TPU v7x, 32 devices: a whole 2x2x4 slice. The times are simulated.
32 devices in a mesh: rep: 2 (over core), shard: 16 (over z, y, x).
Axes of the slice: x: 2, y: 2, z: 4, core: 2. Of those that a mesh axis runs over, the one named last changes fastest.
Arguments:
- content_in: bfloat16 [4, 2048, 768], P('rep', 'shard'), may hold values from -6 to 6
- query_in: bfloat16 [4, 2048, 768], P('rep', 'shard'), may hold values from -6 to 6
- segment_ids: int32 [4, 2048], P('rep', 'shard'), may hold values from 0 to 12, never falling along the last dimension, each value on 1 to 512 neighbouring positions
- parent_ids: int32 [4, 13], P('rep'), may hold values from 0 to 11, as said below
- rank_order: int32 [4, 2048], P('rep', 'shard'), may hold values from 0 to 2047, as said below
- query_flags: int32 [4, 2048], P('rep', 'shard'), may hold values from 0 to 1, as said below
- query_weight: bfloat16 [768, 768], P('shard'), may hold values from -0.21875 to 0.21875
- key_weight: bfloat16 [768, 768], P('shard'), may hold values from -0.21875 to 0.21875
- value_weight: bfloat16 [768, 768], P('shard'), may hold values from -0.21875 to 0.21875
- relative_weight: bfloat16 [768, 768], P('shard'), may hold values from -0.21875 to 0.21875
- output_weight: bfloat16 [768, 768], P('shard'), may hold values from -3 to 3
- inner_weight: bfloat16 [768, 3072], P('shard'), may hold values from -0.21875 to 0.21875
- outer_weight: bfloat16 [3072, 768], P('shard'), may hold values from -0.109375 to 0.109375
- inner_bias: bfloat16 [3072], P('shard'), may hold values from -3 to 3
- outer_bias: bfloat16 [768], P('shard'), may hold values from -2 to 2
- attend_gain: bfloat16 [768], P('shard'), may hold values from 0.5 to 1.5
- attend_shift: bfloat16 [768], P('shard'), may hold values from -2 to 2
- feed_gain: bfloat16 [768], P('shard'), may hold values from 0.5 to 1.5
- feed_shift: bfloat16 [768], P('shard'), may hold values from -2 to 2
- content_bias: bfloat16 [768], P('shard'), may hold values from -3 to 3
- position_bias: bfloat16 [768], P('shard'), may hold values from -3 to 3
- segment_bias: bfloat16 [768], P('shard'), may hold values from -3 to 3
- segment_table: bfloat16 [2, 768], P(None, 'shard'), may hold values from -3 to 3
- content_cot: bfloat16 [4, 2048, 768], P('rep', 'shard'), may hold values from -6 to 6
- query_cot: bfloat16 [4, 2048, 768], P('rep', 'shard'), may hold values from -6 to 6
Outputs:
- content_out: bfloat16 [4, 2048, 768], P('rep', 'shard')
- query_out: bfloat16 [4, 2048, 768], P('rep', 'shard')
- content_grad: bfloat16 [4, 2048, 768], P('rep', 'shard')
- query_grad: bfloat16 [4, 2048, 768], P('rep', 'shard')
- query_weight_grad: float32 [768, 768], P('shard')
- key_weight_grad: float32 [768, 768], P('shard')
- value_weight_grad: float32 [768, 768], P('shard')
- relative_weight_grad: float32 [768, 768], P('shard')
- output_weight_grad: float32 [768, 768], P('shard')
- inner_weight_grad: float32 [768, 3072], P('shard')
- outer_weight_grad: float32 [3072, 768], P('shard')
- inner_bias_grad: float32 [3072], P('shard')
- outer_bias_grad: float32 [768], P('shard')
- attend_gain_grad: float32 [768], P('shard')
- attend_shift_grad: float32 [768], P('shard')
- feed_gain_grad: float32 [768], P('shard')
- feed_shift_grad: float32 [768], P('shard')
- content_bias_grad: float32 [768], P('shard')
- position_bias_grad: float32 [768], P('shard')
- segment_bias_grad: float32 [768], P('shard')
- segment_table_grad: float32 [2, 768], P(None, 'shard')
Inputs may be any that keep to these rules, and one draw needn't show every extreme that they name: `parent_ids`: segment 0 of a tree is its own parent; every other segment's parent is a segment of smaller number; the last segment's parent is the segment before it. `rank_order`: the ranks of one tree are a permutation of 0 to 2047, with rank 0 at position 0. `query_flags`: position 0 of each tree has flag 0.
All inputs are finite; a program needn't handle non-finite values.
Results may differ from a plain program's by a relative error of at most 0.03.
Values may be sent and summed in bfloat16 or wider, within the bound.
No kernel may reach another device: no remote copies, remote signals or barrier semaphores. Data moves between devices by JAX's collectives and lax.ppermute only.
A program may use at most 320 MiB of HBM per device.

v0:
```python
import math

import jax
import jax.numpy as jnp
from jax import lax
from jax.sharding import PartitionSpec as P

H = 12
DH = 64
NS = 13


EPSILON = 1e-05
MASKED = -1e30
HIGHEST = lax.Precision.HIGHEST


def layer_norm(vector, gain_row, shift_row):
    average = jnp.mean(vector, axis=-1, keepdims=True)
    centred = vector - average
    variance = jnp.mean(centred * centred, axis=-1, keepdims=True)
    return centred * lax.rsqrt(variance + EPSILON) * gain_row + shift_row


def gelu_tanh(vector):
    return jax.nn.gelu(vector, approximate=True)


def position_rows(offsets, model_width):
    half_width = model_width // 2
    powers = jnp.arange(half_width, dtype=jnp.float32) * (2.0 / model_width)
    inverse_freq = 1.0 / 10000.0**powers
    angles = offsets[:, None] * inverse_freq[None, :]
    return jnp.concatenate([jnp.sin(angles), jnp.cos(angles)], axis=1)


def skew_rows(full_table, row_count, key_count):
    leading = full_table.shape[0]
    window = row_count + key_count - 1
    flattened = full_table.reshape(leading, row_count * window)
    flattened = lax.slice_in_dim(
        flattened, row_count - 1, row_count - 1 + row_count * (window - 1), axis=1
    )
    return flattened.reshape(leading, row_count, window - 1)[:, :, :key_count]


def unskew_rows(grad_table, row_count, key_count):
    leading = grad_table.shape[0]
    window = row_count + key_count - 1
    padded = jnp.pad(grad_table, ((0, 0), (0, 0), (0, window - 1 - key_count)))
    flattened = padded.reshape(leading, row_count * (window - 1))
    flattened = jnp.pad(flattened, ((0, 0), (row_count - 1, 1)))
    return flattened.reshape(leading, row_count, window)


def ancestry(parents):
    segment_count = parents.shape[0]
    labels = jnp.arange(segment_count, dtype=jnp.int32)
    parent_step = (parents[:, None] == labels[None, :]).astype(jnp.float32)
    reached = jnp.eye(segment_count, dtype=jnp.float32)
    current = reached
    for repeat in range(segment_count - 1):
        current = jnp.dot(current, parent_step, precision=HIGHEST)
        reached = jnp.maximum(reached, current)
    return reached


def guarded(live_block, running):
    result = live_block(running)
    return result


def body(
    content_in,
    query_in,
    segment_ids,
    parent_ids,
    rank_order,
    query_flags,
    query_weight,
    key_weight,
    value_weight,
    relative_weight,
    output_weight,
    inner_weight,
    outer_weight,
    inner_bias,
    outer_bias,
    attend_gain,
    attend_shift,
    feed_gain,
    feed_shift,
    content_bias,
    position_bias,
    segment_bias,
    segment_table,
    content_cot,
    query_cot,
):
    micro_count = content_in.shape[0]
    row_count = content_in.shape[1]
    model_width = content_in.shape[2]
    ff_width = inner_weight.shape[1]
    length = row_count * lax.axis_size("shard")
    key_block = math.gcd(length, 512)
    block_count = length // key_block
    window = row_count + key_block - 1
    score_scale = DH ** (-0.5)
    first_row = lax.axis_index("shard") * row_count
    segment_range = jnp.arange(NS, dtype=jnp.int32)

    def gather_weights():
        return (
            lax.all_gather(query_weight, "shard", axis=0, tiled=True),
            lax.all_gather(key_weight, "shard", axis=0, tiled=True),
            lax.all_gather(value_weight, "shard", axis=0, tiled=True),
            lax.all_gather(relative_weight, "shard", axis=0, tiled=True),
            lax.all_gather(output_weight, "shard", axis=0, tiled=True),
            lax.all_gather(inner_weight, "shard", axis=0, tiled=True),
            lax.all_gather(outer_weight, "shard", axis=0, tiled=True),
            lax.all_gather(inner_bias, "shard", axis=0, tiled=True),
            lax.all_gather(outer_bias, "shard", axis=0, tiled=True),
            lax.all_gather(attend_gain, "shard", axis=0, tiled=True),
            lax.all_gather(attend_shift, "shard", axis=0, tiled=True),
            lax.all_gather(feed_gain, "shard", axis=0, tiled=True),
            lax.all_gather(feed_shift, "shard", axis=0, tiled=True),
            lax.all_gather(content_bias, "shard", axis=0, tiled=True),
            lax.all_gather(position_bias, "shard", axis=0, tiled=True),
            lax.all_gather(segment_bias, "shard", axis=0, tiled=True),
            lax.all_gather(segment_table, "shard", axis=1, tiled=True),
        )

    tree_segments, tree_ranks = (
        lax.all_gather(segment_ids, "shard", axis=1, tiled=True),
        lax.all_gather(rank_order, "shard", axis=1, tiled=True),
    )
    offsets = (first_row + row_count - 1 - jnp.arange(length + row_count, dtype=jnp.int32)).astype(
        jnp.float32
    )
    position_bf = position_rows(offsets, model_width).astype(jnp.bfloat16)
    shapes = [(model_width, model_width)] * 5 + [
        (model_width, ff_width),
        (ff_width, model_width),
        (ff_width,),
    ]
    shapes = shapes + [(model_width,)] * 8 + [(2, model_width)]
    gradients = [jnp.zeros(shape_item, jnp.float32) for shape_item in shapes]
    relative_grad = jnp.zeros((length + row_count, model_width), jnp.float32)
    relative_table = None
    content_outs = []
    query_outs = []
    content_grads = []
    query_grads = []
    for micro_index in range(micro_count):
        gathered = gather_weights()
        (
            query_full,
            key_full,
            value_full,
            relative_full,
            output_full,
            inner_full,
            outer_full,
            inner_shift,
            outer_shift,
            norm_gain,
            norm_shift,
            final_gain,
            final_shift,
            content_shift,
            position_shift,
            segment_shift,
            segment_full,
        ) = gathered
        if micro_index == 0:
            relative_table = jnp.dot(
                position_bf, relative_full, preferred_element_type=jnp.float32
            ).astype(jnp.bfloat16)
        own_content = content_in[micro_index]
        inputs = jnp.concatenate([own_content, query_in[micro_index]], axis=0)
        queries = jnp.dot(inputs, query_full, preferred_element_type=jnp.float32).reshape(
            2, row_count, H, DH
        )
        key_own = jnp.dot(own_content, key_full, preferred_element_type=jnp.float32).astype(
            jnp.bfloat16
        )
        value_own = jnp.dot(own_content, value_full, preferred_element_type=jnp.float32).astype(
            jnp.bfloat16
        )
        keys, values = (
            lax.all_gather(key_own, "shard", axis=0, tiled=True),
            lax.all_gather(value_own, "shard", axis=0, tiled=True),
        )
        query_plain = (queries + content_shift.astype(jnp.float32).reshape(H, DH)).astype(
            jnp.bfloat16
        )
        query_place = (queries + position_shift.astype(jnp.float32).reshape(H, DH)).astype(
            jnp.bfloat16
        )
        query_label = queries + segment_shift.astype(jnp.float32).reshape(H, DH)
        label_table = segment_full.astype(jnp.float32).reshape(2, H, DH)
        label_terms = jnp.einsum("sqhd,thd->sthq", query_label, label_table, precision=HIGHEST)
        row_segments = segment_ids[micro_index]
        row_ranks = rank_order[micro_index]
        limits = jnp.stack([row_ranks, row_ranks - query_flags[micro_index]])
        key_labels = tree_segments[micro_index]
        key_orders = tree_ranks[micro_index]
        reached = ancestry(parent_ids[micro_index])
        row_hot = (row_segments[:, None] == segment_range[None, :]).astype(jnp.float32)
        path_rows = jnp.dot(row_hot, reached, precision=HIGHEST)

        def block_masks(key_start):
            label_block = lax.dynamic_slice_in_dim(key_labels, key_start, key_block)
            order_block = lax.dynamic_slice_in_dim(key_orders, key_start, key_block)
            key_hot = (label_block[:, None] == segment_range[None, :]).astype(jnp.float32)
            on_path = jnp.dot(path_rows, key_hot.T, precision=HIGHEST) > 0.5
            allowed = on_path[None] & (order_block[None, None, :] <= limits[:, :, None])
            same_label = row_segments[:, None] == label_block[None, :]
            return (allowed, same_label)

        def block_scores(key_start, same_label):
            key_heads = lax.dynamic_slice_in_dim(keys, key_start, key_block).reshape(
                key_block, H, DH
            )
            place_heads = lax.dynamic_slice_in_dim(relative_table, key_start, window).reshape(
                window, H, DH
            )
            content_part = jnp.einsum(
                "sqhd,khd->shqk", query_plain, key_heads, preferred_element_type=jnp.float32
            )
            full_part = jnp.einsum(
                "sqhd,chd->shqc", query_place, place_heads, preferred_element_type=jnp.float32
            )
            shifted = skew_rows(
                full_part.reshape(2 * H, row_count, window), row_count, key_block
            ).reshape(2, H, row_count, key_block)
            label_part = jnp.where(
                same_label[None, None], label_terms[:, 0][..., None], label_terms[:, 1][..., None]
            )
            return (content_part + shifted + label_part) * score_scale

        def stats_step(step_index, running):
            key_start = step_index * key_block
            allowed, same_label = block_masks(key_start)

            def live_block(state_in):
                maxima, totals = state_in
                scores = jnp.where(allowed[:, None], block_scores(key_start, same_label), MASKED)
                new_maxima = jnp.maximum(maxima, jnp.max(scores, axis=-1))
                weights_exp = jnp.where(
                    allowed[:, None], jnp.exp(scores - new_maxima[..., None]), 0.0
                )
                return (
                    new_maxima,
                    totals * jnp.exp(maxima - new_maxima) + jnp.sum(weights_exp, axis=-1),
                )

            return guarded(live_block, running)

        start_stats = (
            jnp.full((2, H, row_count), MASKED, jnp.float32),
            jnp.zeros((2, H, row_count), jnp.float32),
        )
        maxima, totals = lax.fori_loop(0, block_count, stats_step, start_stats)
        log_totals = maxima + jnp.log(totals)

        def mix_step(step_index, running):
            key_start = step_index * key_block
            allowed, same_label = block_masks(key_start)

            def live_block(state_in):
                value_heads = lax.dynamic_slice_in_dim(values, key_start, key_block).reshape(
                    key_block, H, DH
                )
                attention = jnp.where(
                    allowed[:, None],
                    jnp.exp(block_scores(key_start, same_label) - log_totals[..., None]),
                    0.0,
                )
                return state_in + jnp.einsum(
                    "shqk,khd->sqhd",
                    attention.astype(jnp.bfloat16),
                    value_heads,
                    preferred_element_type=jnp.float32,
                )

            return guarded(live_block, running)

        mixed = lax.fori_loop(
            0, block_count, mix_step, jnp.zeros((2, row_count, H, DH), jnp.float32)
        )
        mixed_bf = mixed.reshape(2 * row_count, model_width).astype(jnp.bfloat16)
        attended = jnp.dot(mixed_bf, output_full, preferred_element_type=jnp.float32)
        residual = attended + inputs.astype(jnp.float32)
        gain_one = norm_gain.astype(jnp.float32)
        shift_one = norm_shift.astype(jnp.float32)
        gain_two = final_gain.astype(jnp.float32)
        shift_two = final_shift.astype(jnp.float32)
        normed = layer_norm(residual, gain_one, shift_one)
        normed_bf = normed.astype(jnp.bfloat16)
        inner_pre = jnp.dot(
            normed_bf, inner_full, preferred_element_type=jnp.float32
        ) + inner_shift.astype(jnp.float32)
        hidden_bf = gelu_tanh(inner_pre).astype(jnp.bfloat16)
        summed = (
            jnp.dot(hidden_bf, outer_full, preferred_element_type=jnp.float32)
            + outer_shift.astype(jnp.float32)
            + normed
        )
        result = layer_norm(summed, gain_two, shift_two)
        content_outs.append(result[:row_count].astype(jnp.bfloat16))
        query_outs.append(result[row_count:].astype(jnp.bfloat16))
        back_weights = gather_weights()
        back_keys, back_values = (
            lax.all_gather(key_own, "shard", axis=0, tiled=True),
            lax.all_gather(value_own, "shard", axis=0, tiled=True),
        )
        keys, values = (back_keys, back_values)
        (
            query_full,
            key_full,
            value_full,
            relative_full,
            output_full,
            inner_full,
            outer_full,
            inner_shift,
            outer_shift,
            norm_gain,
            norm_shift,
            final_gain,
            final_shift,
            content_shift,
            position_shift,
            segment_shift,
            segment_full,
        ) = back_weights
        cotangent = jnp.concatenate(
            [content_cot[micro_index], query_cot[micro_index]], axis=0
        ).astype(jnp.float32)
        unused, final_back = jax.vjp(layer_norm, summed, gain_two, shift_two)
        grad_summed, grad_final_gain, grad_final_shift = final_back(cotangent)
        grad_summed_bf = grad_summed.astype(jnp.bfloat16)
        grad_outer = jnp.dot(hidden_bf.T, grad_summed_bf, preferred_element_type=jnp.float32)
        grad_hidden = jnp.dot(grad_summed_bf, outer_full.T, preferred_element_type=jnp.float32)
        unused, gelu_back = jax.vjp(gelu_tanh, inner_pre)
        (grad_inner,) = gelu_back(grad_hidden)
        grad_inner_bf = grad_inner.astype(jnp.bfloat16)
        grad_inner_weight = jnp.dot(normed_bf.T, grad_inner_bf, preferred_element_type=jnp.float32)
        grad_normed = (
            jnp.dot(grad_inner_bf, inner_full.T, preferred_element_type=jnp.float32) + grad_summed
        )
        unused, first_back = jax.vjp(layer_norm, residual, gain_one, shift_one)
        grad_residual, grad_norm_gain, grad_norm_shift = first_back(grad_normed)
        grad_residual_bf = grad_residual.astype(jnp.bfloat16)
        grad_output = jnp.dot(mixed_bf.T, grad_residual_bf, preferred_element_type=jnp.float32)
        grad_mixed = jnp.dot(grad_residual_bf, output_full.T, preferred_element_type=jnp.float32)
        grad_mixed = grad_mixed.astype(jnp.bfloat16).reshape(2, row_count, H, DH)
        row_delta = jnp.einsum(
            "sqhd,sqhd->shq", grad_mixed.astype(jnp.float32), mixed, precision=HIGHEST
        )

        def back_step(step_index, running):
            key_start = step_index * key_block
            allowed, same_label = block_masks(key_start)

            def live_block(state_in):
                grad_plain, grad_place, grad_label, grad_keys, grad_values, grad_window_all = (
                    state_in
                )
                key_heads = lax.dynamic_slice_in_dim(keys, key_start, key_block).reshape(
                    key_block, H, DH
                )
                value_heads = lax.dynamic_slice_in_dim(values, key_start, key_block).reshape(
                    key_block, H, DH
                )
                place_heads = lax.dynamic_slice_in_dim(relative_table, key_start, window).reshape(
                    window, H, DH
                )
                scores = block_scores(key_start, same_label)
                attention = jnp.where(
                    allowed[:, None], jnp.exp(scores - log_totals[..., None]), 0.0
                )
                grad_attention = jnp.einsum(
                    "sqhd,khd->shqk", grad_mixed, value_heads, preferred_element_type=jnp.float32
                )
                grad_scores = (attention * (grad_attention - row_delta[..., None])).astype(
                    jnp.bfloat16
                )
                grad_plain = grad_plain + jnp.einsum(
                    "shqk,khd->sqhd", grad_scores, key_heads, preferred_element_type=jnp.float32
                )
                grad_key_heads = jnp.einsum(
                    "shqk,sqhd->khd", grad_scores, query_plain, preferred_element_type=jnp.float32
                )
                grad_full = unskew_rows(
                    grad_scores.reshape(2 * H, row_count, key_block), row_count, key_block
                ).reshape(2, H, row_count, window)
                grad_place = grad_place + jnp.einsum(
                    "shqc,chd->sqhd", grad_full, place_heads, preferred_element_type=jnp.float32
                )
                grad_window = jnp.einsum(
                    "shqc,sqhd->chd", grad_full, query_place, preferred_element_type=jnp.float32
                ).reshape(window, model_width)
                old_window = lax.dynamic_slice_in_dim(grad_window_all, key_start, window)
                grad_window_all = lax.dynamic_update_slice_in_dim(
                    grad_window_all, old_window + grad_window * score_scale, key_start, 0
                )
                grad_wide = grad_scores.astype(jnp.float32)
                same_sum = jnp.sum(jnp.where(same_label[None, None], grad_wide, 0.0), axis=-1)
                other_sum = jnp.sum(jnp.where(same_label[None, None], 0.0, grad_wide), axis=-1)
                grad_label = grad_label + jnp.stack([same_sum, other_sum], axis=1)
                grad_value_heads = jnp.einsum(
                    "shqk,sqhd->khd",
                    attention.astype(jnp.bfloat16),
                    grad_mixed,
                    preferred_element_type=jnp.float32,
                )
                grad_keys = lax.dynamic_update_slice_in_dim(
                    grad_keys,
                    (grad_key_heads * score_scale).reshape(key_block, model_width),
                    key_start,
                    0,
                )
                grad_values = lax.dynamic_update_slice_in_dim(
                    grad_values, grad_value_heads.reshape(key_block, model_width), key_start, 0
                )
                return (grad_plain, grad_place, grad_label, grad_keys, grad_values, grad_window_all)

            return guarded(live_block, running)

        start_back = (
            jnp.zeros((2, row_count, H, DH), jnp.float32),
            jnp.zeros((2, row_count, H, DH), jnp.float32),
            jnp.zeros((2, 2, H, row_count), jnp.float32),
            jnp.zeros((length, model_width), jnp.float32),
            jnp.zeros((length, model_width), jnp.float32),
            relative_grad,
        )
        grad_plain, grad_place, grad_label, grad_keys, grad_values, relative_grad = lax.fori_loop(
            0, block_count, back_step, start_back
        )
        grad_plain = grad_plain * score_scale
        grad_place = grad_place * score_scale
        grad_label = grad_label * score_scale
        grad_through_label = jnp.einsum(
            "sthq,thd->sqhd", grad_label, label_table, precision=HIGHEST
        )
        grad_table = jnp.einsum(
            "sthq,sqhd->thd", grad_label, query_label, precision=HIGHEST
        ).reshape(2, model_width)
        grad_query = (grad_plain + grad_place + grad_through_label).reshape(
            2 * row_count, model_width
        )
        grad_query_bf = grad_query.astype(jnp.bfloat16)
        grad_query_weight = jnp.dot(inputs.T, grad_query_bf, preferred_element_type=jnp.float32)
        grad_inputs = (
            jnp.dot(grad_query_bf, query_full.T, preferred_element_type=jnp.float32) + grad_residual
        )
        own_keys, own_values = (
            lax.psum_scatter(
                grad_keys.astype(jnp.bfloat16), "shard", scatter_dimension=0, tiled=True
            ).astype(jnp.float32),
            lax.psum_scatter(
                grad_values.astype(jnp.bfloat16), "shard", scatter_dimension=0, tiled=True
            ).astype(jnp.float32),
        )
        own_keys_bf = own_keys.astype(jnp.bfloat16)
        own_values_bf = own_values.astype(jnp.bfloat16)
        grad_key_weight = jnp.dot(own_content.T, own_keys_bf, preferred_element_type=jnp.float32)
        grad_value_weight = jnp.dot(
            own_content.T, own_values_bf, preferred_element_type=jnp.float32
        )
        grad_content = (
            grad_inputs[:row_count]
            + jnp.dot(own_keys_bf, key_full.T, preferred_element_type=jnp.float32)
            + jnp.dot(own_values_bf, value_full.T, preferred_element_type=jnp.float32)
        )
        content_grads.append(grad_content.astype(jnp.bfloat16))
        query_grads.append(grad_inputs[row_count:].astype(jnp.bfloat16))
        terms = [
            grad_query_weight,
            grad_key_weight,
            grad_value_weight,
            jnp.zeros_like(gradients[3]),
            grad_output,
            grad_inner_weight,
            grad_outer,
            jnp.sum(grad_inner, axis=0),
            jnp.sum(grad_summed, axis=0),
            grad_norm_gain,
            grad_norm_shift,
            grad_final_gain,
            grad_final_shift,
            jnp.sum(grad_plain.reshape(2 * row_count, model_width), axis=0),
            jnp.sum(grad_place.reshape(2 * row_count, model_width), axis=0),
            jnp.sum(grad_through_label.reshape(2 * row_count, model_width), axis=0),
            grad_table,
        ]
        gradients = [earlier + latest for earlier, latest in zip(gradients, terms)]
    gradients[3] = jnp.dot(position_bf.astype(jnp.float32).T, relative_grad, precision=HIGHEST)
    owned = (
        lax.psum_scatter(
            gradients[0].astype(jnp.bfloat16), "shard", scatter_dimension=0, tiled=True
        ).astype(jnp.float32),
        lax.psum_scatter(
            gradients[1].astype(jnp.bfloat16), "shard", scatter_dimension=0, tiled=True
        ).astype(jnp.float32),
        lax.psum_scatter(
            gradients[2].astype(jnp.bfloat16), "shard", scatter_dimension=0, tiled=True
        ).astype(jnp.float32),
        lax.psum_scatter(
            gradients[3].astype(jnp.bfloat16), "shard", scatter_dimension=0, tiled=True
        ).astype(jnp.float32),
        lax.psum_scatter(
            gradients[4].astype(jnp.bfloat16), "shard", scatter_dimension=0, tiled=True
        ).astype(jnp.float32),
        lax.psum_scatter(
            gradients[5].astype(jnp.bfloat16), "shard", scatter_dimension=0, tiled=True
        ).astype(jnp.float32),
        lax.psum_scatter(
            gradients[6].astype(jnp.bfloat16), "shard", scatter_dimension=0, tiled=True
        ).astype(jnp.float32),
        lax.psum_scatter(
            gradients[7].astype(jnp.bfloat16), "shard", scatter_dimension=0, tiled=True
        ).astype(jnp.float32),
        lax.psum_scatter(
            gradients[8].astype(jnp.bfloat16), "shard", scatter_dimension=0, tiled=True
        ).astype(jnp.float32),
        lax.psum_scatter(
            gradients[9].astype(jnp.bfloat16), "shard", scatter_dimension=0, tiled=True
        ).astype(jnp.float32),
        lax.psum_scatter(
            gradients[10].astype(jnp.bfloat16), "shard", scatter_dimension=0, tiled=True
        ).astype(jnp.float32),
        lax.psum_scatter(
            gradients[11].astype(jnp.bfloat16), "shard", scatter_dimension=0, tiled=True
        ).astype(jnp.float32),
        lax.psum_scatter(
            gradients[12].astype(jnp.bfloat16), "shard", scatter_dimension=0, tiled=True
        ).astype(jnp.float32),
        lax.psum_scatter(
            gradients[13].astype(jnp.bfloat16), "shard", scatter_dimension=0, tiled=True
        ).astype(jnp.float32),
        lax.psum_scatter(
            gradients[14].astype(jnp.bfloat16), "shard", scatter_dimension=0, tiled=True
        ).astype(jnp.float32),
        lax.psum_scatter(
            gradients[15].astype(jnp.bfloat16), "shard", scatter_dimension=0, tiled=True
        ).astype(jnp.float32),
        lax.psum_scatter(
            gradients[16].astype(jnp.bfloat16), "shard", scatter_dimension=1, tiled=True
        ).astype(jnp.float32),
    )
    totals_all = (
        lax.psum(owned[0].astype(jnp.bfloat16), "rep").astype(jnp.float32),
        lax.psum(owned[1].astype(jnp.bfloat16), "rep").astype(jnp.float32),
        lax.psum(owned[2].astype(jnp.bfloat16), "rep").astype(jnp.float32),
        lax.psum(owned[3].astype(jnp.bfloat16), "rep").astype(jnp.float32),
        lax.psum(owned[4].astype(jnp.bfloat16), "rep").astype(jnp.float32),
        lax.psum(owned[5].astype(jnp.bfloat16), "rep").astype(jnp.float32),
        lax.psum(owned[6].astype(jnp.bfloat16), "rep").astype(jnp.float32),
        lax.psum(owned[7].astype(jnp.bfloat16), "rep").astype(jnp.float32),
        lax.psum(owned[8].astype(jnp.bfloat16), "rep").astype(jnp.float32),
        lax.psum(owned[9].astype(jnp.bfloat16), "rep").astype(jnp.float32),
        lax.psum(owned[10].astype(jnp.bfloat16), "rep").astype(jnp.float32),
        lax.psum(owned[11].astype(jnp.bfloat16), "rep").astype(jnp.float32),
        lax.psum(owned[12].astype(jnp.bfloat16), "rep").astype(jnp.float32),
        lax.psum(owned[13].astype(jnp.bfloat16), "rep").astype(jnp.float32),
        lax.psum(owned[14].astype(jnp.bfloat16), "rep").astype(jnp.float32),
        lax.psum(owned[15].astype(jnp.bfloat16), "rep").astype(jnp.float32),
        lax.psum(owned[16].astype(jnp.bfloat16), "rep").astype(jnp.float32),
    )
    return (
        jnp.stack(content_outs),
        jnp.stack(query_outs),
        jnp.stack(content_grads),
        jnp.stack(query_grads),
        totals_all[0],
        totals_all[1],
        totals_all[2],
        totals_all[3],
        totals_all[4],
        totals_all[5],
        totals_all[6],
        totals_all[7],
        totals_all[8],
        totals_all[9],
        totals_all[10],
        totals_all[11],
        totals_all[12],
        totals_all[13],
        totals_all[14],
        totals_all[15],
        totals_all[16],
    )


def solution(mesh):
    in_specs = (
        P("rep", "shard", None),
        P("rep", "shard", None),
        P("rep", "shard"),
        P("rep", None),
        P("rep", "shard"),
        P("rep", "shard"),
        P("shard", None),
        P("shard", None),
        P("shard", None),
        P("shard", None),
        P("shard", None),
        P("shard", None),
        P("shard", None),
        P("shard"),
        P("shard"),
        P("shard"),
        P("shard"),
        P("shard"),
        P("shard"),
        P("shard"),
        P("shard"),
        P("shard"),
        P(None, "shard"),
        P("rep", "shard", None),
        P("rep", "shard", None),
    )
    out_specs = (
        P("rep", "shard", None),
        P("rep", "shard", None),
        P("rep", "shard", None),
        P("rep", "shard", None),
        P("shard", None),
        P("shard", None),
        P("shard", None),
        P("shard", None),
        P("shard", None),
        P("shard", None),
        P("shard", None),
        P("shard"),
        P("shard"),
        P("shard"),
        P("shard"),
        P("shard"),
        P("shard"),
        P("shard"),
        P("shard"),
        P("shard"),
        P(None, "shard"),
    )
    return jax.shard_map(body, mesh=mesh, in_specs=in_specs, out_specs=out_specs, check_vma=False)
```

profile of v0, /device:TPU:9, one launch (start us, length us, event | category | flops | bytes accessed | tf_op | source)
XLA Modules:
  0.0 4223.0 jit_solution(759177239464165868)
XLA Ops:
  10.0 55.9 %all-gather.17.cloned.1.call-done = bf16[768,768]{1,0:T(8,128)(2,1)} async-done(((bf16[48,768]{1,0:T(8,128)(2,1)}), bf16[768,768]{1,0:T(8,128)(2,1)}) %all-gather.17.cloned.1.call-update) | async-done | bytes 1179664 | tf_op jit(solution)/shard_map/all_gather | solution.py:115
  71.0 52.7 %all-gather.13.cloned.1.call-done = bf16[768,768]{1,0:T(8,128)(2,1)} async-done(((bf16[48,768]{1,0:T(8,128)(2,1)}), bf16[768,768]{1,0:T(8,128)(2,1)}) %all-gather.13.cloned.1.call-update) | async-done | bytes 1179664 | tf_op jit(solution)/shard_map/all_gather | solution.py:116
  131.3 26.0 all_gather.48
  159.4 28.8 all_gather.49
  190.1 59.8 %all-reduce.23 = (bf16[768]{0:T(1024)(128)(2,1)S(1)}, bf16[768]{0:T(1024)(128)(2,1)S(1)}, bf16[768]{0:T(1024)(128)(2,1)S(1)}, bf16[3072]{0:T(1024)(128)(2,1)S(1)...) all-reduce(bf16[768]{0:T(1024)(128)(2,1)S(1)} %dynamic-update-slice, ...), channel_id=1, replica_groups=mesh['rep'=2,'shard'=16] {'shard'}, use_global_device_ids=true, to_apply=%add.4 | all-reduce | flops 8448 | bytes 33792
  257.2 29.4 all-gather
  294.2 14.3 fusion.104
  339.7 285.8 %while.114 = (s32[]{:T(128)}, f32[2,12,128]{2,0,1:T(2,128)}, f32[2,12,128]{2,0,1:T(2,128)}, s32[2048]{0:T(1024)}, f32[128,13]{0,1:T(8,128)S(1)}, /*index=5*/s32[...) while((s32[]{:T(128)}, f32[2,12,128]{2,0,1:T(2,128)}, ...), condition=%wide.region_13.14_spmd.clone, body=%wide.region_10.0_spmd.clone.sunk | while | flops 477386240 | bytes 123385760 | solution.py:264
  377.8 12.3 reshape.1061
  448.1 12.3 reshape.1061
  519.8 12.3 reshape.1061
  591.4 12.3 reshape.1061
  630.3 286.0 %while.112 = (s32[]{:T(128)}, f32[2,12,128]{2,0,1:T(2,128)S(1)}, f32[2,12,128]{2,0,1:T(2,128)}, s32[2048]{0:T(1024)}, f32[128,13]{0,1:T(8,128)}, /*index=5*/s32[...) while((s32[]{:T(128)}, f32[2,12,128]{2,0,1:T(2,128)S(1)}, ...), condition=%wide.region_3.4_spmd.clone, body=%wide.region_0.3_spmd.clone.sunk | while | flops 477386240 | bytes 123332448 | solution.py:264
  669.6 12.4 reshape.1057
  924.4 285.0 %while.115 = (s32[]{:T(128)}, f32[2,128,12,64]{1,3,0,2:T(8,128)}, bf16[2048,768]{0,1:T(8,128)(2,1)}, s32[2048]{0:T(1024)}, f32[128,13]{0,1:T(8,128)S(1)}, /*inde...) while((s32[]{:T(128)}, f32[2,128,12,64]{1,3,0,2:T(8,128)}, ...), condition=%wide.region_15.16_spmd.clone, body=%wide.region_14.15_spmd.clone.sunk | while | flops 675944960 | bytes 130158536 | solution.py:289
  1216.5 287.3 %while.113 = (s32[]{:T(128)}, f32[2,128,12,64]{1,3,0,2:T(8,128)}, bf16[2048,768]{0,1:T(8,128)(2,1)}, s32[2048]{0:T(1024)}, f32[128,13]{0,1:T(8,128)}, /*index=5*...) while((s32[]{:T(128)}, f32[2,128,12,64]{1,3,0,2:T(8,128)}, ...), condition=%wide.region_5.6_spmd.clone, body=%wide.region_4.5_spmd.clone.sunk | while | flops 675944960 | bytes 130131872 | solution.py:289
  1575.8 559.1 %while.116 = (s32[]{:T(128)}, f32[2,128,12,64]{1,3,0,2:T(8,128)}, f32[2,128,12,64]{1,3,0,2:T(8,128)}, f32[2,2,12,128]{3,0,2,1:T(2,128)}, bf16[2048,768]{0,1:T(8,...) while((s32[]{:T(128)}, f32[2,128,12,64]{1,3,0,2:T(8,128)}, ...), condition=%wide.region_27.28_spmd.clone, body=%wide.region_24.0_spmd.clone.sunk | while | flops 1797211136 | bytes 287206432 | solution.py:440
  2143.8 541.0 %while.117 = (s32[]{:T(128)}, f32[2,128,12,64]{1,3,0,2:T(8,128)}, f32[2,128,12,64]{1,3,0,2:T(8,128)}, f32[2,2,12,128]{3,0,2,1:T(2,128)}, bf16[2048,768]{0,1:T(8,...) while((s32[]{:T(128)}, f32[2,128,12,64]{1,3,0,2:T(8,128)}, ...), condition=%wide.region_37.38_spmd.clone, body=%wide.region_34.37_spmd.clone.sunk | while | flops 1797211136 | bytes 287206432 | solution.py:440
  2705.4 153.3 %reduce-scatter.41.cloned.1.call-done = bf16[128,768]{1,0:T(8,128)(2,1)} async-done(((bf16[2048,768]{1,0:T(8,128)(2,1)}), bf16[128,768]{1,0:T(8,128)(2,1)}) %reduce-scatter.41.cloned.1.call-update) | async-done | bytes 196624
  2863.6 129.4 %reduce-scatter.39.cloned.1.call-done = bf16[128,768]{1,0:T(8,128)(2,1)} async-done(((bf16[2048,768]{1,0:T(8,128)(2,1)}), bf16[128,768]{1,0:T(8,128)(2,1)}) %reduce-scatter.39.cloned.1.call-update) | async-done | bytes 196624
  2995.8 131.9 %reduce-scatter.43.cloned.1.call-done = bf16[128,768]{1,0:T(8,128)(2,1)} async-done(((bf16[2048,768]{1,0:T(8,128)(2,1)}), bf16[128,768]{1,0:T(8,128)(2,1)}) %reduce-scatter.43.cloned.1.call-update) | async-done | bytes 196624
  3133.9 15.1 fusion.119
  3188.5 55.7 %all-reduce.22 = (bf16[768]{0:T(1024)(128)(2,1)S(1)}, bf16[3072]{0:T(1024)(128)(2,1)S(1)}, bf16[768]{0:T(1024)(128)(2,1)S(1)}, bf16[768]{0:T(1024)(128)(2,1)S(1)...) all-reduce(bf16[768]{0:T(1024)(128)(2,1)} %dynamic-update-slice.8, ...), channel_id=1, replica_groups=mesh['rep'=2,'shard'=16] {'shard'}, use_global_device_ids=true, to_apply=%add.12 | all-reduce | flops 9984 | bytes 39936
  3254.3 18.6 all-reduce.24
  3284.7 96.8 %reduce-scatter.45.cloned.1.call-done = bf16[48,768]{1,0:T(8,128)(2,1)} async-done(((bf16[768,768]{1,0:T(8,128)(2,1)}), bf16[48,768]{1,0:T(8,128)(2,1)}) %reduce-scatter.45.cloned.1.call-update) | async-done | bytes 73744
  3383.2 126.5 %reduce-scatter.47.cloned.1.call-done = bf16[48,768]{1,0:T(8,128)(2,1)} async-done(((bf16[768,768]{1,0:T(8,128)(2,1)}), bf16[48,768]{1,0:T(8,128)(2,1)}) %reduce-scatter.47.cloned.1.call-update) | async-done | bytes 73744
  3511.4 126.5 %reduce-scatter.31.cloned.1.call-done = bf16[48,768]{1,0:T(8,128)(2,1)} async-done(((bf16[768,768]{1,0:T(8,128)(2,1)}), bf16[48,768]{1,0:T(8,128)(2,1)}) %reduce-scatter.31.cloned.1.call-update) | async-done | bytes 73744 | tf_op jit(solution)/shard_map/reduce_scatter | solution.py:515
  3637.9 128.1 %reduce-scatter.29.cloned.1.call-done = bf16[48,768]{1,0:T(8,128)(2,1)} async-done(((bf16[768,768]{1,0:T(8,128)(2,1)}), bf16[48,768]{1,0:T(8,128)(2,1)}) %reduce-scatter.29.cloned.1.call-update) | async-done | bytes 73744 | tf_op jit(solution)/shard_map/reduce_scatter | solution.py:512
  3766.0 128.2 %reduce-scatter.27.cloned.1.call-done = bf16[48,768]{1,0:T(8,128)(2,1)} async-done(((bf16[768,768]{1,0:T(8,128)(2,1)}), bf16[48,768]{1,0:T(8,128)(2,1)}) %reduce-scatter.27.cloned.1.call-update) | async-done | bytes 73744 | tf_op jit(solution)/shard_map/reduce_scatter | solution.py:503
  3894.2 141.9 %reduce-scatter.35.cloned.1.call-done = bf16[192,768]{1,0:T(8,128)(2,1)} async-done(((bf16[3072,768]{1,0:T(8,128)(2,1)}), bf16[192,768]{1,0:T(8,128)(2,1)}) %reduce-scatter.35.cloned.1.call-update) | async-done | bytes 294928 | tf_op jit(solution)/shard_map/reduce_scatter | solution.py:521
  4036.1 142.6 %reduce-scatter.33.cloned.1.call-done = bf16[48,3072]{1,0:T(8,128)(2,1)} async-done(((bf16[768,3072]{1,0:T(8,128)(2,1)}), bf16[48,3072]{1,0:T(8,128)(2,1)}) %reduce-scatter.33.cloned.1.call-update) | async-done | bytes 294928 | tf_op jit(solution)/shard_map/reduce_scatter | solution.py:518
  4183.7 20.5 all-reduce.28.cloned.1.call-done
  (1663 shorter events, 2438.3 us)
Async XLA Ops:
  7.2 58.7 %all-gather.17.cloned.1.call-start = ((), (), s32[]{:S(2)}) async-start(), calls=%async_computation.14 | async-start | bytes 1253376 | tf_op jit(solution)/shard_map/all_gather | solution.py:115
  7.9 115.9 %all-gather.13.cloned.1.call-start = ((), (), s32[]{:S(2)}) async-start(), calls=%async_computation.12 | async-start | bytes 1253376 | tf_op jit(solution)/shard_map/all_gather | solution.py:116
  8.7 299.9 %all-gather.21.cloned.1.call-start = ((), (), s32[]{:S(2)}) async-start(), calls=%async_computation.16 | async-start | bytes 1253376 | tf_op jit(solution)/shard_map/all_gather | solution.py:114
  9.4 315.8 %all-gather.23.cloned.1.call-start = ((), (), s32[]{:S(2)}) async-start(), calls=%async_computation.17 | async-start | bytes 1253376 | tf_op jit(solution)/shard_map/all_gather | solution.py:117
  10.0 325.0 %all-gather.33.cloned.1.call-start = ((), (), s32[]{:S(2)}) async-start(), calls=%async_computation.22 | async-start | bytes 3342336 | tf_op jit(solution)/shard_map/all_gather | solution.py:191
  68.5 557.1 %all-gather.19.cloned.1.call-start = ((), (), s32[]{:S(2)}) async-start(), calls=%async_computation.15 | async-start | bytes 3342336 | tf_op jit(solution)/shard_map/all_gather | solution.py:191
  71.0 186.2 %copy-start.194 = (bf16[2,48]{1,0:T(2,128)(2,1)S(1)}, bf16[2,48]{1,0:T(2,128)(2,1)}, u32[]{:S(2)}) copy-start(bf16[2,48]{1,0:T(2,128)(2,1)} %param.59) | copy-start | bytes 580
  71.0 848.6 %all-gather.31.cloned.1.call-start = ((), (), s32[]{:S(2)}) async-start(), calls=%async_computation.21 | async-start | bytes 3342336 | tf_op jit(solution)/shard_map/all_gather | solution.py:192
  126.1 165.9 %copy-start.130 = (bf16[2,128,768]{2,1,0:T(8,128)(2,1)S(1)}, bf16[2,128,768]{2,1,0:T(8,128)(2,1)}, u32[]{:S(2)}) copy-start(bf16[2,128,768]{2,1,0:T(8,128)(2,1)} %param.60) | copy-start | bytes 1179652
  126.1 166.7 %copy-start.131 = (bf16[2,128,768]{2,1,0:T(8,128)(2,1)S(1)}, bf16[2,128,768]{2,1,0:T(8,128)(2,1)}, u32[]{:S(2)}) copy-start(bf16[2,128,768]{2,1,0:T(8,128)(2,1)} %param.61) | copy-start | bytes 1179652
  126.1 1085.6 %all-gather.15.cloned.1.call-start = ((), (), s32[]{:S(2)}) async-start(), calls=%async_computation.13 | async-start | bytes 3342336 | tf_op jit(solution)/shard_map/all_gather | solution.py:192
  128.6 1377.6 %all-gather.25.cloned.1.call-start = ((), (), s32[]{:S(2)}) async-start(), calls=%async_computation.18 | async-start | bytes 1253376 | tf_op jit(solution)/shard_map/all_gather | solution.py:118
  129.3 1381.8 %all-gather.27.cloned.1.call-start = ((), (), s32[]{:S(2)}) async-start(), calls=%async_computation.19 | async-start | bytes 5013504 | tf_op jit(solution)/shard_map/all_gather | solution.py:119
  129.9 1386.9 %all-gather.29.cloned.1.call-start = ((), (), s32[]{:S(2)}) async-start(), calls=%async_computation.20 | async-start | bytes 5013504 | tf_op jit(solution)/shard_map/all_gather | solution.py:120
  130.6 2573.3 %reduce-scatter.37.cloned.1.call-start = ((), (), s32[]{:S(2)}) async-start(), calls=%async_computation.28 | async-start | bytes 3342336
  2139.6 719.1 %reduce-scatter.41.cloned.1.call-start = ((), (), s32[]{:S(2)}) async-start(), calls=%async_computation.30 | async-start | bytes 3342336
  2689.5 303.5 %reduce-scatter.39.cloned.1.call-start = ((), (), s32[]{:S(2)}) async-start(), calls=%async_computation.29 | async-start | bytes 3342336
  2694.2 433.5 %reduce-scatter.43.cloned.1.call-start = ((), (), s32[]{:S(2)}) async-start(), calls=%async_computation.31 | async-start | bytes 3342336
  2698.9 554.5 %reduce-scatter.49.cloned.1.call-start = ((), (), s32[]{:S(2)}) async-start(), calls=%async_computation.34 | async-start | bytes 208896
  2703.9 677.6 %reduce-scatter.45.cloned.1.call-start = ((), (), s32[]{:S(2)}) async-start(), calls=%async_computation.32 | async-start | bytes 1253376
  2863.5 646.2 %reduce-scatter.47.cloned.1.call-start = ((), (), s32[]{:S(2)}) async-start(), calls=%async_computation.33 | async-start | bytes 1253376
  3131.5 506.4 %reduce-scatter.31.cloned.1.call-start = ((), (), s32[]{:S(2)}) async-start(), calls=%async_computation.25 | async-start | bytes 1253376 | tf_op jit(solution)/shard_map/reduce_scatter | solution.py:515
  3133.8 632.2 %reduce-scatter.29.cloned.1.call-start = ((), (), s32[]{:S(2)}) async-start(), calls=%async_computation.24 | async-start | bytes 1253376 | tf_op jit(solution)/shard_map/reduce_scatter | solution.py:512
  3149.0 745.2 %reduce-scatter.27.cloned.1.call-start = ((), (), s32[]{:S(2)}) async-start(), calls=%async_computation.23 | async-start | bytes 1253376 | tf_op jit(solution)/shard_map/reduce_scatter | solution.py:503
  3157.5 878.6 %reduce-scatter.35.cloned.1.call-start = ((), (), s32[]{:S(2)}) async-start(), calls=%async_computation.27 | async-start | bytes 5013504 | tf_op jit(solution)/shard_map/reduce_scatter | solution.py:521
  3166.0 1012.7 %reduce-scatter.33.cloned.1.call-start = ((), (), s32[]{:S(2)}) async-start(), calls=%async_computation.26 | async-start | bytes 5013504 | tf_op jit(solution)/shard_map/reduce_scatter | solution.py:518
  3174.1 1030.1 %all-reduce.28.cloned.1.call-start = ((), (), s32[]{:S(2)}) async-start(), calls=%async_computation.35 | async-start | bytes 2408448 | tf_op jit(solution)/shard_map/psum | solution.py:557
  3251.5 927.3 %copy-start.45 = (bf16[768,768]{1,0:T(8,128)(2,1)S(1)}, bf16[768,768]{1,0:T(8,128)(2,1)}, u32[]{:S(2)}) copy-start(bf16[768,768]{1,0:T(8,128)(2,1)} %all-gather.17.cloned.1.call-done) | copy-start | bytes 3538948
  3251.5 927.3 %copy-start.123 = (bf16[128,768]{1,0:T(8,128)(2,1)S(1)}, bf16[128,768]{1,0:T(8,128)(2,1)}, u32[]{:S(2)}) copy-start(bf16[128,768]{1,0:T(8,128)(2,1)} %reduce-scatter.41.cloned.1.call-done) | copy-start | bytes 589828
  3251.8 928.5 %copy-start.48 = (bf16[768,768]{1,0:T(8,128)(2,1)S(1)}, bf16[768,768]{1,0:T(8,128)(2,1)}, u32[]{:S(2)}) copy-start(bf16[768,768]{1,0:T(8,128)(2,1)} %all-gather.13.cloned.1.call-done) | copy-start | bytes 3538948
  3253.5 928.3 %copy-start.89 = (f32[256,768]{1,0:T(8,128)S(1)}, f32[256,768]{1,0:T(8,128)}, u32[]{:S(2)}) copy-start(f32[256,768]{1,0:T(8,128)} %copy-done.88) | copy-start | bytes 2359300
  3253.5 928.3 %copy-start.122 = (bf16[128,768]{1,0:T(8,128)(2,1)S(1)}, bf16[128,768]{1,0:T(8,128)(2,1)}, u32[]{:S(2)}) copy-start(bf16[128,768]{1,0:T(8,128)(2,1)} %reduce-scatter.37.cloned.1.call-done) | copy-start | bytes 589828
  (393 other events, 4766.4 us)
Sparse Core Ops, SparseCore 0:
  10.8 55.0 all-gather.16
  68.7 54.9 all-gather.12
  126.6 55.0 all-gather.20
  184.3 55.1 all-gather.22
  242.2 68.6 all-gather.32
  313.5 66.6 all-gather.18
  383.0 66.6 all-gather.30
  452.4 66.6 all-gather.14
  521.9 53.2 all-gather.24
  577.9 80.2 all-gather.26
  661.0 79.1 all-gather.28
  2139.7 169.2 reduce-scatter.36
  2689.6 169.0 reduce-scatter.40
  2863.5 129.4 reduce-scatter.38
  2997.8 129.8 reduce-scatter.42
  3132.8 120.4 reduce-scatter.48
  3257.9 123.5 reduce-scatter.44
  3386.1 123.5 reduce-scatter.46
  3514.5 123.4 reduce-scatter.30
  3642.5 123.4 reduce-scatter.28
  3770.8 123.3 reduce-scatter.26
  3899.4 136.6 reduce-scatter.34
  4042.1 136.5 reduce-scatter.32
  4182.0 22.1 all-reduce.27
where the time goes:
time: 4250 us; the launch traced here: 4220 us
  local copies, waits for them, and re-layouts  1910 us (45%)
  waiting for transfers between devices  1440 us (34%)
  matrix products  455 us (11%)
  blocking collectives  218 us (5%)
  other arithmetic  161 us (4%)
    unnamed x31, waiting for transfers between devices  643 us
    reshape x24, local copies, waits for them, and re-layouts, skew_rows(): return flattened.reshape(leading, row_count, window - 1)[:, :, :key_count]  295 us
    reshape x24, local copies, waits for them, and re-layouts, skew_rows(): flattened = full_table.reshape(leading, row_count * window)  228 us
    transpose x24, local copies, waits for them, and re-layouts, block_scores(): jnp.einsum('sqhd,chd->shqc', query_place, place_heads, preferred_element_...  220 us
    slice x24, local copies, waits for them, and re-layouts, skew_rows(): lax.slice_in_dim(flattened, row_count - 1, row_count - 1 + row_count * (w...  203 us
    reshape x24, local copies, waits for them, and re-layouts, block_scores(): shifted = skew_rows(full_part.reshape(2 * H, row_count, window), row_coun...  160 us
    slice x24, local copies, waits for them, and re-layouts, skew_rows(): return flattened.reshape(leading, row_count, window - 1)[:, :, :key_count]  155 us
    reduce_scatter x1, waiting for transfers between devices, body(): lax.psum_scatter(gradients[5].astype(jnp.bfloat16), 'shard', scatter_dime...  143 us
  transfers between devices with their start and end apart: 24, of which 13 were waited for; matrix products, arithmetic and copies ran while one was open for 45% of the time, Pallas kernels for 0%

commit v1 on v0

v1 whole, which is shorter than its diff:
```python
import functools

import jax
import jax.numpy as jnp
from jax import lax
from jax.experimental import pallas as pl
from jax.experimental.pallas import tpu as pltpu
from jax.sharding import PartitionSpec as P

DH = 64
NS = 13
EPSILON = 1e-05
NEG = -1e30
F32 = jnp.float32
BF = jnp.bfloat16
HIGHEST = lax.Precision.HIGHEST

R = 128
KB = 256
W = R + KB
SCALE = DH**-0.5
LOG2E = 1.4426950408889634
LN2 = 0.6931471805599453
ONES = 32


def mm(a, b, ca=1, cb=0, precision=None):
    return lax.dot_general(
        a, b, (((ca,), (cb,)), ((), ())), preferred_element_type=F32, precision=precision
    )


def row_features(seg_col):
    lane = lax.broadcasted_iota(jnp.int32, (2 * R, 128), 1)
    folded = jnp.where(lane < NS, lane, lane - NS).astype(F32)
    return jnp.where((lane < 2 * NS) & (folded == seg_col), 1.0, 0.0)


def live_list(live_ref, list_ref, block, nkb):
    def step(kb, count):
        list_ref[count] = kb
        return count + live_ref[block * nkb + kb]

    return lax.fori_loop(0, nkb, step, 0)


def forward_kernel(
    nkb,
    base_ref,
    live_ref,
    q_ref,
    vec_ref,
    table_ref,
    info_ref,
    reach_ref,
    kv_ref,
    hot_ref,
    rel_ref,
    rank_ref,
    p_ref,
    o_ref,
    inv_ref,
    qq_scr,
    qr_scr,
    s_scr,
    m_scr,
    acc_scr,
    list_scr,
):
    block = pl.program_id(0)
    base = base_ref[block]
    count = live_list(live_ref, list_scr, block, nkb)
    seg_col = info_ref[:, 0:1]
    limit = info_ref[:, 1:2]
    hot_row = row_features(seg_col)
    lane = lax.broadcasted_iota(jnp.int32, (2 * R, 128), 1)
    reach = mm(jnp.where(lane < NS, hot_row, 0.0).astype(BF), reach_ref[...])
    outside = jnp.where((lane < 2 * NS) & (reach < 0.5), NEG, 0.0)
    zero = jnp.zeros((2 * R, DH), BF)
    for h in range(2):
        half = slice(DH * h, DH * h + DH)
        q = q_ref[:, half]
        plain = ((q + vec_ref[0:1, half]) * (SCALE * LOG2E)).astype(BF)
        place = ((q + vec_ref[1:2, half]) * (SCALE * LOG2E)).astype(BF)
        label = q + vec_ref[2:3, half]
        same = mm(label, table_ref[h, 0], precision=HIGHEST)
        other = mm(label, table_ref[h, 1], precision=HIGHEST)
        term = jnp.where(hot_row > 0.5, same, other) * (SCALE * LOG2E) + outside
        high = term.astype(BF).astype(F32)
        extra = jnp.where(lane < NS, high, jnp.where(lane < 2 * NS, term - high, 0.0))
        qq_scr[h] = jnp.concatenate([plain, zero, extra.astype(BF)], axis=1)
        qr_scr[h] = jnp.concatenate([place, zero] if h == 0 else [zero, place], axis=1)
    m_scr[...] = jnp.full(m_scr.shape, -jnp.inf, F32)
    acc_scr[...] = jnp.zeros(acc_scr.shape, F32)

    def score(n, carry):
        k0 = pl.multiple_of(list_scr[n] * KB, KB)
        ok = rank_ref[:, pl.ds(k0, KB)] <= limit
        window = rel_ref[pl.ds(pl.multiple_of(base + k0, 128), W), :]
        hot = hot_ref[pl.ds(k0, KB), :]
        for h in range(2):
            keys = jnp.concatenate([kv_ref[pl.ds(k0, KB), 128 * h : 128 * h + 128], hot], axis=1)
            s = mm(qq_scr[h], keys, 1, 1)
            full = mm(qr_scr[h], window, 1, 1)
            shifted = [
                pltpu.roll(full[i * R : i * R + R], W - (R - 1), 1, stride=1, stride_axis=0)[
                    :, :KB
                ]
                for i in range(2)
            ]
            s = jnp.where(ok, s + jnp.concatenate(shifted, axis=0), NEG)
            s_scr[h, n] = s
            m_scr[h] = jnp.maximum(m_scr[h], jnp.maximum(s[:, :128], s[:, 128:]))
        return carry

    lax.fori_loop(0, count, score, 0)
    top = [jnp.max(m_scr[h], axis=1, keepdims=True) for h in range(2)]

    def mix(n, carry):
        k0 = pl.multiple_of(list_scr[n] * KB, KB)
        hot = hot_ref[pl.ds(k0, KB), :]
        for h in range(2):
            p = jnp.exp2(s_scr[h, n] - top[h]).astype(BF)
            p_ref[0, 0, h, n] = p
            keys = jnp.concatenate([kv_ref[pl.ds(k0, KB), 128 * h : 128 * h + 128], hot], axis=1)
            acc_scr[h] += mm(p, keys)
        return carry

    lax.fori_loop(0, count, mix, 0)
    for h in range(2):
        half = slice(DH * h, DH * h + DH)
        acc = acc_scr[h]
        inverse = 1.0 / acc[:, 128 + ONES : 129 + ONES]
        o_ref[:, half] = acc[:, DH : 2 * DH] * inverse
        inv_ref[:, half] = jnp.broadcast_to(inverse, (2 * R, DH))


def attend_forward(base, live, q, vec, table, info, reach, kv, hot, rel, rank):
    nb = q.shape[0] // (2 * R)
    pairs = q.shape[1] // 128
    length = kv.shape[0]
    nkb = length // KB
    rows = lambda width: pl.BlockSpec((2 * R, width), lambda b, p, *_: (b, p))
    whole = lambda *shape: pl.BlockSpec(shape, lambda b, p, *_: (0,) * len(shape))
    return pl.pallas_call(
        functools.partial(forward_kernel, nkb),
        grid_spec=pltpu.PrefetchScalarGridSpec(
            num_scalar_prefetch=2,
            grid=(nb, pairs),
            in_specs=[
                rows(128),
                pl.BlockSpec((8, 128), lambda b, p, *_: (0, p)),
                pl.BlockSpec((2, 2, DH, 128), lambda b, p, *_: (p, 0, 0, 0)),
                pl.BlockSpec((2 * R, 2), lambda b, p, *_: (b, 0)),
                whole(128, 128),
                pl.BlockSpec((length, 256), lambda b, p, *_: (0, p)),
                whole(length, 128),
                pl.BlockSpec((2 * length, 128), lambda b, p, *_: (0, p)),
                whole(1, length),
            ],
            out_specs=[
                pl.BlockSpec((1, 1, 2, nkb, 2 * R, KB), lambda b, p, *_: (b, p, 0, 0, 0, 0)),
                rows(128),
                rows(128),
            ],
            scratch_shapes=[
                pltpu.VMEM((2, 2 * R, 256), BF),
                pltpu.VMEM((2, 2 * R, 128), BF),
                pltpu.VMEM((2, nkb, 2 * R, KB), F32),
                pltpu.VMEM((2, 2 * R, 128), F32),
                pltpu.VMEM((2, 2 * R, 256), F32),
                pltpu.SMEM((nkb + 1,), jnp.int32),
            ],
        ),
        out_shape=[
            jax.ShapeDtypeStruct((nb, pairs, 2, nkb, 2 * R, KB), BF),
            jax.ShapeDtypeStruct(q.shape, F32),
            jax.ShapeDtypeStruct(q.shape, F32),
        ],
        compiler_params=pltpu.CompilerParams(
            dimension_semantics=("arbitrary", "arbitrary"), vmem_limit_bytes=58 * 2**20
        ),
        cost_estimate=pl.CostEstimate(
            flops=nb * pairs * nkb * 2 * 2 * 2 * R * KB * 700,
            bytes_accessed=nb * pairs * nkb * 2 * 2 * 2 * R * KB,
            transcendentals=nb * pairs * nkb * 2 * 2 * R * KB,
        ),
        name="attend_forward",
    )(base, live, q, vec, table, info, reach, kv, hot, rel, rank)


def backward_kernel(
    nkb,
    nb,
    base_ref,
    live_ref,
    p_ref,
    q_ref,
    g_ref,
    o_ref,
    inv_ref,
    vec_ref,
    info_ref,
    kv_ref,
    hot_ref,
    rel_ref,
    dq_ref,
    dkv_ref,
    drel_ref,
    small_ref,
    qq_scr,
    qr_scr,
    dd_scr,
    acc_scr,
    accr_scr,
    dkv_scr,
    drel_scr,
    flip_scr,
    list_scr,
):
    block = pl.program_id(1)
    length = nkb * KB
    base = base_ref[block]
    count = live_list(live_ref, list_scr, block, nkb)

    @pl.when(block == 0)
    def start():
        dkv_scr[...] = jnp.zeros(dkv_scr.shape, F32)
        drel_scr[...] = jnp.zeros(drel_scr.shape, F32)
        small_ref[...] = jnp.zeros(small_ref.shape, F32)
        down = lax.broadcasted_iota(jnp.int32, (KB, KB), 0)
        across = lax.broadcasted_iota(jnp.int32, (KB, KB), 1)
        flip_scr[...] = jnp.where(down + across == KB - 1, 1.0, 0.0).astype(BF)

    lane = lax.broadcasted_iota(jnp.int32, (2 * R, 128), 1)
    zero = jnp.zeros((2 * R, DH), BF)
    for h in range(2):
        half = slice(DH * h, DH * h + DH)
        q = q_ref[:, half]
        plain = ((q + vec_ref[0:1, half]) * (SCALE * LOG2E)).astype(BF)
        place = ((q + vec_ref[1:2, half]) * (SCALE * LOG2E)).astype(BF)
        g = g_ref[:, half].astype(F32)
        inverse = inv_ref[:, DH * h : DH * h + 1]
        delta = -jnp.sum(g * o_ref[:, half], axis=1, keepdims=True) * inverse
        high = delta.astype(BF).astype(F32)
        extra = jnp.where(lane == ONES, high, jnp.where(lane == ONES + 1, delta - high, 0.0))
        qq_scr[h] = jnp.concatenate([plain, zero], axis=1)
        qr_scr[h] = jnp.concatenate([place, zero] if h == 0 else [zero, place], axis=1)
        dd_scr[h] = jnp.concatenate([zero, (g * inverse).astype(BF), extra.astype(BF)], axis=1)
    acc_scr[...] = jnp.zeros(acc_scr.shape, F32)
    accr_scr[...] = jnp.zeros(accr_scr.shape, F32)

    def step(n, carry):
        k0 = pl.multiple_of(list_scr[n] * KB, KB)
        r0 = pl.multiple_of(2 * length - base - k0 - W, 128)
        hot = hot_ref[pl.ds(k0, KB), :]
        window = rel_ref[pl.ds(r0, W), :]
        pad = jnp.zeros((R, W - KB), F32)
        for h in range(2):
            lanes = slice(128 * h, 128 * h + 128)
            p = p_ref[0, 0, h, n]
            keys = jnp.concatenate([kv_ref[pl.ds(k0, KB), lanes], hot], axis=1)
            dd = dd_scr[h]
            ds = (p.astype(F32) * mm(dd, keys, 1, 1)).astype(BF)
            acc_scr[h] += mm(ds, keys)
            turned = mm(ds, flip_scr[...])
            full = [
                pltpu.roll(
                    jnp.concatenate([turned[i * R : i * R + R], pad], axis=1),
                    0,
                    1,
                    stride=1,
                    stride_axis=0,
                )
                for i in range(2)
            ]
            full = jnp.concatenate(full, axis=0).astype(BF)
            accr_scr[h] += mm(full, window)
            drel_scr[pl.ds(r0, W), :] += mm(full, qr_scr[h], 0, 0)
            dkv_scr[pl.ds(k0, KB), lanes] += mm(ds, qq_scr[h], 0, 0) + mm(p, dd[:, :128], 0, 0)
        return carry

    lax.fori_loop(0, count, step, 0)
    hot_row = row_features(info_ref[:, 0:1])
    for h in range(2):
        half = slice(DH * h, DH * h + DH)
        acc = acc_scr[h]
        d_plain = acc[:, :DH] * SCALE
        d_place = accr_scr[h][:, half] * SCALE
        sums = jnp.where(lane < NS, acc[:, 128:], 0.0) * SCALE
        same = jnp.sum(sums * hot_row, axis=1, keepdims=True)
        other = jnp.sum(sums, axis=1, keepdims=True) - same
        d_label = same * vec_ref[3:4, half] + other * vec_ref[4:5, half]
        label = q_ref[:, half] + vec_ref[2:3, half]
        dq_ref[:, half] = (d_plain + d_place + d_label).astype(BF)
        terms = [d_plain, d_place, d_label, same * label, other * label]
        for row, term in enumerate(terms):
            small_ref[row : row + 1, half] += jnp.sum(term, axis=0, keepdims=True)

    @pl.when(block == nb - 1)
    def finish():
        across = lax.broadcasted_iota(jnp.int32, (length, 256), 1)
        factor = jnp.where((across % 128) < DH, LN2, 1.0)
        dkv_ref[...] = (dkv_scr[...] * factor).astype(BF)
        drel_ref[...] = (drel_scr[...] * LN2).astype(BF)


def attend_backward(base, live, p, q, g, o, inv, vec, info, kv, hot, rel):
    nb = q.shape[0] // (2 * R)
    pairs = q.shape[1] // 128
    length = kv.shape[0]
    nkb = length // KB
    rows = lambda width: pl.BlockSpec((2 * R, width), lambda p, b, *_: (b, p))
    return pl.pallas_call(
        functools.partial(backward_kernel, nkb, nb),
        grid_spec=pltpu.PrefetchScalarGridSpec(
            num_scalar_prefetch=2,
            grid=(pairs, nb),
            in_specs=[
                pl.BlockSpec((1, 1, 2, nkb, 2 * R, KB), lambda p, b, *_: (b, p, 0, 0, 0, 0)),
                rows(128),
                rows(128),
                rows(128),
                rows(128),
                pl.BlockSpec((8, 128), lambda p, b, *_: (0, p)),
                pl.BlockSpec((2 * R, 2), lambda p, b, *_: (b, 0)),
                pl.BlockSpec((length, 256), lambda p, b, *_: (0, p)),
                pl.BlockSpec((length, 128), lambda p, b, *_: (0, 0)),
                pl.BlockSpec((2 * length, 128), lambda p, b, *_: (0, p)),
            ],
            out_specs=[
                rows(128),
                pl.BlockSpec((length, 256), lambda p, b, *_: (0, p)),
                pl.BlockSpec((2 * length, 128), lambda p, b, *_: (0, p)),
                pl.BlockSpec((8, 128), lambda p, b, *_: (0, p)),
            ],
            scratch_shapes=[
                pltpu.VMEM((2, 2 * R, 128), BF),
                pltpu.VMEM((2, 2 * R, 128), BF),
                pltpu.VMEM((2, 2 * R, 256), BF),
                pltpu.VMEM((2, 2 * R, 256), F32),
                pltpu.VMEM((2, 2 * R, 128), F32),
                pltpu.VMEM((length, 256), F32),
                pltpu.VMEM((2 * length, 128), F32),
                pltpu.VMEM((KB, KB), BF),
                pltpu.SMEM((nkb + 1,), jnp.int32),
            ],
        ),
        out_shape=[
            jax.ShapeDtypeStruct(q.shape, BF),
            jax.ShapeDtypeStruct(kv.shape, BF),
            jax.ShapeDtypeStruct((2 * length, q.shape[1]), BF),
            jax.ShapeDtypeStruct((8, q.shape[1]), F32),
        ],
        compiler_params=pltpu.CompilerParams(
            dimension_semantics=("arbitrary", "arbitrary"), vmem_limit_bytes=58 * 2**20
        ),
        cost_estimate=pl.CostEstimate(
            flops=nb * pairs * nkb * 2 * 2 * 2 * R * KB * 1400,
            bytes_accessed=nb * pairs * nkb * 2 * 2 * 2 * R * KB,
            transcendentals=0,
        ),
        name="attend_backward",
    )(base, live, p, q, g, o, inv, vec, info, kv, hot, rel)


def layer_norm(vector, gain_row, shift_row):
    average = jnp.mean(vector, axis=-1, keepdims=True)
    centred = vector - average
    variance = jnp.mean(centred * centred, axis=-1, keepdims=True)
    return centred * lax.rsqrt(variance + EPSILON) * gain_row + shift_row


def gelu_tanh(vector):
    return jax.nn.gelu(vector, approximate=True)


def position_rows(offsets, model_width):
    half_width = model_width // 2
    powers = jnp.arange(half_width, dtype=F32) * (2.0 / model_width)
    inverse_freq = 1.0 / 10000.0**powers
    angles = offsets[:, None] * inverse_freq[None, :]
    return jnp.concatenate([jnp.sin(angles), jnp.cos(angles)], axis=1)


def body(
    content_in,
    query_in,
    segment_ids,
    parent_ids,
    rank_order,
    query_flags,
    query_weight,
    key_weight,
    value_weight,
    relative_weight,
    output_weight,
    inner_weight,
    outer_weight,
    inner_bias,
    outer_bias,
    attend_gain,
    attend_shift,
    feed_gain,
    feed_shift,
    content_bias,
    position_bias,
    segment_bias,
    segment_table,
    content_cot,
    query_cot,
):
    n = lax.axis_size("shard")
    nr = lax.axis_size("rep")
    trees, r, d = content_in.shape
    groups = 2 * trees
    m = n // groups
    length = r * n
    nkb = length // KB
    rh = r // 2
    ff = inner_weight.shape[1]
    dh = d // 2
    fh = ff // 2
    heads = dh // DH
    ws = query_weight.shape[0]
    fs = outer_weight.shape[0]
    me = lax.axis_index("shard")
    g, c = me // m, me % m
    k = lax.axis_index("rep") % 2
    first = k == 0

    def swap(x):
        return lax.ppermute(x, "rep", [(i, i ^ 1) for i in range(nr)])

    def far(x, step):
        return lax.ppermute(x, "shard", [(i, i ^ (m * step)) for i in range(n)])

    def near(x, step):
        return lax.ppermute(x, "shard", [(i, i ^ step) for i in range(n)])

    def pick(x, index, axis=0):
        return lax.dynamic_index_in_dim(x, index, axis, keepdims=False)

    def put(buffer, x, index, axis=0):
        return lax.dynamic_update_index_in_dim(buffer, x, index, axis)

    def ordered(mine, other, axis):
        return jnp.where(
            first,
            jnp.concatenate([mine, other], axis=axis),
            jnp.concatenate([other, mine], axis=axis),
        )

    def halves(x, axis, size):
        return (
            lax.dynamic_slice_in_dim(x, k * size, size, axis),
            lax.dynamic_slice_in_dim(x, (1 - k) * size, size, axis),
        )

    def gather(x):
        rows = jnp.zeros((groups,) + x.shape, x.dtype)
        for step in range(groups):
            rows = put(rows, far(x, step) if step else x, g ^ step)
        full = jnp.zeros((groups, m) + x.shape, x.dtype)
        for step in range(m):
            full = put(full, near(rows, step) if step else rows, c ^ step, 1)
        return full.reshape((n,) + x.shape)

    def scatter_near(x):
        total = pick(x, c).astype(F32)
        for step in range(1, m):
            total = total + near(pick(x, c ^ step), step).astype(F32)
        return total

    def scatter_far(x):
        total = pick(x, g).astype(F32)
        for step in range(1, groups):
            total = total + far(pick(x, g ^ step), step).astype(F32)
        return total

    def scatter(x):
        x = x.reshape((groups, m) + x.shape[1:])
        part = scatter_near(jnp.swapaxes(x, 0, 1)).astype(BF)
        return scatter_far(part)

    def trade_far(x):
        out = jnp.zeros_like(x)
        for step in range(groups):
            part = pick(x, g ^ step)
            out = put(out, far(part, step) if step else part, g ^ step)
        return out

    def to_trees(x):
        mine, other = halves(x, 1, rh)
        return trade_far(ordered(mine, swap(other), 0))

    def from_trees(x):
        back = trade_far(x)
        mine, other = halves(back, 0, trees)
        return ordered(mine, swap(other), 1)

    kv_shard = jnp.concatenate(
        [
            lax.dynamic_slice_in_dim(key_weight, k * dh, dh, 1).reshape(ws, heads, 1, DH),
            lax.dynamic_slice_in_dim(value_weight, k * dh, dh, 1).reshape(ws, heads, 1, DH),
        ],
        axis=2,
    ).reshape(ws, d)
    proj_shard = jnp.concatenate(
        [
            lax.dynamic_slice_in_dim(query_weight, k * dh, dh, 1),
            kv_shard,
            lax.dynamic_slice_in_dim(relative_weight, k * dh, dh, 1),
        ],
        axis=1,
    )
    vec_shard = jnp.concatenate(
        [
            outer_bias,
            attend_gain,
            attend_shift,
            feed_gain,
            feed_shift,
            content_bias,
            position_bias,
            segment_bias,
            segment_table[0],
            segment_table[1],
            inner_bias,
        ]
    )
    vec_width = vec_shard.shape[0]
    vec_row = jnp.pad(vec_shard, (0, 4 * dh - vec_width))[None]
    proj_all = gather(jnp.concatenate([proj_shard, vec_row], axis=0))
    proj = proj_all[:, :ws].reshape(d, 4 * dh)
    vectors = proj_all[:, ws, :vec_width].astype(F32)
    vecs = vectors[:, : 10 * ws].reshape(n, 10, ws).swapaxes(0, 1).reshape(10, d)
    inner_shift = vectors[:, 10 * ws :].reshape(n, 2, fs // 2).swapaxes(0, 1).reshape(2, fh)
    outer_shift, gain_one, shift_one, gain_two, shift_two = [vecs[i] for i in range(5)]
    head_vecs = lax.dynamic_slice_in_dim(vecs[5:], k * dh, dh, 1)

    codes = jnp.stack(
        [segment_ids, rank_order // 64, rank_order % 64, query_flags], axis=1
    ).astype(BF)
    codes = codes.reshape(trees, 4, 2, rh).swapaxes(1, 2).reshape(trees, 2, 1, 4 * rh)
    codes = jnp.pad(codes, ((0, 0), (0, 0), (0, 0), (0, d - 4 * rh)))
    content_rows = jnp.concatenate([content_in.reshape(trees, 2, rh, d), codes], axis=2)
    mine, other = halves(content_rows, 1, 1)
    content_half = trade_far(ordered(mine[:, 0], swap(other[:, 0]), 0))
    tree_half = jnp.zeros((groups, m, rh + 1, d), BF)
    for step in range(m):
        tree_half = put(tree_half, near(content_half, step) if step else content_half, c ^ step, 1)
    tree_other = swap(tree_half)
    tree_rows = jnp.zeros((groups, m, 2, rh + 1, d), BF)
    tree_rows = put(tree_rows, tree_half, k, 2)
    tree_rows = put(tree_rows, tree_other, 1 - k, 2)
    content_full = tree_rows[:, :, :, :rh].reshape(length, d)
    codes = tree_rows[:, :, :, rh, : 4 * rh].reshape(n, 2, 4, rh).astype(F32)
    key_segs = codes[:, :, 0].reshape(length)
    key_ranks = (codes[:, :, 1] * 64.0 + codes[:, :, 2]).reshape(length)
    key_flags = codes[:, :, 3].reshape(length)
    query_half = to_trees(query_in)
    query_other = swap(query_half)
    own_content = pick(tree_rows, c, 1)[:, :, :rh]
    own_query = ordered(query_half[:, None], query_other[:, None], 1)
    inputs = jnp.stack([own_content, own_query], axis=1).reshape(groups * 2 * r, d)
    half_inputs = jnp.stack([content_half[:, :rh], query_half], axis=1).reshape(groups * r, d)

    parents = ordered(parent_ids, swap(parent_ids), 0)
    parents = pick(parents, g)
    labels = jnp.arange(NS, dtype=jnp.int32)
    reached = jnp.eye(NS, dtype=F32) + (parents[:, None] == labels[None, :]).astype(F32)
    for repeat in range(4):
        reached = jnp.minimum(jnp.dot(reached, reached, precision=HIGHEST), 1.0)
    reach = jnp.pad(jnp.concatenate([reached, reached], axis=1), ((0, 128 - NS), (0, 128 - 2 * NS)))
    reach = reach.astype(BF)
    feature = jnp.arange(128, dtype=jnp.int32)
    folded = jnp.where(feature < 2 * NS, feature % NS, -1).astype(F32)
    ones_lane = (feature == ONES) | (feature == ONES + 1)
    hot = ((key_segs[:, None] == folded[None]) | ones_lane[None]).astype(BF)
    key_present = jnp.max(
        (key_segs.reshape(nkb, KB)[:, :, None] == labels.astype(F32)).astype(F32), axis=1
    )
    by_block = lambda x: pick(x.reshape(groups, m, r), c, 1)
    row_segs, row_ranks, row_flags = by_block(key_segs), by_block(key_ranks), by_block(key_flags)
    row_present = jnp.max((row_segs[:, :, None] == labels.astype(F32)).astype(F32), axis=1)
    seen = jnp.dot(row_present, reached, precision=HIGHEST)
    live = (jnp.dot(seen, key_present.T, precision=HIGHEST) > 0.5).astype(jnp.int32).reshape(-1)
    base = length - R - R * (jnp.arange(groups, dtype=jnp.int32) * m + c)
    limits = jnp.stack([row_ranks, row_ranks - row_flags], axis=1)
    info = jnp.stack([jnp.broadcast_to(row_segs[:, None], limits.shape), limits], axis=-1)
    info = info.reshape(groups * 2 * r, 2)

    offsets = (length - 1 - jnp.arange(2 * length, dtype=jnp.int32)).astype(F32)
    position_bf = position_rows(offsets, d).astype(BF)
    sign = jnp.where(jnp.arange(d) < d // 2, -1.0, 1.0)
    rel_weight = proj[:, 3 * dh :]
    turned_weight = (rel_weight.astype(F32) * sign[:, None]).astype(BF)
    rel = mm(position_bf, rel_weight).astype(BF)
    rel_turned = mm(position_bf, turned_weight).astype(BF)
    queries = mm(inputs, proj[:, :dh])
    kv_weight = proj[:, dh : 3 * dh]
    kv = mm(content_full, kv_weight).astype(BF)
    vec8 = jnp.pad(head_vecs, ((0, 3), (0, 0)))
    table = head_vecs[3:5].reshape(2, heads, DH).swapaxes(0, 1)
    table = jnp.where(feature < 2 * NS, table[..., None], 0.0)
    probs, mixed, inverse = attend_forward(
        base, live, queries, vec8, table, info, reach, kv, hot, rel, key_ranks[None]
    )

    cols = inner_weight.reshape(ws, n, 2, fs // 2)
    inner_shard = pick(cols, k, 2).reshape(ws, fh)
    early = gather(
        jnp.concatenate([lax.dynamic_slice_in_dim(output_weight, k * dh, dh, 1), inner_shard], 1)
    ).reshape(d, dh + fh)
    outer_half = gather(pick(outer_weight.reshape(2, fs // 2, d), k)).reshape(fh, d)
    early_other = swap(early)
    outer_other = swap(outer_half)
    output_full = ordered(early[:, :dh], early_other[:, :dh], 1)
    inner_w = (early[:, dh:], early_other[:, dh:])
    outer_w = (outer_half, outer_other)
    shifts = (pick(inner_shift, k), pick(inner_shift, 1 - k))

    mixed_rows = mixed.astype(BF).reshape(groups * 2, 2, rh, dh)
    mine, other = halves(mixed_rows, 1, 1)
    mixed_bf = ordered(mine, swap(other), 3).reshape(groups * r, d)
    residual = mm(mixed_bf, output_full) + half_inputs.astype(F32)
    normed = layer_norm(residual, gain_one, shift_one)
    normed_bf = normed.astype(BF)
    inner_pre = [mm(normed_bf, w) + s for w, s in zip(inner_w, shifts)]
    hidden_bf = [gelu_tanh(x).astype(BF) for x in inner_pre]
    summed = mm(hidden_bf[0], outer_w[0]) + mm(hidden_bf[1], outer_w[1]) + outer_shift + normed
    result = layer_norm(summed, gain_two, shift_two).astype(BF).reshape(groups, 2, rh, d)
    outs = from_trees(result.reshape(groups, r, d)[:, :rh]), from_trees(
        result.reshape(groups, r, d)[:, rh:]
    )
    cotangent = jnp.stack([to_trees(content_cot), to_trees(query_cot)], axis=1)
    cotangent = cotangent.reshape(groups * r, d).astype(F32)
    unused, final_back = jax.vjp(layer_norm, summed, gain_two, shift_two)
    grad_summed, grad_final_gain, grad_final_shift = final_back(cotangent)
    grad_summed_bf = grad_summed.astype(BF)
    grad_inner = []
    for pre, w in zip(inner_pre, outer_w):
        unused, gelu_back = jax.vjp(gelu_tanh, pre)
        grad_inner.append(gelu_back(mm(grad_summed_bf, w, 1, 1))[0])
    grad_inner_bf = [x.astype(BF) for x in grad_inner]
    grad_normed = (
        mm(grad_inner_bf[0], inner_w[0], 1, 1) + mm(grad_inner_bf[1], inner_w[1], 1, 1) + grad_summed
    )
    unused, first_back = jax.vjp(layer_norm, residual, gain_one, shift_one)
    grad_residual, grad_norm_gain, grad_norm_shift = first_back(grad_normed)
    grad_residual_bf = grad_residual.astype(BF)
    grad_mixed = mm(grad_residual_bf, output_full, 1, 1).astype(BF)
    mine, other = halves(grad_mixed, 1, dh)
    grad_heads = ordered(
        mine.reshape(groups * 2, 1, rh, dh), swap(other).reshape(groups * 2, 1, rh, dh), 1
    ).reshape(groups * 2 * r, dh)

    grad_output = mm(mixed_bf, grad_residual_bf, 0, 0).astype(BF)
    mine_output, other_output = halves(grad_output, 1, dh)
    grad_inner_w = [mm(normed_bf, x, 0, 0).astype(BF) for x in grad_inner_bf]
    grad_outer_w = [mm(x, grad_summed_bf, 0, 0).astype(BF) for x in hidden_bf]
    row_vecs = jnp.stack(
        [
            jnp.sum(grad_summed, axis=0),
            grad_norm_gain,
            grad_norm_shift,
            grad_final_gain,
            grad_final_shift,
        ]
    ).reshape(5, n, ws)
    row_vecs = row_vecs.swapaxes(0, 1).reshape(n, 5 * ws)
    inner_vecs = [jnp.sum(x, axis=0).reshape(n, fs // 2) for x in grad_inner]

    def pack(parts_vec, out_part, inner_part, outer_part):
        vec = jnp.pad(parts_vec, ((0, 0), (0, d - parts_vec.shape[1])))[:, None].astype(BF)
        return jnp.concatenate(
            [
                out_part.reshape(n, ws * dh // d, d),
                inner_part.reshape(n, ws * fh // d, d),
                outer_part.reshape(n, fs // 2, d),
                vec,
            ],
            axis=1,
        )

    vec_halves = [
        jnp.concatenate([row_vecs, inner_vecs[i]], axis=1) for i in range(2)
    ]
    mine_pack = pack(vec_halves[0], mine_output, grad_inner_w[0], grad_outer_w[0])
    other_pack = pack(vec_halves[1], other_output, grad_inner_w[1], grad_outer_w[1])
    pack_sum = (mine_pack.astype(F32) + swap(other_pack).astype(F32)).astype(BF)
    late = scatter(pack_sum)

    dq, dkv, drel, small = attend_backward(
        base, live, probs, queries, grad_heads, mixed, inverse, vec8, info, kv, hot, rel_turned
    )

    grad_q_weight = mm(inputs, dq, 0, 0)
    grad_kv_weight = mm(content_full, dkv, 0, 0)
    grad_rel_weight = mm(position_bf, drel, 0, 0) * sign[:, None]
    proj_grad = jnp.concatenate([grad_q_weight, grad_kv_weight, grad_rel_weight], axis=1)
    small = small[:5].reshape(5, n // 2, ws).swapaxes(0, 1)
    small_rows = jnp.zeros((n, 5 * ws), F32)
    small_rows = lax.dynamic_update_slice_in_dim(
        small_rows, small.reshape(n // 2, 5 * ws), k * (n // 2), 0
    )
    small_rows = jnp.pad(small_rows, ((0, 0), (0, 4 * dh - 5 * ws)))[:, None]
    proj_parts = scatter(
        jnp.concatenate([proj_grad.reshape(n, ws, 4 * dh), small_rows], axis=1).astype(BF)
    )

    content_kv = mm(dkv, kv_weight, 1, 1).astype(BF).reshape(n, 2, rh, d)
    query_part = mm(dq, proj[:, :dh], 1, 1).astype(BF).reshape(groups * 2, 2, rh, d)
    mine_kv, other_kv = halves(content_kv, 1, 1)
    mine_q, other_q = halves(query_part, 1, 1)
    got = swap(jnp.concatenate([other_kv, other_q], axis=0)[:, 0]).astype(F32)
    kv_sum = (mine_kv[:, 0].astype(F32) + got[:n]).astype(BF).reshape(groups, m, rh, d)
    q_sum = (mine_q[:, 0].astype(F32) + got[n:]).reshape(groups, 2, rh, d)
    q_sum = q_sum + grad_residual.reshape(groups, 2, rh, d)
    content_sum = scatter_near(kv_sum.swapaxes(0, 1)) + q_sum[:, 0]
    grads = from_trees(content_sum.astype(BF)), from_trees(q_sum[:, 1].astype(BF))

    bit = 2
    flat = jnp.concatenate([late.reshape(-1), proj_parts.reshape(-1)])
    while bit < nr:
        flat = flat + lax.ppermute(flat, "rep", [(i, i ^ bit) for i in range(nr)])
        bit *= 2
    flat_other = swap(flat)
    late_size = late.size
    both = [
        (x[:late_size].reshape(late.shape), x[late_size:].reshape(proj_parts.shape))
        for x in (flat, flat_other)
    ]
    (late_a, proj_a), (late_b, proj_b) = both
    lo = jnp.where(first, late_a, late_b), jnp.where(first, late_b, late_a)
    pr = jnp.where(first, proj_a, proj_b), jnp.where(first, proj_b, proj_a)
    cut1 = ws * dh // d
    cut2 = cut1 + ws * fh // d
    cut3 = cut2 + fs // 2
    grad_wo = jnp.concatenate([x[:cut1].reshape(ws, dh) for x in lo], axis=1)
    grad_w1 = jnp.stack([x[cut1:cut2].reshape(ws, n, fs // 2) for x in lo], axis=2).reshape(ws, ff)
    grad_w2 = jnp.concatenate([x[cut2:cut3] for x in lo], axis=0)
    vec_lo = [x[cut3] for x in lo]
    vec_rows = vec_lo[0][: 5 * ws].reshape(5, ws)
    grad_b1 = jnp.concatenate([x[5 * ws : 5 * ws + fs // 2] for x in vec_lo])
    grad_wq = jnp.concatenate([x[:ws, :dh] for x in pr], axis=1)
    kv_parts = [x[:ws, dh : 3 * dh].reshape(ws, heads, 2, DH) for x in pr]
    grad_wk = jnp.concatenate([x[:, :, 0].reshape(ws, dh) for x in kv_parts], axis=1)
    grad_wv = jnp.concatenate([x[:, :, 1].reshape(ws, dh) for x in kv_parts], axis=1)
    grad_wr = jnp.concatenate([x[:ws, 3 * dh :] for x in pr], axis=1)
    head_rows = (pr[0][ws, : 5 * ws] + pr[1][ws, : 5 * ws]).reshape(5, ws)
    return (
        outs[0],
        outs[1],
        grads[0],
        grads[1],
        grad_wq,
        grad_wk,
        grad_wv,
        grad_wr,
        grad_wo,
        grad_w1,
        grad_w2,
        grad_b1,
        vec_rows[0],
        vec_rows[1],
        vec_rows[2],
        vec_rows[3],
        vec_rows[4],
        head_rows[0],
        head_rows[1],
        head_rows[2],
        head_rows[3:5],
    )


def solution(mesh):
    in_specs = (
        P("rep", "shard", None),
        P("rep", "shard", None),
        P("rep", "shard"),
        P("rep", None),
        P("rep", "shard"),
        P("rep", "shard"),
        P("shard", None),
        P("shard", None),
        P("shard", None),
        P("shard", None),
        P("shard", None),
        P("shard", None),
        P("shard", None),
        P("shard"),
        P("shard"),
        P("shard"),
        P("shard"),
        P("shard"),
        P("shard"),
        P("shard"),
        P("shard"),
        P("shard"),
        P(None, "shard"),
        P("rep", "shard", None),
        P("rep", "shard", None),
    )
    out_specs = (
        P("rep", "shard", None),
        P("rep", "shard", None),
        P("rep", "shard", None),
        P("rep", "shard", None),
        P("shard", None),
        P("shard", None),
        P("shard", None),
        P("shard", None),
        P("shard", None),
        P("shard", None),
        P("shard", None),
        P("shard"),
        P("shard"),
        P("shard"),
        P("shard"),
        P("shard"),
        P("shard"),
        P("shard"),
        P("shard"),
        P("shard"),
        P(None, "shard"),
    )
    return jax.shard_map(body, mesh=mesh, in_specs=in_specs, out_specs=out_specs, check_vma=False)
```

time: 4250 us -> 757 us (0.18)
  local copies, waits for them, and re-layouts: 1910 us -> 163 us
  waiting for transfers between devices: 1440 us -> 145 us
  matrix products: 455 us -> 82.3 us
  blocking collectives: 218 us -> 0 us
  starting transfers between devices: 1.14 us -> 149 us
  Pallas kernels: 0 us -> 132 us
  other arithmetic: 161 us -> 72.8 us
    reshape x93 -> x32, local copies, waits for them, and re-layouts: 843 us -> 19.8 us  [the longest x3 8.51 us: pack(): inner_part.reshape(n, ws * fh // d, d)]
    reduce_scatter x5 -> x0, waiting for transfers between devices: 667 us -> none  [the longest x1 143 us: body(): lax.psum_scatter(gradients[5].astype(jnp.bfloat16), 'shard', scatter_dime...]
    unnamed x31 -> x0, waiting for transfers between devices: 643 us -> none
    dot_general x198 -> x30, matrix products: 455 us -> 82.3 us  [the longest x24 80.8 us: mm(): lax.dot_general(a, b, (((ca,), (cb,)), ((), ())), preferred_element_type=...]
    slice x51 -> x32, local copies, waits for them, and re-layouts: 360 us -> 14.2 us  [the longest x3 3.01 us: body(): head_vecs = lax.dynamic_slice_in_dim(vecs[5:], k * dh, dh, 1)]
    transpose x24 -> x1, local copies, waits for them, and re-layouts: 220 us -> 1.29 us  [body(): table = head_vecs[3:5].reshape(2, heads, DH).swapaxes(0, 1)]
    ppermute x0 -> x78, starting transfers between devices: none -> 149 us  [the longest x39 58.5 us: far(): return lax.ppermute(x, 'shard', [(i, i ^ m * step) for i in range(n)])]
    ppermute x0 -> x78, waiting for transfers between devices: none -> 145 us  [the longest x21 103 us: near(): return lax.ppermute(x, 'shard', [(i, i ^ step) for i in range(n)])]
  transfers between devices with their start and end apart: 24 -> 78, of which waited for: 13 -> 23; matrix products, arithmetic and copies ran while one was open for 45% -> 32% of each run, Pallas kernels for 0% -> 18%
where the time goes in v1:
time: 757 us; the launch traced here: 747 us
  local copies, waits for them, and re-layouts  163 us (22%)
  starting transfers between devices  149 us (20%)
  waiting for transfers between devices  145 us (19%)
  Pallas kernels  132 us (17%)
  matrix products  82.3 us (11%)
  other arithmetic  72.8 us (10%)
    ppermute x21, waiting for transfers between devices, near(): return lax.ppermute(x, 'shard', [(i, i ^ step) for i in range(n)])  103 us
    pallas_call x1, Pallas kernels, attend_backward(): pl.pallas_call(functools.partial(backward_kernel, nkb, nb), grid_spec=plt...  82 us
    dot_general x24, matrix products, mm(): lax.dot_general(a, b, (((ca,), (cb,)), ((), ())), preferred_element_type=...  80.8 us
    dynamic_update_slice x57, local copies, waits for them, and re-layouts, put(): return lax.dynamic_update_index_in_dim(buffer, x, index, axis)  63 us
    ppermute x39, starting transfers between devices, far(): return lax.ppermute(x, 'shard', [(i, i ^ m * step) for i in range(n)])  58.5 us
    ppermute x18, starting transfers between devices, swap(): return lax.ppermute(x, 'rep', [(i, i ^ 1) for i in range(nr)])  51.5 us
    pallas_call x1, Pallas kernels, attend_forward(): pl.pallas_call(functools.partial(forward_kernel, nkb), grid_spec=pltpu.Pr...  50 us
    ppermute x39, waiting for transfers between devices, far(): return lax.ppermute(x, 'shard', [(i, i ^ m * step) for i in range(n)])  42.4 us
  transfers between devices with their start and end apart: 78, of which 23 were waited for; matrix products, arithmetic and copies ran while one was open for 32% of the time, Pallas kernels for 18%

profile of v1, /device:TPU:9, one launch (start us, length us, event | category | flops | bytes accessed | tf_op | source)
XLA Modules:
  0.0 746.8 jit_solution(15660099415861980595)
XLA Ops:
  1.5 6.1 concatenate.203
  26.4 5.9 dynamic_update_slice.221
  32.4 25.2 %fusion = (bf16[4096,384]{1,0:T(8,128)(2,1)}, bf16[4096,384]{1,0:T(8,128)(2,1)}) fusion(f32[384]{0:T(512)S(1)} %negate_power_fusion, f32[4096]{0:T(1024)S(1)} %subtract_convert_fusion), kind=kLoop, calls=%fused_computation.3 | loop fusion | flops 4718592 | bytes 6309376 | tf_op jit(solution)/shard_map/convert.32
  64.0 6.1 collective-permute-done.29
  84.2 6.0 dynamic_update_slice.222
  90.2 5.9 dynamic_update_slice.223
  96.1 6.1 dynamic_update_slice.224
  121.4 5.5 collective-permute-done.12
  142.1 10.3 %collective-permute-start.13 = (bf16[4,64,768]{2,1,0:T(8,128)(2,1)S(1)}, bf16[4,64,768]{2,1,0:T(8,128)(2,1)S(1)}, u32[]{:S(2)}, u32[]{:S(2)}) collective-permute-start(bf16[4,64,768]{2,1,0:T(8,128)(2,1)S(1)} %bitcast_dynamic-update-slice_fusion.48), channel_id=1, source_target_pairs={{0,16},{16,0},{1,17},{17,1},{2,18},{18,2},{3,19},{19,3},{4,20},{20... | collective-permute-start | bytes 1179656 | tf_op jit(solution)/shard_map/ppermute | solution.py:433
  162.5 20.5 %collective-permute-done.6 = bf16[4,65,768]{2,1,0:T(8,128)(2,1)S(1)} collective-permute-done((bf16[4,65,768]{2,1,0:T(8,128)(2,1)S(1)}, bf16[4,65,768]{2,1,0:T(8,128)(2,1)S(1)}, u32[]{:S(2)}, u32[]{:S(2)}) %collective-permute-start.6) | collective-permute-done | bytes 399392 | tf_op jit(solution)/shard_map/ppermute | solution.py:439
  197.6 23.0 %collective-permute-start.7 = (bf16[4,4,65,768]{3,1,2,0:T(4,128)(2,1)}, bf16[4,4,65,768]{3,1,2,0:T(4,128)(2,1)}, u32[]{:S(2)}, u32[]{:S(2)}) collective-permute-start(bf16[4,4,65,768]{3,1,2,0:T(4,128)(2,1)} %copy.288), channel_id=1, source_target_pairs={{0,16},{16,0},{1,17},{17,1},{2,18},{18,2},{3,19},{19,3},{4,20},{20... | collective-permute-start | bytes 4792328 | tf_op jit(solution)/shard_map/ppermute | solution.py:433
  229.0 8.1 %convolution_convert_fusion.1.rel_ref = bf16[4096,384]{1,0:T(8,128)(2,1)} fusion(bf16[4096,384]{1,0:T(8,128)(2,1)} %get-tuple-element.161, bf16[4096,384]{1,0:T(8,128)(2,1)} %get-tuple-element.160, bf16[768,1536]{1,0:T(8,128)(2,1)} %bitcast.408), kind=kOutput, calls=%fused_computation.11 | convolution fusion | flops 2430074880 | bytes 10027008 | tf_op jit(solution)/shard_map/dot_general | solution.py:28
  267.1 6.2 convolution_convert_fusion.7.kv_ref
  275.1 50.0 %attend_forward.1 = (bf16[4,3,2,8,256,256]{5,4,3,2,1,0:T(8,128)(2,1)}, f32[1024,384]{1,0:T(8,128)}, f32[1024,384]{1,0:T(8,128)}) custom-call(s32[4]{0:T(128)} %multiply_subtract_fusion.base_ref, s32[32]{0:T(128)} %reshape.627.live_ref, f32[1024,384]{1,0:T(8,128)} %fusion.58.q_ref, f32[8,384]{1,0:T(8,128)} %pad.33.vec_ref, ...), custom_call_target="tpu_custom_call" | custom-call | flops 17616076800 | bytes 25165824 | tf_op jit(solution)/shard_map/attend_forward/pallas_call | solution.py:145
  327.7 7.2 convolution_convert_fusion.rel_ref
  356.1 4.7 fusion.98
  366.8 4.9 fusion.96
  389.7 4.2 collective-permute-start.36
  415.8 5.2 pad_maximum_fusion.1
  428.9 82.0 %attend_backward.1 = (bf16[1024,384]{1,0:T(8,128)(2,1)}, bf16[2048,768]{1,0:T(8,128)(2,1)}, bf16[4096,384]{1,0:T(8,128)(2,1)}, f32[8,384]{1,0:T(8,128)}) custom-call(s32[4]{0:T(128)} %multiply_subtract_fusion.base_ref, s32[32]{0:T(128)} %reshape.627.live_ref, bf16[4,3,2,8,256,256]{5,4,3,2,1,0:T(8,128)(2,1)} %get-tuple-element.29.p_ref, ...), custom_call_target="tpu_custom_call" | custom-call | flops 35232153600 | bytes 25165824 | tf_op jit(solution)/shard_map/attend_backward/pallas_call | solution.py:314
  510.9 4.7 convolution_convert_fusion.6
  534.5 15.1 %collective-permute-start.66 = (bf16[4,49,1536]{2,0,1:T(4,128)(2,1)S(1)}, bf16[4,49,1536]{2,0,1:T(4,128)(2,1)S(1)}, u32[]{:S(2)}, u32[]{:S(2)}) collective-permute-start(bf16[4,49,1536]{2,0,1:T(4,128)(2,1)S(1)} %bitcast.432), channel_id=1, source_target_pairs={{0,3},{1,2},{2,1},{3,0},{4,7},{5,6},{6,5},{7,4},{8,11},{9,10},{10,... | collective-permute-start | bytes 1806344 | tf_op jit(solution)/shard_map/ppermute | solution.py:439
  549.6 6.2 collective-permute-start.65
  564.8 16.4 %collective-permute-done.65 = bf16[4,49,1536]{2,0,1:T(4,128)(2,1)S(1)} collective-permute-done((bf16[4,49,1536]{2,0,1:T(4,128)(2,1)S(1)}, bf16[4,49,1536]{2,0,1:T(4,128)(2,1)S(1)}, u32[]{:S(2)}, u32[]{:S(2)}) %collective-permute-start.65) | collective-permute-done | bytes 602144 | tf_op jit(solution)/shard_map/ppermute | solution.py:439
  583.4 9.9 %collective-permute-start.69 = (bf16[49,1536]{1,0:T(8,128)(2,1)S(1)}, bf16[49,1536]{1,0:T(8,128)(2,1)S(1)}, u32[]{:S(2)}, u32[]{:S(2)}) collective-permute-start(bf16[49,1536]{1,0:T(8,128)(2,1)S(1)} %get-tuple-element.102), channel_id=1, source_target_pairs={{0,12},{1,13},{2,14},{3,15},{4,8},{5,9},{6,10},{7,11},{8,4},{9,5},... | collective-permute-start | bytes 451592 | tf_op jit(solution)/shard_map/ppermute | solution.py:436
  599.2 4.7 collective-permute-start.42
  610.2 5.1 add_convert_fusion
  633.2 13.7 %collective-permute-done.73 = bf16[4,217,768]{2,0,1:T(4,128)(2,1)S(1)} collective-permute-done((bf16[4,217,768]{2,0,1:T(4,128)(2,1)S(1)}, bf16[4,217,768]{2,0,1:T(4,128)(2,1)S(1)}, u32[]{:S(2)}, u32[]{:S(2)}) %collective-permute-start.73) | collective-permute-done | bytes 1333280 | tf_op jit(solution)/shard_map/ppermute | solution.py:439
  647.1 32.2 %collective-permute-done.72 = bf16[4,217,768]{2,0,1:T(4,128)(2,1)S(1)} collective-permute-done((bf16[4,217,768]{2,0,1:T(4,128)(2,1)S(1)}, bf16[4,217,768]{2,0,1:T(4,128)(2,1)S(1)}, u32[]{:S(2)}, u32[]{:S(2)}) %collective-permute-start.72) | collective-permute-done | bytes 1333280 | tf_op jit(solution)/shard_map/ppermute | solution.py:439
  684.8 9.4 %collective-permute-done.54 = bf16[4,64,768]{2,1,0:T(8,128)(2,1)S(1)} collective-permute-done((bf16[4,64,768]{2,1,0:T(8,128)(2,1)S(1)}, bf16[4,64,768]{2,1,0:T(8,128)(2,1)S(1)}, u32[]{:S(2)}, u32[]{:S(2)}) %collective-permute-start.54) | collective-permute-done | bytes 393248 | tf_op jit(solution)/shard_map/ppermute | solution.py:439
  698.1 9.0 %collective-permute-done.76 = bf16[217,768]{1,0:T(8,128)(2,1)S(1)} collective-permute-done((bf16[217,768]{1,0:T(8,128)(2,1)S(1)}, bf16[217,768]{1,0:T(8,128)(2,1)S(1)}, u32[]{:S(2)}, u32[]{:S(2)}) %collective-permute-start.76) | collective-permute-done | bytes 333344 | tf_op jit(solution)/shard_map/ppermute | solution.py:436
  707.1 4.7 collective-permute-done.75
  (599 shorter events, 320.4 us)
Async XLA Ops:
  10.5 67.9 %collective-permute-start.14 = (bf16[49,1536]{1,0:T(8,128)(2,1)}, bf16[49,1536]{1,0:T(8,128)(2,1)}, u32[]{:S(2)}, u32[]{:S(2)}) collective-permute-start(bf16[49,1536]{1,0:T(8,128)(2,1)} %get-tuple-element.155), channel_id=1, source_target_pairs={{0,4},{1,5},{2,6},{3,7},{4,0},{5,1},{6,2},{7,3},{8,12},{9,13},{10,... | collective-permute-start | bytes 451592 | tf_op jit(solution)/shard_map/ppermute | solution.py:436
  10.5 70.2 %collective-permute-start.15 = (bf16[49,1536]{1,0:T(8,128)(2,1)}, bf16[49,1536]{1,0:T(8,128)(2,1)}, u32[]{:S(2)}, u32[]{:S(2)}) collective-permute-start(bf16[49,1536]{1,0:T(8,128)(2,1)} %get-tuple-element.155), channel_id=1, source_target_pairs={{0,8},{1,9},{2,10},{3,11},{4,12},{5,13},{6,14},{7,15},{8,0},{9,1},... | collective-permute-start | bytes 451592 | tf_op jit(solution)/shard_map/ppermute | solution.py:436
  13.0 70.0 %collective-permute-start.16 = (bf16[49,1536]{1,0:T(8,128)(2,1)}, bf16[49,1536]{1,0:T(8,128)(2,1)}, u32[]{:S(2)}, u32[]{:S(2)}) collective-permute-start(bf16[49,1536]{1,0:T(8,128)(2,1)} %get-tuple-element.155), channel_id=1, source_target_pairs={{0,12},{1,13},{2,14},{3,15},{4,8},{5,9},{6,10},{7,11},{8,4},{9,5},... | collective-permute-start | bytes 451592 | tf_op jit(solution)/shard_map/ppermute | solution.py:436
  13.2 44.5 %collective-permute-start.8 = (s32[2,13]{1,0:T(2,128)}, s32[2,13]{1,0:T(2,128)S(1)}, u32[]{:S(2)}, u32[]{:S(2)}) collective-permute-start(s32[2,13]{1,0:T(2,128)} %param.28), channel_id=1, source_target_pairs={{0,16},{16,0},{1,17},{17,1},{2,18},{18,2},{3,19},{19,3},{4,20},{20... | collective-permute-start | bytes 320 | tf_op jit(solution)/shard_map/ppermute | solution.py:433
  16.3 45.8 %collective-permute-start.28 = (bf16[96,768]{1,0:T(8,128)(2,1)}, bf16[96,768]{1,0:T(8,128)(2,1)}, u32[]{:S(2)}, u32[]{:S(2)}) collective-permute-start(bf16[96,768]{1,0:T(8,128)(2,1)} %get-tuple-element.153), channel_id=1, source_target_pairs={{0,4},{1,5},{2,6},{3,7},{4,0},{5,1},{6,2},{7,3},{8,12},{9,13},{10,... | collective-permute-start | bytes 442376 | tf_op jit(solution)/shard_map/ppermute | solution.py:436
  70.0 34.2 %collective-permute-start.21 = (bf16[48,1920]{1,0:T(8,128)(2,1)S(1)}, bf16[48,1920]{1,0:T(8,128)(2,1)S(1)}, u32[]{:S(2)}, u32[]{:S(2)}) collective-permute-start(bf16[48,1920]{1,0:T(8,128)(2,1)S(1)} %copy-done.42), channel_id=1, source_target_pairs={{0,4},{1,5},{2,6},{3,7},{4,0},{5,1},{6,2},{7,3},{8,12},{9,13},{10,... | collective-permute-start | bytes 552968 | tf_op jit(solution)/shard_map/ppermute | solution.py:436
  83.0 34.0 %collective-permute-start = (bf16[2,65,768]{2,1,0:T(8,128)(2,1)S(1)}, bf16[2,65,768]{2,1,0:T(8,128)(2,1)S(1)}, u32[]{:S(2)}, u32[]{:S(2)}) collective-permute-start(bf16[2,65,768]{2,1,0:T(8,128)(2,1)S(1)} %get-tuple-element.109), channel_id=1, source_target_pairs={{0,16},{16,0},{1,17},{17,1},{2,18},{18,2},{3,19},{19,3},{4,20},{20... | collective-permute-start | bytes 599048 | tf_op jit(solution)/shard_map/ppermute | solution.py:433
  107.2 79.2 %collective-permute-start.31 = (bf16[4,96,768]{2,1,0:T(8,128)(2,1)}, bf16[4,96,768]{2,1,0:T(8,128)(2,1)}, u32[]{:S(2)}, u32[]{:S(2)}) collective-permute-start(bf16[4,96,768]{2,1,0:T(8,128)(2,1)} %bitcast_dynamic-update-slice_fusion.21), channel_id=1, source_target_pairs={{0,1},{1,0},{2,3},{3,2},{4,5},{5,4},{6,7},{7,6},{8,9},{9,8},{10,11... | collective-permute-start | bytes 1769480 | tf_op jit(solution)/shard_map/ppermute | solution.py:439
  111.5 78.4 %collective-permute-start.32 = (bf16[4,96,768]{2,1,0:T(8,128)(2,1)}, bf16[4,96,768]{2,1,0:T(8,128)(2,1)}, u32[]{:S(2)}, u32[]{:S(2)}) collective-permute-start(bf16[4,96,768]{2,1,0:T(8,128)(2,1)} %bitcast_dynamic-update-slice_fusion.21), channel_id=1, source_target_pairs={{0,2},{1,3},{2,0},{3,1},{4,6},{5,7},{6,4},{7,5},{8,10},{9,11},{10,... | collective-permute-start | bytes 1769480 | tf_op jit(solution)/shard_map/ppermute | solution.py:439
  155.0 36.8 %collective-permute-start.33 = (bf16[4,96,768]{2,1,0:T(8,128)(2,1)}, bf16[4,96,768]{2,1,0:T(8,128)(2,1)S(1)}, u32[]{:S(2)}, u32[]{:S(2)}) collective-permute-start(bf16[4,96,768]{2,1,0:T(8,128)(2,1)} %bitcast_dynamic-update-slice_fusion.21), channel_id=1, source_target_pairs={{0,3},{1,2},{2,1},{3,0},{4,7},{5,6},{6,5},{7,4},{8,11},{9,10},{10,... | collective-permute-start | bytes 1769480 | tf_op jit(solution)/shard_map/ppermute | solution.py:439
  162.3 33.5 %collective-permute-start.17 = (bf16[4,49,1536]{2,0,1:T(4,128)(2,1)}, bf16[4,49,1536]{2,0,1:T(4,128)(2,1)S(1)}, u32[]{:S(2)}, u32[]{:S(2)}) collective-permute-start(bf16[4,49,1536]{2,0,1:T(4,128)(2,1)} %dynamic_update_slice.224), channel_id=1, source_target_pairs={{0,1},{1,0},{2,3},{3,2},{4,5},{5,4},{6,7},{7,6},{8,9},{9,8},{10,11... | collective-permute-start | bytes 1806344 | tf_op jit(solution)/shard_map/ppermute | solution.py:439
  186.4 35.0 %collective-permute-start.19 = (bf16[4,49,1536]{2,0,1:T(4,128)(2,1)}, bf16[4,49,1536]{2,0,1:T(4,128)(2,1)S(1)}, u32[]{:S(2)}, u32[]{:S(2)}) collective-permute-start(bf16[4,49,1536]{2,0,1:T(4,128)(2,1)} %dynamic_update_slice.224), channel_id=1, source_target_pairs={{0,3},{1,2},{2,1},{3,0},{4,7},{5,6},{6,5},{7,4},{8,11},{9,10},{10,... | collective-permute-start | bytes 1806344 | tf_op jit(solution)/shard_map/ppermute | solution.py:439
  189.9 55.5 %collective-permute-start.24 = (bf16[4,48,1920]{2,1,0:T(8,128)(2,1)}, bf16[4,48,1920]{2,1,0:T(8,128)(2,1)}, u32[]{:S(2)}, u32[]{:S(2)}) collective-permute-start(bf16[4,48,1920]{2,1,0:T(8,128)(2,1)} %bitcast_dynamic-update-slice_fusion.17), channel_id=1, source_target_pairs={{0,1},{1,0},{2,3},{3,2},{4,5},{5,4},{6,7},{7,6},{8,9},{9,8},{10,11... | collective-permute-start | bytes 2211848 | tf_op jit(solution)/shard_map/ppermute | solution.py:439
  191.8 55.6 %collective-permute-start.25 = (bf16[4,48,1920]{2,1,0:T(8,128)(2,1)}, bf16[4,48,1920]{2,1,0:T(8,128)(2,1)}, u32[]{:S(2)}, u32[]{:S(2)}) collective-permute-start(bf16[4,48,1920]{2,1,0:T(8,128)(2,1)} %bitcast_dynamic-update-slice_fusion.17), channel_id=1, source_target_pairs={{0,2},{1,3},{2,0},{3,1},{4,6},{5,7},{6,4},{7,5},{8,10},{9,11},{10,... | collective-permute-start | bytes 2211848 | tf_op jit(solution)/shard_map/ppermute | solution.py:439
  195.8 53.7 %collective-permute-start.26 = (bf16[4,48,1920]{2,1,0:T(8,128)(2,1)}, bf16[4,48,1920]{2,1,0:T(8,128)(2,1)}, u32[]{:S(2)}, u32[]{:S(2)}) collective-permute-start(bf16[4,48,1920]{2,1,0:T(8,128)(2,1)} %bitcast_dynamic-update-slice_fusion.17), channel_id=1, source_target_pairs={{0,3},{1,2},{2,1},{3,0},{4,7},{5,6},{6,5},{7,4},{8,11},{9,10},{10,... | collective-permute-start | bytes 2211848 | tf_op jit(solution)/shard_map/ppermute | solution.py:439
  197.6 54.5 %collective-permute-start.7 = (bf16[4,4,65,768]{3,1,2,0:T(4,128)(2,1)}, bf16[4,4,65,768]{3,1,2,0:T(4,128)(2,1)}, u32[]{:S(2)}, u32[]{:S(2)}) collective-permute-start(bf16[4,4,65,768]{3,1,2,0:T(4,128)(2,1)} %copy.288), channel_id=1, source_target_pairs={{0,16},{16,0},{1,17},{17,1},{2,18},{18,2},{3,19},{19,3},{4,20},{20... | collective-permute-start | bytes 4792328 | tf_op jit(solution)/shard_map/ppermute | solution.py:433
  221.4 124.8 %collective-permute-start.34 = (bf16[1536,768]{1,0:T(8,128)(2,1)}, bf16[1536,768]{1,0:T(8,128)(2,1)}, u32[]{:S(2)}, u32[]{:S(2)}) collective-permute-start(bf16[1536,768]{1,0:T(8,128)(2,1)} %bitcast.81), channel_id=1, source_target_pairs={{0,16},{16,0},{1,17},{17,1},{2,18},{18,2},{3,19},{19,3},{4,20},{20... | collective-permute-start | bytes 7077896 | tf_op jit(solution)/shard_map/ppermute | solution.py:433
  251.6 85.9 %collective-permute-start.27 = (bf16[768,1920]{1,0:T(8,128)(2,1)}, bf16[768,1920]{1,0:T(8,128)(2,1)}, u32[]{:S(2)}, u32[]{:S(2)}) collective-permute-start(bf16[768,1920]{1,0:T(8,128)(2,1)} %bitcast.404), channel_id=1, source_target_pairs={{0,16},{16,0},{1,17},{17,1},{2,18},{18,2},{3,19},{19,3},{4,20},{20... | collective-permute-start | bytes 8847368 | tf_op jit(solution)/shard_map/ppermute | solution.py:433
  389.7 33.0 %collective-permute-start.36 = (bf16[64,768]{1,0:T(8,128)(2,1)}, bf16[64,768]{1,0:T(8,128)(2,1)}, u32[]{:S(2)}, u32[]{:S(2)}) collective-permute-start(bf16[64,768]{1,0:T(8,128)(2,1)} %get-tuple-element.140), channel_id=1, source_target_pairs={{0,8},{1,9},{2,10},{3,11},{4,12},{5,13},{6,14},{7,15},{8,0},{9,1},... | collective-permute-start | bytes 294920 | tf_op jit(solution)/shard_map/ppermute | solution.py:436
  393.9 32.3 %collective-permute-start.37 = (bf16[64,768]{1,0:T(8,128)(2,1)}, bf16[64,768]{1,0:T(8,128)(2,1)}, u32[]{:S(2)}, u32[]{:S(2)}) collective-permute-start(bf16[64,768]{1,0:T(8,128)(2,1)} %get-tuple-element.139), channel_id=1, source_target_pairs={{0,12},{1,13},{2,14},{3,15},{4,8},{5,9},{6,10},{7,11},{8,4},{9,5},... | collective-permute-start | bytes 294920 | tf_op jit(solution)/shard_map/ppermute | solution.py:436
  395.4 139.0 %collective-permute-start.39 = (bf16[64,768]{1,0:T(8,128)(2,1)}, bf16[64,768]{1,0:T(8,128)(2,1)}, u32[]{:S(2)}, u32[]{:S(2)}) collective-permute-start(bf16[64,768]{1,0:T(8,128)(2,1)} %get-tuple-element.135), channel_id=1, source_target_pairs={{0,4},{1,5},{2,6},{3,7},{4,0},{5,1},{6,2},{7,3},{8,12},{9,13},{10,... | collective-permute-start | bytes 294920 | tf_op jit(solution)/shard_map/ppermute | solution.py:436
  396.6 153.0 %collective-permute-start.40 = (bf16[64,768]{1,0:T(8,128)(2,1)}, bf16[64,768]{1,0:T(8,128)(2,1)}, u32[]{:S(2)}, u32[]{:S(2)}) collective-permute-start(bf16[64,768]{1,0:T(8,128)(2,1)} %get-tuple-element.134), channel_id=1, source_target_pairs={{0,8},{1,9},{2,10},{3,11},{4,12},{5,13},{6,14},{7,15},{8,0},{9,1},... | collective-permute-start | bytes 294920 | tf_op jit(solution)/shard_map/ppermute | solution.py:436
  421.1 134.7 %collective-permute-start.41 = (bf16[64,768]{1,0:T(8,128)(2,1)S(1)}, bf16[64,768]{1,0:T(8,128)(2,1)S(1)}, u32[]{:S(2)}, u32[]{:S(2)}) collective-permute-start(bf16[64,768]{1,0:T(8,128)(2,1)S(1)} %copy-done.43), channel_id=1, source_target_pairs={{0,12},{1,13},{2,14},{3,15},{4,8},{5,9},{6,10},{7,11},{8,4},{9,5},... | collective-permute-start | bytes 294920 | tf_op jit(solution)/shard_map/ppermute | solution.py:436
  426.2 183.2 %collective-permute-start.70 = (bf16[16,217,768]{2,0,1:T(8,128)(2,1)}, bf16[16,217,768]{2,0,1:T(8,128)(2,1)}, u32[]{:S(2)}, u32[]{:S(2)}) collective-permute-start(bf16[16,217,768]{2,0,1:T(8,128)(2,1)} %pad_maximum_fusion.1), channel_id=1, source_target_pairs={{0,16},{16,0},{1,17},{17,1},{2,18},{18,2},{3,19},{19,3},{4,20},{20... | collective-permute-start | bytes 15998984 | tf_op jit(solution)/shard_map/ppermute | solution.py:433
  522.0 82.0 %collective-permute-start.52 = (bf16[24,64,768]{2,1,0:T(8,128)(2,1)}, bf16[24,64,768]{2,1,0:T(8,128)(2,1)}, u32[]{:S(2)}, u32[]{:S(2)}) collective-permute-start(bf16[24,64,768]{2,1,0:T(8,128)(2,1)} %maximum_bitcast_fusion), channel_id=1, source_target_pairs={{0,16},{16,0},{1,17},{17,1},{2,18},{18,2},{3,19},{19,3},{4,20},{20... | collective-permute-start | bytes 7077896 | tf_op jit(solution)/shard_map/ppermute | solution.py:433
  549.6 31.6 %collective-permute-start.65 = (bf16[4,49,1536]{2,0,1:T(4,128)(2,1)S(1)}, bf16[4,49,1536]{2,0,1:T(4,128)(2,1)S(1)}, u32[]{:S(2)}, u32[]{:S(2)}) collective-permute-start(bf16[4,49,1536]{2,0,1:T(4,128)(2,1)S(1)} %bitcast.431), channel_id=1, source_target_pairs={{0,2},{1,3},{2,0},{3,1},{4,6},{5,7},{6,4},{7,5},{8,10},{9,11},{10,... | collective-permute-start | bytes 1806344 | tf_op jit(solution)/shard_map/ppermute | solution.py:439
  599.2 127.8 %collective-permute-start.42 = (bf16[2,64,768]{2,1,0:T(8,128)(2,1)S(1)}, bf16[2,64,768]{2,1,0:T(8,128)(2,1)}, u32[]{:S(2)}, u32[]{:S(2)}) collective-permute-start(bf16[2,64,768]{2,1,0:T(8,128)(2,1)S(1)} %get-tuple-element.132), channel_id=1, source_target_pairs={{0,16},{16,0},{1,17},{17,1},{2,18},{18,2},{3,19},{19,3},{4,20},{20... | collective-permute-start | bytes 589832 | tf_op jit(solution)/shard_map/ppermute | solution.py:433
  617.9 61.4 %collective-permute-start.72 = (bf16[4,217,768]{2,0,1:T(4,128)(2,1)S(1)}, bf16[4,217,768]{2,0,1:T(4,128)(2,1)S(1)}, u32[]{:S(2)}, u32[]{:S(2)}) collective-permute-start(bf16[4,217,768]{2,0,1:T(4,128)(2,1)S(1)} %copy.336), channel_id=1, source_target_pairs={{0,2},{1,3},{2,0},{3,1},{4,6},{5,7},{6,4},{7,5},{8,10},{9,11},{10,... | collective-permute-start | bytes 3999752 | tf_op jit(solution)/shard_map/ppermute | solution.py:439
  621.1 59.0 %collective-permute-start.71 = (bf16[4,217,768]{2,0,1:T(4,128)(2,1)S(1)}, bf16[4,217,768]{2,0,1:T(4,128)(2,1)S(1)}, u32[]{:S(2)}, u32[]{:S(2)}) collective-permute-start(bf16[4,217,768]{2,0,1:T(4,128)(2,1)S(1)} %copy.334), channel_id=1, source_target_pairs={{0,1},{1,0},{2,3},{3,2},{4,5},{5,4},{6,7},{7,6},{8,9},{9,8},{10,11... | collective-permute-start | bytes 3999752 | tf_op jit(solution)/shard_map/ppermute | solution.py:439
  632.1 51.8 %collective-permute-start.55 = (bf16[4,64,768]{2,1,0:T(8,128)(2,1)S(1)}, bf16[4,64,768]{2,1,0:T(8,128)(2,1)S(1)}, u32[]{:S(2)}, u32[]{:S(2)}) collective-permute-start(bf16[4,64,768]{2,1,0:T(8,128)(2,1)S(1)} %get-tuple-element.75), channel_id=1, source_target_pairs={{0,3},{1,2},{2,1},{3,0},{4,7},{5,6},{6,5},{7,4},{8,11},{9,10},{10,... | collective-permute-start | bytes 1179656 | tf_op jit(solution)/shard_map/ppermute | solution.py:439
  646.8 47.4 %collective-permute-start.54 = (bf16[4,64,768]{2,1,0:T(8,128)(2,1)S(1)}, bf16[4,64,768]{2,1,0:T(8,128)(2,1)S(1)}, u32[]{:S(2)}, u32[]{:S(2)}) collective-permute-start(bf16[4,64,768]{2,1,0:T(8,128)(2,1)S(1)} %get-tuple-element.76), channel_id=1, source_target_pairs={{0,2},{1,3},{2,0},{3,1},{4,6},{5,7},{6,4},{7,5},{8,10},{9,11},{10,... | collective-permute-start | bytes 1179656 | tf_op jit(solution)/shard_map/ppermute | solution.py:439
  680.1 48.7 %collective-permute-start.63 = (bf16[2,64,768]{2,1,0:T(8,128)(2,1)}, bf16[2,64,768]{2,1,0:T(8,128)(2,1)}, u32[]{:S(2)}, u32[]{:S(2)}) collective-permute-start(bf16[2,64,768]{2,1,0:T(8,128)(2,1)} %get-tuple-element.111), channel_id=1, source_target_pairs={{0,16},{16,0},{1,17},{17,1},{2,18},{18,2},{3,19},{19,3},{4,20},{20... | collective-permute-start | bytes 589832 | tf_op jit(solution)/shard_map/ppermute | solution.py:433
  (106 other events, 1168.5 us)

commit v2 on v1

v2 whole, which is shorter than its diff:
```python
import functools
import math

import jax
import jax.numpy as jnp
from jax import lax
from jax.experimental import pallas as pl
from jax.experimental.pallas import tpu as pltpu
from jax.sharding import PartitionSpec as P

DH = 64
NS = 13
EPSILON = 1e-05
NEG = -1e30
F32 = jnp.float32
BF = jnp.bfloat16
HIGHEST = lax.Precision.HIGHEST

R = 128
KB = 256
W = R + KB
SCALE = DH**-0.5
LOG2E = 1.4426950408889634
LN2 = 0.6931471805599453
ONES = 32


def mm(a, b, ca=1, cb=0, precision=None):
    return lax.dot_general(
        a, b, (((ca,), (cb,)), ((), ())), preferred_element_type=F32, precision=precision
    )


def row_features(seg_col):
    lane = lax.broadcasted_iota(jnp.int32, (2 * R, 128), 1)
    folded = jnp.where(lane < NS, lane, lane - NS).astype(F32)
    return jnp.where((lane < 2 * NS) & (folded == seg_col), 1.0, 0.0)


def live_list(live_ref, list_ref, row, nkb):
    per = KB // R

    def step(kb, count):
        list_ref[count] = kb
        live = live_ref[row, kb * per]
        for i in range(1, per):
            live = jnp.maximum(live, live_ref[row, kb * per + i])
        return count + live

    return lax.fori_loop(0, nkb, step, 0)


def ordered(kernel, count, extra):
    def run(*refs):
        kernel(*refs[:count], *refs[count + extra :])

    return run


def forward_kernel(
    nkb,
    base_ref,
    live_ref,
    q_ref,
    vec_ref,
    table_ref,
    info_ref,
    reach_ref,
    kv_ref,
    hot_ref,
    rel_ref,
    rank_ref,
    p_ref,
    o_ref,
    inv_ref,
    ob_ref,
    qq_scr,
    qr_scr,
    s_scr,
    m_scr,
    acc_scr,
    list_scr,
):
    block = pl.program_id(0)
    row = base_ref[0] + base_ref[1] * block
    base = nkb * KB - R - R * row
    count = live_list(live_ref, list_scr, row, nkb)
    seg_col = info_ref[:, 0:1]
    limit = info_ref[:, 1:2]
    hot_row = row_features(seg_col)
    lane = lax.broadcasted_iota(jnp.int32, (2 * R, 128), 1)
    reach = mm(jnp.where(lane < NS, hot_row, 0.0).astype(BF), reach_ref[...])
    outside = jnp.where((lane < 2 * NS) & (reach < 0.5), NEG, 0.0)
    zero = jnp.zeros((2 * R, DH), BF)
    for h in range(2):
        half = slice(DH * h, DH * h + DH)
        q = q_ref[:, half]
        plain = ((q + vec_ref[0:1, half]) * (SCALE * LOG2E)).astype(BF)
        place = ((q + vec_ref[1:2, half]) * (SCALE * LOG2E)).astype(BF)
        label = q + vec_ref[2:3, half]
        same = mm(label, table_ref[h, 0], precision=HIGHEST)
        other = mm(label, table_ref[h, 1], precision=HIGHEST)
        term = jnp.where(hot_row > 0.5, same, other) * (SCALE * LOG2E) + outside
        high = term.astype(BF).astype(F32)
        extra = jnp.where(lane < NS, high, jnp.where(lane < 2 * NS, term - high, 0.0))
        side = lambda x: [x, zero] if h == 0 else [zero, x]
        qq_scr[h] = jnp.concatenate(side(plain) + [extra.astype(BF)], axis=1)
        qr_scr[h] = jnp.concatenate(side(place), axis=1)
    m_scr[...] = jnp.full(m_scr.shape, -jnp.inf, F32)
    acc_scr[...] = jnp.zeros(acc_scr.shape, F32)

    def score(n, carry):
        k0 = pl.multiple_of(list_scr[n] * KB, KB)
        ok = rank_ref[:, pl.ds(k0, KB)] <= limit
        window = rel_ref[pl.ds(pl.multiple_of(base + k0, 128), W), :]
        keys = jnp.concatenate([kv_ref[pl.ds(k0, KB), :128], hot_ref[pl.ds(k0, KB), :]], axis=1)
        for h in range(2):
            s = mm(qq_scr[h], keys, 1, 1)
            full = mm(qr_scr[h], window, 1, 1)
            shifted = [
                pltpu.roll(full[i * R : i * R + R], W - (R - 1), 1, stride=1, stride_axis=0)[
                    :, :KB
                ]
                for i in range(2)
            ]
            s = jnp.where(ok, s + jnp.concatenate(shifted, axis=0), NEG)
            s_scr[h, n] = s
            m_scr[h] = jnp.maximum(m_scr[h], jnp.maximum(s[:, :128], s[:, 128:]))
        return carry

    lax.fori_loop(0, count, score, 0)
    top = [jnp.max(m_scr[h], axis=1, keepdims=True) for h in range(2)]

    def mix(n, carry):
        k0 = pl.multiple_of(list_scr[n] * KB, KB)
        values = jnp.concatenate([kv_ref[pl.ds(k0, KB), 128:], hot_ref[pl.ds(k0, KB), :]], axis=1)
        for h in range(2):
            p = jnp.exp2(s_scr[h, n] - top[h]).astype(BF)
            p_ref[0, h, n] = p
            acc_scr[h] += mm(p, values)
        return carry

    lax.fori_loop(0, count, mix, 0)
    for h in range(2):
        half = slice(DH * h, DH * h + DH)
        acc = acc_scr[h]
        inverse = 1.0 / acc[:, 128 + ONES : 129 + ONES]
        mixed = acc[:, half] * inverse
        o_ref[:, half] = mixed
        ob_ref[:, half] = mixed.astype(BF)
        inv_ref[:, half] = jnp.broadcast_to(inverse, (2 * R, DH))


def attend_forward(pair, after, base, live, q, vec, table, info, reach, kv, hot, rel, rank):
    nb = q.shape[0] // (2 * R)
    length = kv.shape[0]
    nkb = length // KB
    whole = lambda *shape: pl.BlockSpec(shape, lambda b, *_: (0,) * len(shape))
    return pl.pallas_call(
        ordered(functools.partial(forward_kernel, nkb), 11, len(after)),
        grid_spec=pltpu.PrefetchScalarGridSpec(
            num_scalar_prefetch=2,
            grid=(nb,),
            in_specs=[
                pl.BlockSpec((2 * R, 128), lambda b, *_: (b, pair)),
                pl.BlockSpec((8, 128), lambda b, *_: (0, pair)),
                pl.BlockSpec((2, 2, DH, 128), lambda b, *_: (pair, 0, 0, 0)),
                pl.BlockSpec((2 * R, 128), lambda b, *_: (b, 0)),
                whole(128, 128),
                pl.BlockSpec((length, 256), lambda b, *_: (0, pair)),
                whole(length, 128),
                pl.BlockSpec((2 * length, 128), lambda b, *_: (0, pair)),
                whole(1, length),
            ]
            + [pl.BlockSpec(memory_space=pl.ANY)] * len(after),
            out_specs=[
                pl.BlockSpec((1, 2, nkb, 2 * R, KB), lambda b, *_: (b, 0, 0, 0, 0)),
                pl.BlockSpec((2 * R, 128), lambda b, *_: (b, 0)),
                pl.BlockSpec((2 * R, 128), lambda b, *_: (b, 0)),
                pl.BlockSpec((2 * R, 128), lambda b, *_: (b, 0)),
            ],
            scratch_shapes=[
                pltpu.VMEM((2, 2 * R, 256), BF),
                pltpu.VMEM((2, 2 * R, 128), BF),
                pltpu.VMEM((2, nkb, 2 * R, KB), F32),
                pltpu.VMEM((2, 2 * R, 128), F32),
                pltpu.VMEM((2, 2 * R, 256), F32),
                pltpu.SMEM((nkb + 1,), jnp.int32),
            ],
        ),
        out_shape=[
            jax.ShapeDtypeStruct((nb, 2, nkb, 2 * R, KB), BF),
            jax.ShapeDtypeStruct((q.shape[0], 128), F32),
            jax.ShapeDtypeStruct((q.shape[0], 128), F32),
            jax.ShapeDtypeStruct((q.shape[0], 128), BF),
        ],
        compiler_params=pltpu.CompilerParams(
            dimension_semantics=("arbitrary",), vmem_limit_bytes=58 * 2**20
        ),
        cost_estimate=pl.CostEstimate(
            flops=10**8, bytes_accessed=10**6, transcendentals=0
        ),
        name="attend_forward",
    )(base, live, q, vec, table, info, reach, kv, hot, rel, rank, *after)


def backward_kernel(
    nkb,
    nb,
    base_ref,
    live_ref,
    p_ref,
    q_ref,
    g_ref,
    o_ref,
    inv_ref,
    vec_ref,
    info_ref,
    kv_ref,
    hot_ref,
    rel_ref,
    dq_ref,
    dkv_ref,
    drel_ref,
    small_ref,
    qq_scr,
    qr_scr,
    dd_scr,
    acc_scr,
    accr_scr,
    dkv_scr,
    drel_scr,
    flip_scr,
    list_scr,
):
    block = pl.program_id(0)
    length = nkb * KB
    row = base_ref[0] + base_ref[1] * block
    base = nkb * KB - R - R * row
    count = live_list(live_ref, list_scr, row, nkb)

    @pl.when(block == 0)
    def start():
        dkv_scr[...] = jnp.zeros(dkv_scr.shape, F32)
        drel_scr[...] = jnp.zeros(drel_scr.shape, F32)
        small_ref[...] = jnp.zeros(small_ref.shape, F32)
        down = lax.broadcasted_iota(jnp.int32, (KB, KB), 0)
        across = lax.broadcasted_iota(jnp.int32, (KB, KB), 1)
        flip_scr[...] = jnp.where(down + across == KB - 1, 1.0, 0.0).astype(BF)

    lane = lax.broadcasted_iota(jnp.int32, (2 * R, 128), 1)
    zero = jnp.zeros((2 * R, DH), BF)
    for h in range(2):
        half = slice(DH * h, DH * h + DH)
        q = q_ref[:, half]
        plain = ((q + vec_ref[0:1, half]) * (SCALE * LOG2E)).astype(BF)
        place = ((q + vec_ref[1:2, half]) * (SCALE * LOG2E)).astype(BF)
        g = g_ref[:, half].astype(F32)
        inverse = inv_ref[:, DH * h : DH * h + 1]
        delta = -jnp.sum(g * o_ref[:, half], axis=1, keepdims=True) * inverse
        high = delta.astype(BF).astype(F32)
        extra = jnp.where(lane == ONES, high, jnp.where(lane == ONES + 1, delta - high, 0.0))
        side = lambda x: [x, zero] if h == 0 else [zero, x]
        qq_scr[h] = jnp.concatenate(side(plain), axis=1)
        qr_scr[h] = jnp.concatenate(side(place), axis=1)
        dd_scr[h] = jnp.concatenate(side((g * inverse).astype(BF)) + [extra.astype(BF)], axis=1)
    acc_scr[...] = jnp.zeros(acc_scr.shape, F32)
    accr_scr[...] = jnp.zeros(accr_scr.shape, F32)

    def step(n, carry):
        k0 = pl.multiple_of(list_scr[n] * KB, KB)
        r0 = pl.multiple_of(2 * length - base - k0 - W, 128)
        hot = hot_ref[pl.ds(k0, KB), :]
        window = rel_ref[pl.ds(r0, W), :]
        pad = jnp.zeros((R, W - KB), F32)
        keys = jnp.concatenate([kv_ref[pl.ds(k0, KB), :128], hot], axis=1)
        values = jnp.concatenate([kv_ref[pl.ds(k0, KB), 128:], hot], axis=1)
        d_keys = d_values = d_rel = 0.0
        for h in range(2):
            p = p_ref[0, h, n]
            dd = dd_scr[h]
            ds = (p.astype(F32) * mm(dd, values, 1, 1)).astype(BF)
            acc_scr[h] += mm(ds, keys)
            turned = mm(ds, flip_scr[...])
            full = [
                pltpu.roll(
                    jnp.concatenate([turned[i * R : i * R + R], pad], axis=1),
                    0,
                    1,
                    stride=1,
                    stride_axis=0,
                )
                for i in range(2)
            ]
            full = jnp.concatenate(full, axis=0).astype(BF)
            accr_scr[h] += mm(full, window)
            d_rel += mm(full, qr_scr[h], 0, 0)
            d_keys += mm(ds, qq_scr[h], 0, 0)
            d_values += mm(p, dd[:, :128], 0, 0)
        drel_scr[pl.ds(r0, W), :] += d_rel
        dkv_scr[pl.ds(k0, KB), :128] += d_keys
        dkv_scr[pl.ds(k0, KB), 128:] += d_values
        return carry

    lax.fori_loop(0, count, step, 0)
    hot_row = row_features(info_ref[:, 0:1])
    for h in range(2):
        half = slice(DH * h, DH * h + DH)
        acc = acc_scr[h]
        d_plain = acc[:, half] * SCALE
        d_place = accr_scr[h][:, half] * SCALE
        sums = jnp.where(lane < NS, acc[:, 128:], 0.0) * SCALE
        same = jnp.sum(sums * hot_row, axis=1, keepdims=True)
        other = jnp.sum(sums, axis=1, keepdims=True) - same
        d_label = same * vec_ref[3:4, half] + other * vec_ref[4:5, half]
        label = q_ref[:, half] + vec_ref[2:3, half]
        dq_ref[:, half] = (d_plain + d_place + d_label).astype(BF)
        terms = [d_plain, d_place, d_label, same * label, other * label]
        for row, term in enumerate(terms):
            small_ref[row : row + 1, half] += jnp.sum(term, axis=0, keepdims=True)

    @pl.when(block == nb - 1)
    def finish():
        across = lax.broadcasted_iota(jnp.int32, (length, 256), 1)
        factor = jnp.where(across < 128, LN2, 1.0)
        dkv_ref[...] = (dkv_scr[...] * factor).astype(BF)
        drel_ref[...] = (drel_scr[...] * LN2).astype(BF)


def attend_backward(pair, after, base, live, p, q, g, o, inv, vec, info, kv, hot, rel):
    nb = q.shape[0] // (2 * R)
    length = kv.shape[0]
    nkb = length // KB
    own = pl.BlockSpec((2 * R, 128), lambda b, *_: (b, 0))
    rows = pl.BlockSpec((2 * R, 128), lambda b, *_: (b, pair))
    return pl.pallas_call(
        ordered(functools.partial(backward_kernel, nkb, nb), 12, len(after)),
        grid_spec=pltpu.PrefetchScalarGridSpec(
            num_scalar_prefetch=2,
            grid=(nb,),
            in_specs=[
                pl.BlockSpec((1, 2, nkb, 2 * R, KB), lambda b, *_: (b, 0, 0, 0, 0)),
                rows,
                rows,
                own,
                own,
                pl.BlockSpec((8, 128), lambda b, *_: (0, pair)),
                pl.BlockSpec((2 * R, 128), lambda b, *_: (b, 0)),
                pl.BlockSpec((length, 256), lambda b, *_: (0, pair)),
                pl.BlockSpec((length, 128), lambda b, *_: (0, 0)),
                pl.BlockSpec((2 * length, 128), lambda b, *_: (0, pair)),
            ]
            + [pl.BlockSpec(memory_space=pl.ANY)] * len(after),
            out_specs=[
                own,
                pl.BlockSpec((length, 256), lambda b, *_: (0, 0)),
                pl.BlockSpec((2 * length, 128), lambda b, *_: (0, 0)),
                pl.BlockSpec((8, 128), lambda b, *_: (0, 0)),
            ],
            scratch_shapes=[
                pltpu.VMEM((2, 2 * R, 128), BF),
                pltpu.VMEM((2, 2 * R, 128), BF),
                pltpu.VMEM((2, 2 * R, 256), BF),
                pltpu.VMEM((2, 2 * R, 256), F32),
                pltpu.VMEM((2, 2 * R, 128), F32),
                pltpu.VMEM((length, 256), F32),
                pltpu.VMEM((2 * length, 128), F32),
                pltpu.VMEM((KB, KB), BF),
                pltpu.SMEM((nkb + 1,), jnp.int32),
            ],
        ),
        out_shape=[
            jax.ShapeDtypeStruct((q.shape[0], 128), BF),
            jax.ShapeDtypeStruct((length, 256), BF),
            jax.ShapeDtypeStruct((2 * length, 128), BF),
            jax.ShapeDtypeStruct((8, 128), F32),
        ],
        compiler_params=pltpu.CompilerParams(
            dimension_semantics=("arbitrary",), vmem_limit_bytes=58 * 2**20
        ),
        cost_estimate=pl.CostEstimate(
            flops=10**8, bytes_accessed=10**6, transcendentals=0
        ),
        name="attend_backward",
    )(base, live, p, q, g, o, inv, vec, info, kv, hot, rel, *after)


def whole_block(x):
    return pl.BlockSpec(x.shape, lambda i: (0,) * len(x.shape))


def pack_kernel(r, ws, low_ref, content_ref, seg_ref, rank_ref, flag_ref, parent_ref, *refs):
    vec_refs, weight_refs, (a_ref, b_ref, scr) = refs[:4], refs[4:8], refs[8:]
    low = low_ref[0]
    for e, out in enumerate((a_ref, b_ref)):
        tree = jnp.bitwise_xor(low, e)
        out[:r, :] = content_ref[tree]
        scr[...] = jnp.zeros(scr.shape, F32)
        row = lambda ref: ref[pl.ds(tree, 1), :]
        rank = row(rank_ref)
        scr[0:1, :r] = row(seg_ref).astype(F32)
        scr[0:1, r : 2 * r] = lax.shift_right_logical(rank, 6).astype(F32)
        scr[0:1, 2 * r : 3 * r] = jnp.bitwise_and(rank, 63).astype(F32)
        scr[0:1, 3 * r : 4 * r] = row(flag_ref).astype(F32)
        scr[0:1, 4 * r : 4 * r + NS] = row(parent_ref).astype(F32)
        for i in range(3):
            scr[i + 1 : i + 2, :ws] = vec_refs[i][...].astype(F32)
        scr[4:6, :ws] = vec_refs[3][...].astype(F32)
        out[r : r + 16, :] = scr[...].astype(BF)
        for i in range(4):
            out[r + 16 + i * ws : r + 16 + (i + 1) * ws, :] = weight_refs[i][...]


def pack(low, content, segs, ranks, flags, parents, vecs, weights):
    trees, r, d = content.shape
    ws = weights[0].shape[0]
    shape = jax.ShapeDtypeStruct((r + 16 + 4 * ws, d), BF)
    return pl.pallas_call(
        functools.partial(pack_kernel, r, ws),
        grid=(1,),
        in_specs=[pl.BlockSpec(memory_space=pltpu.SMEM), whole_block(content)]
        + [whole_block(x) for x in (segs, ranks, flags, parents, *vecs, *weights)],
        out_specs=[whole_block(shape)] * 2,
        out_shape=[shape, shape],
        scratch_shapes=[pltpu.VMEM((16, d), F32)],
        compiler_params=pltpu.CompilerParams(vmem_limit_bytes=24 * 2**20),
        name="pack",
    )(low, content, segs, ranks, flags, parents, *vecs, *weights)


def assemble_kernel(r, ws, dh, m, at_ref, a0, a1, t0, t1, q_own, q_other, *outs):
    content_ref, codes_ref, wq_ref, wkv_ref, wr_ref, inputs_ref = outs
    k, low, c = at_ref[0], at_ref[1], at_ref[2]
    h, zl = pl.program_id(0), pl.program_id(1)
    column = lambda start: pl.multiple_of(k * dh + start, 128)

    def fill(src, query):
        inputs_ref[0, 0, 0] = src[0, :r, :]
        inputs_ref[0, 0, 1] = query[...]
        for step in range(m):
            to = jnp.bitwise_xor(c, step)
            rows = lambda i: slice(r + 16 + i * ws, r + 16 + (i + 1) * ws)
            content_ref[0, 0, to] = src[step, :r, :]
            codes_ref[0, 0, to] = src[step, r : r + 16, :]
            wq_ref[0, 0, to] = src[step, rows(0), pl.ds(column(0), dh)]
            wr_ref[0, 0, to] = src[step, rows(3), pl.ds(column(0), dh)]
            for p in range(dh // 128):
                for i in range(2):
                    wkv_ref[0, 0, to, :, 256 * p + 128 * i : 256 * p + 128 * i + 128] = src[
                        step, rows(1 + i), pl.ds(column(128 * p), 128)
                    ]

    for mine in (True, False):
        for e in range(2):
            src = ((a0, a1) if mine else (t0, t1))[e]
            query = (q_own if mine else q_other).at[e]

            @pl.when(((h == k) == mine) & (jnp.bitwise_xor(zl, low) == e))
            def case(src=src, query=query):
                fill(src, query)


def assemble(at, near_rows, their_rows, q_own, q_other, r, ws):
    m, rows, d = near_rows[0].shape
    dh = d // 2
    sizes = [(m, r, d), (m, 16, d), (m, ws, dh), (m, ws, d), (m, ws, dh), (2, r, d)]
    return pl.pallas_call(
        functools.partial(assemble_kernel, r, ws, dh, m),
        grid=(2, 2),
        in_specs=[pl.BlockSpec(memory_space=pltpu.SMEM)]
        + [pl.BlockSpec((m, rows, d), lambda h, z: (0, 0, 0))] * 4
        + [pl.BlockSpec((2, r, d), lambda h, z: (0, 0, 0))] * 2,
        out_specs=[pl.BlockSpec((1, 1) + size, lambda h, z: (h, z, 0, 0, 0)) for size in sizes],
        out_shape=[jax.ShapeDtypeStruct((2, 2) + size, BF) for size in sizes],
        compiler_params=pltpu.CompilerParams(vmem_limit_bytes=48 * 2**20),
        name="assemble",
    )(at, *near_rows, *their_rows, q_own, q_other)


def pack_late_kernel(ws, w1_ref, wo_ref, w2_ref, *refs):
    vec_refs, out, scr = refs[:-2], refs[-2], refs[-1]
    d = wo_ref.shape[1]
    parts = w1_ref.shape[1] // d
    for j in range(parts):
        out[j * ws : (j + 1) * ws, :] = w1_ref[:, j * d : (j + 1) * d]
    out[parts * ws : (parts + 1) * ws, :] = wo_ref[...]
    out[(parts + 1) * ws : (2 * parts + 1) * ws, :] = w2_ref[...]
    scr[...] = jnp.zeros(scr.shape, F32)
    row = 0
    for ref in vec_refs:
        scr[row : row + ref.shape[0], :ws] = ref[...].astype(F32)
        row += ref.shape[0]
    out[(2 * parts + 1) * ws :, :] = scr[...].astype(BF)


def pack_late(w1, wo, w2, vecs):
    ws, d = wo.shape
    rows = ws + w1.shape[1] // d * ws + w2.shape[0] + 16
    return pl.pallas_call(
        functools.partial(pack_late_kernel, ws),
        grid=(1,),
        in_specs=[whole_block(x) for x in (w1, wo, w2, *vecs)],
        out_specs=pl.BlockSpec((rows, d), lambda i: (0, 0)),
        out_shape=jax.ShapeDtypeStruct((rows, d), BF),
        scratch_shapes=[pltpu.VMEM((16, d), F32)],
        compiler_params=pltpu.CompilerParams(vmem_limit_bytes=24 * 2**20),
        name="pack_late",
    )(w1, wo, w2, *vecs)


def assemble_late_kernel(ws, m, at_ref, *refs):
    mine_refs, their_refs, (w1_ref, wo_ref, w2_ref, vec_ref) = refs[:m], refs[m : 2 * m], refs[2 * m :]
    k, low, c = at_ref[0], at_ref[1], at_ref[2]
    h, zl = pl.program_id(0), pl.program_id(1)
    d = wo_ref.shape[-1]
    parts = w1_ref.shape[-1] // d
    e = jnp.bitwise_xor(zl, low)

    def fill(refs):
        for step, src in enumerate(refs):
            to = jnp.bitwise_xor(c, step)
            for j in range(parts):
                w1_ref[0, 0, to, :, j * d : (j + 1) * d] = src[e, j * ws : (j + 1) * ws, :]
            wo_ref[0, 0, to] = src[e, parts * ws : (parts + 1) * ws, :]
            w2_ref[0, 0, to] = src[e, (parts + 1) * ws : (2 * parts + 1) * ws, :]
            vec_ref[0, 0, to] = src[e, (2 * parts + 1) * ws :, :]

    @pl.when(h == k)
    def own():
        fill(mine_refs)

    @pl.when(h != k)
    def other():
        fill(their_refs)


def assemble_late(at, mine, theirs, ws, parts):
    m = len(mine)
    two, rows, d = mine[0].shape
    sizes = [(m, ws, parts * d), (m, ws, d), (m, parts * ws, d), (m, 16, d)]
    return pl.pallas_call(
        functools.partial(assemble_late_kernel, ws, m),
        grid=(2, 2),
        in_specs=[pl.BlockSpec(memory_space=pltpu.SMEM)]
        + [pl.BlockSpec((2, rows, d), lambda h, z: (0, 0, 0))] * (2 * m),
        out_specs=[pl.BlockSpec((1, 1) + size, lambda h, z: (h, z, 0, 0, 0)) for size in sizes],
        out_shape=[jax.ShapeDtypeStruct((2, 2) + size, BF) for size in sizes],
        compiler_params=pltpu.CompilerParams(vmem_limit_bytes=56 * 2**20),
        name="assemble_late",
    )(at, *mine, *theirs)


def relative_kernel(sa_ref, ca_ref, sb_ref, cb_ref, w_ref, pos_ref, rel_ref, turned_ref):
    half = sb_ref.shape[1]
    fine = sb_ref.shape[0]
    for i in range(KB // fine):
        rows = slice(i * fine, (i + 1) * fine)
        sa, ca = sa_ref[0, i : i + 1, :], ca_ref[0, i : i + 1, :]
        sine = sa * cb_ref[...] - ca * sb_ref[...]
        cosine = ca * cb_ref[...] + sa * sb_ref[...]
        pos_ref[rows, :half] = sine.astype(BF)
        pos_ref[rows, half:] = cosine.astype(BF)
    from_sine = mm(pos_ref[:, :half], w_ref[:half, :])
    from_cosine = mm(pos_ref[:, half:], w_ref[half:, :])
    rel_ref[...] = (from_cosine + from_sine).astype(BF)
    turned_ref[...] = (from_cosine - from_sine).astype(BF)


def relative(wr, length):
    d, width = wr.shape
    half, fine = d // 2, 64
    powers = jnp.arange(half, dtype=F32) * (2.0 / d)
    inverse_freq = 1.0 / 10000.0**powers
    coarse = (length - 1 - fine * jnp.arange(2 * length // fine, dtype=jnp.int32)).astype(F32)
    a = coarse[:, None] * inverse_freq[None]
    b = jnp.arange(fine, dtype=F32)[:, None] * inverse_freq[None]
    per = KB // fine
    tables = [jnp.sin(a).reshape(-1, per, half), jnp.cos(a).reshape(-1, per, half), jnp.sin(b), jnp.cos(b)]
    rows = lambda w: pl.BlockSpec((KB, w), lambda i: (i, 0))
    return pl.pallas_call(
        relative_kernel,
        grid=(2 * length // KB,),
        in_specs=[pl.BlockSpec((1, per, half), lambda i: (i, 0, 0))] * 2
        + [pl.BlockSpec((fine, half), lambda i: (0, 0))] * 2
        + [pl.BlockSpec((d, width), lambda i: (0, 0))],
        out_specs=[rows(d), rows(width), rows(width)],
        out_shape=[
            jax.ShapeDtypeStruct((2 * length, d), BF),
            jax.ShapeDtypeStruct((2 * length, width), BF),
            jax.ShapeDtypeStruct((2 * length, width), BF),
        ],
        compiler_params=pltpu.CompilerParams(vmem_limit_bytes=24 * 2**20),
        cost_estimate=pl.CostEstimate(
            flops=4 * length * d * width, bytes_accessed=8 * length * d, transcendentals=0
        ),
        name="relative",
    )(*tables, wr)


def input_grad_kernel(count, at_ref, *refs):
    parts, w_ref, out_ref = refs[:count], refs[count], refs[-1]
    total = 0.0
    start = 0
    for ref in parts:
        width = ref.shape[1]
        total += mm(ref[...], w_ref[:, start : start + width], 1, 1)
        start += width
    out_ref[...] = total.astype(out_ref.dtype)


def input_grad(half, parts, w, dtype, after):
    rows = parts[0].shape[0] // 2
    block = math.gcd(rows, 256)
    d = w.shape[0]
    return pl.pallas_call(
        ordered(functools.partial(input_grad_kernel, len(parts)), len(parts) + 2, len(after)),
        grid_spec=pltpu.PrefetchScalarGridSpec(
            num_scalar_prefetch=1,
            grid=(rows // block,),
            in_specs=[
                pl.BlockSpec((block, x.shape[1]), lambda i, at: (at[0] * (rows // block) + i, 0))
                for x in parts
            ]
            + [pl.BlockSpec(w.shape, lambda i, at: (0, 0))]
            + [pl.BlockSpec(memory_space=pl.ANY)] * len(after),
            out_specs=pl.BlockSpec((block, d), lambda i, at: (i, 0)),
        ),
        out_shape=jax.ShapeDtypeStruct((rows, d), dtype),
        compiler_params=pltpu.CompilerParams(vmem_limit_bytes=24 * 2**20),
        cost_estimate=pl.CostEstimate(
            flops=2 * rows * d * w.shape[1], bytes_accessed=4 * rows * d, transcendentals=0
        ),
        name="input_grad",
    )(half, *parts, w, *after)


def mask_kernel(n, m, r, c_ref, codes_ref, rank_ref, hot_ref, info_ref, reach_ref, live_ref):
    c = c_ref[0]
    iota = lambda shape, axis: lax.broadcasted_iota(jnp.int32, shape, axis)
    choose = iota((n, 16 * n), 1) == 16 * iota((n, 16 * n), 0)
    rows = mm(choose.astype(F32).astype(BF), codes_ref[...])
    part = lambda i: rows[:, i * r : (i + 1) * r]
    segs = part(0)
    ranks = part(1) * 64.0 + part(2)
    flags = part(3)
    seg_cols, rank_cols, flag_cols = segs.T, ranks.T, flags.T
    parent_col = rows[:, 4 * r : 4 * r + 128].T[:, 0:1]
    lane = iota((128, 128), 1)
    down = iota((128, 128), 0)
    feature = jnp.where(lane < NS, lane, jnp.where(lane < 2 * NS, lane - NS, -1))
    folded = feature.astype(F32)
    ones_lane = (lane == ONES) | (lane == ONES + 1)
    for i in range(n):
        rank_ref[0:1, i * r : (i + 1) * r] = ranks[i : i + 1, :]
        hit = (folded == seg_cols[:, i : i + 1]) | ones_lane
        hot_ref[i * r : (i + 1) * r, :] = jnp.where(hit, 1.0, 0.0).astype(BF)
    mine = iota((r, n), 1)
    for b in range(n // m):
        column = lambda x: jnp.sum(jnp.where(mine == b * m + c, x, 0.0), axis=1, keepdims=True)
        seg, limit = column(seg_cols), column(rank_cols)
        lower = limit - column(flag_cols)
        for i, value in enumerate((limit, lower)):
            start = (2 * b + i) * r
            info_ref[start : start + r, :] = jnp.where(lane == 0, seg, value)
    inside = (down < NS) & (lane < NS)
    link = inside & ((down == lane) | (parent_col == lane.astype(F32)))
    reached = jnp.where(link, 1.0, 0.0)
    for repeat in range(4):
        half = reached.astype(BF)
        reached = jnp.minimum(mm(half, half), 1.0)
    reached = reached.astype(BF)
    twice = jnp.where(down == feature, 1.0, 0.0).astype(BF)
    reach_ref[...] = mm(reached, twice).astype(BF)
    spot = iota((n, 128), 1)
    present = jnp.zeros((n, 128), F32)
    for t in range(NS):
        any_t = jnp.max(jnp.where(segs == t, 1.0, 0.0), axis=1, keepdims=True)
        present = jnp.where(spot == t, any_t, present)
    present = present.astype(BF)
    seen = jnp.minimum(mm(present, reached), 1.0).astype(BF)
    live_ref[...] = jnp.minimum(mm(seen, present, 1, 1), 1.0).astype(jnp.int32)


def masks(c, codes, m, r):
    n, length = codes.shape[0] // 16, codes.shape[0] // 16 * r
    return pl.pallas_call(
        functools.partial(mask_kernel, n, m, r),
        grid=(1,),
        in_specs=[pl.BlockSpec(memory_space=pltpu.SMEM), whole_block(codes)],
        out_specs=[
            pl.BlockSpec(size, lambda i: (0, 0))
            for size in ((1, length), (length, 128), (n // m * 2 * r, 128), (128, 128), (n, n))
        ],
        out_shape=[
            jax.ShapeDtypeStruct((1, length), F32),
            jax.ShapeDtypeStruct((length, 128), BF),
            jax.ShapeDtypeStruct((n // m * 2 * r, 128), F32),
            jax.ShapeDtypeStruct((128, 128), BF),
            jax.ShapeDtypeStruct((n, n), jnp.int32),
        ],
        compiler_params=pltpu.CompilerParams(vmem_limit_bytes=24 * 2**20),
        name="masks",
    )(c, codes)


def hold_kernel(a_ref, b_ref, out_ref):
    out_ref[0] = a_ref[...]
    out_ref[1] = b_ref[...]


def hold(a, b, after):
    spec = pl.BlockSpec(a.shape, lambda i: (0, 0))
    return pl.pallas_call(
        ordered(hold_kernel, 2, len(after)),
        grid=(1,),
        in_specs=[spec, spec] + [pl.BlockSpec(memory_space=pl.ANY)] * len(after),
        out_specs=pl.BlockSpec((2,) + a.shape, lambda i: (0, 0, 0)),
        out_shape=jax.ShapeDtypeStruct((2,) + a.shape, a.dtype),
        compiler_params=pltpu.CompilerParams(vmem_limit_bytes=24 * 2**20),
        name="hold",
    )(a, b, *after)


def proj_grad_kernel(count, steps, x_ref, c_ref, pos_ref, *refs):
    dq, dkv, drel = refs[:count], refs[count : 2 * count], refs[2 * count : 3 * count]
    extra = refs[3 * count : -4]
    out_ref, q_scr, kv_scr, r_scr = refs[-4:]
    i = pl.program_id(0)

    @pl.when(i == 0)
    def start():
        for scr in (q_scr, kv_scr, r_scr):
            scr[...] = jnp.zeros(scr.shape, F32)

    for p in range(count):
        r_scr[p] += mm(drel[p][...], pos_ref[...], 0, 0)

    @pl.when(i < steps[1])
    def keys():
        for p in range(count):
            kv_scr[p] += mm(dkv[p][...], c_ref[...], 0, 0)

    @pl.when(i < steps[0])
    def queries():
        for p in range(count):
            q_scr[p] += mm(dq[p][...], x_ref[...], 0, 0)

    @pl.when(i == steps[2] - 1)
    def finish():
        d = pos_ref.shape[1]
        lane = lax.broadcasted_iota(jnp.int32, (128, d), 1)
        for p in range(count):
            at = 512 * p
            out_ref[:, at : at + 128] = q_scr[p].T.astype(BF)
            out_ref[:, at + 128 : at + 384] = kv_scr[p].T.astype(BF)
            turned = jnp.where(lane < d // 2, -r_scr[p], r_scr[p])
            out_ref[:, at + 384 : at + 512] = turned.T.astype(BF)
        for ref in extra:
            out_ref[:, 512 * count :] = ref[...]


def proj_grads(x, content, position, parts, extra, after):
    count = len(parts)
    d = x.shape[1]
    steps = [a.shape[0] // KB for a in (x, content, position)]
    spec = lambda width, kind: pl.BlockSpec(
        (KB, width), lambda i: (jnp.minimum(i, steps[kind] - 1), 0)
    )
    operands = [x, content, position]
    specs = [spec(d, kind) for kind in range(3)]
    for index, width, kind in ((0, 128, 0), (1, 256, 1), (2, 128, 2)):
        operands += [b[index] for b in parts]
        specs += [spec(width, kind)] * count
    operands += extra
    specs += [pl.BlockSpec(e.shape, lambda i: (0, 0)) for e in extra]
    width = 512 * count + sum(e.shape[1] for e in extra)
    total = len(operands)
    return pl.pallas_call(
        ordered(functools.partial(proj_grad_kernel, count, steps), total, len(after)),
        grid=(steps[2],),
        in_specs=specs + [pl.BlockSpec(memory_space=pl.ANY)] * len(after),
        out_specs=pl.BlockSpec((d, width), lambda i: (0, 0)),
        out_shape=jax.ShapeDtypeStruct((d, width), BF),
        scratch_shapes=[
            pltpu.VMEM((count, 128, d), F32),
            pltpu.VMEM((count, 256, d), F32),
            pltpu.VMEM((count, 128, d), F32),
        ],
        compiler_params=pltpu.CompilerParams(vmem_limit_bytes=32 * 2**20),
        cost_estimate=pl.CostEstimate(flops=10**9, bytes_accessed=10**6, transcendentals=0),
        name="proj_grads",
    )(*operands, *after)


def add_kernel(count, *refs):
    total = refs[0][...].astype(F32)
    for ref in refs[1:count]:
        total += ref[...].astype(F32)
    refs[-1][...] = total.astype(refs[-1].dtype)


def add_up(parts, dtype, after):
    shape = parts[0].shape
    rows = parts[0].size // shape[-1]
    flat = [x.reshape(rows, shape[-1]) for x in parts]
    block = rows // 2 if rows % 32 == 0 else rows
    spec = pl.BlockSpec((block, shape[-1]), lambda i: (i, 0))
    out = pl.pallas_call(
        ordered(functools.partial(add_kernel, len(parts)), len(parts), len(after)),
        grid=(rows // block,),
        in_specs=[spec] * len(parts) + [pl.BlockSpec(memory_space=pl.ANY)] * len(after),
        out_specs=spec,
        out_shape=jax.ShapeDtypeStruct((rows, shape[-1]), dtype),
        compiler_params=pltpu.CompilerParams(vmem_limit_bytes=32 * 2**20),
        cost_estimate=pl.CostEstimate(flops=rows, bytes_accessed=10**6, transcendentals=0),
        name="add_up",
    )(*flat, *after)
    return out.reshape(shape)


def layer_norm(vector, gain_row, shift_row):
    average = jnp.mean(vector, axis=-1, keepdims=True)
    centred = vector - average
    variance = jnp.mean(centred * centred, axis=-1, keepdims=True)
    return centred * lax.rsqrt(variance + EPSILON) * gain_row + shift_row


def gelu_tanh(vector):
    return jax.nn.gelu(vector, approximate=True)


def position_rows(offsets, model_width):
    half_width = model_width // 2
    powers = jnp.arange(half_width, dtype=F32) * (2.0 / model_width)
    inverse_freq = 1.0 / 10000.0**powers
    angles = offsets[:, None] * inverse_freq[None, :]
    return jnp.concatenate([jnp.sin(angles), jnp.cos(angles)], axis=1)


def body(
    content_in,
    query_in,
    segment_ids,
    parent_ids,
    rank_order,
    query_flags,
    query_weight,
    key_weight,
    value_weight,
    relative_weight,
    output_weight,
    inner_weight,
    outer_weight,
    inner_bias,
    outer_bias,
    attend_gain,
    attend_shift,
    feed_gain,
    feed_shift,
    content_bias,
    position_bias,
    segment_bias,
    segment_table,
    content_cot,
    query_cot,
):
    n = lax.axis_size("shard")
    nr = lax.axis_size("rep")
    trees, r, d = content_in.shape
    groups = 2 * trees
    m = n // groups
    length = r * n
    nkb = length // KB
    ff = inner_weight.shape[1]
    dh = d // 2
    heads = dh // DH
    pairs = heads // 2
    ws = query_weight.shape[0]
    fs = outer_weight.shape[0]
    me = lax.axis_index("shard")
    g, c = me // m, me % m
    low = g % 2
    k = lax.axis_index("rep") % 2
    first = k == 0
    tie = lax.optimization_barrier

    def swap(x):
        return lax.ppermute(x, "rep", [(i, i ^ 1) for i in range(nr)])

    def far(x, step):
        return lax.ppermute(x, "shard", [(i, i ^ (m * step)) for i in range(n)])

    def near(x, step):
        return lax.ppermute(x, "shard", [(i, i ^ step) for i in range(n)])

    def across(x, e):
        moves = []
        for i in range(nr):
            for j in range(n):
                z = j // m
                to = (i - i % 2 + z // 2) * n + (2 * (i % 2) + (z % 2 ^ e)) * m + j % m
                moves.append((i * n + j, to))
        return lax.ppermute(x, ("rep", "shard"), moves)

    def pick(x, index, axis=0):
        return lax.dynamic_index_in_dim(x, index, axis, keepdims=False)

    def put(buffer, x, index, axis=0):
        return lax.dynamic_update_index_in_dim(buffer, x, index, axis)

    def pair_of(mine, other, index, axis=0):
        return put(jnp.stack([mine, mine], axis), other, 1 - index, axis)

    def cross(parts):
        got = [across(pick(parts, low ^ e), e) for e in range(2)]
        return pair_of(got[0], got[1], low)

    def near_gather(x, downward):
        bits = [b for b in range(m.bit_length() - 1)]
        held = {0: x}
        for b in bits[::-1] if downward else bits:
            held.update({o | 1 << b: near(y, 1 << b) for o, y in list(held.items())})
        return jnp.stack([held[o] for o in range(m)])

    def near_parts(x, axis):
        sent = [near(pick(x, c ^ step, axis), step) for step in range(1, m)]
        return [pick(x, c, axis)] + sent

    def far_sum(x):
        total = pick(x, g).astype(F32)
        for step in range(1, groups):
            total = total + far(pick(x, g ^ step), step).astype(F32)
        return total

    weights = [query_weight, key_weight, value_weight, relative_weight]
    low_array = low.astype(jnp.int32).reshape(1)
    vec_rows = [x.reshape(1, ws) for x in (content_bias, position_bias, segment_bias)]
    packed = pack(
        low_array,
        content_in,
        segment_ids,
        rank_order,
        query_flags,
        parent_ids,
        vec_rows + [segment_table],
        weights,
    )
    at = jnp.stack([k, low, c]).astype(jnp.int32)
    got = [across(packed[e], e) for e in range(2)]
    own_query = jnp.stack([across(pick(query_in, low ^ e), e) for e in range(2)])
    near_rows = [near_gather(got[e], e) for e in range(2)]
    their_rows = [swap(x) for x in near_rows]
    content_full, codes, wq, kv_weight, wr, inputs = assemble(
        at, near_rows, their_rows, own_query, swap(own_query), r, ws
    )
    content_full = content_full.reshape(length, d)
    wq, kv_weight, wr = wq.reshape(d, dh), kv_weight.reshape(d, d), wr.reshape(d, dh)
    own_inputs = pick(inputs, k).reshape(groups * r, d)
    inputs = inputs.reshape(groups * 2 * r, d)
    codes = codes.reshape(n, 16, d)
    key_ranks, hot, info, reach, live = masks(
        c.astype(jnp.int32).reshape(1), codes.reshape(n * 16, d), m, r
    )
    base = jnp.stack([c, m]).astype(jnp.int32)
    vectors = codes[:, 1:6, :ws].astype(F32).swapaxes(0, 1).reshape(5, 2, dh)
    head_vecs = jnp.where(first, vectors[:, 0], vectors[:, 1])

    late_pack = pack_late(
        inner_weight,
        output_weight,
        outer_weight,
        [x.reshape(1, ws) for x in (outer_bias, attend_gain, attend_shift, feed_gain, feed_shift)]
        + [inner_bias.reshape(fs // ws, ws)],
    )
    late_pack, unused = tie((late_pack, got[1]))
    late = [across(late_pack, e) for e in range(2)]
    content_cot, query_cot, unused = tie((content_cot, query_cot, content_full))
    cots = cross(jnp.stack([content_cot, query_cot], axis=1))

    position_bf, rel, rel_turned = relative(wr, length)
    queries = mm(inputs, wq)
    kv = mm(content_full, kv_weight).astype(BF)
    vec8 = jnp.pad(head_vecs, ((0, 3), (0, 0)))
    table = head_vecs[3:5].reshape(2, heads, DH).swapaxes(0, 1)
    table = jnp.where(jnp.arange(128) < 2 * NS, table[..., None], 0.0)
    late = hold(late[0], late[1], [content_full, wr])
    late_near = [late] + [near(late, step) for step in range(1, m)]
    late_theirs = [swap(x) for x in late_near]
    forward = []
    got_mixed = []
    for pair in range(pairs):
        after = [[late], [], late_near + [cots]][min(pair, 2)]
        after = after + [f[1] for f in forward[-1:]]
        forward.append(
            attend_forward(
                pair,
                after,
                base,
                live,
                queries,
                vec8,
                table,
                info,
                reach,
                kv,
                hot,
                rel,
                key_ranks,
            )
        )
        got_mixed.append(swap(pick(forward[-1][3].reshape(2, groups * r, 128), 1 - k)))

    inner_w, output_w, outer_w, vecs = assemble_late(at, late_near, late_theirs, ws, ff // d)
    inner_w, output_w = inner_w.reshape(d, ff), output_w.reshape(d, d)
    outer_w = outer_w.reshape(ff, d)
    vecs = vecs.reshape(n, 16, d)[:, : 5 + fs // ws, :ws].astype(F32)
    inner_shift = vecs[:, 5:].reshape(ff)
    vecs = vecs[:, :5].swapaxes(0, 1).reshape(5, d)
    outer_shift, gain_one, shift_one, gain_two, shift_two = [vecs[i] for i in range(5)]

    own_mixed = [pick(f[3].reshape(2, groups * r, 128), k) for f in forward]
    mixed_bf = jnp.where(
        first,
        jnp.concatenate(own_mixed + got_mixed, axis=1),
        jnp.concatenate(got_mixed + own_mixed, axis=1),
    )
    residual = mm(mixed_bf, output_w) + own_inputs.astype(F32)
    normed = layer_norm(residual, gain_one, shift_one)
    normed_bf = normed.astype(BF)
    inner_pre = mm(normed_bf, inner_w) + inner_shift
    hidden_bf = gelu_tanh(inner_pre).astype(BF)
    summed = mm(hidden_bf, outer_w) + outer_shift + normed
    result = layer_norm(summed, gain_two, shift_two).astype(BF).reshape(2, 2, r, d)
    outs = cross(result)
    cotangent = cots.reshape(groups * r, d).astype(F32)
    unused, final_back = jax.vjp(layer_norm, summed, gain_two, shift_two)
    grad_summed, grad_final_gain, grad_final_shift = final_back(cotangent)
    grad_summed_bf = grad_summed.astype(BF)
    unused, gelu_back = jax.vjp(gelu_tanh, inner_pre)
    (grad_inner,) = gelu_back(mm(grad_summed_bf, outer_w, 1, 1))
    grad_inner_bf = grad_inner.astype(BF)
    grad_normed = mm(grad_inner_bf, inner_w, 1, 1) + grad_summed
    unused, first_back = jax.vjp(layer_norm, residual, gain_one, shift_one)
    grad_residual, grad_norm_gain, grad_norm_shift = first_back(grad_normed)
    grad_residual_bf = grad_residual.astype(BF)
    grad_mixed = mm(grad_residual_bf, output_w, 1, 1).astype(BF)
    mine_grad = lax.dynamic_slice_in_dim(grad_mixed, k * dh, dh, 1)
    got_grad = swap(lax.dynamic_slice_in_dim(grad_mixed, (1 - k) * dh, dh, 1))
    grad_heads = pair_of(mine_grad, got_grad, k).reshape(groups * 2 * r, dh)

    grad_late = mm(hidden_bf, grad_summed_bf, 0, 0).astype(BF).reshape(2, ff // 2, d)
    row_vecs = jnp.stack(
        [
            jnp.sum(grad_summed, axis=0),
            grad_norm_gain,
            grad_norm_shift,
            grad_final_gain,
            grad_final_shift,
        ],
        axis=1,
    )
    inner_vecs = jnp.sum(grad_inner, axis=0).reshape(n, fs // ws, ws).swapaxes(1, 2)
    row_vecs = jnp.concatenate([row_vecs, inner_vecs.reshape(d, fs // ws)], axis=1)
    row_vecs = jnp.pad(row_vecs, ((0, 0), (0, 128 - row_vecs.shape[1])))
    grad_early = jnp.concatenate(
        [
            mm(normed_bf, grad_inner_bf, 0, 0).astype(BF),
            mm(mixed_bf, grad_residual_bf, 0, 0).astype(BF),
            row_vecs.astype(BF),
        ],
        axis=1,
    ).reshape(2, d // 2, ff + d + 128)

    def cross_parts(x):
        return [across(pick(x, low ^ e), e) for e in range(2)]

    backward = []

    def back(pair, after):
        f = forward[pair]
        after = after + [b[0] for b in backward[-1:]]
        backward.append(
            attend_backward(
                pair,
                after,
                base,
                live,
                f[0],
                queries,
                grad_heads,
                f[1],
                f[2],
                vec8,
                info,
                kv,
                hot,
                rel_turned,
            )
        )

    def half_sum(x, rows, after):
        half = add_up([pick(x, k), swap(pick(x, 1 - k))], BF, after)
        return half.reshape(2, m, rows, x.shape[-1])

    def proj_some(some, extra, after):
        return proj_grads(
            inputs, content_full, position_bf, [backward[p] for p in some], extra, after
        ).reshape(groups, m, ws, -1)

    late_half = half_sum(grad_late, fs, [])
    late_parts = near_parts(late_half, 1)
    back(0, [late_half])
    after = [backward[0][0]]
    late_near = add_up(late_parts, BF, after)
    late_cross = cross_parts(late_near)
    early_half = half_sum(grad_early, ws, after)
    early_parts = near_parts(early_half, 1)
    back(1, [early_half, late_near, outs])
    some_grads = proj_some(range(pairs - 1), [], early_parts[1:] + late_cross)
    some_parts = near_parts(some_grads, 1)
    early_near = add_up(early_parts, BF, [])
    early_cross = cross_parts(early_near)
    back(2, [early_near, some_grads])

    which = [jnp.asarray(x, jnp.int32).reshape(1) for x in (k, 1 - k)]
    dkv_parts = [b[1] for b in backward]
    dq_parts = [b[0] for b in backward]
    got_kv = swap(input_grad(which[1], dkv_parts, kv_weight, BF, some_parts[1:] + early_cross))
    got_q = swap(input_grad(which[1], dq_parts, wq, BF, []))
    own_kv = input_grad(which[0], dkv_parts, kv_weight, F32, [])
    own_q = input_grad(which[0], dq_parts, wq, F32, [])
    kv_sum = add_up([own_kv, got_kv], BF, [])
    content_parts = near_parts(kv_sum.reshape(2, m, r, d), 1)
    q_sum = own_q + got_q.astype(F32) + grad_residual
    q_sum = q_sum.reshape(2, 2, r, d)
    query_grads = cross(q_sum[:, 1].astype(BF))

    small = jnp.concatenate([b[3][:5] for b in backward], axis=1)
    small = jnp.where(
        first,
        jnp.concatenate([small, jnp.zeros_like(small)], axis=1),
        jnp.concatenate([jnp.zeros_like(small), small], axis=1),
    )
    small = jnp.pad(small.T, ((0, 0), (0, 128 - 5))).astype(BF)
    last_grads = proj_some([pairs - 1], [small], [kv_sum])
    last_parts = near_parts(last_grads, 1)
    late_sum = add_up(late_cross, BF, [kv_sum])
    early_sum = add_up(early_cross, BF, [kv_sum])
    late_total = late_sum.astype(F32) + swap(late_sum).astype(F32)
    content_sum = sum([x.astype(F32) for x in content_parts]) + q_sum[:, 0]
    content_grads = cross(content_sum.astype(BF))
    some_near, last_near = [
        sum([x.astype(F32) for x in parts]).astype(BF) for parts in (some_parts, last_parts)
    ]
    proj_sum = far_sum(jnp.concatenate([some_near, last_near], axis=2))

    early_total = early_sum.astype(F32) + swap(early_sum).astype(F32)
    bit = 2
    while bit < nr:
        turn = [(i, i ^ bit) for i in range(nr)]
        early_total = early_total + lax.ppermute(early_total, "rep", turn)
        late_total = late_total + lax.ppermute(late_total, "rep", turn)
        proj_sum = proj_sum + lax.ppermute(proj_sum, "rep", turn)
        bit *= 2
    proj_other = swap(proj_sum)
    halves = jnp.where(first, proj_sum, proj_other), jnp.where(first, proj_other, proj_sum)

    def columns(index):
        return jnp.concatenate(
            [
                x[:, 512 * p + 128 * index : 512 * p + 128 * index + 128]
                for x in halves
                for p in range(pairs)
            ],
            axis=1,
        )

    vec_cols = early_total[:, ff + d :]
    head_cols = (proj_sum + proj_other)[:, 512 * pairs :]
    return (
        outs[:, 0],
        outs[:, 1],
        content_grads,
        query_grads,
        columns(0),
        columns(1),
        columns(2),
        columns(3),
        early_total[:, ff : ff + d],
        early_total[:, :ff],
        late_total,
        vec_cols[:, 5 : 5 + fs // ws].T.reshape(fs),
        vec_cols[:, 0],
        vec_cols[:, 1],
        vec_cols[:, 2],
        vec_cols[:, 3],
        vec_cols[:, 4],
        head_cols[:, 0],
        head_cols[:, 1],
        head_cols[:, 2],
        head_cols[:, 3:5].T,
    )


def solution(mesh):
    in_specs = (
        P("rep", "shard", None),
        P("rep", "shard", None),
        P("rep", "shard"),
        P("rep", None),
        P("rep", "shard"),
        P("rep", "shard"),
        P("shard", None),
        P("shard", None),
        P("shard", None),
        P("shard", None),
        P("shard", None),
        P("shard", None),
        P("shard", None),
        P("shard"),
        P("shard"),
        P("shard"),
        P("shard"),
        P("shard"),
        P("shard"),
        P("shard"),
        P("shard"),
        P("shard"),
        P(None, "shard"),
        P("rep", "shard", None),
        P("rep", "shard", None),
    )
    out_specs = (
        P("rep", "shard", None),
        P("rep", "shard", None),
        P("rep", "shard", None),
        P("rep", "shard", None),
        P("shard", None),
        P("shard", None),
        P("shard", None),
        P("shard", None),
        P("shard", None),
        P("shard", None),
        P("shard", None),
        P("shard"),
        P("shard"),
        P("shard"),
        P("shard"),
        P("shard"),
        P("shard"),
        P("shard"),
        P("shard"),
        P("shard"),
        P(None, "shard"),
    )
    return jax.shard_map(body, mesh=mesh, in_specs=in_specs, out_specs=out_specs, check_vma=False)
```

time: 757 us -> 571 us (0.75)
  Pallas kernels: 132 us -> 215 us
  local copies, waits for them, and re-layouts: 163 us -> 85.5 us
  waiting for transfers between devices: 145 us -> 88.5 us
  starting transfers between devices: 149 us -> 93.4 us
  other arithmetic: 72.8 us -> 32.8 us
  matrix products: 82.3 us -> 44.2 us
    pallas_call x2 -> x26, Pallas kernels: 132 us -> 215 us  [the longest x3 96.3 us: attend_backward(): pl.pallas_call(ordered(functools.partial(backward_kernel, nkb, nb), 12, l...]
    ppermute x21 -> x24, waiting for transfers between devices: 103 us -> 37.8 us  [near(): return lax.ppermute(x, 'shard', [(i, i ^ step) for i in range(n)])]
    dynamic_update_slice x57 -> x5, local copies, waits for them, and re-layouts: 63 us -> 2.64 us  [put(): return lax.dynamic_update_index_in_dim(buffer, x, index, axis)]
    ppermute x39 -> x3, starting transfers between devices: 58.5 us -> 3.55 us  [far(): return lax.ppermute(x, 'shard', [(i, i ^ m * step) for i in range(n)])]
    ppermute x0 -> x18, waiting for transfers between devices: none -> 50.5 us  [across(): return lax.ppermute(x, ('rep', 'shard'), moves)]
    ppermute x18, starting transfers between devices: 51.5 us -> 4.42 us  [swap(): return lax.ppermute(x, 'rep', [(i, i ^ 1) for i in range(nr)])]
    ppermute x39 -> x3, waiting for transfers between devices: 42.4 us -> 0.01 us  [far(): return lax.ppermute(x, 'shard', [(i, i ^ m * step) for i in range(n)])]
    ppermute x0 -> x18, starting transfers between devices: none -> 41.9 us  [across(): return lax.ppermute(x, ('rep', 'shard'), moves)]
  transfers between devices with their start and end apart: 78 -> 63, of which waited for: 23 -> 17; matrix products, arithmetic and copies ran while one was open for 32% -> 11% of each run, Pallas kernels for 18% -> 35%
where the time goes in v2:
time: 571 us; the launch traced here: 562 us
  Pallas kernels  215 us (38%)
  starting transfers between devices  93.4 us (16%)
  waiting for transfers between devices  88.5 us (15%)
  local copies, waits for them, and re-layouts  85.5 us (15%)
  matrix products  44.2 us (8%)
  other arithmetic  32.8 us (6%)
    pallas_call x3, Pallas kernels, attend_backward(): pl.pallas_call(ordered(functools.partial(backward_kernel, nkb, nb), 12, l...  96.3 us
    pallas_call x3, Pallas kernels, attend_forward(): pl.pallas_call(ordered(functools.partial(forward_kernel, nkb), 11, len(af...  58.6 us
    unnamed x227, local copies, waits for them, and re-layouts  51.3 us
    ppermute x18, waiting for transfers between devices, across(): return lax.ppermute(x, ('rep', 'shard'), moves)  50.5 us
    dot_general x11, matrix products, mm(): lax.dot_general(a, b, (((ca,), (cb,)), ((), ())), preferred_element_type=...  44.2 us
    ppermute x24, starting transfers between devices, near(): return lax.ppermute(x, 'shard', [(i, i ^ step) for i in range(n)])  43.5 us
    ppermute x18, starting transfers between devices, across(): return lax.ppermute(x, ('rep', 'shard'), moves)  41.9 us
    ppermute x24, waiting for transfers between devices, near(): return lax.ppermute(x, 'shard', [(i, i ^ step) for i in range(n)])  37.8 us
  transfers between devices with their start and end apart: 63, of which 17 were waited for; matrix products, arithmetic and copies ran while one was open for 11% of the time, Pallas kernels for 35%

profile of v2, /device:TPU:9, one launch (start us, length us, event | category | flops | bytes accessed | tf_op | source)
XLA Modules:
  0.0 561.7 jit_solution(13703450027086150851)
XLA Ops:
  15.5 8.6 %collective-permute-done.4 = bf16[336,768]{1,0:T(8,128)(2,1)S(1)} collective-permute-done((bf16[336,768]{1,0:T(8,128)(2,1)S(1)}, bf16[336,768]{1,0:T(8,128)(2,1)S(1)}, u32[]{:S(2)}, u32[]{:S(2)}) %collective-permute-start.4) | collective-permute-done | bytes 516128 | tf_op jit(solution)/shard_map/ppermute | solution.py:903
  25.4 9.9 %collective-permute-done = bf16[336,768]{1,0:T(8,128)(2,1)S(1)} collective-permute-done((bf16[336,768]{1,0:T(8,128)(2,1)S(1)}, bf16[336,768]{1,0:T(8,128)(2,1)S(1)}, u32[]{:S(2)}, u32[]{:S(2)}) %collective-permute-start) | collective-permute-done | bytes 516128 | tf_op jit(solution)/shard_map/ppermute | solution.py:903
  39.5 9.5 %collective-permute-done.1 = bf16[336,768]{1,0:T(8,128)(2,1)S(1)} collective-permute-done((bf16[336,768]{1,0:T(8,128)(2,1)S(1)}, bf16[336,768]{1,0:T(8,128)(2,1)S(1)}, u32[]{:S(2)}, u32[]{:S(2)}) %collective-permute-start.1) | collective-permute-done | bytes 516128 | tf_op jit(solution)/shard_map/ppermute | solution.py:894
  49.3 7.6 %collective-permute-done.5 = bf16[336,768]{1,0:T(8,128)(2,1)S(1)} collective-permute-done((bf16[336,768]{1,0:T(8,128)(2,1)S(1)}, bf16[336,768]{1,0:T(8,128)(2,1)S(1)}, u32[]{:S(2)}, u32[]{:S(2)}) %collective-permute-start.5) | collective-permute-done | bytes 516128 | tf_op jit(solution)/shard_map/ppermute | solution.py:894
  56.9 5.5 collective-permute-done.7
  71.4 4.9 collective-permute-done.10
  80.9 5.9 %assemble.1 = (bf16[2,2,4,128,768]{4,3,2,1,0:T(8,128)(2,1)}, bf16[2,2,4,16,768]{4,3,2,1,0:T(8,128)(2,1)S(1)}, bf16[2,2,4,48,384]{4,3,2,1,0:T(8,128)(2,1)S(1)}, b...) custom-call(s32[3]{0:T(128)S(1)} %pad_add_fusion.1.at_ref, ...), custom_call_target="tpu_custom_call" | custom-call | tf_op jit(solution)/shard_map/assemble/pallas_call | solution.py:467
  86.9 15.3 %collective-permute-done.14.refs_1_ = bf16[448,768]{1,0:T(8,128)(2,1)S(1)} collective-permute-done((bf16[448,768]{1,0:T(8,128)(2,1)S(1)}, bf16[448,768]{1,0:T(8,128)(2,1)S(1)}, u32[]{:S(2)}, u32[]{:S(2)}) %collective-permute-start.14) | collective-permute-done | bytes 688160 | tf_op jit(solution)/shard_map/ppermute | solution.py:903
  102.1 4.4 collective-permute-done.13.refs_0_
  116.9 5.5 collective-permute-start.18
  130.7 6.4 %relative.1 = (bf16[4096,768]{1,0:T(8,128)(2,1)S(1)}, bf16[4096,384]{1,0:T(8,128)(2,1)S(1)}, bf16[4096,384]{1,0:T(8,128)(2,1)S(1)}) custom-call(f32[16,4,384]{2,1,0:T(4,128)S(1)} %copy-done.55, f32[16,4,384]{2,1,0:T(4,128)S(1)} %copy-done.54, f32[64,384]{1,0:T(8,128)S(1)} %copy-done.53, f32[64,384]{1,0:T(8,128)S(1)} %copy-done.52, bf16[768,384]{1,0:T(8,128)(2,1)S(1)} %bitcast.261), custom_call_target="tpu_custom_call" | custom-call | flops 2415919104 | bytes 12582912 | tf_op jit(solution)/shard_map/relative/pallas_call | solution.py:580
  148.2 19.5 %attend_forward.3 = (bf16[4,2,8,256,256]{4,3,2,1,0:T(8,128)(2,1)}, f32[1024,128]{1,0:T(8,128)}, f32[1024,128]{1,0:T(8,128)}, bf16[1024,128]{1,0:T(8,128)(2,1)}) custom-call(s32[2]{0:T(128)} %pad_add_fusion.refs_0_, s32[16,16]{1,0:T(8,128)} %copy-done.49, f32[1024,384]{1,0:T(8,128)} %fusion.59.refs_2_.refs_3_, f32[8,384]{1,0:T(8,128)} %pad.14.refs_3_.refs_7_, ...), custom_call_target="tpu_custom_call" | custom-call | flops 100000000 | bytes 1000000 | tf_op jit(solution)/shard_map/attend_forward/pallas_call | solution.py:159
  168.6 19.5 %attend_forward.4 = (bf16[4,2,8,256,256]{4,3,2,1,0:T(8,128)(2,1)}, f32[1024,128]{1,0:T(8,128)}, f32[1024,128]{1,0:T(8,128)}, bf16[1024,128]{1,0:T(8,128)(2,1)}) custom-call(s32[2]{0:T(128)} %pad_add_fusion.refs_0_, s32[16,16]{1,0:T(8,128)} %copy-done.49, f32[1024,384]{1,0:T(8,128)} %fusion.59.refs_2_.refs_3_, f32[8,384]{1,0:T(8,128)} %pad.14.refs_3_.refs_7_, ...), custom_call_target="tpu_custom_call" | custom-call | flops 100000000 | bytes 1000000 | tf_op jit(solution)/shard_map/attend_forward/pallas_call | solution.py:159
  195.4 19.6 %attend_forward.5 = (bf16[4,2,8,256,256]{4,3,2,1,0:T(8,128)(2,1)}, f32[1024,128]{1,0:T(8,128)}, f32[1024,128]{1,0:T(8,128)}, bf16[1024,128]{1,0:T(8,128)(2,1)}) custom-call(s32[2]{0:T(128)} %pad_add_fusion.refs_0_, s32[16,16]{1,0:T(8,128)} %copy-done.49, f32[1024,384]{1,0:T(8,128)} %fusion.59.refs_2_.refs_3_, f32[8,384]{1,0:T(8,128)} %pad.14.refs_3_.refs_7_, ...), custom_call_target="tpu_custom_call" | custom-call | flops 100000000 | bytes 1000000 | tf_op jit(solution)/shard_map/attend_forward/pallas_call | solution.py:159
  225.8 9.0 %assemble_late.1 = (bf16[2,2,4,48,3072]{4,3,2,1,0:T(8,128)(2,1)}, bf16[2,2,4,48,768]{4,3,2,1,0:T(8,128)(2,1)}, bf16[2,2,4,192,768]{4,3,2,1,0:T(8,128)(2,1)}, bf16[2,2,4,16,768]{4,3,2,1,0:T(8,128)(2,1)}) custom-call(s32[3]{0:T(128)} %copy-done.62, bf16[2,448,768]{2,1,0:T(8,128)(2,1)} %hold.1.refs_11_.refs_0_, ...), custom_call_target="tpu_custom_call" | custom-call | tf_op jit(solution)/shard_map/assemble_late/pallas_call | solution.py:541
  251.5 8.3 %fusion.58 = (bf16[3072]{0:T(1024)(128)(2,1)S(1)}, bf16[512,3072]{1,0:T(8,128)(2,1)S(1)}) fusion(f32[512,3072]{1,0:T(8,128)S(1)} %fusion.50, f32[3072]{0:T(1024)S(1)} %add.270, bf16[3072,768]{1,0:T(8,128)(2,1)S(1)} %bitcast.313, f32[512,768]{1,0:T(8,128)S(1)} %get-tuple-element.220, f32[512]{0:T(512)S(1)} %negate_multiply_fusion.1), kind=kOutput, calls=%fused_computation.231 | convolution fusion | flops 2451305472 | bytes 15749120 | tf_op jit(solution)/shard_map/dot_general | solution.py:29
  259.8 5.7 %convolution_convert_fusion.1 = bf16[3072,768]{1,0:T(8,128)(2,1)} fusion(f32[512,768]{1,0:T(8,128)S(1)} %get-tuple-element.220, f32[512]{0:T(512)S(1)} %negate_multiply_fusion.1, f32[512,3072]{1,0:T(8,128)S(1)} %fusion.50, f32[3072]{0:T(1024)S(1)} %add.270), kind=kOutput, calls=%fused_computation.13 | convolution fusion | flops 2434793472 | bytes 12597248 | tf_op jit(solution)/shard_map/dot_general | solution.py:29
  268.8 4.9 convolution_convert_fusion
  299.3 9.3 %collective-permute-start.34 = (bf16[2,192,768]{2,1,0:T(8,128)(2,1)}, bf16[2,192,768]{2,1,0:T(8,128)(2,1)S(1)}, u32[]{:S(2)}, u32[]{:S(2)}) collective-permute-start(bf16[2,192,768]{2,1,0:T(8,128)(2,1)} %get-tuple-element.229), channel_id=1, source_target_pairs={{0,3},{1,2},{2,1},{3,0},{4,7},{5,6},{6,5},{7,4},{8,11},{9,10},{10,... | collective-permute-start | bytes 1769480 | tf_op jit(solution)/shard_map/ppermute | solution.py:894
  310.4 32.1 %attend_backward.3 = (bf16[1024,128]{1,0:T(8,128)(2,1)}, bf16[2048,256]{1,0:T(8,128)(2,1)}, bf16[4096,128]{1,0:T(8,128)(2,1)}, f32[8,128]{1,0:T(8,128)}) custom-call(s32[2]{0:T(128)} %pad_add_fusion.refs_0_, s32[16,16]{1,0:T(8,128)} %copy-done.49, bf16[4,2,8,256,256]{4,3,2,1,0:T(8,128)(2,1)} %get-tuple-element.94.refs_2_, ...), custom_call_target="tpu_custom_call" | custom-call | flops 100000000 | bytes 1000000 | tf_op jit(solution)/shard_map/attend_backward/pallas_call | solution.py:336
  352.3 7.0 %collective-permute-start.37 = (bf16[2,48,3968]{2,1,0:T(8,128)(2,1)}, bf16[2,48,3968]{2,1,0:T(8,128)(2,1)}, u32[]{:S(2)}, u32[]{:S(2)}) collective-permute-start(bf16[2,48,3968]{2,1,0:T(8,128)(2,1)} %get-tuple-element.225), channel_id=1, source_target_pairs={{0,3},{1,2},{2,1},{3,0},{4,7},{5,6},{6,5},{7,4},{8,11},{9,10},{10,... | collective-permute-start | bytes 2285576 | tf_op jit(solution)/shard_map/ppermute | solution.py:894
  362.8 4.8 collective-permute-start.38
  368.7 31.9 %attend_backward.4 = (bf16[1024,128]{1,0:T(8,128)(2,1)}, bf16[2048,256]{1,0:T(8,128)(2,1)}, bf16[4096,128]{1,0:T(8,128)(2,1)}, f32[8,128]{1,0:T(8,128)}) custom-call(s32[2]{0:T(128)} %pad_add_fusion.refs_0_, s32[16,16]{1,0:T(8,128)} %copy-done.49, bf16[4,2,8,256,256]{4,3,2,1,0:T(8,128)(2,1)} %get-tuple-element.98.refs_2_, ...), custom_call_target="tpu_custom_call" | custom-call | flops 100000000 | bytes 1000000 | tf_op jit(solution)/shard_map/attend_backward/pallas_call | solution.py:336
  408.1 10.1 %proj_grads.2 = bf16[768,1024]{1,0:T(8,128)(2,1)S(1)} custom-call(bf16[1024,768]{1,0:T(8,128)(2,1)S(1)} %bitcast.244, bf16[2048,768]{1,0:T(8,128)(2,1)S(1)} %bitcast.232, bf16[4096,768]{1,0:T(8,128)(2,1)S(1)} %copy-done.7, bf16[1024,128]{1,0:T(8,128)(2,1)S(1)} %copy-done.18, bf16[1024,128]{1,0:T(8,128)(2,1)S(1)} %copy-done.31, ...), custom_call_target="tpu_custom_call" | custom-call | flops 1000000000 | bytes 1000000 | tf_op jit(solution)/shard_map/proj_grads/pallas_call | solution.py:778
  420.5 7.8 %collective-permute-start.42 = (bf16[4,48,1024]{2,1,0:T(8,128)(2,1)}, bf16[4,48,1024]{2,1,0:T(8,128)(2,1)}, u32[]{:S(2)}, u32[]{:S(2)}) collective-permute-start(bf16[4,48,1024]{2,1,0:T(8,128)(2,1)} %get-tuple-element.237), channel_id=1, source_target_pairs={{0,3},{1,2},{2,1},{3,0},{4,7},{5,6},{6,5},{7,4},{8,11},{9,10},{10,... | collective-permute-start | bytes 1179656 | tf_op jit(solution)/shard_map/ppermute | solution.py:894
  432.0 4.4 collective-permute-start.43
  436.4 32.2 %attend_backward.5 = (bf16[1024,128]{1,0:T(8,128)(2,1)}, bf16[2048,256]{1,0:T(8,128)(2,1)}, bf16[4096,128]{1,0:T(8,128)(2,1)}, f32[8,128]{1,0:T(8,128)}) custom-call(s32[2]{0:T(128)} %pad_add_fusion.refs_0_, s32[16,16]{1,0:T(8,128)} %copy-done.49, bf16[4,2,8,256,256]{4,3,2,1,0:T(8,128)(2,1)} %get-tuple-element.102.refs_2_, ...), custom_call_target="tpu_custom_call" | custom-call | flops 100000000 | bytes 1000000 | tf_op jit(solution)/shard_map/attend_backward/pallas_call | solution.py:336
  499.3 7.8 %proj_grads.3 = bf16[768,640]{1,0:T(8,128)(2,1)S(1)} custom-call(bf16[1024,768]{1,0:T(8,128)(2,1)S(1)} %bitcast.245, bf16[2048,768]{1,0:T(8,128)(2,1)S(1)} %bitcast.233, bf16[4096,768]{1,0:T(8,128)(2,1)S(1)} %bitcast.237, bf16[1024,128]{1,0:T(8,128)(2,1)S(1)} %copy-done.37, bf16[2048,256]{1,0:T(8,128)(2,1)S(1)} %copy-done.24, ...), custom_call_target="tpu_custom_call" | custom-call | flops 1000000000 | bytes 1000000 | tf_op jit(solution)/shard_map/proj_grads/pallas_call | solution.py:778
  507.2 4.6 collective-permute-start.54
  520.2 4.4 collective-permute-done.56
  541.5 4.5 collective-permute-done.47
  548.8 5.8 %collective-permute-start.50 = (bf16[128,768]{1,0:T(8,128)(2,1)S(1)}, bf16[128,768]{1,0:T(8,128)(2,1)S(1)}, u32[]{:S(2)}, u32[]{:S(2)}) collective-permute-start(bf16[128,768]{1,0:T(8,128)(2,1)S(1)} %get-tuple-element.264), channel_id=1, source_target_pairs={{0,0},{1,1},{2,2},{3,3},{4,4},{5,5},{6,6},{7,7},{8,16},{9,17},{10,... | collective-permute-start | bytes 589832 | tf_op jit(solution)/shard_map/ppermute | solution.py:903
  (478 shorter events, 222.3 us)
Async XLA Ops:
  37.0 25.3 %collective-permute-start.7 = (bf16[336,768]{1,0:T(8,128)(2,1)S(1)}, bf16[336,768]{1,0:T(8,128)(2,1)S(1)}, u32[]{:S(2)}, u32[]{:S(2)}) collective-permute-start(bf16[336,768]{1,0:T(8,128)(2,1)S(1)} %collective-permute-done.6), channel_id=1, source_target_pairs={{0,1},{1,0},{2,3},{3,2},{4,5},{5,4},{6,7},{7,6},{8,9},{9,8},{10,11... | collective-permute-start | bytes 1548296 | tf_op jit(solution)/shard_map/ppermute | solution.py:894
  38.3 25.7 %collective-permute-start.2 = (bf16[336,768]{1,0:T(8,128)(2,1)S(1)}, bf16[336,768]{1,0:T(8,128)(2,1)S(1)}, u32[]{:S(2)}, u32[]{:S(2)}) collective-permute-start(bf16[336,768]{1,0:T(8,128)(2,1)S(1)} %collective-permute-done), channel_id=1, source_target_pairs={{0,2},{1,3},{2,0},{3,1},{4,6},{5,7},{6,4},{7,5},{8,10},{9,11},{10,... | collective-permute-start | bytes 1548296 | tf_op jit(solution)/shard_map/ppermute | solution.py:894
  71.3 30.8 %collective-permute-start.14 = (bf16[448,768]{1,0:T(8,128)(2,1)S(1)}, bf16[448,768]{1,0:T(8,128)(2,1)S(1)}, u32[]{:S(2)}, u32[]{:S(2)}) collective-permute-start(bf16[448,768]{1,0:T(8,128)(2,1)S(1)} %pack_late.1), channel_id=1, source_target_pairs={{0,4},{1,5},{2,6},{3,7},{4,0},{5,1},{6,2},{7,3},{8,20},{9,21},{10,... | collective-permute-start | bytes 2064392 | tf_op jit(solution)/shard_map/ppermute | solution.py:903
  76.3 30.3 %collective-permute-start.13 = (bf16[448,768]{1,0:T(8,128)(2,1)S(1)}, bf16[448,768]{1,0:T(8,128)(2,1)S(1)}, u32[]{:S(2)}, u32[]{:S(2)}) collective-permute-start(bf16[448,768]{1,0:T(8,128)(2,1)S(1)} %pack_late.1), channel_id=1, source_target_pairs={{0,0},{1,1},{2,2},{3,3},{4,4},{5,5},{6,6},{7,7},{8,16},{9,17},{10,... | collective-permute-start | bytes 2064392 | tf_op jit(solution)/shard_map/ppermute | solution.py:903
  109.7 83.0 %collective-permute-start.17 = (bf16[2,448,768]{2,1,0:T(8,128)(2,1)}, bf16[2,448,768]{2,1,0:T(8,128)(2,1)}, u32[]{:S(2)}, u32[]{:S(2)}) collective-permute-start(bf16[2,448,768]{2,1,0:T(8,128)(2,1)} %hold.1.refs_11_.refs_0_), channel_id=1, source_target_pairs={{0,3},{1,2},{2,1},{3,0},{4,7},{5,6},{6,5},{7,4},{8,11},{9,10},{10,... | collective-permute-start | bytes 4128776 | tf_op jit(solution)/shard_map/ppermute | solution.py:894
  110.9 82.2 %collective-permute-start.16 = (bf16[2,448,768]{2,1,0:T(8,128)(2,1)}, bf16[2,448,768]{2,1,0:T(8,128)(2,1)}, u32[]{:S(2)}, u32[]{:S(2)}) collective-permute-start(bf16[2,448,768]{2,1,0:T(8,128)(2,1)} %hold.1.refs_11_.refs_0_), channel_id=1, source_target_pairs={{0,2},{1,3},{2,0},{3,1},{4,6},{5,7},{6,4},{7,5},{8,10},{9,11},{10,... | collective-permute-start | bytes 4128776 | tf_op jit(solution)/shard_map/ppermute | solution.py:894
  111.8 81.3 %collective-permute-start.15 = (bf16[2,448,768]{2,1,0:T(8,128)(2,1)}, bf16[2,448,768]{2,1,0:T(8,128)(2,1)}, u32[]{:S(2)}, u32[]{:S(2)}) collective-permute-start(bf16[2,448,768]{2,1,0:T(8,128)(2,1)} %hold.1.refs_11_.refs_0_), channel_id=1, source_target_pairs={{0,1},{1,0},{2,3},{3,2},{4,5},{5,4},{6,7},{7,6},{8,9},{9,8},{10,11... | collective-permute-start | bytes 4128776 | tf_op jit(solution)/shard_map/ppermute | solution.py:894
  113.6 78.9 %collective-permute-start.19 = (bf16[2,128,768]{2,1,0:T(8,128)(2,1)}, bf16[2,128,768]{2,1,0:T(8,128)(2,1)}, u32[]{:S(2)}, u32[]{:S(2)}) collective-permute-start(bf16[2,128,768]{2,1,0:T(8,128)(2,1)} %get-tuple-element.249), channel_id=1, source_target_pairs={{0,4},{1,5},{2,6},{3,7},{4,0},{5,1},{6,2},{7,3},{8,20},{9,21},{10,... | collective-permute-start | bytes 1179656 | tf_op jit(solution)/shard_map/ppermute | solution.py:903
  116.9 73.1 %collective-permute-start.18 = (bf16[2,128,768]{2,1,0:T(8,128)(2,1)}, bf16[2,128,768]{2,1,0:T(8,128)(2,1)}, u32[]{:S(2)}, u32[]{:S(2)}) collective-permute-start(bf16[2,128,768]{2,1,0:T(8,128)(2,1)} %get-tuple-element.250), channel_id=1, source_target_pairs={{0,0},{1,1},{2,2},{3,3},{4,4},{5,5},{6,6},{7,7},{8,16},{9,17},{10,... | collective-permute-start | bytes 1179656 | tf_op jit(solution)/shard_map/ppermute | solution.py:903
  192.0 33.8 %collective-permute-start.23 = (bf16[2,448,768]{2,1,0:T(8,128)(2,1)}, bf16[2,448,768]{2,1,0:T(8,128)(2,1)}, u32[]{:S(2)}, u32[]{:S(2)}) collective-permute-start(bf16[2,448,768]{2,1,0:T(8,128)(2,1)} %hold.1.refs_11_.refs_0_), channel_id=1, source_target_pairs={{0,16},{16,0},{1,17},{17,1},{2,18},{18,2},{3,19},{19,3},{4,20},{20... | collective-permute-start | bytes 4128776 | tf_op jit(solution)/shard_map/ppermute | solution.py:888
  192.6 23.9 %collective-permute-start.21 = (bf16[512,128]{1,0:T(8,128)(2,1)S(1)}, bf16[512,128]{1,0:T(8,128)(2,1)S(1)}, u32[]{:S(2)}, u32[]{:S(2)}) collective-permute-start(bf16[512,128]{1,0:T(8,128)(2,1)S(1)} %dynamic-slice_bitcast_fusion.33), channel_id=1, source_target_pairs={{0,16},{16,0},{1,17},{17,1},{2,18},{18,2},{3,19},{19,3},{4,20},{20... | collective-permute-start | bytes 393224 | tf_op jit(solution)/shard_map/ppermute | solution.py:888
  192.6 33.2 %collective-permute-start.26 = (bf16[2,448,768]{2,1,0:T(8,128)(2,1)}, bf16[2,448,768]{2,1,0:T(8,128)(2,1)}, u32[]{:S(2)}, u32[]{:S(2)}) collective-permute-start(bf16[2,448,768]{2,1,0:T(8,128)(2,1)} %collective-permute-done.17.refs_14_.refs_3_), channel_id=1, source_target_pairs={{0,16},{16,0},{1,17},{17,1},{2,18},{18,2},{3,19},{19,3},{4,20},{20... | collective-permute-start | bytes 4128776 | tf_op jit(solution)/shard_map/ppermute | solution.py:888
  193.1 32.8 %collective-permute-start.25 = (bf16[2,448,768]{2,1,0:T(8,128)(2,1)}, bf16[2,448,768]{2,1,0:T(8,128)(2,1)}, u32[]{:S(2)}, u32[]{:S(2)}) collective-permute-start(bf16[2,448,768]{2,1,0:T(8,128)(2,1)} %collective-permute-done.16.refs_13_.refs_2_), channel_id=1, source_target_pairs={{0,16},{16,0},{1,17},{17,1},{2,18},{18,2},{3,19},{19,3},{4,20},{20... | collective-permute-start | bytes 4128776 | tf_op jit(solution)/shard_map/ppermute | solution.py:888
  193.1 32.7 %collective-permute-start.24 = (bf16[2,448,768]{2,1,0:T(8,128)(2,1)}, bf16[2,448,768]{2,1,0:T(8,128)(2,1)}, u32[]{:S(2)}, u32[]{:S(2)}) collective-permute-start(bf16[2,448,768]{2,1,0:T(8,128)(2,1)} %collective-permute-done.15.refs_12_.refs_1_), channel_id=1, source_target_pairs={{0,16},{16,0},{1,17},{17,1},{2,18},{18,2},{3,19},{19,3},{4,20},{20... | collective-permute-start | bytes 4128776 | tf_op jit(solution)/shard_map/ppermute | solution.py:888
  285.3 57.3 %collective-permute-start.31 = (bf16[384,3968]{1,0:T(8,128)(2,1)}, bf16[384,3968]{1,0:T(8,128)(2,1)}, u32[]{:S(2)}, u32[]{:S(2)}) collective-permute-start(bf16[384,3968]{1,0:T(8,128)(2,1)} %get-tuple-element.221), channel_id=1, source_target_pairs={{0,16},{16,0},{1,17},{17,1},{2,18},{18,2},{3,19},{19,3},{4,20},{20... | collective-permute-start | bytes 9142280 | tf_op jit(solution)/shard_map/ppermute | solution.py:888
  293.8 68.1 %collective-permute-start.28 = (bf16[2,128,768]{2,1,0:T(8,128)(2,1)}, bf16[2,128,768]{2,1,0:T(8,128)(2,1)S(1)}, u32[]{:S(2)}, u32[]{:S(2)}) collective-permute-start(bf16[2,128,768]{2,1,0:T(8,128)(2,1)} %get-tuple-element.247), channel_id=1, source_target_pairs={{0,4},{1,5},{2,6},{3,7},{4,0},{5,1},{6,2},{7,3},{8,20},{9,21},{10,... | collective-permute-start | bytes 1179656 | tf_op jit(solution)/shard_map/ppermute | solution.py:903
  299.3 53.0 %collective-permute-start.34 = (bf16[2,192,768]{2,1,0:T(8,128)(2,1)}, bf16[2,192,768]{2,1,0:T(8,128)(2,1)S(1)}, u32[]{:S(2)}, u32[]{:S(2)}) collective-permute-start(bf16[2,192,768]{2,1,0:T(8,128)(2,1)} %get-tuple-element.229), channel_id=1, source_target_pairs={{0,3},{1,2},{2,1},{3,0},{4,7},{5,6},{6,5},{7,4},{8,11},{9,10},{10,... | collective-permute-start | bytes 1769480 | tf_op jit(solution)/shard_map/ppermute | solution.py:894
  308.6 50.8 %collective-permute-start.33 = (bf16[2,192,768]{2,1,0:T(8,128)(2,1)}, bf16[2,192,768]{2,1,0:T(8,128)(2,1)S(1)}, u32[]{:S(2)}, u32[]{:S(2)}) collective-permute-start(bf16[2,192,768]{2,1,0:T(8,128)(2,1)} %get-tuple-element.230), channel_id=1, source_target_pairs={{0,2},{1,3},{2,0},{3,1},{4,6},{5,7},{6,4},{7,5},{8,10},{9,11},{10,... | collective-permute-start | bytes 1769480 | tf_op jit(solution)/shard_map/ppermute | solution.py:894
  308.6 50.8 %collective-permute-start.32 = (bf16[2,192,768]{2,1,0:T(8,128)(2,1)}, bf16[2,192,768]{2,1,0:T(8,128)(2,1)S(1)}, u32[]{:S(2)}, u32[]{:S(2)}) collective-permute-start(bf16[2,192,768]{2,1,0:T(8,128)(2,1)} %get-tuple-element.231), channel_id=1, source_target_pairs={{0,1},{1,0},{2,3},{3,2},{4,5},{5,4},{6,7},{7,6},{8,9},{9,8},{10,11... | collective-permute-start | bytes 1769480 | tf_op jit(solution)/shard_map/ppermute | solution.py:894
  352.3 48.3 %collective-permute-start.37 = (bf16[2,48,3968]{2,1,0:T(8,128)(2,1)}, bf16[2,48,3968]{2,1,0:T(8,128)(2,1)}, u32[]{:S(2)}, u32[]{:S(2)}) collective-permute-start(bf16[2,48,3968]{2,1,0:T(8,128)(2,1)} %get-tuple-element.225), channel_id=1, source_target_pairs={{0,3},{1,2},{2,1},{3,0},{4,7},{5,6},{6,5},{7,4},{8,11},{9,10},{10,... | collective-permute-start | bytes 2285576 | tf_op jit(solution)/shard_map/ppermute | solution.py:894
  359.4 41.3 %collective-permute-start.36 = (bf16[2,48,3968]{2,1,0:T(8,128)(2,1)}, bf16[2,48,3968]{2,1,0:T(8,128)(2,1)}, u32[]{:S(2)}, u32[]{:S(2)}) collective-permute-start(bf16[2,48,3968]{2,1,0:T(8,128)(2,1)} %get-tuple-element.226), channel_id=1, source_target_pairs={{0,2},{1,3},{2,0},{3,1},{4,6},{5,7},{6,4},{7,5},{8,10},{9,11},{10,... | collective-permute-start | bytes 2285576 | tf_op jit(solution)/shard_map/ppermute | solution.py:894
  359.4 41.3 %collective-permute-start.35 = (bf16[2,48,3968]{2,1,0:T(8,128)(2,1)}, bf16[2,48,3968]{2,1,0:T(8,128)(2,1)}, u32[]{:S(2)}, u32[]{:S(2)}) collective-permute-start(bf16[2,48,3968]{2,1,0:T(8,128)(2,1)} %get-tuple-element.227), channel_id=1, source_target_pairs={{0,1},{1,0},{2,3},{3,2},{4,5},{5,4},{6,7},{7,6},{8,9},{9,8},{10,11... | collective-permute-start | bytes 2285576 | tf_op jit(solution)/shard_map/ppermute | solution.py:894
  361.9 38.7 %collective-permute-start.39 = (bf16[192,768]{1,0:T(8,128)(2,1)}, bf16[192,768]{1,0:T(8,128)(2,1)}, u32[]{:S(2)}, u32[]{:S(2)}) collective-permute-start(bf16[192,768]{1,0:T(8,128)(2,1)} %get-tuple-element.259), channel_id=1, source_target_pairs={{0,4},{1,5},{2,6},{3,7},{4,0},{5,1},{6,2},{7,3},{8,20},{9,21},{10,... | collective-permute-start | bytes 884744 | tf_op jit(solution)/shard_map/ppermute | solution.py:903
  362.8 37.8 %collective-permute-start.38 = (bf16[192,768]{1,0:T(8,128)(2,1)}, bf16[192,768]{1,0:T(8,128)(2,1)}, u32[]{:S(2)}, u32[]{:S(2)}) collective-permute-start(bf16[192,768]{1,0:T(8,128)(2,1)} %get-tuple-element.260), channel_id=1, source_target_pairs={{0,0},{1,1},{2,2},{3,3},{4,4},{5,5},{6,6},{7,7},{8,16},{9,17},{10,... | collective-permute-start | bytes 884744 | tf_op jit(solution)/shard_map/ppermute | solution.py:903
  420.5 51.4 %collective-permute-start.42 = (bf16[4,48,1024]{2,1,0:T(8,128)(2,1)}, bf16[4,48,1024]{2,1,0:T(8,128)(2,1)}, u32[]{:S(2)}, u32[]{:S(2)}) collective-permute-start(bf16[4,48,1024]{2,1,0:T(8,128)(2,1)} %get-tuple-element.237), channel_id=1, source_target_pairs={{0,3},{1,2},{2,1},{3,0},{4,7},{5,6},{6,5},{7,4},{8,11},{9,10},{10,... | collective-permute-start | bytes 1179656 | tf_op jit(solution)/shard_map/ppermute | solution.py:894
  428.3 43.6 %collective-permute-start.41 = (bf16[4,48,1024]{2,1,0:T(8,128)(2,1)}, bf16[4,48,1024]{2,1,0:T(8,128)(2,1)}, u32[]{:S(2)}, u32[]{:S(2)}) collective-permute-start(bf16[4,48,1024]{2,1,0:T(8,128)(2,1)} %get-tuple-element.238), channel_id=1, source_target_pairs={{0,2},{1,3},{2,0},{3,1},{4,6},{5,7},{6,4},{7,5},{8,10},{9,11},{10,... | collective-permute-start | bytes 1179656 | tf_op jit(solution)/shard_map/ppermute | solution.py:894
  428.3 43.6 %collective-permute-start.40 = (bf16[4,48,1024]{2,1,0:T(8,128)(2,1)}, bf16[4,48,1024]{2,1,0:T(8,128)(2,1)}, u32[]{:S(2)}, u32[]{:S(2)}) collective-permute-start(bf16[4,48,1024]{2,1,0:T(8,128)(2,1)} %get-tuple-element.239), channel_id=1, source_target_pairs={{0,1},{1,0},{2,3},{3,2},{4,5},{5,4},{6,7},{7,6},{8,9},{9,8},{10,11... | collective-permute-start | bytes 1179656 | tf_op jit(solution)/shard_map/ppermute | solution.py:894
  431.4 40.1 %collective-permute-start.44 = (bf16[48,3968]{1,0:T(8,128)(2,1)}, bf16[48,3968]{1,0:T(8,128)(2,1)}, u32[]{:S(2)}, u32[]{:S(2)}) collective-permute-start(bf16[48,3968]{1,0:T(8,128)(2,1)} %get-tuple-element.251), channel_id=1, source_target_pairs={{0,4},{1,5},{2,6},{3,7},{4,0},{5,1},{6,2},{7,3},{8,20},{9,21},{10,... | collective-permute-start | bytes 1142792 | tf_op jit(solution)/shard_map/ppermute | solution.py:903
  432.0 39.9 %collective-permute-start.43 = (bf16[48,3968]{1,0:T(8,128)(2,1)}, bf16[48,3968]{1,0:T(8,128)(2,1)}, u32[]{:S(2)}, u32[]{:S(2)}) collective-permute-start(bf16[48,3968]{1,0:T(8,128)(2,1)} %get-tuple-element.252), channel_id=1, source_target_pairs={{0,0},{1,1},{2,2},{3,3},{4,4},{5,5},{6,6},{7,7},{8,16},{9,17},{10,... | collective-permute-start | bytes 1142792 | tf_op jit(solution)/shard_map/ppermute | solution.py:903
  491.6 24.1 %collective-permute-start.53 = (bf16[128,768]{1,0:T(8,128)(2,1)S(1)}, bf16[128,768]{1,0:T(8,128)(2,1)S(1)}, u32[]{:S(2)}, u32[]{:S(2)}) collective-permute-start(bf16[128,768]{1,0:T(8,128)(2,1)S(1)} %get-tuple-element.261), channel_id=1, source_target_pairs={{0,4},{1,5},{2,6},{3,7},{4,0},{5,1},{6,2},{7,3},{8,20},{9,21},{10,... | collective-permute-start | bytes 589832 | tf_op jit(solution)/shard_map/ppermute | solution.py:903
  527.9 26.7 %collective-permute-start.57 = (bf16[48,1664]{1,0:T(8,128)(2,1)}, bf16[48,1664]{1,0:T(8,128)(2,1)}, u32[]{:S(2)}, u32[]{:S(2)}) collective-permute-start(bf16[48,1664]{1,0:T(8,128)(2,1)} %get-tuple-element.256), channel_id=1, source_target_pairs={{0,4},{1,5},{2,6},{3,7},{4,0},{5,1},{6,2},{7,3},{8,12},{9,13},{10,... | collective-permute-start | bytes 479240 | tf_op jit(solution)/shard_map/ppermute | solution.py:891
  531.1 23.6 %collective-permute-start.58 = (bf16[48,1664]{1,0:T(8,128)(2,1)}, bf16[48,1664]{1,0:T(8,128)(2,1)}, u32[]{:S(2)}, u32[]{:S(2)}) collective-permute-start(bf16[48,1664]{1,0:T(8,128)(2,1)} %get-tuple-element.257), channel_id=1, source_target_pairs={{0,8},{1,9},{2,10},{3,11},{4,12},{5,13},{6,14},{7,15},{8,0},{9,1},... | collective-permute-start | bytes 479240 | tf_op jit(solution)/shard_map/ppermute | solution.py:891
  (138 other events, 1040.7 us)

commit v3 on v2

--- a/solution.py
+++ b/solution.py
@@ -22,6 +22,8 @@
 SCALE = DH**-0.5
 LOG2E = 1.4426950408889634
 LN2 = 0.6931471805599453
+VMEM = 60 * 2**20
+SMALL = 32 * 2**20
 ONES = 32
 
 
@@ -195,7 +197,7 @@
             jax.ShapeDtypeStruct((q.shape[0], 128), BF),
         ],
         compiler_params=pltpu.CompilerParams(
-            dimension_semantics=("arbitrary",), vmem_limit_bytes=58 * 2**20
+            dimension_semantics=("arbitrary",), vmem_limit_bytes=VMEM
         ),
         cost_estimate=pl.CostEstimate(
             flops=10**8, bytes_accessed=10**6, transcendentals=0
@@ -223,8 +225,7 @@
     dkv_ref,
     drel_ref,
     small_ref,
-    qq_scr,
-    qr_scr,
+    turn_scr,
     dd_scr,
     acc_scr,
     accr_scr,
@@ -253,17 +254,18 @@
     for h in range(2):
         half = slice(DH * h, DH * h + DH)
         q = q_ref[:, half]
-        plain = ((q + vec_ref[0:1, half]) * (SCALE * LOG2E)).astype(BF)
-        place = ((q + vec_ref[1:2, half]) * (SCALE * LOG2E)).astype(BF)
+        plain = (q + vec_ref[0:1, half]) * (SCALE * LOG2E)
+        place = (q + vec_ref[1:2, half]) * (SCALE * LOG2E)
         g = g_ref[:, half].astype(F32)
         inverse = inv_ref[:, DH * h : DH * h + 1]
         delta = -jnp.sum(g * o_ref[:, half], axis=1, keepdims=True) * inverse
         high = delta.astype(BF).astype(F32)
         extra = jnp.where(lane == ONES, high, jnp.where(lane == ONES + 1, delta - high, 0.0))
         side = lambda x: [x, zero] if h == 0 else [zero, x]
-        qq_scr[h] = jnp.concatenate(side(plain), axis=1)
-        qr_scr[h] = jnp.concatenate(side(place), axis=1)
-        dd_scr[h] = jnp.concatenate(side((g * inverse).astype(BF)) + [extra.astype(BF)], axis=1)
+        scaled = g * inverse
+        dd_scr[h] = jnp.concatenate(side(scaled.astype(BF)) + [extra.astype(BF)], axis=1)
+        for i, x in enumerate((plain, scaled, place)):
+            turn_scr[h, i] = x.T.astype(BF)
     acc_scr[...] = jnp.zeros(acc_scr.shape, F32)
     accr_scr[...] = jnp.zeros(accr_scr.shape, F32)
 
@@ -275,7 +277,6 @@
         pad = jnp.zeros((R, W - KB), F32)
         keys = jnp.concatenate([kv_ref[pl.ds(k0, KB), :128], hot], axis=1)
         values = jnp.concatenate([kv_ref[pl.ds(k0, KB), 128:], hot], axis=1)
-        d_keys = d_values = d_rel = 0.0
         for h in range(2):
             p = p_ref[0, h, n]
             dd = dd_scr[h]
@@ -294,12 +295,10 @@
             ]
             full = jnp.concatenate(full, axis=0).astype(BF)
             accr_scr[h] += mm(full, window)
-            d_rel += mm(full, qr_scr[h], 0, 0)
-            d_keys += mm(ds, qq_scr[h], 0, 0)
-            d_values += mm(p, dd[:, :128], 0, 0)
-        drel_scr[pl.ds(r0, W), :] += d_rel
-        dkv_scr[pl.ds(k0, KB), :128] += d_keys
-        dkv_scr[pl.ds(k0, KB), 128:] += d_values
+            low, high = DH * h, DH * h + DH
+            dkv_scr[low:high, pl.ds(k0, KB)] += mm(turn_scr[h, 0], ds)
+            dkv_scr[128 + low : 128 + high, pl.ds(k0, KB)] += mm(turn_scr[h, 1], p)
+            drel_scr[low:high, pl.ds(r0, W)] += mm(turn_scr[h, 2], full)
         return carry
 
     lax.fori_loop(0, count, step, 0)
@@ -321,9 +320,8 @@
 
     @pl.when(block == nb - 1)
     def finish():
-        across = lax.broadcasted_iota(jnp.int32, (length, 256), 1)
-        factor = jnp.where(across < 128, LN2, 1.0)
-        dkv_ref[...] = (dkv_scr[...] * factor).astype(BF)
+        dkv_ref[:128, :] = (dkv_scr[:128, :] * LN2).astype(BF)
+        dkv_ref[128:, :] = dkv_scr[128:, :].astype(BF)
         drel_ref[...] = (drel_scr[...] * LN2).astype(BF)
 
 
@@ -353,30 +351,29 @@
             + [pl.BlockSpec(memory_space=pl.ANY)] * len(after),
             out_specs=[
                 own,
-                pl.BlockSpec((length, 256), lambda b, *_: (0, 0)),
-                pl.BlockSpec((2 * length, 128), lambda b, *_: (0, 0)),
+                pl.BlockSpec((256, length), lambda b, *_: (0, 0)),
+                pl.BlockSpec((128, 2 * length), lambda b, *_: (0, 0)),
                 pl.BlockSpec((8, 128), lambda b, *_: (0, 0)),
             ],
             scratch_shapes=[
-                pltpu.VMEM((2, 2 * R, 128), BF),
-                pltpu.VMEM((2, 2 * R, 128), BF),
+                pltpu.VMEM((2, 3, DH, 2 * R), BF),
                 pltpu.VMEM((2, 2 * R, 256), BF),
                 pltpu.VMEM((2, 2 * R, 256), F32),
                 pltpu.VMEM((2, 2 * R, 128), F32),
-                pltpu.VMEM((length, 256), F32),
-                pltpu.VMEM((2 * length, 128), F32),
+                pltpu.VMEM((256, length), F32),
+                pltpu.VMEM((128, 2 * length), F32),
                 pltpu.VMEM((KB, KB), BF),
                 pltpu.SMEM((nkb + 1,), jnp.int32),
             ],
         ),
         out_shape=[
             jax.ShapeDtypeStruct((q.shape[0], 128), BF),
-            jax.ShapeDtypeStruct((length, 256), BF),
-            jax.ShapeDtypeStruct((2 * length, 128), BF),
+            jax.ShapeDtypeStruct((256, length), BF),
+            jax.ShapeDtypeStruct((128, 2 * length), BF),
             jax.ShapeDtypeStruct((8, 128), F32),
         ],
         compiler_params=pltpu.CompilerParams(
-            dimension_semantics=("arbitrary",), vmem_limit_bytes=58 * 2**20
+            dimension_semantics=("arbitrary",), vmem_limit_bytes=VMEM
         ),
         cost_estimate=pl.CostEstimate(
             flops=10**8, bytes_accessed=10**6, transcendentals=0
@@ -423,7 +420,7 @@
         out_specs=[whole_block(shape)] * 2,
         out_shape=[shape, shape],
         scratch_shapes=[pltpu.VMEM((16, d), F32)],
-        compiler_params=pltpu.CompilerParams(vmem_limit_bytes=24 * 2**20),
+        compiler_params=pltpu.CompilerParams(vmem_limit_bytes=VMEM),
         name="pack",
     )(low, content, segs, ranks, flags, parents, *vecs, *weights)
 
@@ -460,21 +457,22 @@
                 fill(src, query)
 
 
-def assemble(at, near_rows, their_rows, q_own, q_other, r, ws):
+def assemble(at, near_rows, their_rows, q_own, q_other, r, ws, after):
     m, rows, d = near_rows[0].shape
     dh = d // 2
     sizes = [(m, r, d), (m, 16, d), (m, ws, dh), (m, ws, d), (m, ws, dh), (2, r, d)]
     return pl.pallas_call(
-        functools.partial(assemble_kernel, r, ws, dh, m),
+        ordered(functools.partial(assemble_kernel, r, ws, dh, m), 7, len(after)),
         grid=(2, 2),
         in_specs=[pl.BlockSpec(memory_space=pltpu.SMEM)]
         + [pl.BlockSpec((m, rows, d), lambda h, z: (0, 0, 0))] * 4
-        + [pl.BlockSpec((2, r, d), lambda h, z: (0, 0, 0))] * 2,
+        + [pl.BlockSpec((2, r, d), lambda h, z: (0, 0, 0))] * 2
+        + [pl.BlockSpec(memory_space=pl.ANY)] * len(after),
         out_specs=[pl.BlockSpec((1, 1) + size, lambda h, z: (h, z, 0, 0, 0)) for size in sizes],
         out_shape=[jax.ShapeDtypeStruct((2, 2) + size, BF) for size in sizes],
-        compiler_params=pltpu.CompilerParams(vmem_limit_bytes=48 * 2**20),
+        compiler_params=pltpu.CompilerParams(vmem_limit_bytes=SMALL),
         name="assemble",
-    )(at, *near_rows, *their_rows, q_own, q_other)
+    )(at, *near_rows, *their_rows, q_own, q_other, *after)
 
 
 def pack_late_kernel(ws, w1_ref, wo_ref, w2_ref, *refs):
@@ -488,7 +486,7 @@
     scr[...] = jnp.zeros(scr.shape, F32)
     row = 0
     for ref in vec_refs:
-        scr[row : row + ref.shape[0], :ws] = ref[...].astype(F32)
+        scr[row : row + ref.shape[0], : ref.shape[1]] = ref[...].astype(F32)
         row += ref.shape[0]
     out[(2 * parts + 1) * ws :, :] = scr[...].astype(BF)
 
@@ -503,7 +501,7 @@
         out_specs=pl.BlockSpec((rows, d), lambda i: (0, 0)),
         out_shape=jax.ShapeDtypeStruct((rows, d), BF),
         scratch_shapes=[pltpu.VMEM((16, d), F32)],
-        compiler_params=pltpu.CompilerParams(vmem_limit_bytes=24 * 2**20),
+        compiler_params=pltpu.CompilerParams(vmem_limit_bytes=SMALL),
         name="pack_late",
     )(w1, wo, w2, *vecs)
 
@@ -545,7 +543,7 @@
         + [pl.BlockSpec((2, rows, d), lambda h, z: (0, 0, 0))] * (2 * m),
         out_specs=[pl.BlockSpec((1, 1) + size, lambda h, z: (h, z, 0, 0, 0)) for size in sizes],
         out_shape=[jax.ShapeDtypeStruct((2, 2) + size, BF) for size in sizes],
-        compiler_params=pltpu.CompilerParams(vmem_limit_bytes=56 * 2**20),
+        compiler_params=pltpu.CompilerParams(vmem_limit_bytes=SMALL),
         name="assemble_late",
     )(at, *mine, *theirs)
 
@@ -589,7 +587,7 @@
             jax.ShapeDtypeStruct((2 * length, width), BF),
             jax.ShapeDtypeStruct((2 * length, width), BF),
         ],
-        compiler_params=pltpu.CompilerParams(vmem_limit_bytes=24 * 2**20),
+        compiler_params=pltpu.CompilerParams(vmem_limit_bytes=SMALL),
         cost_estimate=pl.CostEstimate(
             flops=4 * length * d * width, bytes_accessed=8 * length * d, transcendentals=0
         ),
@@ -597,28 +595,33 @@
     )(*tables, wr)
 
 
-def input_grad_kernel(count, at_ref, *refs):
+def input_grad_kernel(count, turned, at_ref, *refs):
     parts, w_ref, out_ref = refs[:count], refs[count], refs[-1]
     total = 0.0
     start = 0
     for ref in parts:
-        width = ref.shape[1]
-        total += mm(ref[...], w_ref[:, start : start + width], 1, 1)
+        width = ref.shape[0 if turned else 1]
+        total += mm(ref[...], w_ref[:, start : start + width], 0 if turned else 1, 1)
         start += width
     out_ref[...] = total.astype(out_ref.dtype)
 
 
-def input_grad(half, parts, w, dtype, after):
-    rows = parts[0].shape[0] // 2
+def input_grad(half, parts, w, dtype, after, turned=False):
+    rows = parts[0].shape[1 if turned else 0] // 2
     block = math.gcd(rows, 256)
+    blocks = rows // block
     d = w.shape[0]
     return pl.pallas_call(
-        ordered(functools.partial(input_grad_kernel, len(parts)), len(parts) + 2, len(after)),
+        ordered(
+            functools.partial(input_grad_kernel, len(parts), turned), len(parts) + 2, len(after)
+        ),
         grid_spec=pltpu.PrefetchScalarGridSpec(
             num_scalar_prefetch=1,
             grid=(rows // block,),
             in_specs=[
-                pl.BlockSpec((block, x.shape[1]), lambda i, at: (at[0] * (rows // block) + i, 0))
+                pl.BlockSpec((x.shape[0], block), lambda i, at: (0, at[0] * blocks + i))
+                if turned
+                else pl.BlockSpec((block, x.shape[1]), lambda i, at: (at[0] * blocks + i, 0))
                 for x in parts
             ]
             + [pl.BlockSpec(w.shape, lambda i, at: (0, 0))]
@@ -626,7 +629,7 @@
             out_specs=pl.BlockSpec((block, d), lambda i, at: (i, 0)),
         ),
         out_shape=jax.ShapeDtypeStruct((rows, d), dtype),
-        compiler_params=pltpu.CompilerParams(vmem_limit_bytes=24 * 2**20),
+        compiler_params=pltpu.CompilerParams(vmem_limit_bytes=SMALL),
         cost_estimate=pl.CostEstimate(
             flops=2 * rows * d * w.shape[1], bytes_accessed=4 * rows * d, transcendentals=0
         ),
@@ -698,7 +701,7 @@
             jax.ShapeDtypeStruct((128, 128), BF),
             jax.ShapeDtypeStruct((n, n), jnp.int32),
         ],
-        compiler_params=pltpu.CompilerParams(vmem_limit_bytes=24 * 2**20),
+        compiler_params=pltpu.CompilerParams(vmem_limit_bytes=SMALL),
         name="masks",
     )(c, codes)
 
@@ -716,7 +719,7 @@
         in_specs=[spec, spec] + [pl.BlockSpec(memory_space=pl.ANY)] * len(after),
         out_specs=pl.BlockSpec((2,) + a.shape, lambda i: (0, 0, 0)),
         out_shape=jax.ShapeDtypeStruct((2,) + a.shape, a.dtype),
-        compiler_params=pltpu.CompilerParams(vmem_limit_bytes=24 * 2**20),
+        compiler_params=pltpu.CompilerParams(vmem_limit_bytes=SMALL),
         name="hold",
     )(a, b, *after)
 
@@ -732,18 +735,16 @@
         for scr in (q_scr, kv_scr, r_scr):
             scr[...] = jnp.zeros(scr.shape, F32)
 
-    for p in range(count):
-        r_scr[p] += mm(drel[p][...], pos_ref[...], 0, 0)
+    beside = lambda refs, axis: jnp.concatenate([ref[...] for ref in refs], axis=axis)
+    r_scr[...] += mm(beside(drel, 0), pos_ref[...])
 
     @pl.when(i < steps[1])
     def keys():
-        for p in range(count):
-            kv_scr[p] += mm(dkv[p][...], c_ref[...], 0, 0)
+        kv_scr[...] += mm(beside(dkv, 0), c_ref[...])
 
     @pl.when(i < steps[0])
     def queries():
-        for p in range(count):
-            q_scr[p] += mm(dq[p][...], x_ref[...], 0, 0)
+        q_scr[...] += mm(beside(dq, 1), x_ref[...], 0, 0)
 
     @pl.when(i == steps[2] - 1)
     def finish():
@@ -751,9 +752,10 @@
         lane = lax.broadcasted_iota(jnp.int32, (128, d), 1)
         for p in range(count):
             at = 512 * p
-            out_ref[:, at : at + 128] = q_scr[p].T.astype(BF)
-            out_ref[:, at + 128 : at + 384] = kv_scr[p].T.astype(BF)
-            turned = jnp.where(lane < d // 2, -r_scr[p], r_scr[p])
+            rows = slice(128 * p, 128 * p + 128)
+            out_ref[:, at : at + 128] = q_scr[rows, :].T.astype(BF)
+            out_ref[:, at + 128 : at + 384] = kv_scr[256 * p : 256 * p + 256, :].T.astype(BF)
+            turned = jnp.where(lane < d // 2, -r_scr[rows, :], r_scr[rows, :])
             out_ref[:, at + 384 : at + 512] = turned.T.astype(BF)
         for ref in extra:
             out_ref[:, 512 * count :] = ref[...]
@@ -762,15 +764,19 @@
 def proj_grads(x, content, position, parts, extra, after):
     count = len(parts)
     d = x.shape[1]
-    steps = [a.shape[0] // KB for a in (x, content, position)]
+    size = 512
+    steps = [a.shape[0] // size for a in (x, content, position)]
     spec = lambda width, kind: pl.BlockSpec(
-        (KB, width), lambda i: (jnp.minimum(i, steps[kind] - 1), 0)
+        (size, width), lambda i: (jnp.minimum(i, steps[kind] - 1), 0)
+    )
+    turned = lambda width, kind: pl.BlockSpec(
+        (width, size), lambda i: (0, jnp.minimum(i, steps[kind] - 1))
     )
     operands = [x, content, position]
     specs = [spec(d, kind) for kind in range(3)]
-    for index, width, kind in ((0, 128, 0), (1, 256, 1), (2, 128, 2)):
+    for index, one in enumerate((spec(128, 0), turned(256, 1), turned(128, 2))):
         operands += [b[index] for b in parts]
-        specs += [spec(width, kind)] * count
+        specs += [one] * count
     operands += extra
     specs += [pl.BlockSpec(e.shape, lambda i: (0, 0)) for e in extra]
     width = 512 * count + sum(e.shape[1] for e in extra)
@@ -782,11 +788,11 @@
         out_specs=pl.BlockSpec((d, width), lambda i: (0, 0)),
         out_shape=jax.ShapeDtypeStruct((d, width), BF),
         scratch_shapes=[
-            pltpu.VMEM((count, 128, d), F32),
-            pltpu.VMEM((count, 256, d), F32),
-            pltpu.VMEM((count, 128, d), F32),
+            pltpu.VMEM((count * 128, d), F32),
+            pltpu.VMEM((count * 256, d), F32),
+            pltpu.VMEM((count * 128, d), F32),
         ],
-        compiler_params=pltpu.CompilerParams(vmem_limit_bytes=32 * 2**20),
+        compiler_params=pltpu.CompilerParams(vmem_limit_bytes=VMEM),
         cost_estimate=pl.CostEstimate(flops=10**9, bytes_accessed=10**6, transcendentals=0),
         name="proj_grads",
     )(*operands, *after)
@@ -811,30 +817,377 @@
         in_specs=[spec] * len(parts) + [pl.BlockSpec(memory_space=pl.ANY)] * len(after),
         out_specs=spec,
         out_shape=jax.ShapeDtypeStruct((rows, shape[-1]), dtype),
-        compiler_params=pltpu.CompilerParams(vmem_limit_bytes=32 * 2**20),
+        compiler_params=pltpu.CompilerParams(vmem_limit_bytes=SMALL),
         cost_estimate=pl.CostEstimate(flops=rows, bytes_accessed=10**6, transcendentals=0),
         name="add_up",
     )(*flat, *after)
     return out.reshape(shape)
 
 
-def layer_norm(vector, gain_row, shift_row):
-    average = jnp.mean(vector, axis=-1, keepdims=True)
-    centred = vector - average
-    variance = jnp.mean(centred * centred, axis=-1, keepdims=True)
-    return centred * lax.rsqrt(variance + EPSILON) * gain_row + shift_row
-
-
-def gelu_tanh(vector):
-    return jax.nn.gelu(vector, approximate=True)
-
-
-def position_rows(offsets, model_width):
-    half_width = model_width // 2
-    powers = jnp.arange(half_width, dtype=F32) * (2.0 / model_width)
-    inverse_freq = 1.0 / 10000.0**powers
-    angles = offsets[:, None] * inverse_freq[None, :]
-    return jnp.concatenate([jnp.sin(angles), jnp.cos(angles)], axis=1)
+def fold_kernel(m, count, at_ref, *refs):
+    for step in range(m):
+        total = refs[step * count][0, 0].astype(F32)
+        for ref in refs[step * count + 1 : (step + 1) * count]:
+            total += ref[0, 0].astype(F32)
+        refs[m * count + step][0] = total.astype(BF)
+
+
+def fold(at, arrays, after):
+    two, m, rows, width = arrays[0].shape
+    count = len(arrays)
+    spec = lambda step: pl.BlockSpec(
+        (1, 1, rows, width), lambda i, at: (i, jnp.bitwise_xor(at[2], step), 0, 0)
+    )
+    return pl.pallas_call(
+        ordered(functools.partial(fold_kernel, m, count), m * count + 1, len(after)),
+        grid_spec=pltpu.PrefetchScalarGridSpec(
+            num_scalar_prefetch=1,
+            grid=(2,),
+            in_specs=[spec(step) for step in range(m) for x in arrays]
+            + [pl.BlockSpec(memory_space=pl.ANY)] * len(after),
+            out_specs=[pl.BlockSpec((1, rows, width), lambda i, at: (i, 0, 0))] * m,
+        ),
+        out_shape=[jax.ShapeDtypeStruct((2, rows, width), BF)] * m,
+        compiler_params=pltpu.CompilerParams(vmem_limit_bytes=SMALL),
+        cost_estimate=pl.CostEstimate(flops=rows, bytes_accessed=10**6, transcendentals=0),
+        name="fold",
+    )(at, *(list(arrays) * m), *after)
+
+
+def join_kernel(count, at_ref, *refs):
+    for e in range(2):
+        total = refs[e * count][0].astype(F32)
+        for ref in refs[e * count + 1 : (e + 1) * count]:
+            total += ref[0].astype(F32)
+        refs[2 * count + e][...] = total.astype(BF)
+
+
+def join(at, arrays, after):
+    two, rows, width = arrays[0].shape
+    count = len(arrays)
+    spec = lambda e: pl.BlockSpec(
+        (1, rows, width), lambda i, at: (jnp.bitwise_xor(at[1], e), 0, 0)
+    )
+    return pl.pallas_call(
+        ordered(functools.partial(join_kernel, count), 2 * count + 1, len(after)),
+        grid_spec=pltpu.PrefetchScalarGridSpec(
+            num_scalar_prefetch=1,
+            grid=(1,),
+            in_specs=[spec(e) for e in range(2) for x in arrays]
+            + [pl.BlockSpec(memory_space=pl.ANY)] * len(after),
+            out_specs=[pl.BlockSpec((rows, width), lambda i, at: (0, 0))] * 2,
+        ),
+        out_shape=[jax.ShapeDtypeStruct((rows, width), BF)] * 2,
+        compiler_params=pltpu.CompilerParams(vmem_limit_bytes=SMALL),
+        cost_estimate=pl.CostEstimate(flops=rows, bytes_accessed=10**6, transcendentals=0),
+        name="join",
+    )(at, *(list(arrays) * 2), *after)
+
+
+GELU_A = 0.7978845608028654
+GELU_B = 0.044715
+
+
+def gelu_and_slope(v):
+    square = v * v
+    t = jnp.tanh(GELU_A * (v + GELU_B * (v * square)))
+    half = 0.5 + 0.5 * t
+    slope = half + 0.5 * v * (1.0 - t * t) * (GELU_A * (1.0 + 3.0 * GELU_B * square))
+    return v * half, slope
+
+
+def norm_forward(x):
+    average = jnp.mean(x, axis=1, keepdims=True)
+    centred = x - average
+    inverse = lax.rsqrt(jnp.mean(centred * centred, axis=1, keepdims=True) + EPSILON)
+    return centred * inverse, inverse
+
+
+def norm_backward(grad, gain, unit, inverse):
+    scaled = grad * gain
+    pull = jnp.mean(scaled, axis=1, keepdims=True)
+    twist = jnp.mean(scaled * unit, axis=1, keepdims=True)
+    return inverse * (scaled - pull - unit * twist)
+
+
+def dense_kernel(m, n, ws, pairs, at_ref, *refs):
+    own_mixed, got_mixed = refs[:pairs], refs[pairs : 2 * pairs]
+    x_ref, cot_ref = refs[2 * pairs : 2 * pairs + 2]
+    pieces = refs[2 * pairs + 2 : 2 * pairs + 2 + 2 * m]
+    rest = refs[2 * pairs + 2 + 2 * m :]
+    result_ref, gr_ref, gm_own, gm_other, vec_ref, b1_ref = rest[:6]
+    early_own, early_other, late_own, late_other = rest[6:10]
+    w1, w2, wo, vp, slope, hidden, unit_bf, mixed, early, late, bias, sems, out_sems = rest[10:]
+    k, low, c = at_ref[0], at_ref[1], at_ref[2]
+    d = x_ref.shape[1]
+    ff = w1.shape[1]
+    parts = ff // d
+    fs = parts * ws
+    places = []
+    for index, piece in enumerate(pieces):
+        h = k if index < m else 1 - k
+        for e in range(2):
+            s = (2 * h + jnp.bitwise_xor(low, e)) * m + jnp.bitwise_xor(c, index % m)
+            places.append((piece.at[e], s))
+    kinds = 2 + parts + 1
+
+    def load(i, kind, j=0):
+        src, s = places[i]
+        to = pl.ds(pl.multiple_of(s * ws, 16), ws)
+        if kind == 0:
+            pair = (src.at[pl.ds(parts * ws, ws), :], wo.at[to, :])
+        elif kind == 1:
+            pair = (src.at[pl.ds((2 * parts + 1) * ws, 16), :], vp.at[s])
+        elif kind == 2:
+            rows = pl.ds(pl.multiple_of(j * ws, 16), ws)
+            pair = (src.at[rows, :], w1.at[to, pl.ds(pl.multiple_of(j * d, 128), d)])
+        else:
+            to = pl.ds(pl.multiple_of(s * fs, 16), fs)
+            pair = (src.at[pl.ds((parts + 1) * ws, fs), :], w2.at[to, :])
+        at = i * kinds + (kind if kind < 2 else 2 + j if kind == 2 else kinds - 1)
+        return pltpu.make_async_copy(*pair, sems.at[at])
+
+    count = len(places)
+    for kind in (0, 1):
+        for i in range(count):
+            load(i, kind).start()
+    for j in range(parts):
+        for i in range(count):
+            load(i, 2, j).start()
+    for i in range(count):
+        load(i, 3).start()
+
+    for p in range(pairs):
+        lanes = slice(128 * p, 128 * p + 128)
+        other = slice(d // 2 + 128 * p, d // 2 + 128 * p + 128)
+
+        @pl.when(k == 0)
+        def low_core():
+            mixed[:, lanes] = own_mixed[p][...]
+            mixed[:, other] = got_mixed[p][...]
+
+        @pl.when(k != 0)
+        def high_core():
+            mixed[:, lanes] = got_mixed[p][...]
+            mixed[:, other] = own_mixed[p][...]
+
+    for kind in (0, 1):
+        for i in range(count):
+            load(i, kind).wait()
+    spot = lax.broadcasted_iota(jnp.int32, (128, d), 1)
+    down = lax.broadcasted_iota(jnp.int32, (128, d), 0)
+    vecs = jnp.zeros((16, d), F32)
+    for s in range(n):
+        place = jnp.where((spot == s * ws + down) & (down < ws), 1.0, 0.0).astype(BF)
+        vecs += mm(vp[s, :, :128], place)
+    per = (d // 2) // fs
+    spot = lax.broadcasted_iota(jnp.int32, (256, d // 2), 1)
+    down = lax.broadcasted_iota(jnp.int32, (256, d // 2), 0)
+    place = [
+        jnp.where((spot == t * fs + down) & (down < fs), 1.0, 0.0).astype(BF) for t in range(per)
+    ]
+    for q in range(n // per):
+        row = sum(mm(vp[q * per + t, :, :256], place[t]) for t in range(per))
+        bias[:, q * (d // 2) : (q + 1) * (d // 2)] = row[:8]
+    outer_shift, gain_one, shift_one, gain_two, shift_two = [vecs[i : i + 1] for i in range(5)]
+
+    residual = mm(mixed[...], wo[...]) + x_ref[...].astype(F32)
+    unit_one, inverse_one = norm_forward(residual)
+    normed = unit_one * gain_one + shift_one
+    unit_bf[...] = normed.astype(BF)
+    total = normed + outer_shift
+
+    def wait_chunk(j):
+        for i in range(count):
+            load(i, 2, j).wait()
+
+    for j in range(parts):
+        wait_chunk(j)
+        cols = slice(j * d, (j + 1) * d)
+        value, slant = gelu_and_slope(mm(unit_bf[...], w1[:, cols]) + bias[5:6, cols])
+        hidden[:, cols] = value.astype(BF)
+        slope[:, cols] = slant
+    for i in range(count):
+        load(i, 3).wait()
+    summed = total + mm(hidden[...], w2[...])
+    unit_two, inverse_two = norm_forward(summed)
+    result_ref[...] = (unit_two * gain_two + shift_two).astype(BF)
+    cot = cot_ref[...].astype(F32)
+    grad_summed = norm_backward(cot, gain_two, unit_two, inverse_two)
+    row_sum = lambda x: jnp.sum(x, axis=0, keepdims=True)
+    vec_ref[0:1, :] = row_sum(grad_summed)
+    vec_ref[3:4, :] = row_sum(cot * unit_two)
+    vec_ref[4:5, :] = row_sum(cot)
+    grad_bf = grad_summed.astype(BF)
+    grad_normed = grad_summed
+    copies = []
+    deep = early.shape[0] // 2
+    split = ff // 2 // d
+
+    def send(half, src, own, other):
+        sem = out_sems.at[len(copies)]
+        copies.append(pltpu.make_async_copy(src, own, sem))
+
+        @pl.when(k == half)
+        def keep():
+            pltpu.make_async_copy(src, own, sem).start()
+
+        @pl.when(k != half)
+        def give():
+            pltpu.make_async_copy(src, other, sem).start()
+
+    def send_early(cols):
+        for half in range(2):
+            src = early.at[half * deep : (half + 1) * deep, cols]
+            send(half, src, early_own.at[:, cols], early_other.at[:, cols])
+
+    for j in range(parts):
+        cols = slice(j * d, (j + 1) * d)
+        grad_inner = mm(grad_bf, w2[cols, :], 1, 1) * slope[:, cols]
+        b1_ref[0:1, cols] = row_sum(grad_inner)
+        inner_bf = grad_inner.astype(BF)
+        late[cols, :] = mm(hidden[:, cols], grad_bf, 0, 0).astype(BF)
+        to = pl.ds((j % split) * d, d)
+        send(j // split, late.at[cols, :], late_own.at[to, :], late_other.at[to, :])
+        early[:, cols] = mm(unit_bf[...], inner_bf, 0, 0).astype(BF)
+        send_early(cols)
+        grad_normed += mm(inner_bf, w1[:, cols], 1, 1)
+    vec_ref[1:2, :] = row_sum(grad_normed * unit_one)
+    vec_ref[2:3, :] = row_sum(grad_normed)
+    grad_residual = norm_backward(grad_normed, gain_one, unit_one, inverse_one)
+    gr_ref[...] = grad_residual
+    residual_bf = grad_residual.astype(BF)
+    early[:, ff:] = mm(mixed[...], residual_bf, 0, 0).astype(BF)
+    send_early(slice(ff, ff + d))
+    grad_mixed = mm(residual_bf, wo[...], 1, 1).astype(BF)
+    for half in range(2):
+        part = grad_mixed[:, half * (d // 2) : (half + 1) * (d // 2)]
+
+        @pl.when(k == half)
+        def keep(part=part):
+            gm_own[...] = part
+
+        @pl.when(k != half)
+        def give(part=part):
+            gm_other[...] = part
+
+    for copy in copies:
+        copy.wait()
+
+
+def dense(at, own_mixed, got_mixed, inputs, cots, mine, theirs, ws, ff):
+    m = len(mine)
+    pairs = len(own_mixed)
+    rows, d = cots.shape
+    n = d // ws
+    parts = ff // d
+    anywhere = pl.BlockSpec(memory_space=pl.ANY)
+    half = lambda width: pl.BlockSpec((rows, width), lambda i, at: (at[0], 0))
+    fixed = lambda *shape: pl.BlockSpec(shape, lambda i, at: (0,) * len(shape))
+    return pl.pallas_call(
+        functools.partial(dense_kernel, m, n, ws, pairs),
+        grid_spec=pltpu.PrefetchScalarGridSpec(
+            num_scalar_prefetch=1,
+            grid=(1,),
+            in_specs=[half(128)] * pairs
+            + [fixed(rows, 128)] * pairs
+            + [half(d), fixed(rows, d)]
+            + [anywhere] * (2 * m),
+            out_specs=[
+                fixed(rows, d),
+                fixed(rows, d),
+                fixed(rows, d // 2),
+                fixed(rows, d // 2),
+                fixed(8, d),
+                fixed(8, ff),
+            ]
+            + [anywhere] * 4,
+            scratch_shapes=[
+                pltpu.VMEM((d, ff), BF),
+                pltpu.VMEM((ff, d), BF),
+                pltpu.VMEM((d, d), BF),
+                pltpu.VMEM((n, 16, d), BF),
+                pltpu.VMEM((rows, ff), F32),
+                pltpu.VMEM((rows, ff), BF),
+                pltpu.VMEM((rows, d), BF),
+                pltpu.VMEM((rows, d), BF),
+                pltpu.VMEM((d, ff + d), BF),
+                pltpu.VMEM((ff, d), BF),
+                pltpu.VMEM((8, ff), F32),
+                pltpu.SemaphoreType.DMA((4 * m * (3 + parts),)),
+                pltpu.SemaphoreType.DMA((3 * parts + 2,)),
+            ],
+        ),
+        out_shape=[
+            jax.ShapeDtypeStruct((rows, d), BF),
+            jax.ShapeDtypeStruct((rows, d), F32),
+            jax.ShapeDtypeStruct((rows, d // 2), BF),
+            jax.ShapeDtypeStruct((rows, d // 2), BF),
+            jax.ShapeDtypeStruct((8, d), F32),
+            jax.ShapeDtypeStruct((8, ff), F32),
+            jax.ShapeDtypeStruct((d // 2, ff + d), BF),
+            jax.ShapeDtypeStruct((d // 2, ff + d), BF),
+            jax.ShapeDtypeStruct((ff // 2, d), BF),
+            jax.ShapeDtypeStruct((ff // 2, d), BF),
+        ],
+        compiler_params=pltpu.CompilerParams(vmem_limit_bytes=VMEM),
+        cost_estimate=pl.CostEstimate(flops=10**9, bytes_accessed=10**6, transcendentals=0),
+        name="dense",
+    )(at, *own_mixed, *got_mixed, inputs, cots, *mine, *theirs)
+
+
+def dense_plain(at, own_mixed, got_mixed, inputs, cots, mine, theirs, ws, ff):
+    rows, d = cots.shape
+    n, fs = d // ws, ff * ws // d
+    k = at[0]
+    mine_half = lambda x: lax.dynamic_slice_in_dim(x, k * rows, rows, 0)
+    inner_w, output_w, outer_w, vecs = assemble_late(at, mine, theirs, ws, ff // d)
+    inner_w, output_w = inner_w.reshape(d, ff), output_w.reshape(d, d)
+    outer_w = outer_w.reshape(ff, d)
+    vecs = vecs.reshape(n, 16, d).astype(F32)
+    inner_shift = vecs[:, 5, :fs].reshape(ff)
+    vecs = vecs[:, :5, :ws].swapaxes(0, 1).reshape(5, d)
+    outer_shift, gain_one, shift_one, gain_two, shift_two = [vecs[i] for i in range(5)]
+    own = [mine_half(x) for x in own_mixed]
+    mixed = jnp.where(
+        k == 0,
+        jnp.concatenate(own + got_mixed, axis=1),
+        jnp.concatenate(got_mixed + own, axis=1),
+    )
+    residual = mm(mixed, output_w) + mine_half(inputs).astype(F32)
+    unit_one, inverse_one = norm_forward(residual)
+    normed = unit_one * gain_one + shift_one
+    normed_bf = normed.astype(BF)
+    value, slope = gelu_and_slope(mm(normed_bf, inner_w) + inner_shift)
+    hidden = value.astype(BF)
+    summed = mm(hidden, outer_w) + outer_shift + normed
+    unit_two, inverse_two = norm_forward(summed)
+    result = (unit_two * gain_two + shift_two).astype(BF)
+    cot = cots.astype(F32)
+    grad_summed = norm_backward(cot, gain_two, unit_two, inverse_two)
+    grad_bf = grad_summed.astype(BF)
+    grad_inner = mm(grad_bf, outer_w, 1, 1) * slope
+    inner_bf = grad_inner.astype(BF)
+    grad_normed = mm(inner_bf, inner_w, 1, 1) + grad_summed
+    grad_residual = norm_backward(grad_normed, gain_one, unit_one, inverse_one)
+    residual_bf = grad_residual.astype(BF)
+    grad_mixed = mm(residual_bf, output_w, 1, 1).astype(BF)
+    terms = [grad_summed, grad_normed * unit_one, grad_normed, cot * unit_two, cot]
+    early = jnp.concatenate([mm(normed_bf, inner_bf, 0, 0), mm(mixed, residual_bf, 0, 0)], axis=1)
+
+    def halves(x, axis):
+        size = x.shape[axis] // 2
+        return [lax.dynamic_slice_in_dim(x, i * size, size, axis).astype(BF) for i in (k, 1 - k)]
+
+    return (
+        result,
+        grad_residual,
+        *halves(grad_mixed, 1),
+        jnp.stack([jnp.sum(x, axis=0) for x in terms]),
+        jnp.sum(grad_inner, axis=0)[None],
+        *halves(early, 0),
+        *halves(mm(hidden, grad_bf, 0, 0), 0),
+    )
 
 
 def body(
@@ -950,12 +1303,20 @@
     own_query = jnp.stack([across(pick(query_in, low ^ e), e) for e in range(2)])
     near_rows = [near_gather(got[e], e) for e in range(2)]
     their_rows = [swap(x) for x in near_rows]
+    late_pack = pack_late(
+        inner_weight,
+        output_weight,
+        outer_weight,
+        [x.reshape(1, ws) for x in (outer_bias, attend_gain, attend_shift, feed_gain, feed_shift)]
+        + [inner_bias.reshape(1, fs)],
+    )
+    late_pack, unused = tie((late_pack, got[1]))
+    late = [across(late_pack, e) for e in range(2)]
     content_full, codes, wq, kv_weight, wr, inputs = assemble(
-        at, near_rows, their_rows, own_query, swap(own_query), r, ws
+        at, near_rows, their_rows, own_query, swap(own_query), r, ws, []
     )
     content_full = content_full.reshape(length, d)
     wq, kv_weight, wr = wq.reshape(d, dh), kv_weight.reshape(d, d), wr.reshape(d, dh)
-    own_inputs = pick(inputs, k).reshape(groups * r, d)
     inputs = inputs.reshape(groups * 2 * r, d)
     codes = codes.reshape(n, 16, d)
     key_ranks, hot, info, reach, live = masks(
@@ -965,15 +1326,7 @@
     vectors = codes[:, 1:6, :ws].astype(F32).swapaxes(0, 1).reshape(5, 2, dh)
     head_vecs = jnp.where(first, vectors[:, 0], vectors[:, 1])
 
-    late_pack = pack_late(
-        inner_weight,
-        output_weight,
-        outer_weight,
-        [x.reshape(1, ws) for x in (outer_bias, attend_gain, attend_shift, feed_gain, feed_shift)]
-        + [inner_bias.reshape(fs // ws, ws)],
-    )
-    late_pack, unused = tie((late_pack, got[1]))
-    late = [across(late_pack, e) for e in range(2)]
+
     content_cot, query_cot, unused = tie((content_cot, query_cot, content_full))
     cots = cross(jnp.stack([content_cot, query_cot], axis=1))
 
@@ -983,13 +1336,15 @@
     vec8 = jnp.pad(head_vecs, ((0, 3), (0, 0)))
     table = head_vecs[3:5].reshape(2, heads, DH).swapaxes(0, 1)
     table = jnp.where(jnp.arange(128) < 2 * NS, table[..., None], 0.0)
-    late = hold(late[0], late[1], [content_full, wr])
+    late = hold(late[0], late[1], [content_full])
     late_near = [late] + [near(late, step) for step in range(1, m)]
-    late_theirs = [swap(x) for x in late_near]
     forward = []
     got_mixed = []
     for pair in range(pairs):
-        after = [[late], [], late_near + [cots]][min(pair, 2)]
+        after = [[late], [cots], late_near[1:]][min(pair, 2)]
+        if pair == 2:
+            *held, unused = tie((*late_near, forward[1][1]))
+            late_theirs = [swap(x) for x in held]
         after = after + [f[1] for f in forward[-1:]]
         forward.append(
             attend_forward(
@@ -1010,69 +1365,29 @@
         )
         got_mixed.append(swap(pick(forward[-1][3].reshape(2, groups * r, 128), 1 - k)))
 
-    inner_w, output_w, outer_w, vecs = assemble_late(at, late_near, late_theirs, ws, ff // d)
-    inner_w, output_w = inner_w.reshape(d, ff), output_w.reshape(d, d)
-    outer_w = outer_w.reshape(ff, d)
-    vecs = vecs.reshape(n, 16, d)[:, : 5 + fs // ws, :ws].astype(F32)
-    inner_shift = vecs[:, 5:].reshape(ff)
-    vecs = vecs[:, :5].swapaxes(0, 1).reshape(5, d)
-    outer_shift, gain_one, shift_one, gain_two, shift_two = [vecs[i] for i in range(5)]
-
-    own_mixed = [pick(f[3].reshape(2, groups * r, 128), k) for f in forward]
-    mixed_bf = jnp.where(
-        first,
-        jnp.concatenate(own_mixed + got_mixed, axis=1),
-        jnp.concatenate(got_mixed + own_mixed, axis=1),
+    (
+        result,
+        grad_residual,
+        mine_grad,
+        other_grad,
+        row_vecs,
+        inner_vecs,
+        early_mine,
+        early_other,
+        late_mine,
+        late_other,
+    ) = (dense if ws % 16 == 0 else dense_plain)(
+        at,
+        [f[3] for f in forward],
+        got_mixed,
+        inputs,
+        cots.reshape(groups * r, d),
+        late_near,
+        late_theirs,
+        ws,
+        ff,
     )
-    residual = mm(mixed_bf, output_w) + own_inputs.astype(F32)
-    normed = layer_norm(residual, gain_one, shift_one)
-    normed_bf = normed.astype(BF)
-    inner_pre = mm(normed_bf, inner_w) + inner_shift
-    hidden_bf = gelu_tanh(inner_pre).astype(BF)
-    summed = mm(hidden_bf, outer_w) + outer_shift + normed
-    result = layer_norm(summed, gain_two, shift_two).astype(BF).reshape(2, 2, r, d)
-    outs = cross(result)
-    cotangent = cots.reshape(groups * r, d).astype(F32)
-    unused, final_back = jax.vjp(layer_norm, summed, gain_two, shift_two)
-    grad_summed, grad_final_gain, grad_final_shift = final_back(cotangent)
-    grad_summed_bf = grad_summed.astype(BF)
-    unused, gelu_back = jax.vjp(gelu_tanh, inner_pre)
-    (grad_inner,) = gelu_back(mm(grad_summed_bf, outer_w, 1, 1))
-    grad_inner_bf = grad_inner.astype(BF)
-    grad_normed = mm(grad_inner_bf, inner_w, 1, 1) + grad_summed
-    unused, first_back = jax.vjp(layer_norm, residual, gain_one, shift_one)
-    grad_residual, grad_norm_gain, grad_norm_shift = first_back(grad_normed)
-    grad_residual_bf = grad_residual.astype(BF)
-    grad_mixed = mm(grad_residual_bf, output_w, 1, 1).astype(BF)
-    mine_grad = lax.dynamic_slice_in_dim(grad_mixed, k * dh, dh, 1)
-    got_grad = swap(lax.dynamic_slice_in_dim(grad_mixed, (1 - k) * dh, dh, 1))
-    grad_heads = pair_of(mine_grad, got_grad, k).reshape(groups * 2 * r, dh)
-
-    grad_late = mm(hidden_bf, grad_summed_bf, 0, 0).astype(BF).reshape(2, ff // 2, d)
-    row_vecs = jnp.stack(
-        [
-            jnp.sum(grad_summed, axis=0),
-            grad_norm_gain,
-            grad_norm_shift,
-            grad_final_gain,
-            grad_final_shift,
-        ],
-        axis=1,
-    )
-    inner_vecs = jnp.sum(grad_inner, axis=0).reshape(n, fs // ws, ws).swapaxes(1, 2)
-    row_vecs = jnp.concatenate([row_vecs, inner_vecs.reshape(d, fs // ws)], axis=1)
-    row_vecs = jnp.pad(row_vecs, ((0, 0), (0, 128 - row_vecs.shape[1])))
-    grad_early = jnp.concatenate(
-        [
-            mm(normed_bf, grad_inner_bf, 0, 0).astype(BF),
-            mm(mixed_bf, grad_residual_bf, 0, 0).astype(BF),
-            row_vecs.astype(BF),
-        ],
-        axis=1,
-    ).reshape(2, d // 2, ff + d + 128)
-
-    def cross_parts(x):
-        return [across(pick(x, low ^ e), e) for e in range(2)]
+    grad_heads = pair_of(mine_grad, swap(other_grad), k).reshape(groups * 2 * r, dh)
 
     backward = []
 
@@ -1098,42 +1413,32 @@
             )
         )
 
-    def half_sum(x, rows, after):
-        half = add_up([pick(x, k), swap(pick(x, 1 - k))], BF, after)
-        return half.reshape(2, m, rows, x.shape[-1])
+    def near_fold(arrays, rows, after):
+        parts = fold(at, [x.reshape(2, m, rows, x.shape[-1]) for x in arrays], after)
+        return [parts[0]] + [near(parts[step], step) for step in range(1, m)]
+
+    def cross_join(parts, after):
+        return [across(x, e) for e, x in enumerate(join(at, parts, after))]
 
     def proj_some(some, extra, after):
         return proj_grads(
             inputs, content_full, position_bf, [backward[p] for p in some], extra, after
         ).reshape(groups, m, ws, -1)
 
-    late_half = half_sum(grad_late, fs, [])
-    late_parts = near_parts(late_half, 1)
-    back(0, [late_half])
+    late_parts = near_fold([late_mine, swap(late_other)], fs, [])
+    back(0, late_parts[:1])
     after = [backward[0][0]]
-    late_near = add_up(late_parts, BF, after)
-    late_cross = cross_parts(late_near)
-    early_half = half_sum(grad_early, ws, after)
-    early_parts = near_parts(early_half, 1)
-    back(1, [early_half, late_near, outs])
-    some_grads = proj_some(range(pairs - 1), [], early_parts[1:] + late_cross)
+    early_parts = near_fold([early_mine, swap(early_other)], ws, after)
+    late_cross = cross_join(late_parts, after)
+    result, unused = tie((result, backward[0][0]))
+    outs = cross(result.reshape(2, 2, r, d))
+    back(1, [early_parts[0]])
+    some_grads = proj_some(range(pairs - 1), [], early_parts[1:] + late_cross + [outs])
     some_parts = near_parts(some_grads, 1)
-    early_near = add_up(early_parts, BF, [])
-    early_cross = cross_parts(early_near)
-    back(2, [early_near, some_grads])
-
-    which = [jnp.asarray(x, jnp.int32).reshape(1) for x in (k, 1 - k)]
-    dkv_parts = [b[1] for b in backward]
-    dq_parts = [b[0] for b in backward]
-    got_kv = swap(input_grad(which[1], dkv_parts, kv_weight, BF, some_parts[1:] + early_cross))
-    got_q = swap(input_grad(which[1], dq_parts, wq, BF, []))
-    own_kv = input_grad(which[0], dkv_parts, kv_weight, F32, [])
-    own_q = input_grad(which[0], dq_parts, wq, F32, [])
-    kv_sum = add_up([own_kv, got_kv], BF, [])
-    content_parts = near_parts(kv_sum.reshape(2, m, r, d), 1)
-    q_sum = own_q + got_q.astype(F32) + grad_residual
-    q_sum = q_sum.reshape(2, 2, r, d)
-    query_grads = cross(q_sum[:, 1].astype(BF))
+    early_cross = cross_join(early_parts, [])
+    late_sum = add_up(late_cross, BF, [some_grads])
+    late_got = swap(late_sum)
+    back(2, [some_grads])
 
     small = jnp.concatenate([b[3][:5] for b in backward], axis=1)
     small = jnp.where(
@@ -1141,20 +1446,35 @@
         jnp.concatenate([small, jnp.zeros_like(small)], axis=1),
         jnp.concatenate([jnp.zeros_like(small), small], axis=1),
     )
-    small = jnp.pad(small.T, ((0, 0), (0, 128 - 5))).astype(BF)
-    last_grads = proj_some([pairs - 1], [small], [kv_sum])
+    inner_vecs = inner_vecs[0].reshape(n, fs // ws, ws).swapaxes(1, 2).reshape(d, fs // ws)
+    small = jnp.concatenate([small.T, row_vecs[:5].T, inner_vecs], axis=1)
+    small = jnp.pad(small, ((0, 0), (0, 128 - small.shape[1]))).astype(BF)
+    last_grads = proj_some([pairs - 1], [small], some_parts[1:] + early_cross + [late_got])
+    early_sum = add_up(early_cross, BF, [last_grads])
+    late_sum, late_got, unused = tie((late_sum, late_got, last_grads))
+    early_got = swap(early_sum)
     last_parts = near_parts(last_grads, 1)
-    late_sum = add_up(late_cross, BF, [kv_sum])
-    early_sum = add_up(early_cross, BF, [kv_sum])
-    late_total = late_sum.astype(F32) + swap(late_sum).astype(F32)
+    which = [jnp.asarray(x, jnp.int32).reshape(1) for x in (k, 1 - k)]
+    dkv_parts = [b[1] for b in backward]
+    dq_parts = [b[0] for b in backward]
+    got_kv = swap(input_grad(which[1], dkv_parts, kv_weight, BF, [last_grads], True))
+    got_q = swap(input_grad(which[1], dq_parts, wq, BF, [last_grads]))
+    own_kv = input_grad(which[0], dkv_parts, kv_weight, F32, [last_grads], True)
+    own_q = input_grad(which[0], dq_parts, wq, F32, [last_grads])
+    content_parts = near_fold([own_kv, got_kv], r, [own_q, early_got] + last_parts[1:])
+    q_sum = own_q + got_q.astype(F32) + grad_residual
+    q_sum = q_sum.reshape(2, 2, r, d)
+    query_rows, unused = tie((q_sum[:, 1].astype(BF), content_parts[1]))
+    query_grads = cross(query_rows)
+    late_total = late_sum.astype(F32) + late_got.astype(F32)
     content_sum = sum([x.astype(F32) for x in content_parts]) + q_sum[:, 0]
     content_grads = cross(content_sum.astype(BF))
     some_near, last_near = [
-        sum([x.astype(F32) for x in parts]).astype(BF) for parts in (some_parts, last_parts)
+        add_up(parts, BF, content_parts[:1]) for parts in (some_parts, last_parts)
     ]
     proj_sum = far_sum(jnp.concatenate([some_near, last_near], axis=2))
 
-    early_total = early_sum.astype(F32) + swap(early_sum).astype(F32)
+    early_total = early_sum.astype(F32) + early_got.astype(F32)
     bit = 2
     while bit < nr:
         turn = [(i, i ^ bit) for i in range(nr)]
@@ -1175,8 +1495,8 @@
             axis=1,
         )
 
-    vec_cols = early_total[:, ff + d :]
     head_cols = (proj_sum + proj_other)[:, 512 * pairs :]
+    vec_cols = head_cols[:, 5:]
     return (
         outs[:, 0],
         outs[:, 1],

time: 571 us -> 511 us (0.89); the launches traced: 562 us -> 512 us
  local copies, waits for them, and re-layouts: 85.5 us -> 44.4 us
  matrix products: 44.2 us -> 8.45 us
  other arithmetic: 32.8 us -> 11.2 us
  Pallas kernels: 215 us -> 235 us
  starting transfers between devices: 93.4 us -> 112 us
  waiting for transfers between devices: 88.5 us -> 98.3 us
    dot_general x11 -> x2, matrix products: 44.2 us -> 8.45 us  [mm(): lax.dot_general(a, b, (((ca,), (cb,)), ((), ())), preferred_element_type=...]
    pallas_call x6 -> x11, Pallas kernels: 22.7 us -> 53.3 us  [the longest x1 32.7 us: dense(): pl.pallas_call(functools.partial(dense_kernel, m, n, ws, pairs), grid_spe...]
    unnamed x227 -> x210, local copies, waits for them, and re-layouts: 51.3 us -> 27.7 us
    squeeze x16 -> x7, local copies, waits for them, and re-layouts: 17.8 us -> 3.98 us  [pick(): return lax.dynamic_index_in_dim(x, index, axis, keepdims=False)]
    ppermute x3, waiting for transfers between devices: 0.01 us -> 11.1 us  [far(): return lax.ppermute(x, 'shard', [(i, i ^ m * step) for i in range(n)])]
    ppermute x18, waiting for transfers between devices: 0.22 us -> 11 us  [swap(): return lax.ppermute(x, 'rep', [(i, i ^ 1) for i in range(nr)])]
    ppermute x24, waiting for transfers between devices: 37.8 us -> 27.1 us  [near(): return lax.ppermute(x, 'shard', [(i, i ^ step) for i in range(n)])]
    ppermute x18, starting transfers between devices: 41.9 us -> 52 us  [across(): return lax.ppermute(x, ('rep', 'shard'), moves)]
  transfers between devices with their start and end apart: 63 -> 63, of which waited for: 17 -> 22; matrix products, arithmetic and copies ran while one was open for 11% -> 7% of each run, Pallas kernels for 35% -> 34%
where the time goes in v3:
time: 511 us; the launch traced here: 512 us
  Pallas kernels  235 us (46%)
  starting transfers between devices  112 us (22%)
  waiting for transfers between devices  98.3 us (19%)
  local copies, waits for them, and re-layouts  44.4 us (9%)
  other arithmetic  11.2 us (2%)
  matrix products  8.45 us (2%)
    pallas_call x3, Pallas kernels, attend_backward(): pl.pallas_call(ordered(functools.partial(backward_kernel, nkb, nb), 12, l...  87.9 us
    pallas_call x3, Pallas kernels, attend_forward(): pl.pallas_call(ordered(functools.partial(forward_kernel, nkb), 11, len(af...  56.6 us
    ppermute x18, starting transfers between devices, across(): return lax.ppermute(x, ('rep', 'shard'), moves)  52 us
    ppermute x24, starting transfers between devices, near(): return lax.ppermute(x, 'shard', [(i, i ^ step) for i in range(n)])  49.3 us
    ppermute x18, waiting for transfers between devices, across(): return lax.ppermute(x, ('rep', 'shard'), moves)  49.1 us
    pallas_call x1, Pallas kernels, dense(): pl.pallas_call(functools.partial(dense_kernel, m, n, ws, pairs), grid_spe...  32.7 us
    unnamed x210, local copies, waits for them, and re-layouts  27.7 us
    ppermute x24, waiting for transfers between devices, near(): return lax.ppermute(x, 'shard', [(i, i ^ step) for i in range(n)])  27.1 us
  transfers between devices with their start and end apart: 63, of which 22 were waited for; matrix products, arithmetic and copies ran while one was open for 7% of the time, Pallas kernels for 34%

profile of v3, /device:TPU:9, one launch (start us, length us, event | category | flops | bytes accessed | tf_op | source)
XLA Modules:
  0.0 511.6 jit_solution(6987705934636920531)
XLA Ops:
  7.7 8.8 %collective-permute-done.4 = bf16[336,768]{1,0:T(8,128)(2,1)S(1)} collective-permute-done((bf16[336,768]{1,0:T(8,128)(2,1)}, bf16[336,768]{1,0:T(8,128)(2,1)S(1)}, u32[]{:S(2)}, u32[]{:S(2)}) %collective-permute-start.4) | collective-permute-done | bytes 516128 | tf_op jit(solution)/shard_map/ppermute | solution.py:1256
  17.8 10.0 %collective-permute-done = bf16[336,768]{1,0:T(8,128)(2,1)S(1)} collective-permute-done((bf16[336,768]{1,0:T(8,128)(2,1)}, bf16[336,768]{1,0:T(8,128)(2,1)S(1)}, u32[]{:S(2)}, u32[]{:S(2)}) %collective-permute-start) | collective-permute-done | bytes 516128 | tf_op jit(solution)/shard_map/ppermute | solution.py:1256
  31.9 9.6 %collective-permute-done.1 = bf16[336,768]{1,0:T(8,128)(2,1)S(1)} collective-permute-done((bf16[336,768]{1,0:T(8,128)(2,1)S(1)}, bf16[336,768]{1,0:T(8,128)(2,1)S(1)}, u32[]{:S(2)}, u32[]{:S(2)}) %collective-permute-start.1) | collective-permute-done | bytes 516128 | tf_op jit(solution)/shard_map/ppermute | solution.py:1247
  41.7 7.6 %collective-permute-done.5 = bf16[336,768]{1,0:T(8,128)(2,1)S(1)} collective-permute-done((bf16[336,768]{1,0:T(8,128)(2,1)S(1)}, bf16[336,768]{1,0:T(8,128)(2,1)S(1)}, u32[]{:S(2)}, u32[]{:S(2)}) %collective-permute-start.5) | collective-permute-done | bytes 516128 | tf_op jit(solution)/shard_map/ppermute | solution.py:1247
  49.2 5.5 %collective-permute-done.7 = bf16[336,768]{1,0:T(8,128)(2,1)S(1)} collective-permute-done((bf16[336,768]{1,0:T(8,128)(2,1)S(1)}, bf16[336,768]{1,0:T(8,128)(2,1)S(1)}, u32[]{:S(2)}, u32[]{:S(2)}) %collective-permute-start.7) | collective-permute-done | bytes 516128 | tf_op jit(solution)/shard_map/ppermute | solution.py:1247
  64.5 3.7 collective-permute-start.13
  69.7 4.3 collective-permute-done.11
  84.1 7.0 %collective-permute-done.13.refs_0_ = bf16[448,768]{1,0:T(8,128)(2,1)} collective-permute-done((bf16[448,768]{1,0:T(8,128)(2,1)}, bf16[448,768]{1,0:T(8,128)(2,1)}, u32[]{:S(2)}, u32[]{:S(2)}) %collective-permute-start.13) | collective-permute-done | bytes 688160 | tf_op jit(solution)/shard_map/ppermute | solution.py:1256
  91.1 10.7 %collective-permute-done.14.refs_1_ = bf16[448,768]{1,0:T(8,128)(2,1)} collective-permute-done((bf16[448,768]{1,0:T(8,128)(2,1)}, bf16[448,768]{1,0:T(8,128)(2,1)}, u32[]{:S(2)}, u32[]{:S(2)}) %collective-permute-start.14) | collective-permute-done | bytes 688160 | tf_op jit(solution)/shard_map/ppermute | solution.py:1256
  114.7 6.4 %relative.1 = (bf16[4096,768]{1,0:T(8,128)(2,1)S(1)}, bf16[4096,384]{1,0:T(8,128)(2,1)S(1)}, bf16[4096,384]{1,0:T(8,128)(2,1)S(1)}) custom-call(f32[16,4,384]{2,1,0:T(4,128)S(1)} %copy-done.63, f32[16,4,384]{2,1,0:T(4,128)S(1)} %copy-done.62, f32[64,384]{1,0:T(8,128)S(1)} %copy-done.61, f32[64,384]{1,0:T(8,128)S(1)} %copy-done.60, bf16[768,384]{1,0:T(8,128)(2,1)S(1)} %bitcast.217), custom_call_target="tpu_custom_call" | custom-call | flops 2415919104 | bytes 12582912 | tf_op jit(solution)/shard_map/relative/pallas_call | solution.py:578
  121.2 4.7 convolution_convert_fusion.refs_7_.refs_9_
  132.8 18.8 %attend_forward.3 = (bf16[4,2,8,256,256]{4,3,2,1,0:T(8,128)(2,1)}, f32[1024,128]{1,0:T(8,128)}, f32[1024,128]{1,0:T(8,128)}, bf16[1024,128]{1,0:T(8,128)(2,1)}) custom-call(s32[2]{0:T(128)} %pad_add_fusion.1.refs_0_, s32[16,16]{1,0:T(8,128)} %copy-done.59, f32[1024,384]{1,0:T(8,128)} %fusion.25.refs_2_.refs_3_, f32[8,384]{1,0:T(8,128)} %pad.9.refs_3_.refs_7_, ...), custom_call_target="tpu_custom_call" | custom-call | flops 100000000 | bytes 1000000 | tf_op jit(solution)/shard_map/attend_forward/pallas_call | solution.py:161
  154.7 19.0 %attend_forward.4 = (bf16[4,2,8,256,256]{4,3,2,1,0:T(8,128)(2,1)}, f32[1024,128]{1,0:T(8,128)}, f32[1024,128]{1,0:T(8,128)}, bf16[1024,128]{1,0:T(8,128)(2,1)}) custom-call(s32[2]{0:T(128)} %pad_add_fusion.1.refs_0_, s32[16,16]{1,0:T(8,128)} %copy-done.59, f32[1024,384]{1,0:T(8,128)} %fusion.25.refs_2_.refs_3_, f32[8,384]{1,0:T(8,128)} %pad.9.refs_3_.refs_7_, ...), custom_call_target="tpu_custom_call" | custom-call | flops 100000000 | bytes 1000000 | tf_op jit(solution)/shard_map/attend_forward/pallas_call | solution.py:161
  177.6 18.8 %attend_forward.5 = (bf16[4,2,8,256,256]{4,3,2,1,0:T(8,128)(2,1)}, f32[1024,128]{1,0:T(8,128)}, f32[1024,128]{1,0:T(8,128)}, bf16[1024,128]{1,0:T(8,128)(2,1)}) custom-call(s32[2]{0:T(128)} %pad_add_fusion.1.refs_0_, s32[16,16]{1,0:T(8,128)} %copy-done.59, f32[1024,384]{1,0:T(8,128)} %fusion.25.refs_2_.refs_3_, f32[8,384]{1,0:T(8,128)} %pad.9.refs_3_.refs_7_, ...), custom_call_target="tpu_custom_call" | custom-call | flops 100000000 | bytes 1000000 | tf_op jit(solution)/shard_map/attend_forward/pallas_call | solution.py:161
  200.4 32.7 %dense.1 = (bf16[512,768]{1,0:T(8,128)(2,1)}, f32[512,768]{1,0:T(8,128)}, bf16[512,384]{1,0:T(8,128)(2,1)}, bf16[512,384]{1,0:T(8,128)(2,1)}, f32[8,768]{1,0:T(8...) custom-call(s32[3]{0:T(128)} %copy-done.66, ...), custom_call_target="tpu_custom_call" | custom-call | flops 1000000000 | bytes 1000000 | tf_op jit(solution)/shard_map/dense/pallas_call | solution.py:1087
  234.1 8.1 %collective-permute-done.28 = bf16[1536,768]{1,0:T(8,128)(2,1)S(1)} collective-permute-done((bf16[1536,768]{1,0:T(8,128)(2,1)}, bf16[1536,768]{1,0:T(8,128)(2,1)S(1)}, u32[]{:S(2)}, u32[]{:S(2)}) %collective-permute-start.28) | collective-permute-done | bytes 2359328 | tf_op jit(solution)/shard_map/ppermute | solution.py:1241
  247.8 10.0 %collective-permute-start.36 = (bf16[2,192,768]{2,1,0:T(8,128)(2,1)}, bf16[2,192,768]{2,1,0:T(8,128)(2,1)}, u32[]{:S(2)}, u32[]{:S(2)}) collective-permute-start(bf16[2,192,768]{2,1,0:T(8,128)(2,1)} %get-tuple-element.153), channel_id=1, source_target_pairs={{0,2},{1,3},{2,0},{3,1},{4,6},{5,7},{6,4},{7,5},{8,10},{9,11},{10,... | collective-permute-start | bytes 1769480 | tf_op jit(solution)/shard_map/ppermute | solution.py:1247
  258.8 29.4 %attend_backward.3 = (bf16[1024,128]{1,0:T(8,128)(2,1)}, bf16[256,2048]{1,0:T(8,128)(2,1)}, bf16[128,4096]{1,0:T(8,128)(2,1)}, f32[8,128]{1,0:T(8,128)}) custom-call(s32[2]{0:T(128)} %pad_add_fusion.1.refs_0_, s32[16,16]{1,0:T(8,128)} %copy-done.59, bf16[4,2,8,256,256]{4,3,2,1,0:T(8,128)(2,1)} %get-tuple-element.125.refs_2_, ...), custom_call_target="tpu_custom_call" | custom-call | flops 100000000 | bytes 1000000 | tf_op jit(solution)/shard_map/attend_backward/pallas_call | solution.py:334
  292.2 11.6 %collective-permute-start.30 = (bf16[2,128,768]{2,1,0:T(8,128)(2,1)}, bf16[2,128,768]{2,1,0:T(8,128)(2,1)}, u32[]{:S(2)}, u32[]{:S(2)}) collective-permute-start(bf16[2,128,768]{2,1,0:T(8,128)(2,1)} %get-tuple-element.277), channel_id=1, source_target_pairs={{0,4},{1,5},{2,6},{3,7},{4,0},{5,1},{6,2},{7,3},{8,20},{9,21},{10,... | collective-permute-start | bytes 1179656 | tf_op jit(solution)/shard_map/ppermute | solution.py:1256
  309.3 4.9 collective-permute-start.32
  314.2 4.0 collective-permute-start.33
  328.0 29.3 %attend_backward.4 = (bf16[1024,128]{1,0:T(8,128)(2,1)}, bf16[256,2048]{1,0:T(8,128)(2,1)}, bf16[128,4096]{1,0:T(8,128)(2,1)}, f32[8,128]{1,0:T(8,128)}) custom-call(s32[2]{0:T(128)} %pad_add_fusion.1.refs_0_, s32[16,16]{1,0:T(8,128)} %copy-done.59, bf16[4,2,8,256,256]{4,3,2,1,0:T(8,128)(2,1)} %get-tuple-element.136.refs_2_, ...), custom_call_target="tpu_custom_call" | custom-call | flops 100000000 | bytes 1000000 | tf_op jit(solution)/shard_map/attend_backward/pallas_call | solution.py:334
  358.9 12.4 %proj_grads.2 = bf16[768,1024]{1,0:T(8,128)(2,1)} custom-call(bf16[1024,768]{1,0:T(8,128)(2,1)} %bitcast.190, bf16[2048,768]{1,0:T(8,128)(2,1)} %bitcast.179, bf16[4096,768]{1,0:T(8,128)(2,1)} %copy-done.9, bf16[1024,128]{1,0:T(8,128)(2,1)} %get-tuple-element.133.refs_9_.refs_13_.refs_3_.refs_1_, ...), custom_call_target="tpu_custom_call" | custom-call | flops 1000000000 | bytes 1000000 | tf_op jit(solution)/shard_map/proj_grads/pallas_call | solution.py:784
  382.0 5.0 collective-permute-start.44
  388.0 5.0 collective-permute-start.40
  393.0 3.9 collective-permute-start.41
  398.6 29.2 %attend_backward.5 = (bf16[1024,128]{1,0:T(8,128)(2,1)}, bf16[256,2048]{1,0:T(8,128)(2,1)}, bf16[128,4096]{1,0:T(8,128)(2,1)}, f32[8,128]{1,0:T(8,128)}) custom-call(s32[2]{0:T(128)} %pad_add_fusion.1.refs_0_, s32[16,16]{1,0:T(8,128)} %copy-done.59, bf16[4,2,8,256,256]{4,3,2,1,0:T(8,128)(2,1)} %get-tuple-element.142.refs_2_, ...), custom_call_target="tpu_custom_call" | custom-call | flops 100000000 | bytes 1000000 | tf_op jit(solution)/shard_map/attend_backward/pallas_call | solution.py:334
  432.3 10.8 %proj_grads.3 = bf16[768,640]{1,0:T(8,128)(2,1)} custom-call(bf16[1024,768]{1,0:T(8,128)(2,1)} %bitcast.191, bf16[2048,768]{1,0:T(8,128)(2,1)} %bitcast.180, bf16[4096,768]{1,0:T(8,128)(2,1)} %copy-done.9, bf16[1024,128]{1,0:T(8,128)(2,1)} %get-tuple-element.158.refs_3_, bf16[256,2048]{1,0:T(8,128)(2,1)} %get-tuple-element.157.refs_4_.refs_3_, ...), custom_call_target="tpu_custom_call" | custom-call | flops 1000000000 | bytes 1000000 | tf_op jit(solution)/shard_map/proj_grads/pallas_call | solution.py:784
  452.3 6.5 %collective-permute-start.49 = (bf16[4,48,640]{2,1,0:T(8,128)(2,1)S(1)}, bf16[4,48,640]{2,1,0:T(8,128)(2,1)S(1)}, u32[]{:S(2)}, u32[]{:S(2)}) collective-permute-start(bf16[4,48,640]{2,1,0:T(8,128)(2,1)S(1)} %get-tuple-element.273), channel_id=1, source_target_pairs={{0,2},{1,3},{2,0},{3,1},{4,6},{5,7},{6,4},{7,5},{8,10},{9,11},{10,... | collective-permute-start | bytes 737288 | tf_op jit(solution)/shard_map/ppermute | solution.py:1247
  478.6 9.6 %collective-permute-done.61 = bf16[48,1664]{1,0:T(8,128)(2,1)S(1)} collective-permute-done((bf16[48,1664]{1,0:T(8,128)(2,1)S(1)}, bf16[48,1664]{1,0:T(8,128)(2,1)S(1)}, u32[]{:S(2)}, u32[]{:S(2)}) %collective-permute-start.61) | collective-permute-done | bytes 159776 | tf_op jit(solution)/shard_map/ppermute | solution.py:1244
  493.0 5.9 %collective-permute-start.55 = (bf16[128,768]{1,0:T(8,128)(2,1)S(1)}, bf16[128,768]{1,0:T(8,128)(2,1)S(1)}, u32[]{:S(2)}, u32[]{:S(2)}) collective-permute-start(bf16[128,768]{1,0:T(8,128)(2,1)S(1)} %get-tuple-element.290), channel_id=1, source_target_pairs={{0,0},{1,1},{2,2},{3,3},{4,4},{5,5},{6,6},{7,7},{8,16},{9,17},{10,... | collective-permute-start | bytes 589832 | tf_op jit(solution)/shard_map/ppermute | solution.py:1256
  502.2 5.0 collective-permute-done.55
  (405 shorter events, 150.9 us)
Async XLA Ops:
  4.8 22.9 %collective-permute-start = (bf16[336,768]{1,0:T(8,128)(2,1)}, bf16[336,768]{1,0:T(8,128)(2,1)S(1)}, u32[]{:S(2)}, u32[]{:S(2)}) collective-permute-start(bf16[336,768]{1,0:T(8,128)(2,1)} %get-tuple-element.98), channel_id=1, source_target_pairs={{0,0},{1,1},{2,2},{3,3},{4,4},{5,5},{6,6},{7,7},{8,16},{9,17},{10,... | collective-permute-start | bytes 1548296 | tf_op jit(solution)/shard_map/ppermute | solution.py:1256
  29.4 25.3 %collective-permute-start.7 = (bf16[336,768]{1,0:T(8,128)(2,1)S(1)}, bf16[336,768]{1,0:T(8,128)(2,1)S(1)}, u32[]{:S(2)}, u32[]{:S(2)}) collective-permute-start(bf16[336,768]{1,0:T(8,128)(2,1)S(1)} %collective-permute-done.6), channel_id=1, source_target_pairs={{0,1},{1,0},{2,3},{3,2},{4,5},{5,4},{6,7},{7,6},{8,9},{9,8},{10,11... | collective-permute-start | bytes 1548296 | tf_op jit(solution)/shard_map/ppermute | solution.py:1247
  30.7 24.5 %collective-permute-start.2 = (bf16[336,768]{1,0:T(8,128)(2,1)S(1)}, bf16[336,768]{1,0:T(8,128)(2,1)S(1)}, u32[]{:S(2)}, u32[]{:S(2)}) collective-permute-start(bf16[336,768]{1,0:T(8,128)(2,1)S(1)} %collective-permute-done), channel_id=1, source_target_pairs={{0,2},{1,3},{2,0},{3,1},{4,6},{5,7},{6,4},{7,5},{8,10},{9,11},{10,... | collective-permute-start | bytes 1548296 | tf_op jit(solution)/shard_map/ppermute | solution.py:1247
  64.5 26.6 %collective-permute-start.13 = (bf16[448,768]{1,0:T(8,128)(2,1)}, bf16[448,768]{1,0:T(8,128)(2,1)}, u32[]{:S(2)}, u32[]{:S(2)}) collective-permute-start(bf16[448,768]{1,0:T(8,128)(2,1)} %pack_late.1), channel_id=1, source_target_pairs={{0,0},{1,1},{2,2},{3,3},{4,4},{5,5},{6,6},{7,7},{8,16},{9,17},{10,... | collective-permute-start | bytes 2064392 | tf_op jit(solution)/shard_map/ppermute | solution.py:1256
  68.3 33.6 %collective-permute-start.14 = (bf16[448,768]{1,0:T(8,128)(2,1)}, bf16[448,768]{1,0:T(8,128)(2,1)}, u32[]{:S(2)}, u32[]{:S(2)}) collective-permute-start(bf16[448,768]{1,0:T(8,128)(2,1)} %pack_late.1), channel_id=1, source_target_pairs={{0,4},{1,5},{2,6},{3,7},{4,0},{5,1},{6,2},{7,3},{8,20},{9,21},{10,... | collective-permute-start | bytes 2064392 | tf_op jit(solution)/shard_map/ppermute | solution.py:1256
  104.5 69.2 %collective-permute-start.17 = (bf16[2,448,768]{2,1,0:T(8,128)(2,1)}, bf16[2,448,768]{2,1,0:T(8,128)(2,1)}, u32[]{:S(2)}, u32[]{:S(2)}) collective-permute-start(bf16[2,448,768]{2,1,0:T(8,128)(2,1)} %hold.1.refs_11_.refs_8_), channel_id=1, source_target_pairs={{0,1},{1,0},{2,3},{3,2},{4,5},{5,4},{6,7},{7,6},{8,9},{9,8},{10,11... | collective-permute-start | bytes 4128776 | tf_op jit(solution)/shard_map/ppermute | solution.py:1247
  104.5 69.2 %collective-permute-start.18 = (bf16[2,448,768]{2,1,0:T(8,128)(2,1)}, bf16[2,448,768]{2,1,0:T(8,128)(2,1)}, u32[]{:S(2)}, u32[]{:S(2)}) collective-permute-start(bf16[2,448,768]{2,1,0:T(8,128)(2,1)} %hold.1.refs_11_.refs_8_), channel_id=1, source_target_pairs={{0,2},{1,3},{2,0},{3,1},{4,6},{5,7},{6,4},{7,5},{8,10},{9,11},{10,... | collective-permute-start | bytes 4128776 | tf_op jit(solution)/shard_map/ppermute | solution.py:1247
  106.0 67.8 %collective-permute-start.19 = (bf16[2,448,768]{2,1,0:T(8,128)(2,1)}, bf16[2,448,768]{2,1,0:T(8,128)(2,1)}, u32[]{:S(2)}, u32[]{:S(2)}) collective-permute-start(bf16[2,448,768]{2,1,0:T(8,128)(2,1)} %hold.1.refs_11_.refs_8_), channel_id=1, source_target_pairs={{0,3},{1,2},{2,1},{3,0},{4,7},{5,6},{6,5},{7,4},{8,11},{9,10},{10,... | collective-permute-start | bytes 4128776 | tf_op jit(solution)/shard_map/ppermute | solution.py:1247
  108.1 43.5 %collective-permute-start.15 = (bf16[2,128,768]{2,1,0:T(8,128)(2,1)}, bf16[2,128,768]{2,1,0:T(8,128)(2,1)}, u32[]{:S(2)}, u32[]{:S(2)}) collective-permute-start(bf16[2,128,768]{2,1,0:T(8,128)(2,1)} %get-tuple-element.280), channel_id=1, source_target_pairs={{0,0},{1,1},{2,2},{3,3},{4,4},{5,5},{6,6},{7,7},{8,16},{9,17},{10,... | collective-permute-start | bytes 1179656 | tf_op jit(solution)/shard_map/ppermute | solution.py:1256
  110.3 42.5 %collective-permute-start.16 = (bf16[2,128,768]{2,1,0:T(8,128)(2,1)}, bf16[2,128,768]{2,1,0:T(8,128)(2,1)}, u32[]{:S(2)}, u32[]{:S(2)}) collective-permute-start(bf16[2,128,768]{2,1,0:T(8,128)(2,1)} %get-tuple-element.279), channel_id=1, source_target_pairs={{0,4},{1,5},{2,6},{3,7},{4,0},{5,1},{6,2},{7,3},{8,20},{9,21},{10,... | collective-permute-start | bytes 1179656 | tf_op jit(solution)/shard_map/ppermute | solution.py:1256
  173.7 25.1 %collective-permute-start.23 = (bf16[2,448,768]{2,1,0:T(8,128)(2,1)}, bf16[2,448,768]{2,1,0:T(8,128)(2,1)S(1)}, u32[]{:S(2)}, u32[]{:S(2)}) collective-permute-start(bf16[2,448,768]{2,1,0:T(8,128)(2,1)} %hold.1.refs_11_.refs_8_), channel_id=1, source_target_pairs={{0,16},{16,0},{1,17},{17,1},{2,18},{18,2},{3,19},{19,3},{4,20},{20... | collective-permute-start | bytes 4128776 | tf_op jit(solution)/shard_map/ppermute | solution.py:1241
  173.8 25.0 %collective-permute-start.24 = (bf16[2,448,768]{2,1,0:T(8,128)(2,1)}, bf16[2,448,768]{2,1,0:T(8,128)(2,1)S(1)}, u32[]{:S(2)}, u32[]{:S(2)}) collective-permute-start(bf16[2,448,768]{2,1,0:T(8,128)(2,1)} %collective-permute-done.17.refs_11_.refs_9_), channel_id=1, source_target_pairs={{0,16},{16,0},{1,17},{17,1},{2,18},{18,2},{3,19},{19,3},{4,20},{20... | collective-permute-start | bytes 4128776 | tf_op jit(solution)/shard_map/ppermute | solution.py:1241
  174.3 24.5 %collective-permute-start.25 = (bf16[2,448,768]{2,1,0:T(8,128)(2,1)}, bf16[2,448,768]{2,1,0:T(8,128)(2,1)}, u32[]{:S(2)}, u32[]{:S(2)}) collective-permute-start(bf16[2,448,768]{2,1,0:T(8,128)(2,1)} %collective-permute-done.18.refs_12_.refs_10_), channel_id=1, source_target_pairs={{0,16},{16,0},{1,17},{17,1},{2,18},{18,2},{3,19},{19,3},{4,20},{20... | collective-permute-start | bytes 4128776 | tf_op jit(solution)/shard_map/ppermute | solution.py:1241
  174.4 24.5 %collective-permute-start.26 = (bf16[2,448,768]{2,1,0:T(8,128)(2,1)}, bf16[2,448,768]{2,1,0:T(8,128)(2,1)}, u32[]{:S(2)}, u32[]{:S(2)}) collective-permute-start(bf16[2,448,768]{2,1,0:T(8,128)(2,1)} %collective-permute-done.19.refs_13_.refs_11_), channel_id=1, source_target_pairs={{0,16},{16,0},{1,17},{17,1},{2,18},{18,2},{3,19},{19,3},{4,20},{20... | collective-permute-start | bytes 4128776 | tf_op jit(solution)/shard_map/ppermute | solution.py:1241
  233.2 59.0 %collective-permute-start.31 = (bf16[384,3840]{1,0:T(8,128)(2,1)}, bf16[384,3840]{1,0:T(8,128)(2,1)}, u32[]{:S(2)}, u32[]{:S(2)}) collective-permute-start(bf16[384,3840]{1,0:T(8,128)(2,1)} %get-tuple-element.139), channel_id=1, source_target_pairs={{0,16},{16,0},{1,17},{17,1},{2,18},{18,2},{3,19},{19,3},{4,20},{20... | collective-permute-start | bytes 8847368 | tf_op jit(solution)/shard_map/ppermute | solution.py:1241
  233.7 24.1 %collective-permute-start.27 = (bf16[512,384]{1,0:T(8,128)(2,1)}, bf16[512,384]{1,0:T(8,128)(2,1)S(1)}, u32[]{:S(2)}, u32[]{:S(2)}) collective-permute-start(bf16[512,384]{1,0:T(8,128)(2,1)} %get-tuple-element.127), channel_id=1, source_target_pairs={{0,16},{16,0},{1,17},{17,1},{2,18},{18,2},{3,19},{19,3},{4,20},{20... | collective-permute-start | bytes 1179656 | tf_op jit(solution)/shard_map/ppermute | solution.py:1241
  245.8 63.5 %collective-permute-start.35 = (bf16[2,192,768]{2,1,0:T(8,128)(2,1)}, bf16[2,192,768]{2,1,0:T(8,128)(2,1)}, u32[]{:S(2)}, u32[]{:S(2)}) collective-permute-start(bf16[2,192,768]{2,1,0:T(8,128)(2,1)} %get-tuple-element.152), channel_id=1, source_target_pairs={{0,1},{1,0},{2,3},{3,2},{4,5},{5,4},{6,7},{7,6},{8,9},{9,8},{10,11... | collective-permute-start | bytes 1769480 | tf_op jit(solution)/shard_map/ppermute | solution.py:1247
  247.8 66.4 %collective-permute-start.36 = (bf16[2,192,768]{2,1,0:T(8,128)(2,1)}, bf16[2,192,768]{2,1,0:T(8,128)(2,1)}, u32[]{:S(2)}, u32[]{:S(2)}) collective-permute-start(bf16[2,192,768]{2,1,0:T(8,128)(2,1)} %get-tuple-element.153), channel_id=1, source_target_pairs={{0,2},{1,3},{2,0},{3,1},{4,6},{5,7},{6,4},{7,5},{8,10},{9,11},{10,... | collective-permute-start | bytes 1769480 | tf_op jit(solution)/shard_map/ppermute | solution.py:1247
  257.7 60.4 %collective-permute-start.37 = (bf16[2,192,768]{2,1,0:T(8,128)(2,1)}, bf16[2,192,768]{2,1,0:T(8,128)(2,1)}, u32[]{:S(2)}, u32[]{:S(2)}) collective-permute-start(bf16[2,192,768]{2,1,0:T(8,128)(2,1)} %get-tuple-element.154), channel_id=1, source_target_pairs={{0,3},{1,2},{2,1},{3,0},{4,7},{5,6},{6,5},{7,4},{8,11},{9,10},{10,... | collective-permute-start | bytes 1769480 | tf_op jit(solution)/shard_map/ppermute | solution.py:1247
  290.3 32.0 %collective-permute-start.29 = (bf16[2,128,768]{2,1,0:T(8,128)(2,1)}, bf16[2,128,768]{2,1,0:T(8,128)(2,1)}, u32[]{:S(2)}, u32[]{:S(2)}) collective-permute-start(bf16[2,128,768]{2,1,0:T(8,128)(2,1)} %get-tuple-element.278), channel_id=1, source_target_pairs={{0,0},{1,1},{2,2},{3,3},{4,4},{5,5},{6,6},{7,7},{8,16},{9,17},{10,... | collective-permute-start | bytes 1179656 | tf_op jit(solution)/shard_map/ppermute | solution.py:1256
  292.2 33.4 %collective-permute-start.30 = (bf16[2,128,768]{2,1,0:T(8,128)(2,1)}, bf16[2,128,768]{2,1,0:T(8,128)(2,1)}, u32[]{:S(2)}, u32[]{:S(2)}) collective-permute-start(bf16[2,128,768]{2,1,0:T(8,128)(2,1)} %get-tuple-element.277), channel_id=1, source_target_pairs={{0,4},{1,5},{2,6},{3,7},{4,0},{5,1},{6,2},{7,3},{8,20},{9,21},{10,... | collective-permute-start | bytes 1179656 | tf_op jit(solution)/shard_map/ppermute | solution.py:1256
  309.3 48.1 %collective-permute-start.32 = (bf16[2,48,3840]{2,1,0:T(8,128)(2,1)}, bf16[2,48,3840]{2,1,0:T(8,128)(2,1)S(1)}, u32[]{:S(2)}, u32[]{:S(2)}) collective-permute-start(bf16[2,48,3840]{2,1,0:T(8,128)(2,1)} %get-tuple-element.149), channel_id=1, source_target_pairs={{0,1},{1,0},{2,3},{3,2},{4,5},{5,4},{6,7},{7,6},{8,9},{9,8},{10,11... | collective-permute-start | bytes 2211848 | tf_op jit(solution)/shard_map/ppermute | solution.py:1247
  314.2 43.2 %collective-permute-start.33 = (bf16[2,48,3840]{2,1,0:T(8,128)(2,1)}, bf16[2,48,3840]{2,1,0:T(8,128)(2,1)S(1)}, u32[]{:S(2)}, u32[]{:S(2)}) collective-permute-start(bf16[2,48,3840]{2,1,0:T(8,128)(2,1)} %get-tuple-element.150), channel_id=1, source_target_pairs={{0,2},{1,3},{2,0},{3,1},{4,6},{5,7},{6,4},{7,5},{8,10},{9,11},{10,... | collective-permute-start | bytes 2211848 | tf_op jit(solution)/shard_map/ppermute | solution.py:1247
  318.2 39.3 %collective-permute-start.34 = (bf16[2,48,3840]{2,1,0:T(8,128)(2,1)}, bf16[2,48,3840]{2,1,0:T(8,128)(2,1)S(1)}, u32[]{:S(2)}, u32[]{:S(2)}) collective-permute-start(bf16[2,48,3840]{2,1,0:T(8,128)(2,1)} %get-tuple-element.151), channel_id=1, source_target_pairs={{0,3},{1,2},{2,1},{3,0},{4,7},{5,6},{6,5},{7,4},{8,11},{9,10},{10,... | collective-permute-start | bytes 2211848 | tf_op jit(solution)/shard_map/ppermute | solution.py:1247
  322.3 35.1 %collective-permute-start.38 = (bf16[192,768]{1,0:T(8,128)(2,1)}, bf16[192,768]{1,0:T(8,128)(2,1)S(1)}, u32[]{:S(2)}, u32[]{:S(2)}) collective-permute-start(bf16[192,768]{1,0:T(8,128)(2,1)} %get-tuple-element.155), channel_id=1, source_target_pairs={{0,0},{1,1},{2,2},{3,3},{4,4},{5,5},{6,6},{7,7},{8,16},{9,17},{10,... | collective-permute-start | bytes 884744 | tf_op jit(solution)/shard_map/ppermute | solution.py:1256
  325.6 31.7 %collective-permute-start.39 = (bf16[192,768]{1,0:T(8,128)(2,1)}, bf16[192,768]{1,0:T(8,128)(2,1)S(1)}, u32[]{:S(2)}, u32[]{:S(2)}) collective-permute-start(bf16[192,768]{1,0:T(8,128)(2,1)} %get-tuple-element.156), channel_id=1, source_target_pairs={{0,4},{1,5},{2,6},{3,7},{4,0},{5,1},{6,2},{7,3},{8,20},{9,21},{10,... | collective-permute-start | bytes 884744 | tf_op jit(solution)/shard_map/ppermute | solution.py:1256
  374.8 22.1 %collective-permute-start.45 = (bf16[192,768]{1,0:T(8,128)(2,1)S(1)}, bf16[192,768]{1,0:T(8,128)(2,1)S(1)}, u32[]{:S(2)}, u32[]{:S(2)}) collective-permute-start(bf16[192,768]{1,0:T(8,128)(2,1)S(1)} %add_up.4), channel_id=1, source_target_pairs={{0,16},{16,0},{1,17},{17,1},{2,18},{18,2},{3,19},{19,3},{4,20},{20... | collective-permute-start | bytes 884744 | tf_op jit(solution)/shard_map/ppermute | solution.py:1241
  378.3 52.7 %collective-permute-start.43 = (bf16[48,3840]{1,0:T(8,128)(2,1)S(1)}, bf16[48,3840]{1,0:T(8,128)(2,1)S(1)}, u32[]{:S(2)}, u32[]{:S(2)}) collective-permute-start(bf16[48,3840]{1,0:T(8,128)(2,1)S(1)} %get-tuple-element.165), channel_id=1, source_target_pairs={{0,0},{1,1},{2,2},{3,3},{4,4},{5,5},{6,6},{7,7},{8,16},{9,17},{10,... | collective-permute-start | bytes 1105928 | tf_op jit(solution)/shard_map/ppermute | solution.py:1256
  382.0 49.1 %collective-permute-start.44 = (bf16[48,3840]{1,0:T(8,128)(2,1)S(1)}, bf16[48,3840]{1,0:T(8,128)(2,1)S(1)}, u32[]{:S(2)}, u32[]{:S(2)}) collective-permute-start(bf16[48,3840]{1,0:T(8,128)(2,1)S(1)} %get-tuple-element.166), channel_id=1, source_target_pairs={{0,4},{1,5},{2,6},{3,7},{4,0},{5,1},{6,2},{7,3},{8,20},{9,21},{10,... | collective-permute-start | bytes 1105928 | tf_op jit(solution)/shard_map/ppermute | solution.py:1256
  388.0 43.1 %collective-permute-start.40 = (bf16[4,48,1024]{2,1,0:T(8,128)(2,1)}, bf16[4,48,1024]{2,1,0:T(8,128)(2,1)S(1)}, u32[]{:S(2)}, u32[]{:S(2)}) collective-permute-start(bf16[4,48,1024]{2,1,0:T(8,128)(2,1)} %get-tuple-element.270), channel_id=1, source_target_pairs={{0,1},{1,0},{2,3},{3,2},{4,5},{5,4},{6,7},{7,6},{8,9},{9,8},{10,11... | collective-permute-start | bytes 1179656 | tf_op jit(solution)/shard_map/ppermute | solution.py:1247
  393.0 38.1 %collective-permute-start.41 = (bf16[4,48,1024]{2,1,0:T(8,128)(2,1)}, bf16[4,48,1024]{2,1,0:T(8,128)(2,1)S(1)}, u32[]{:S(2)}, u32[]{:S(2)}) collective-permute-start(bf16[4,48,1024]{2,1,0:T(8,128)(2,1)} %get-tuple-element.269), channel_id=1, source_target_pairs={{0,2},{1,3},{2,0},{3,1},{4,6},{5,7},{6,4},{7,5},{8,10},{9,11},{10,... | collective-permute-start | bytes 1179656 | tf_op jit(solution)/shard_map/ppermute | solution.py:1247
  397.6 33.4 %collective-permute-start.42 = (bf16[4,48,1024]{2,1,0:T(8,128)(2,1)}, bf16[4,48,1024]{2,1,0:T(8,128)(2,1)S(1)}, u32[]{:S(2)}, u32[]{:S(2)}) collective-permute-start(bf16[4,48,1024]{2,1,0:T(8,128)(2,1)} %get-tuple-element.268), channel_id=1, source_target_pairs={{0,3},{1,2},{2,1},{3,0},{4,7},{5,6},{6,5},{7,4},{8,11},{9,10},{10,... | collective-permute-start | bytes 1179656 | tf_op jit(solution)/shard_map/ppermute | solution.py:1247
  (133 other events, 1077.9 us)

commit v4 on v3

--- a/solution.py
+++ b/solution.py
@@ -57,6 +57,24 @@
         kernel(*refs[:count], *refs[count + extra :])
 
     return run
+
+
+def reversal():
+    down = lax.broadcasted_iota(jnp.int32, (KB, KB), 0)
+    across = lax.broadcasted_iota(jnp.int32, (KB, KB), 1)
+    return jnp.where(down + across == KB - 1, 1.0, 0.0).astype(BF)
+
+
+def by_two(count, work):
+    def step(i, carry):
+        work([2 * i, 2 * i + 1])
+        return carry
+
+    lax.fori_loop(0, count // 2, step, 0)
+
+    @pl.when(count % 2 == 1)
+    def last():
+        work([count - 1])
 
 
 def forward_kernel(
@@ -81,9 +99,15 @@
     s_scr,
     m_scr,
     acc_scr,
+    flip_scr,
     list_scr,
 ):
     block = pl.program_id(0)
+
+    @pl.when(block == 0)
+    def start():
+        flip_scr[...] = reversal()
+
     row = base_ref[0] + base_ref[1] * block
     base = nkb * KB - R - R * row
     count = live_list(live_ref, list_scr, row, nkb)
@@ -100,8 +124,10 @@
         plain = ((q + vec_ref[0:1, half]) * (SCALE * LOG2E)).astype(BF)
         place = ((q + vec_ref[1:2, half]) * (SCALE * LOG2E)).astype(BF)
         label = q + vec_ref[2:3, half]
-        same = mm(label, table_ref[h, 0], precision=HIGHEST)
-        other = mm(label, table_ref[h, 1], precision=HIGHEST)
+        top_part = label.astype(BF)
+        rest = (label - top_part.astype(F32)).astype(BF)
+        both = mm(jnp.concatenate([top_part, rest], axis=1), table_ref[h])
+        same, other = both[:, :128], both[:, 128:]
         term = jnp.where(hot_row > 0.5, same, other) * (SCALE * LOG2E) + outside
         high = term.astype(BF).astype(F32)
         extra = jnp.where(lane < NS, high, jnp.where(lane < 2 * NS, term - high, 0.0))
@@ -111,38 +137,48 @@
     m_scr[...] = jnp.full(m_scr.shape, -jnp.inf, F32)
     acc_scr[...] = jnp.zeros(acc_scr.shape, F32)
 
-    def score(n, carry):
-        k0 = pl.multiple_of(list_scr[n] * KB, KB)
-        ok = rank_ref[:, pl.ds(k0, KB)] <= limit
-        window = rel_ref[pl.ds(pl.multiple_of(base + k0, 128), W), :]
-        keys = jnp.concatenate([kv_ref[pl.ds(k0, KB), :128], hot_ref[pl.ds(k0, KB), :]], axis=1)
+    def score(blocks):
+        highest = [m_scr[h] for h in range(2)]
+        for n in blocks:
+            k0 = pl.multiple_of(list_scr[n] * KB, KB)
+            ok = rank_ref[:, pl.ds(k0, KB)] <= limit
+            window = rel_ref[pl.ds(pl.multiple_of(base + k0, 128), W), :]
+            keys = jnp.concatenate(
+                [kv_ref[pl.ds(k0, KB), :128], hot_ref[pl.ds(k0, KB), :]], axis=1
+            )
+            for h in range(2):
+                s = mm(qq_scr[h], keys, 1, 1)
+                full = mm(qr_scr[h], window, 1, 1)
+                shifted = [
+                    pltpu.roll(
+                        full[i * R : i * R + R], W - (R - 1), 1, stride=1, stride_axis=0
+                    )[:, :KB]
+                    for i in range(2)
+                ]
+                s = jnp.where(ok, s + jnp.concatenate(shifted, axis=0), NEG)
+                s_scr[h, n] = s
+                highest[h] = jnp.maximum(highest[h], jnp.maximum(s[:, :128], s[:, 128:]))
         for h in range(2):
-            s = mm(qq_scr[h], keys, 1, 1)
-            full = mm(qr_scr[h], window, 1, 1)
-            shifted = [
-                pltpu.roll(full[i * R : i * R + R], W - (R - 1), 1, stride=1, stride_axis=0)[
-                    :, :KB
-                ]
-                for i in range(2)
-            ]
-            s = jnp.where(ok, s + jnp.concatenate(shifted, axis=0), NEG)
-            s_scr[h, n] = s
-            m_scr[h] = jnp.maximum(m_scr[h], jnp.maximum(s[:, :128], s[:, 128:]))
-        return carry
-
-    lax.fori_loop(0, count, score, 0)
+            m_scr[h] = highest[h]
+
+    by_two(count, score)
     top = [jnp.max(m_scr[h], axis=1, keepdims=True) for h in range(2)]
 
-    def mix(n, carry):
-        k0 = pl.multiple_of(list_scr[n] * KB, KB)
-        values = jnp.concatenate([kv_ref[pl.ds(k0, KB), 128:], hot_ref[pl.ds(k0, KB), :]], axis=1)
+    def mix(blocks):
+        totals = [0.0, 0.0]
+        for n in blocks:
+            k0 = pl.multiple_of(list_scr[n] * KB, KB)
+            values = jnp.concatenate(
+                [kv_ref[pl.ds(k0, KB), 128:], hot_ref[pl.ds(k0, KB), :]], axis=1
+            )
+            for h in range(2):
+                p = jnp.exp2(s_scr[h, n] - top[h]).astype(BF)
+                p_ref[0, h, n] = mm(p, flip_scr[...]).astype(BF)
+                totals[h] += mm(p, values)
         for h in range(2):
-            p = jnp.exp2(s_scr[h, n] - top[h]).astype(BF)
-            p_ref[0, h, n] = p
-            acc_scr[h] += mm(p, values)
-        return carry
-
-    lax.fori_loop(0, count, mix, 0)
+            acc_scr[h] += totals[h]
+
+    by_two(count, mix)
     for h in range(2):
         half = slice(DH * h, DH * h + DH)
         acc = acc_scr[h]
@@ -166,7 +202,7 @@
             in_specs=[
                 pl.BlockSpec((2 * R, 128), lambda b, *_: (b, pair)),
                 pl.BlockSpec((8, 128), lambda b, *_: (0, pair)),
-                pl.BlockSpec((2, 2, DH, 128), lambda b, *_: (pair, 0, 0, 0)),
+                pl.BlockSpec((2, 2 * DH, 256), lambda b, *_: (pair, 0, 0)),
                 pl.BlockSpec((2 * R, 128), lambda b, *_: (b, 0)),
                 whole(128, 128),
                 pl.BlockSpec((length, 256), lambda b, *_: (0, pair)),
@@ -187,6 +223,7 @@
                 pltpu.VMEM((2, nkb, 2 * R, KB), F32),
                 pltpu.VMEM((2, 2 * R, 128), F32),
                 pltpu.VMEM((2, 2 * R, 256), F32),
+                pltpu.VMEM((KB, KB), BF),
                 pltpu.SMEM((nkb + 1,), jnp.int32),
             ],
         ),
@@ -231,6 +268,7 @@
     accr_scr,
     dkv_scr,
     drel_scr,
+    keys_scr,
     flip_scr,
     list_scr,
 ):
@@ -245,9 +283,12 @@
         dkv_scr[...] = jnp.zeros(dkv_scr.shape, F32)
         drel_scr[...] = jnp.zeros(drel_scr.shape, F32)
         small_ref[...] = jnp.zeros(small_ref.shape, F32)
-        down = lax.broadcasted_iota(jnp.int32, (KB, KB), 0)
-        across = lax.broadcasted_iota(jnp.int32, (KB, KB), 1)
-        flip_scr[...] = jnp.where(down + across == KB - 1, 1.0, 0.0).astype(BF)
+        flip = reversal()
+        flip_scr[...] = flip
+        for kb in range(nkb):
+            rows = slice(kb * KB, (kb + 1) * KB)
+            keys_scr[rows, :256] = mm(flip, kv_ref[rows, :]).astype(BF)
+            keys_scr[rows, 256:] = mm(flip, hot_ref[rows, :]).astype(BF)
 
     lane = lax.broadcasted_iota(jnp.int32, (2 * R, 128), 1)
     zero = jnp.zeros((2 * R, DH), BF)
@@ -269,39 +310,44 @@
     acc_scr[...] = jnp.zeros(acc_scr.shape, F32)
     accr_scr[...] = jnp.zeros(accr_scr.shape, F32)
 
-    def step(n, carry):
-        k0 = pl.multiple_of(list_scr[n] * KB, KB)
-        r0 = pl.multiple_of(2 * length - base - k0 - W, 128)
-        hot = hot_ref[pl.ds(k0, KB), :]
-        window = rel_ref[pl.ds(r0, W), :]
+    def step(blocks):
         pad = jnp.zeros((R, W - KB), F32)
-        keys = jnp.concatenate([kv_ref[pl.ds(k0, KB), :128], hot], axis=1)
-        values = jnp.concatenate([kv_ref[pl.ds(k0, KB), 128:], hot], axis=1)
+        d_query = [0.0, 0.0]
+        d_place = [0.0, 0.0]
+        for n in blocks:
+            k0 = pl.multiple_of(list_scr[n] * KB, KB)
+            r0 = pl.multiple_of(2 * length - base - k0 - W, 128)
+            window = rel_ref[pl.ds(r0, W), :]
+            keys = jnp.concatenate(
+                [keys_scr[pl.ds(k0, KB), :128], keys_scr[pl.ds(k0, KB), 256:]], axis=1
+            )
+            values = keys_scr[pl.ds(k0, KB), 128:]
+            for h in range(2):
+                p = p_ref[0, h, n]
+                wide = p.astype(F32) * mm(dd_scr[h], values, 1, 1)
+                ds = wide.astype(BF)
+                d_query[h] += mm(ds, keys)
+                full = [
+                    pltpu.roll(
+                        jnp.concatenate([wide[i * R : i * R + R], pad], axis=1),
+                        0,
+                        1,
+                        stride=1,
+                        stride_axis=0,
+                    )
+                    for i in range(2)
+                ]
+                full = jnp.concatenate(full, axis=0).astype(BF)
+                d_place[h] += mm(full, window)
+                low, high = DH * h, DH * h + DH
+                dkv_scr[low:high, pl.ds(k0, KB)] += mm(turn_scr[h, 0], ds)
+                dkv_scr[128 + low : 128 + high, pl.ds(k0, KB)] += mm(turn_scr[h, 1], p)
+                drel_scr[low:high, pl.ds(r0, W)] += mm(turn_scr[h, 2], full)
         for h in range(2):
-            p = p_ref[0, h, n]
-            dd = dd_scr[h]
-            ds = (p.astype(F32) * mm(dd, values, 1, 1)).astype(BF)
-            acc_scr[h] += mm(ds, keys)
-            turned = mm(ds, flip_scr[...])
-            full = [
-                pltpu.roll(
-                    jnp.concatenate([turned[i * R : i * R + R], pad], axis=1),
-                    0,
-                    1,
-                    stride=1,
-                    stride_axis=0,
-                )
-                for i in range(2)
-            ]
-            full = jnp.concatenate(full, axis=0).astype(BF)
-            accr_scr[h] += mm(full, window)
-            low, high = DH * h, DH * h + DH
-            dkv_scr[low:high, pl.ds(k0, KB)] += mm(turn_scr[h, 0], ds)
-            dkv_scr[128 + low : 128 + high, pl.ds(k0, KB)] += mm(turn_scr[h, 1], p)
-            drel_scr[low:high, pl.ds(r0, W)] += mm(turn_scr[h, 2], full)
-        return carry
-
-    lax.fori_loop(0, count, step, 0)
+            acc_scr[h] += d_query[h]
+            accr_scr[h] += d_place[h]
+
+    by_two(count, step)
     hot_row = row_features(info_ref[:, 0:1])
     for h in range(2):
         half = slice(DH * h, DH * h + DH)
@@ -320,8 +366,11 @@
 
     @pl.when(block == nb - 1)
     def finish():
-        dkv_ref[:128, :] = (dkv_scr[:128, :] * LN2).astype(BF)
-        dkv_ref[128:, :] = dkv_scr[128:, :].astype(BF)
+        down = lax.broadcasted_iota(jnp.int32, (256, KB), 0)
+        factor = jnp.where(down < 128, LN2, 1.0)
+        for kb in range(nkb):
+            cols = slice(kb * KB, (kb + 1) * KB)
+            dkv_ref[:, cols] = mm((dkv_scr[:, cols] * factor).astype(BF), flip_scr[...]).astype(BF)
         drel_ref[...] = (drel_scr[...] * LN2).astype(BF)
 
 
@@ -362,6 +411,7 @@
                 pltpu.VMEM((2, 2 * R, 128), F32),
                 pltpu.VMEM((256, length), F32),
                 pltpu.VMEM((128, 2 * length), F32),
+                pltpu.VMEM((length, 384), BF),
                 pltpu.VMEM((KB, KB), BF),
                 pltpu.SMEM((nkb + 1,), jnp.int32),
             ],
@@ -1334,9 +1384,10 @@
     queries = mm(inputs, wq)
     kv = mm(content_full, kv_weight).astype(BF)
     vec8 = jnp.pad(head_vecs, ((0, 3), (0, 0)))
-    table = head_vecs[3:5].reshape(2, heads, DH).swapaxes(0, 1)
-    table = jnp.where(jnp.arange(128) < 2 * NS, table[..., None], 0.0)
-    late = hold(late[0], late[1], [content_full])
+    table = head_vecs[3:5].reshape(2, heads, DH).transpose(1, 2, 0)[..., None]
+    table = jnp.where(jnp.arange(128) < 2 * NS, table, 0.0).astype(BF)
+    table = jnp.tile(table.reshape(heads, DH, 256), (1, 2, 1))
+    late = hold(late[0], late[1], [rel])
     late_near = [late] + [near(late, step) for step in range(1, m)]
     forward = []
     got_mixed = []
@@ -1425,19 +1476,17 @@
             inputs, content_full, position_bf, [backward[p] for p in some], extra, after
         ).reshape(groups, m, ws, -1)
 
-    late_parts = near_fold([late_mine, swap(late_other)], fs, [])
-    back(0, late_parts[:1])
+    result = result.reshape(2, 2, r, d)
+    outs_got = [across(pick(result, low ^ e), e) for e in range(2)]
+    back(0, [])
     after = [backward[0][0]]
+    late_parts = near_fold([late_mine, swap(late_other)], fs, after + outs_got)
     early_parts = near_fold([early_mine, swap(early_other)], ws, after)
-    late_cross = cross_join(late_parts, after)
-    result, unused = tie((result, backward[0][0]))
-    outs = cross(result.reshape(2, 2, r, d))
-    back(1, [early_parts[0]])
-    some_grads = proj_some(range(pairs - 1), [], early_parts[1:] + late_cross + [outs])
+    back(1, [early_parts[0], late_parts[0]])
+    some_grads = proj_some(range(pairs - 1), [], [])
     some_parts = near_parts(some_grads, 1)
-    early_cross = cross_join(early_parts, [])
-    late_sum = add_up(late_cross, BF, [some_grads])
-    late_got = swap(late_sum)
+    late_cross = cross_join(late_parts, [some_grads])
+    early_cross = cross_join(early_parts, [some_grads])
     back(2, [some_grads])
 
     small = jnp.concatenate([b[3][:5] for b in backward], axis=1)
@@ -1449,10 +1498,12 @@
     inner_vecs = inner_vecs[0].reshape(n, fs // ws, ws).swapaxes(1, 2).reshape(d, fs // ws)
     small = jnp.concatenate([small.T, row_vecs[:5].T, inner_vecs], axis=1)
     small = jnp.pad(small, ((0, 0), (0, 128 - small.shape[1]))).astype(BF)
-    last_grads = proj_some([pairs - 1], [small], some_parts[1:] + early_cross + [late_got])
+    last_grads = proj_some([pairs - 1], [small], some_parts[1:] + late_cross + early_cross)
     early_sum = add_up(early_cross, BF, [last_grads])
-    late_sum, late_got, unused = tie((late_sum, late_got, last_grads))
-    early_got = swap(early_sum)
+    late_sum = add_up(late_cross, BF, [last_grads])
+    early_got, late_got = swap(early_sum), swap(late_sum)
+    *outs_got, unused = tie((*outs_got, last_grads))
+    outs = pair_of(outs_got[0], outs_got[1], low)
     last_parts = near_parts(last_grads, 1)
     which = [jnp.asarray(x, jnp.int32).reshape(1) for x in (k, 1 - k)]
     dkv_parts = [b[1] for b in backward]
@@ -1461,7 +1512,7 @@
     got_q = swap(input_grad(which[1], dq_parts, wq, BF, [last_grads]))
     own_kv = input_grad(which[0], dkv_parts, kv_weight, F32, [last_grads], True)
     own_q = input_grad(which[0], dq_parts, wq, F32, [last_grads])
-    content_parts = near_fold([own_kv, got_kv], r, [own_q, early_got] + last_parts[1:])
+    content_parts = near_fold([own_kv, got_kv], r, [own_q, early_got, late_got] + last_parts[1:])
     q_sum = own_q + got_q.astype(F32) + grad_residual
     q_sum = q_sum.reshape(2, 2, r, d)
     query_rows, unused = tie((q_sum[:, 1].astype(BF), content_parts[1]))

time: 511 us -> 465 us (0.910)
  Pallas kernels: 235 us -> 214 us
  waiting for transfers between devices: 98.3 us -> 77.9 us
    pallas_call x3, Pallas kernels: 87.9 us -> 70.3 us  [attend_backward(): pl.pallas_call(ordered(functools.partial(backward_kernel, nkb, nb), 12, l...]
    ppermute x18, waiting for transfers between devices: 49.1 us -> 37.5 us  [across(): return lax.ppermute(x, ('rep', 'shard'), moves)]
    ppermute x24, starting transfers between devices: 49.3 us -> 41.9 us  [near(): return lax.ppermute(x, 'shard', [(i, i ^ step) for i in range(n)])]
    ppermute x18, waiting for transfers between devices: 11 us -> 4.26 us  [swap(): return lax.ppermute(x, 'rep', [(i, i ^ 1) for i in range(nr)])]
    pallas_call x3, Pallas kernels: 56.6 us -> 50.2 us  [attend_forward(): pl.pallas_call(ordered(functools.partial(forward_kernel, nkb), 11, len(af...]
    ppermute x3, starting transfers between devices: 3.17 us -> 8.76 us  [far(): return lax.ppermute(x, 'shard', [(i, i ^ m * step) for i in range(n)])]
    unnamed x210 -> x170, local copies, waits for them, and re-layouts: 27.7 us -> 26.8 us
  transfers between devices with their start and end apart: 63 -> 63, of which waited for: 22 -> 18; matrix products, arithmetic and copies ran while one was open for 7% -> 7% of each run, Pallas kernels for 34% -> 35%
where the time goes in v4:
time: 465 us
  Pallas kernels  214 us (46%)
  starting transfers between devices  110 us (24%)
  waiting for transfers between devices  77.9 us (17%)
  local copies, waits for them, and re-layouts  44.4 us (10%)
  other arithmetic  10.1 us (2%)
  matrix products  6.08 us (1%)
    pallas_call x3, Pallas kernels, attend_backward(): pl.pallas_call(ordered(functools.partial(backward_kernel, nkb, nb), 12, l...  70.3 us
    ppermute x18, starting transfers between devices, across(): return lax.ppermute(x, ('rep', 'shard'), moves)  52 us
    pallas_call x3, Pallas kernels, attend_forward(): pl.pallas_call(ordered(functools.partial(forward_kernel, nkb), 11, len(af...  50.2 us
    ppermute x24, starting transfers between devices, near(): return lax.ppermute(x, 'shard', [(i, i ^ step) for i in range(n)])  41.9 us
    ppermute x18, waiting for transfers between devices, across(): return lax.ppermute(x, ('rep', 'shard'), moves)  37.5 us
    pallas_call x1, Pallas kernels, dense(): pl.pallas_call(functools.partial(dense_kernel, m, n, ws, pairs), grid_spe...  32.6 us
    unnamed x170, local copies, waits for them, and re-layouts  26.8 us
    ppermute x24, waiting for transfers between devices, near(): return lax.ppermute(x, 'shard', [(i, i ^ step) for i in range(n)])  25.7 us
  transfers between devices with their start and end apart: 63, of which 18 were waited for; matrix products, arithmetic and copies ran while one was open for 7% of the time, Pallas kernels for 35%

profile of v4, /device:TPU:9, one launch (start us, length us, event | category | flops | bytes accessed | tf_op | source)
XLA Modules:
  0.0 465.4 jit_solution(7839740750840060812)
XLA Ops:
  7.7 8.8 %collective-permute-done.4 = bf16[336,768]{1,0:T(8,128)(2,1)S(1)} collective-permute-done((bf16[336,768]{1,0:T(8,128)(2,1)}, bf16[336,768]{1,0:T(8,128)(2,1)S(1)}, u32[]{:S(2)}, u32[]{:S(2)}) %collective-permute-start.4) | collective-permute-done | bytes 516128 | tf_op jit(solution)/shard_map/ppermute | solution.py:1306
  17.7 10.0 %collective-permute-done = bf16[336,768]{1,0:T(8,128)(2,1)S(1)} collective-permute-done((bf16[336,768]{1,0:T(8,128)(2,1)}, bf16[336,768]{1,0:T(8,128)(2,1)S(1)}, u32[]{:S(2)}, u32[]{:S(2)}) %collective-permute-start) | collective-permute-done | bytes 516128 | tf_op jit(solution)/shard_map/ppermute | solution.py:1306
  31.9 9.6 %collective-permute-done.1 = bf16[336,768]{1,0:T(8,128)(2,1)S(1)} collective-permute-done((bf16[336,768]{1,0:T(8,128)(2,1)S(1)}, bf16[336,768]{1,0:T(8,128)(2,1)S(1)}, u32[]{:S(2)}, u32[]{:S(2)}) %collective-permute-start.1) | collective-permute-done | bytes 516128 | tf_op jit(solution)/shard_map/ppermute | solution.py:1297
  41.7 7.6 %collective-permute-done.5 = bf16[336,768]{1,0:T(8,128)(2,1)S(1)} collective-permute-done((bf16[336,768]{1,0:T(8,128)(2,1)S(1)}, bf16[336,768]{1,0:T(8,128)(2,1)S(1)}, u32[]{:S(2)}, u32[]{:S(2)}) %collective-permute-start.5) | collective-permute-done | bytes 516128 | tf_op jit(solution)/shard_map/ppermute | solution.py:1297
  49.2 5.5 %collective-permute-done.7 = bf16[336,768]{1,0:T(8,128)(2,1)S(1)} collective-permute-done((bf16[336,768]{1,0:T(8,128)(2,1)S(1)}, bf16[336,768]{1,0:T(8,128)(2,1)S(1)}, u32[]{:S(2)}, u32[]{:S(2)}) %collective-permute-start.7) | collective-permute-done | bytes 516128 | tf_op jit(solution)/shard_map/ppermute | solution.py:1297
  65.7 3.7 collective-permute-start.13
  70.6 4.7 %collective-permute-done.11 = bf16[128,768]{1,0:T(8,128)(2,1)S(1)} collective-permute-done((bf16[128,768]{1,0:T(8,128)(2,1)S(1)}, bf16[128,768]{1,0:T(8,128)(2,1)S(1)}, u32[]{:S(2)}, u32[]{:S(2)}) %collective-permute-start.11) | collective-permute-done | bytes 196640 | tf_op jit(solution)/shard_map/ppermute | solution.py:1306
  78.7 3.7 assemble.1
  85.2 6.4 %relative.1 = (bf16[4096,768]{1,0:T(8,128)(2,1)S(1)}, bf16[4096,384]{1,0:T(8,128)(2,1)S(1)}, bf16[4096,384]{1,0:T(8,128)(2,1)S(1)}) custom-call(f32[16,4,384]{2,1,0:T(4,128)S(1)} %get-tuple-element.318.sa_ref, f32[16,4,384]{2,1,0:T(4,128)S(1)} %get-tuple-element.317.ca_ref, f32[64,384]{1,0:T(8,128)S(1)} %copy-done.50, ...), custom_call_target="tpu_custom_call" | custom-call | flops 2415919104 | bytes 12582912 | tf_op jit(solution)/shard_map/relative/pallas_call | solution.py:628
  96.0 6.7 %collective-permute-done.14.refs_1_ = bf16[448,768]{1,0:T(8,128)(2,1)} collective-permute-done((bf16[448,768]{1,0:T(8,128)(2,1)}, bf16[448,768]{1,0:T(8,128)(2,1)}, u32[]{:S(2)}, u32[]{:S(2)}) %collective-permute-start.14) | collective-permute-done | bytes 688160 | tf_op jit(solution)/shard_map/ppermute | solution.py:1306
  114.8 4.0 convolution_convert_fusion.refs_7_.refs_9_
  125.7 16.7 %attend_forward.3 = (bf16[4,2,8,256,256]{4,3,2,1,0:T(8,128)(2,1)}, f32[1024,128]{1,0:T(8,128)}, f32[1024,128]{1,0:T(8,128)}, bf16[1024,128]{1,0:T(8,128)(2,1)}) custom-call(s32[2]{0:T(128)} %pad_add_fusion.1.refs_0_, s32[16,16]{1,0:T(8,128)} %copy-done.49, f32[1024,384]{1,0:T(8,128)} %fusion.25.refs_2_.refs_3_, f32[8,384]{1,0:T(8,128)} %pad.9.refs_3_.refs_7_, ...), custom_call_target="tpu_custom_call" | custom-call | flops 100000000 | bytes 1000000 | tf_op jit(solution)/shard_map/attend_forward/pallas_call | solution.py:197
  145.5 16.8 %attend_forward.4 = (bf16[4,2,8,256,256]{4,3,2,1,0:T(8,128)(2,1)}, f32[1024,128]{1,0:T(8,128)}, f32[1024,128]{1,0:T(8,128)}, bf16[1024,128]{1,0:T(8,128)(2,1)}) custom-call(s32[2]{0:T(128)} %pad_add_fusion.1.refs_0_, s32[16,16]{1,0:T(8,128)} %copy-done.49, f32[1024,384]{1,0:T(8,128)} %fusion.25.refs_2_.refs_3_, f32[8,384]{1,0:T(8,128)} %pad.9.refs_3_.refs_7_, ...), custom_call_target="tpu_custom_call" | custom-call | flops 100000000 | bytes 1000000 | tf_op jit(solution)/shard_map/attend_forward/pallas_call | solution.py:197
  167.2 16.7 %attend_forward.5 = (bf16[4,2,8,256,256]{4,3,2,1,0:T(8,128)(2,1)}, f32[1024,128]{1,0:T(8,128)}, f32[1024,128]{1,0:T(8,128)}, bf16[1024,128]{1,0:T(8,128)(2,1)}) custom-call(s32[2]{0:T(128)} %pad_add_fusion.1.refs_0_, s32[16,16]{1,0:T(8,128)} %copy-done.49, f32[1024,384]{1,0:T(8,128)} %fusion.25.refs_2_.refs_3_, f32[8,384]{1,0:T(8,128)} %pad.9.refs_3_.refs_7_, ...), custom_call_target="tpu_custom_call" | custom-call | flops 100000000 | bytes 1000000 | tf_op jit(solution)/shard_map/attend_forward/pallas_call | solution.py:197
  187.5 32.6 %dense.1 = (bf16[512,768]{1,0:T(8,128)(2,1)}, f32[512,768]{1,0:T(8,128)}, bf16[512,384]{1,0:T(8,128)(2,1)}, bf16[512,384]{1,0:T(8,128)(2,1)}, f32[8,768]{1,0:T(8...) custom-call(s32[3]{0:T(128)} %copy-done.53, ...), custom_call_target="tpu_custom_call" | custom-call | flops 1000000000 | bytes 1000000 | tf_op jit(solution)/shard_map/dense/pallas_call | solution.py:1137
  223.1 7.7 %collective-permute-start.27 = (bf16[2,128,768]{2,1,0:T(8,128)(2,1)}, bf16[2,128,768]{2,1,0:T(8,128)(2,1)S(1)}, u32[]{:S(2)}, u32[]{:S(2)}) collective-permute-start(bf16[2,128,768]{2,1,0:T(8,128)(2,1)} %get-tuple-element.276), channel_id=1, source_target_pairs={{0,0},{1,1},{2,2},{3,3},{4,4},{5,5},{6,6},{7,7},{8,16},{9,17},{10,... | collective-permute-start | bytes 1179656 | tf_op jit(solution)/shard_map/ppermute | solution.py:1306
  233.0 23.6 %attend_backward.3 = (bf16[1024,128]{1,0:T(8,128)(2,1)}, bf16[256,2048]{1,0:T(8,128)(2,1)}, bf16[128,4096]{1,0:T(8,128)(2,1)}, f32[8,128]{1,0:T(8,128)}) custom-call(s32[2]{0:T(128)} %pad_add_fusion.1.refs_0_, s32[16,16]{1,0:T(8,128)} %copy-done.49, bf16[4,2,8,256,256]{4,3,2,1,0:T(8,128)(2,1)} %get-tuple-element.131.refs_2_, ...), custom_call_target="tpu_custom_call" | custom-call | flops 100000000 | bytes 1000000 | tf_op jit(solution)/shard_map/attend_backward/pallas_call | solution.py:383
  259.6 3.4 fold.4
  264.8 8.8 %collective-permute-start.36 = (bf16[2,192,768]{2,1,0:T(8,128)(2,1)}, bf16[2,192,768]{2,1,0:T(8,128)(2,1)}, u32[]{:S(2)}, u32[]{:S(2)}) collective-permute-start(bf16[2,192,768]{2,1,0:T(8,128)(2,1)} %get-tuple-element.156), channel_id=1, source_target_pairs={{0,2},{1,3},{2,0},{3,1},{4,6},{5,7},{6,4},{7,5},{8,10},{9,11},{10,... | collective-permute-start | bytes 1769480 | tf_op jit(solution)/shard_map/ppermute | solution.py:1297
  280.1 9.5 %collective-permute-start.42 = (bf16[2,48,3840]{2,1,0:T(8,128)(2,1)}, bf16[2,48,3840]{2,1,0:T(8,128)(2,1)}, u32[]{:S(2)}, u32[]{:S(2)}) collective-permute-start(bf16[2,48,3840]{2,1,0:T(8,128)(2,1)} %get-tuple-element.162), channel_id=1, source_target_pairs={{0,3},{1,2},{2,1},{3,0},{4,7},{5,6},{6,5},{7,4},{8,11},{9,10},{10,... | collective-permute-start | bytes 2211848 | tf_op jit(solution)/shard_map/ppermute | solution.py:1297
  289.6 23.4 %attend_backward.4 = (bf16[1024,128]{1,0:T(8,128)(2,1)}, bf16[256,2048]{1,0:T(8,128)(2,1)}, bf16[128,4096]{1,0:T(8,128)(2,1)}, f32[8,128]{1,0:T(8,128)}) custom-call(s32[2]{0:T(128)} %pad_add_fusion.1.refs_0_, s32[16,16]{1,0:T(8,128)} %copy-done.49, bf16[4,2,8,256,256]{4,3,2,1,0:T(8,128)(2,1)} %get-tuple-element.134.refs_2_, ...), custom_call_target="tpu_custom_call" | custom-call | flops 100000000 | bytes 1000000 | tf_op jit(solution)/shard_map/attend_backward/pallas_call | solution.py:383
  313.0 12.7 %proj_grads.2 = bf16[768,1024]{1,0:T(8,128)(2,1)} custom-call(bf16[1024,768]{1,0:T(8,128)(2,1)} %bitcast.191, bf16[2048,768]{1,0:T(8,128)(2,1)} %bitcast.193, bf16[4096,768]{1,0:T(8,128)(2,1)} %copy-done.8, bf16[1024,128]{1,0:T(8,128)(2,1)} %get-tuple-element.133.refs_9_.refs_14_.refs_3_.refs_1_, ...), custom_call_target="tpu_custom_call" | custom-call | flops 1000000000 | bytes 1000000 | tf_op jit(solution)/shard_map/proj_grads/pallas_call | solution.py:834
  331.0 11.7 %collective-permute-start.38 = (bf16[192,768]{1,0:T(8,128)(2,1)}, bf16[192,768]{1,0:T(8,128)(2,1)}, u32[]{:S(2)}, u32[]{:S(2)}) collective-permute-start(bf16[192,768]{1,0:T(8,128)(2,1)} %get-tuple-element.158), channel_id=1, source_target_pairs={{0,0},{1,1},{2,2},{3,3},{4,4},{5,5},{6,6},{7,7},{8,16},{9,17},{10,... | collective-permute-start | bytes 884744 | tf_op jit(solution)/shard_map/ppermute | solution.py:1306
  358.1 23.3 %attend_backward.5 = (bf16[1024,128]{1,0:T(8,128)(2,1)}, bf16[256,2048]{1,0:T(8,128)(2,1)}, bf16[128,4096]{1,0:T(8,128)(2,1)}, f32[8,128]{1,0:T(8,128)}) custom-call(s32[2]{0:T(128)} %pad_add_fusion.1.refs_0_, s32[16,16]{1,0:T(8,128)} %copy-done.49, bf16[4,2,8,256,256]{4,3,2,1,0:T(8,128)(2,1)} %get-tuple-element.125.refs_2_, ...), custom_call_target="tpu_custom_call" | custom-call | flops 100000000 | bytes 1000000 | tf_op jit(solution)/shard_map/attend_backward/pallas_call | solution.py:383
  384.0 10.8 %proj_grads.3 = bf16[768,640]{1,0:T(8,128)(2,1)} custom-call(bf16[1024,768]{1,0:T(8,128)(2,1)} %bitcast.192, bf16[2048,768]{1,0:T(8,128)(2,1)} %bitcast.194, bf16[4096,768]{1,0:T(8,128)(2,1)} %copy-done.8, bf16[1024,128]{1,0:T(8,128)(2,1)} %get-tuple-element.147.refs_3_, bf16[256,2048]{1,0:T(8,128)(2,1)} %get-tuple-element.148.refs_4_.refs_3_, ...), custom_call_target="tpu_custom_call" | custom-call | flops 1000000000 | bytes 1000000 | tf_op jit(solution)/shard_map/proj_grads/pallas_call | solution.py:834
  418.7 4.6 collective-permute-start.59
  423.3 3.9 collective-permute-start.60
  430.2 6.6 %collective-permute-done.60 = bf16[48,1664]{1,0:T(8,128)(2,1)S(1)} collective-permute-done((bf16[48,1664]{1,0:T(8,128)(2,1)S(1)}, bf16[48,1664]{1,0:T(8,128)(2,1)S(1)}, u32[]{:S(2)}, u32[]{:S(2)}) %collective-permute-start.60) | collective-permute-done | bytes 159776 | tf_op jit(solution)/shard_map/ppermute | solution.py:1294
  436.9 3.8 collective-permute-done.61
  443.0 3.8 collective-permute-start.57
  447.2 6.9 %collective-permute-start.55 = (bf16[128,768]{1,0:T(8,128)(2,1)S(1)}, bf16[128,768]{1,0:T(8,128)(2,1)S(1)}, u32[]{:S(2)}, u32[]{:S(2)}) collective-permute-start(bf16[128,768]{1,0:T(8,128)(2,1)S(1)} %get-tuple-element.288), channel_id=1, source_target_pairs={{0,0},{1,1},{2,2},{3,3},{4,4},{5,5},{6,6},{7,7},{8,16},{9,17},{10,... | collective-permute-start | bytes 589832 | tf_op jit(solution)/shard_map/ppermute | solution.py:1306
  456.9 5.3 %collective-permute-done.55 = bf16[128,768]{1,0:T(8,128)(2,1)S(1)} collective-permute-done((bf16[128,768]{1,0:T(8,128)(2,1)S(1)}, bf16[128,768]{1,0:T(8,128)(2,1)S(1)}, u32[]{:S(2)}, u32[]{:S(2)}) %collective-permute-start.55) | collective-permute-done | bytes 196640 | tf_op jit(solution)/shard_map/ppermute | solution.py:1306
  (369 shorter events, 139.5 us)
Async XLA Ops:
  4.8 22.9 %collective-permute-start = (bf16[336,768]{1,0:T(8,128)(2,1)}, bf16[336,768]{1,0:T(8,128)(2,1)S(1)}, u32[]{:S(2)}, u32[]{:S(2)}) collective-permute-start(bf16[336,768]{1,0:T(8,128)(2,1)} %get-tuple-element.97), channel_id=1, source_target_pairs={{0,0},{1,1},{2,2},{3,3},{4,4},{5,5},{6,6},{7,7},{8,16},{9,17},{10,... | collective-permute-start | bytes 1548296 | tf_op jit(solution)/shard_map/ppermute | solution.py:1306
  28.9 20.3 %collective-permute-start.5 = (bf16[336,768]{1,0:T(8,128)(2,1)S(1)}, bf16[336,768]{1,0:T(8,128)(2,1)S(1)}, u32[]{:S(2)}, u32[]{:S(2)}) collective-permute-start(bf16[336,768]{1,0:T(8,128)(2,1)S(1)} %collective-permute-done.4), channel_id=1, source_target_pairs={{0,1},{1,0},{2,3},{3,2},{4,5},{5,4},{6,7},{7,6},{8,9},{9,8},{10,11... | collective-permute-start | bytes 1548296 | tf_op jit(solution)/shard_map/ppermute | solution.py:1297
  29.4 25.3 %collective-permute-start.7 = (bf16[336,768]{1,0:T(8,128)(2,1)S(1)}, bf16[336,768]{1,0:T(8,128)(2,1)S(1)}, u32[]{:S(2)}, u32[]{:S(2)}) collective-permute-start(bf16[336,768]{1,0:T(8,128)(2,1)S(1)} %collective-permute-done.6), channel_id=1, source_target_pairs={{0,1},{1,0},{2,3},{3,2},{4,5},{5,4},{6,7},{7,6},{8,9},{9,8},{10,11... | collective-permute-start | bytes 1548296 | tf_op jit(solution)/shard_map/ppermute | solution.py:1297
  30.7 24.5 %collective-permute-start.2 = (bf16[336,768]{1,0:T(8,128)(2,1)S(1)}, bf16[336,768]{1,0:T(8,128)(2,1)S(1)}, u32[]{:S(2)}, u32[]{:S(2)}) collective-permute-start(bf16[336,768]{1,0:T(8,128)(2,1)S(1)} %collective-permute-done), channel_id=1, source_target_pairs={{0,2},{1,3},{2,0},{3,1},{4,6},{5,7},{6,4},{7,5},{8,10},{9,11},{10,... | collective-permute-start | bytes 1548296 | tf_op jit(solution)/shard_map/ppermute | solution.py:1297
  55.0 22.1 %collective-permute-start.9 = (bf16[4,336,768]{2,1,0:T(8,128)(2,1)S(1)}, bf16[4,336,768]{2,1,0:T(8,128)(2,1)}, u32[]{:S(2)}, u32[]{:S(2)}) collective-permute-start(bf16[4,336,768]{2,1,0:T(8,128)(2,1)S(1)} %pad_maximum_fusion.1.refs_2_), channel_id=1, source_target_pairs={{0,16},{16,0},{1,17},{17,1},{2,18},{18,2},{3,19},{19,3},{4,20},{20... | collective-permute-start | bytes 6193160 | tf_op jit(solution)/shard_map/ppermute | solution.py:1291
  57.0 20.1 %collective-permute-start.8 = (bf16[4,336,768]{2,1,0:T(8,128)(2,1)}, bf16[4,336,768]{2,1,0:T(8,128)(2,1)}, u32[]{:S(2)}, u32[]{:S(2)}) collective-permute-start(bf16[4,336,768]{2,1,0:T(8,128)(2,1)} %pad_maximum_fusion.refs_1_), channel_id=1, source_target_pairs={{0,16},{16,0},{1,17},{17,1},{2,18},{18,2},{3,19},{19,3},{4,20},{20... | collective-permute-start | bytes 6193160 | tf_op jit(solution)/shard_map/ppermute | solution.py:1291
  65.7 30.2 %collective-permute-start.13 = (bf16[448,768]{1,0:T(8,128)(2,1)}, bf16[448,768]{1,0:T(8,128)(2,1)}, u32[]{:S(2)}, u32[]{:S(2)}) collective-permute-start(bf16[448,768]{1,0:T(8,128)(2,1)} %pack_late.1), channel_id=1, source_target_pairs={{0,0},{1,1},{2,2},{3,3},{4,4},{5,5},{6,6},{7,7},{8,16},{9,17},{10,... | collective-permute-start | bytes 2064392 | tf_op jit(solution)/shard_map/ppermute | solution.py:1306
  69.5 33.2 %collective-permute-start.14 = (bf16[448,768]{1,0:T(8,128)(2,1)}, bf16[448,768]{1,0:T(8,128)(2,1)}, u32[]{:S(2)}, u32[]{:S(2)}) collective-permute-start(bf16[448,768]{1,0:T(8,128)(2,1)} %pack_late.1), channel_id=1, source_target_pairs={{0,4},{1,5},{2,6},{3,7},{4,0},{5,1},{6,2},{7,3},{8,20},{9,21},{10,... | collective-permute-start | bytes 2064392 | tf_op jit(solution)/shard_map/ppermute | solution.py:1306
  104.2 58.1 %collective-permute-start.17 = (bf16[2,448,768]{2,1,0:T(8,128)(2,1)S(1)}, bf16[2,448,768]{2,1,0:T(8,128)(2,1)}, u32[]{:S(2)}, u32[]{:S(2)}) collective-permute-start(bf16[2,448,768]{2,1,0:T(8,128)(2,1)S(1)} %hold.1.refs_11_.refs_8_), channel_id=1, source_target_pairs={{0,1},{1,0},{2,3},{3,2},{4,5},{5,4},{6,7},{7,6},{8,9},{9,8},{10,11... | collective-permute-start | bytes 4128776 | tf_op jit(solution)/shard_map/ppermute | solution.py:1297
  104.3 58.0 %collective-permute-start.18 = (bf16[2,448,768]{2,1,0:T(8,128)(2,1)S(1)}, bf16[2,448,768]{2,1,0:T(8,128)(2,1)}, u32[]{:S(2)}, u32[]{:S(2)}) collective-permute-start(bf16[2,448,768]{2,1,0:T(8,128)(2,1)S(1)} %hold.1.refs_11_.refs_8_), channel_id=1, source_target_pairs={{0,2},{1,3},{2,0},{3,1},{4,6},{5,7},{6,4},{7,5},{8,10},{9,11},{10,... | collective-permute-start | bytes 4128776 | tf_op jit(solution)/shard_map/ppermute | solution.py:1297
  105.7 56.6 %collective-permute-start.19 = (bf16[2,448,768]{2,1,0:T(8,128)(2,1)S(1)}, bf16[2,448,768]{2,1,0:T(8,128)(2,1)}, u32[]{:S(2)}, u32[]{:S(2)}) collective-permute-start(bf16[2,448,768]{2,1,0:T(8,128)(2,1)S(1)} %hold.1.refs_11_.refs_8_), channel_id=1, source_target_pairs={{0,3},{1,2},{2,1},{3,0},{4,7},{5,6},{6,5},{7,4},{8,11},{9,10},{10,... | collective-permute-start | bytes 4128776 | tf_op jit(solution)/shard_map/ppermute | solution.py:1297
  107.9 34.5 %collective-permute-start.15 = (bf16[2,128,768]{2,1,0:T(8,128)(2,1)}, bf16[2,128,768]{2,1,0:T(8,128)(2,1)}, u32[]{:S(2)}, u32[]{:S(2)}) collective-permute-start(bf16[2,128,768]{2,1,0:T(8,128)(2,1)} %get-tuple-element.278), channel_id=1, source_target_pairs={{0,0},{1,1},{2,2},{3,3},{4,4},{5,5},{6,6},{7,7},{8,16},{9,17},{10,... | collective-permute-start | bytes 1179656 | tf_op jit(solution)/shard_map/ppermute | solution.py:1306
  110.0 33.5 %collective-permute-start.16 = (bf16[2,128,768]{2,1,0:T(8,128)(2,1)}, bf16[2,128,768]{2,1,0:T(8,128)(2,1)}, u32[]{:S(2)}, u32[]{:S(2)}) collective-permute-start(bf16[2,128,768]{2,1,0:T(8,128)(2,1)} %get-tuple-element.277), channel_id=1, source_target_pairs={{0,4},{1,5},{2,6},{3,7},{4,0},{5,1},{6,2},{7,3},{8,20},{9,21},{10,... | collective-permute-start | bytes 1179656 | tf_op jit(solution)/shard_map/ppermute | solution.py:1306
  162.3 24.0 %collective-permute-start.23 = (bf16[2,448,768]{2,1,0:T(8,128)(2,1)S(1)}, bf16[2,448,768]{2,1,0:T(8,128)(2,1)S(1)}, u32[]{:S(2)}, u32[]{:S(2)}) collective-permute-start(bf16[2,448,768]{2,1,0:T(8,128)(2,1)S(1)} %copy-done.15), channel_id=1, source_target_pairs={{0,16},{16,0},{1,17},{17,1},{2,18},{18,2},{3,19},{19,3},{4,20},{20... | collective-permute-start | bytes 4128776 | tf_op jit(solution)/shard_map/ppermute | solution.py:1291
  162.4 23.9 %collective-permute-start.24 = (bf16[2,448,768]{2,1,0:T(8,128)(2,1)}, bf16[2,448,768]{2,1,0:T(8,128)(2,1)}, u32[]{:S(2)}, u32[]{:S(2)}) collective-permute-start(bf16[2,448,768]{2,1,0:T(8,128)(2,1)} %collective-permute-done.17.refs_11_.refs_9_), channel_id=1, source_target_pairs={{0,16},{16,0},{1,17},{17,1},{2,18},{18,2},{3,19},{19,3},{4,20},{20... | collective-permute-start | bytes 4128776 | tf_op jit(solution)/shard_map/ppermute | solution.py:1291
  162.9 23.4 %collective-permute-start.25 = (bf16[2,448,768]{2,1,0:T(8,128)(2,1)}, bf16[2,448,768]{2,1,0:T(8,128)(2,1)}, u32[]{:S(2)}, u32[]{:S(2)}) collective-permute-start(bf16[2,448,768]{2,1,0:T(8,128)(2,1)} %collective-permute-done.18.refs_12_.refs_10_), channel_id=1, source_target_pairs={{0,16},{16,0},{1,17},{17,1},{2,18},{18,2},{3,19},{19,3},{4,20},{20... | collective-permute-start | bytes 4128776 | tf_op jit(solution)/shard_map/ppermute | solution.py:1291
  163.0 23.3 %collective-permute-start.26 = (bf16[2,448,768]{2,1,0:T(8,128)(2,1)}, bf16[2,448,768]{2,1,0:T(8,128)(2,1)}, u32[]{:S(2)}, u32[]{:S(2)}) collective-permute-start(bf16[2,448,768]{2,1,0:T(8,128)(2,1)} %collective-permute-done.19.refs_13_.refs_11_), channel_id=1, source_target_pairs={{0,16},{16,0},{1,17},{17,1},{2,18},{18,2},{3,19},{19,3},{4,20},{20... | collective-permute-start | bytes 4128776 | tf_op jit(solution)/shard_map/ppermute | solution.py:1291
  220.1 54.6 %collective-permute-start.30 = (bf16[384,3840]{1,0:T(8,128)(2,1)}, bf16[384,3840]{1,0:T(8,128)(2,1)S(1)}, u32[]{:S(2)}, u32[]{:S(2)}) collective-permute-start(bf16[384,3840]{1,0:T(8,128)(2,1)} %get-tuple-element.137), channel_id=1, source_target_pairs={{0,16},{16,0},{1,17},{17,1},{2,18},{18,2},{3,19},{19,3},{4,20},{20... | collective-permute-start | bytes 8847368 | tf_op jit(solution)/shard_map/ppermute | solution.py:1291
  220.5 36.2 %collective-permute-start.31 = (bf16[1536,768]{1,0:T(8,128)(2,1)}, bf16[1536,768]{1,0:T(8,128)(2,1)}, u32[]{:S(2)}, u32[]{:S(2)}) collective-permute-start(bf16[1536,768]{1,0:T(8,128)(2,1)} %get-tuple-element.140), channel_id=1, source_target_pairs={{0,16},{16,0},{1,17},{17,1},{2,18},{18,2},{3,19},{19,3},{4,20},{20... | collective-permute-start | bytes 7077896 | tf_op jit(solution)/shard_map/ppermute | solution.py:1291
  223.1 33.6 %collective-permute-start.27 = (bf16[2,128,768]{2,1,0:T(8,128)(2,1)}, bf16[2,128,768]{2,1,0:T(8,128)(2,1)S(1)}, u32[]{:S(2)}, u32[]{:S(2)}) collective-permute-start(bf16[2,128,768]{2,1,0:T(8,128)(2,1)} %get-tuple-element.276), channel_id=1, source_target_pairs={{0,0},{1,1},{2,2},{3,3},{4,4},{5,5},{6,6},{7,7},{8,16},{9,17},{10,... | collective-permute-start | bytes 1179656 | tf_op jit(solution)/shard_map/ppermute | solution.py:1306
  230.8 25.9 %collective-permute-start.28 = (bf16[2,128,768]{2,1,0:T(8,128)(2,1)}, bf16[2,128,768]{2,1,0:T(8,128)(2,1)S(1)}, u32[]{:S(2)}, u32[]{:S(2)}) collective-permute-start(bf16[2,128,768]{2,1,0:T(8,128)(2,1)} %get-tuple-element.275), channel_id=1, source_target_pairs={{0,4},{1,5},{2,6},{3,7},{4,0},{5,1},{6,2},{7,3},{8,20},{9,21},{10,... | collective-permute-start | bytes 1179656 | tf_op jit(solution)/shard_map/ppermute | solution.py:1306
  264.8 60.9 %collective-permute-start.36 = (bf16[2,192,768]{2,1,0:T(8,128)(2,1)}, bf16[2,192,768]{2,1,0:T(8,128)(2,1)}, u32[]{:S(2)}, u32[]{:S(2)}) collective-permute-start(bf16[2,192,768]{2,1,0:T(8,128)(2,1)} %get-tuple-element.156), channel_id=1, source_target_pairs={{0,2},{1,3},{2,0},{3,1},{4,6},{5,7},{6,4},{7,5},{8,10},{9,11},{10,... | collective-permute-start | bytes 1769480 | tf_op jit(solution)/shard_map/ppermute | solution.py:1297
  273.6 52.1 %collective-permute-start.37 = (bf16[2,192,768]{2,1,0:T(8,128)(2,1)}, bf16[2,192,768]{2,1,0:T(8,128)(2,1)}, u32[]{:S(2)}, u32[]{:S(2)}) collective-permute-start(bf16[2,192,768]{2,1,0:T(8,128)(2,1)} %get-tuple-element.157), channel_id=1, source_target_pairs={{0,3},{1,2},{2,1},{3,0},{4,7},{5,6},{6,5},{7,4},{8,11},{9,10},{10,... | collective-permute-start | bytes 1769480 | tf_op jit(solution)/shard_map/ppermute | solution.py:1297
  277.7 67.3 %collective-permute-start.40 = (bf16[2,48,3840]{2,1,0:T(8,128)(2,1)}, bf16[2,48,3840]{2,1,0:T(8,128)(2,1)S(1)}, u32[]{:S(2)}, u32[]{:S(2)}) collective-permute-start(bf16[2,48,3840]{2,1,0:T(8,128)(2,1)} %get-tuple-element.160), channel_id=1, source_target_pairs={{0,1},{1,0},{2,3},{3,2},{4,5},{5,4},{6,7},{7,6},{8,9},{9,8},{10,11... | collective-permute-start | bytes 2211848 | tf_op jit(solution)/shard_map/ppermute | solution.py:1297
  278.0 69.8 %collective-permute-start.41 = (bf16[2,48,3840]{2,1,0:T(8,128)(2,1)}, bf16[2,48,3840]{2,1,0:T(8,128)(2,1)}, u32[]{:S(2)}, u32[]{:S(2)}) collective-permute-start(bf16[2,48,3840]{2,1,0:T(8,128)(2,1)} %get-tuple-element.161), channel_id=1, source_target_pairs={{0,2},{1,3},{2,0},{3,1},{4,6},{5,7},{6,4},{7,5},{8,10},{9,11},{10,... | collective-permute-start | bytes 2211848 | tf_op jit(solution)/shard_map/ppermute | solution.py:1297
  280.1 69.3 %collective-permute-start.42 = (bf16[2,48,3840]{2,1,0:T(8,128)(2,1)}, bf16[2,48,3840]{2,1,0:T(8,128)(2,1)}, u32[]{:S(2)}, u32[]{:S(2)}) collective-permute-start(bf16[2,48,3840]{2,1,0:T(8,128)(2,1)} %get-tuple-element.162), channel_id=1, source_target_pairs={{0,3},{1,2},{2,1},{3,0},{4,7},{5,6},{6,5},{7,4},{8,11},{9,10},{10,... | collective-permute-start | bytes 2211848 | tf_op jit(solution)/shard_map/ppermute | solution.py:1297
  331.0 22.5 %collective-permute-start.38 = (bf16[192,768]{1,0:T(8,128)(2,1)}, bf16[192,768]{1,0:T(8,128)(2,1)}, u32[]{:S(2)}, u32[]{:S(2)}) collective-permute-start(bf16[192,768]{1,0:T(8,128)(2,1)} %get-tuple-element.158), channel_id=1, source_target_pairs={{0,0},{1,1},{2,2},{3,3},{4,4},{5,5},{6,6},{7,7},{8,16},{9,17},{10,... | collective-permute-start | bytes 884744 | tf_op jit(solution)/shard_map/ppermute | solution.py:1306
  345.0 38.1 %collective-permute-start.32 = (bf16[4,48,1024]{2,1,0:T(8,128)(2,1)}, bf16[4,48,1024]{2,1,0:T(8,128)(2,1)}, u32[]{:S(2)}, u32[]{:S(2)}) collective-permute-start(bf16[4,48,1024]{2,1,0:T(8,128)(2,1)} %get-tuple-element.268), channel_id=1, source_target_pairs={{0,1},{1,0},{2,3},{3,2},{4,5},{5,4},{6,7},{7,6},{8,9},{9,8},{10,11... | collective-permute-start | bytes 1179656 | tf_op jit(solution)/shard_map/ppermute | solution.py:1297
  347.8 35.3 %collective-permute-start.33 = (bf16[4,48,1024]{2,1,0:T(8,128)(2,1)}, bf16[4,48,1024]{2,1,0:T(8,128)(2,1)}, u32[]{:S(2)}, u32[]{:S(2)}) collective-permute-start(bf16[4,48,1024]{2,1,0:T(8,128)(2,1)} %get-tuple-element.267), channel_id=1, source_target_pairs={{0,2},{1,3},{2,0},{3,1},{4,6},{5,7},{6,4},{7,5},{8,10},{9,11},{10,... | collective-permute-start | bytes 1179656 | tf_op jit(solution)/shard_map/ppermute | solution.py:1297
  349.3 33.8 %collective-permute-start.34 = (bf16[4,48,1024]{2,1,0:T(8,128)(2,1)}, bf16[4,48,1024]{2,1,0:T(8,128)(2,1)}, u32[]{:S(2)}, u32[]{:S(2)}) collective-permute-start(bf16[4,48,1024]{2,1,0:T(8,128)(2,1)} %get-tuple-element.266), channel_id=1, source_target_pairs={{0,3},{1,2},{2,1},{3,0},{4,7},{5,6},{6,5},{7,4},{8,11},{9,10},{10,... | collective-permute-start | bytes 1179656 | tf_op jit(solution)/shard_map/ppermute | solution.py:1297
  353.5 29.6 %collective-permute-start.43 = (bf16[48,3840]{1,0:T(8,128)(2,1)}, bf16[48,3840]{1,0:T(8,128)(2,1)S(1)}, u32[]{:S(2)}, u32[]{:S(2)}) collective-permute-start(bf16[48,3840]{1,0:T(8,128)(2,1)} %get-tuple-element.163), channel_id=1, source_target_pairs={{0,0},{1,1},{2,2},{3,3},{4,4},{5,5},{6,6},{7,7},{8,16},{9,17},{10,... | collective-permute-start | bytes 1105928 | tf_op jit(solution)/shard_map/ppermute | solution.py:1306
  356.0 27.1 %collective-permute-start.44 = (bf16[48,3840]{1,0:T(8,128)(2,1)}, bf16[48,3840]{1,0:T(8,128)(2,1)S(1)}, u32[]{:S(2)}, u32[]{:S(2)}) collective-permute-start(bf16[48,3840]{1,0:T(8,128)(2,1)} %get-tuple-element.164), channel_id=1, source_target_pairs={{0,4},{1,5},{2,6},{3,7},{4,0},{5,1},{6,2},{7,3},{8,20},{9,21},{10,... | collective-permute-start | bytes 1105928 | tf_op jit(solution)/shard_map/ppermute | solution.py:1306
  (113 other events, 944.3 us)

commit v5 on v4

--- a/solution.py
+++ b/solution.py
@@ -601,7 +601,7 @@
 def relative_kernel(sa_ref, ca_ref, sb_ref, cb_ref, w_ref, pos_ref, rel_ref, turned_ref):
     half = sb_ref.shape[1]
     fine = sb_ref.shape[0]
-    for i in range(KB // fine):
+    for i in range(pos_ref.shape[0] // fine):
         rows = slice(i * fine, (i + 1) * fine)
         sa, ca = sa_ref[0, i : i + 1, :], ca_ref[0, i : i + 1, :]
         sine = sa * cb_ref[...] - ca * sb_ref[...]
@@ -622,12 +622,13 @@
     coarse = (length - 1 - fine * jnp.arange(2 * length // fine, dtype=jnp.int32)).astype(F32)
     a = coarse[:, None] * inverse_freq[None]
     b = jnp.arange(fine, dtype=F32)[:, None] * inverse_freq[None]
-    per = KB // fine
+    size = 1024
+    per = size // fine
     tables = [jnp.sin(a).reshape(-1, per, half), jnp.cos(a).reshape(-1, per, half), jnp.sin(b), jnp.cos(b)]
-    rows = lambda w: pl.BlockSpec((KB, w), lambda i: (i, 0))
+    rows = lambda w: pl.BlockSpec((size, w), lambda i: (i, 0))
     return pl.pallas_call(
         relative_kernel,
-        grid=(2 * length // KB,),
+        grid=(2 * length // size,),
         in_specs=[pl.BlockSpec((1, per, half), lambda i: (i, 0, 0))] * 2
         + [pl.BlockSpec((fine, half), lambda i: (0, 0))] * 2
         + [pl.BlockSpec((d, width), lambda i: (0, 0))],
@@ -658,7 +659,7 @@
 
 def input_grad(half, parts, w, dtype, after, turned=False):
     rows = parts[0].shape[1 if turned else 0] // 2
-    block = math.gcd(rows, 256)
+    block = math.gcd(rows, 512)
     blocks = rows // block
     d = w.shape[0]
     return pl.pallas_call(
@@ -814,7 +815,7 @@
 def proj_grads(x, content, position, parts, extra, after):
     count = len(parts)
     d = x.shape[1]
-    size = 512
+    size = 1024
     steps = [a.shape[0] // size for a in (x, content, position)]
     spec = lambda width, kind: pl.BlockSpec(
         (size, width), lambda i: (jnp.minimum(i, steps[kind] - 1), 0)
@@ -1053,6 +1054,7 @@
 
     for j in range(parts):
         wait_chunk(j)
+    for j in range(parts):
         cols = slice(j * d, (j + 1) * d)
         value, slant = gelu_and_slope(mm(unit_bf[...], w1[:, cols]) + bias[5:6, cols])
         hidden[:, cols] = value.astype(BF)

time: 465 us -> 456 us (0.981); the launches traced: 465 us -> 448 us
  starting transfers between devices: 110 us -> 97.5 us
  Pallas kernels: 214 us -> 202 us
  waiting for transfers between devices: 77.9 us -> 86.7 us
    ppermute x18, starting transfers between devices: 52 us -> 43.6 us  [across(): return lax.ppermute(x, ('rep', 'shard'), moves)]
    ppermute x3, starting transfers between devices: 8.76 us -> 2.88 us  [far(): return lax.ppermute(x, 'shard', [(i, i ^ m * step) for i in range(n)])]
  transfers between devices with their start and end apart: 63 -> 63, of which waited for: 18 -> 20; matrix products, arithmetic and copies ran while one was open for 7% -> 8% of each run, Pallas kernels for 35% -> 34%
where the time goes in v5:
time: 456 us; the launch traced here: 448 us
  Pallas kernels  202 us (44%)
  starting transfers between devices  97.5 us (21%)
  waiting for transfers between devices  86.7 us (19%)
  local copies, waits for them, and re-layouts  44.4 us (10%)
  other arithmetic  9.79 us (2%)
  matrix products  6.08 us (1%)
    pallas_call x3, Pallas kernels, attend_backward(): pl.pallas_call(ordered(functools.partial(backward_kernel, nkb, nb), 12, l...  66.9 us
    pallas_call x3, Pallas kernels, attend_forward(): pl.pallas_call(ordered(functools.partial(forward_kernel, nkb), 11, len(af...  47.9 us
    ppermute x24, starting transfers between devices, near(): return lax.ppermute(x, 'shard', [(i, i ^ step) for i in range(n)])  44 us
    ppermute x18, starting transfers between devices, across(): return lax.ppermute(x, ('rep', 'shard'), moves)  43.6 us
    ppermute x18, waiting for transfers between devices, across(): return lax.ppermute(x, ('rep', 'shard'), moves)  40.4 us
    pallas_call x1, Pallas kernels, dense(): pl.pallas_call(functools.partial(dense_kernel, m, n, ws, pairs), grid_spe...  32.6 us
    ppermute x24, waiting for transfers between devices, near(): return lax.ppermute(x, 'shard', [(i, i ^ step) for i in range(n)])  29.4 us
    unnamed x170, local copies, waits for them, and re-layouts  26.9 us
  transfers between devices with their start and end apart: 63, of which 20 were waited for; matrix products, arithmetic and copies ran while one was open for 8% of the time, Pallas kernels for 34%

profile of v5, /device:TPU:9, one launch (start us, length us, event | category | flops | bytes accessed | tf_op | source)
XLA Modules:
  0.0 448.4 jit_solution(17348530109705589534)
XLA Ops:
  7.7 8.8 %collective-permute-done.4 = bf16[336,768]{1,0:T(8,128)(2,1)S(1)} collective-permute-done((bf16[336,768]{1,0:T(8,128)(2,1)}, bf16[336,768]{1,0:T(8,128)(2,1)S(1)}, u32[]{:S(2)}, u32[]{:S(2)}) %collective-permute-start.4) | collective-permute-done | bytes 516128 | tf_op jit(solution)/shard_map/ppermute | solution.py:1308
  17.7 10.0 %collective-permute-done = bf16[336,768]{1,0:T(8,128)(2,1)S(1)} collective-permute-done((bf16[336,768]{1,0:T(8,128)(2,1)}, bf16[336,768]{1,0:T(8,128)(2,1)S(1)}, u32[]{:S(2)}, u32[]{:S(2)}) %collective-permute-start) | collective-permute-done | bytes 516128 | tf_op jit(solution)/shard_map/ppermute | solution.py:1308
  31.9 9.6 %collective-permute-done.1 = bf16[336,768]{1,0:T(8,128)(2,1)S(1)} collective-permute-done((bf16[336,768]{1,0:T(8,128)(2,1)S(1)}, bf16[336,768]{1,0:T(8,128)(2,1)S(1)}, u32[]{:S(2)}, u32[]{:S(2)}) %collective-permute-start.1) | collective-permute-done | bytes 516128 | tf_op jit(solution)/shard_map/ppermute | solution.py:1299
  41.7 7.6 %collective-permute-done.5 = bf16[336,768]{1,0:T(8,128)(2,1)S(1)} collective-permute-done((bf16[336,768]{1,0:T(8,128)(2,1)S(1)}, bf16[336,768]{1,0:T(8,128)(2,1)S(1)}, u32[]{:S(2)}, u32[]{:S(2)}) %collective-permute-start.5) | collective-permute-done | bytes 516128 | tf_op jit(solution)/shard_map/ppermute | solution.py:1299
  49.2 5.5 %collective-permute-done.7 = bf16[336,768]{1,0:T(8,128)(2,1)S(1)} collective-permute-done((bf16[336,768]{1,0:T(8,128)(2,1)S(1)}, bf16[336,768]{1,0:T(8,128)(2,1)S(1)}, u32[]{:S(2)}, u32[]{:S(2)}) %collective-permute-start.7) | collective-permute-done | bytes 516128 | tf_op jit(solution)/shard_map/ppermute | solution.py:1299
  65.7 3.7 collective-permute-start.13
  70.6 4.7 %collective-permute-done.11 = bf16[128,768]{1,0:T(8,128)(2,1)S(1)} collective-permute-done((bf16[128,768]{1,0:T(8,128)(2,1)S(1)}, bf16[128,768]{1,0:T(8,128)(2,1)S(1)}, u32[]{:S(2)}, u32[]{:S(2)}) %collective-permute-start.11) | collective-permute-done | bytes 196640 | tf_op jit(solution)/shard_map/ppermute | solution.py:1308
  78.7 3.7 assemble.1
  85.2 4.7 %relative.1 = (bf16[4096,768]{1,0:T(8,128)(2,1)S(1)}, bf16[4096,384]{1,0:T(8,128)(2,1)S(1)}, bf16[4096,384]{1,0:T(8,128)(2,1)S(1)}) custom-call(f32[4,16,384]{2,1,0:T(8,128)S(1)} %get-tuple-element.318.sa_ref, f32[4,16,384]{2,1,0:T(8,128)S(1)} %get-tuple-element.317.ca_ref, f32[64,384]{1,0:T(8,128)S(1)} %copy-done.50, ...), custom_call_target="tpu_custom_call" | custom-call | flops 2415919104 | bytes 12582912 | tf_op jit(solution)/shard_map/relative/pallas_call | solution.py:629
  94.2 8.5 %collective-permute-done.14.refs_1_ = bf16[448,768]{1,0:T(8,128)(2,1)} collective-permute-done((bf16[448,768]{1,0:T(8,128)(2,1)}, bf16[448,768]{1,0:T(8,128)(2,1)}, u32[]{:S(2)}, u32[]{:S(2)}) %collective-permute-start.14) | collective-permute-done | bytes 688160 | tf_op jit(solution)/shard_map/ppermute | solution.py:1308
  114.7 4.0 convolution_convert_fusion.refs_7_.refs_9_
  125.6 15.9 %attend_forward.3 = (bf16[4,2,8,256,256]{4,3,2,1,0:T(8,128)(2,1)}, f32[1024,128]{1,0:T(8,128)}, f32[1024,128]{1,0:T(8,128)}, bf16[1024,128]{1,0:T(8,128)(2,1)}) custom-call(s32[2]{0:T(128)} %pad_add_fusion.1.refs_0_, s32[16,16]{1,0:T(8,128)} %copy-done.49, f32[1024,384]{1,0:T(8,128)} %fusion.25.refs_2_.refs_3_, f32[8,384]{1,0:T(8,128)} %pad.9.refs_3_.refs_7_, ...), custom_call_target="tpu_custom_call" | custom-call | flops 100000000 | bytes 1000000 | tf_op jit(solution)/shard_map/attend_forward/pallas_call | solution.py:197
  144.7 16.1 %attend_forward.4 = (bf16[4,2,8,256,256]{4,3,2,1,0:T(8,128)(2,1)}, f32[1024,128]{1,0:T(8,128)}, f32[1024,128]{1,0:T(8,128)}, bf16[1024,128]{1,0:T(8,128)(2,1)}) custom-call(s32[2]{0:T(128)} %pad_add_fusion.1.refs_0_, s32[16,16]{1,0:T(8,128)} %copy-done.49, f32[1024,384]{1,0:T(8,128)} %fusion.25.refs_2_.refs_3_, f32[8,384]{1,0:T(8,128)} %pad.9.refs_3_.refs_7_, ...), custom_call_target="tpu_custom_call" | custom-call | flops 100000000 | bytes 1000000 | tf_op jit(solution)/shard_map/attend_forward/pallas_call | solution.py:197
  165.6 15.9 %attend_forward.5 = (bf16[4,2,8,256,256]{4,3,2,1,0:T(8,128)(2,1)}, f32[1024,128]{1,0:T(8,128)}, f32[1024,128]{1,0:T(8,128)}, bf16[1024,128]{1,0:T(8,128)(2,1)}) custom-call(s32[2]{0:T(128)} %pad_add_fusion.1.refs_0_, s32[16,16]{1,0:T(8,128)} %copy-done.49, f32[1024,384]{1,0:T(8,128)} %fusion.25.refs_2_.refs_3_, f32[8,384]{1,0:T(8,128)} %pad.9.refs_3_.refs_7_, ...), custom_call_target="tpu_custom_call" | custom-call | flops 100000000 | bytes 1000000 | tf_op jit(solution)/shard_map/attend_forward/pallas_call | solution.py:197
  185.2 32.6 %dense.1 = (bf16[512,768]{1,0:T(8,128)(2,1)}, f32[512,768]{1,0:T(8,128)}, bf16[512,384]{1,0:T(8,128)(2,1)}, bf16[512,384]{1,0:T(8,128)(2,1)}, f32[8,768]{1,0:T(8...) custom-call(s32[3]{0:T(128)} %copy-done.53, ...), custom_call_target="tpu_custom_call" | custom-call | flops 1000000000 | bytes 1000000 | tf_op jit(solution)/shard_map/dense/pallas_call | solution.py:1139
  220.7 7.8 %collective-permute-start.27 = (bf16[2,128,768]{2,1,0:T(8,128)(2,1)}, bf16[2,128,768]{2,1,0:T(8,128)(2,1)S(1)}, u32[]{:S(2)}, u32[]{:S(2)}) collective-permute-start(bf16[2,128,768]{2,1,0:T(8,128)(2,1)} %get-tuple-element.276), channel_id=1, source_target_pairs={{0,0},{1,1},{2,2},{3,3},{4,4},{5,5},{6,6},{7,7},{8,16},{9,17},{10,... | collective-permute-start | bytes 1179656 | tf_op jit(solution)/shard_map/ppermute | solution.py:1308
  230.9 22.3 %attend_backward.3 = (bf16[1024,128]{1,0:T(8,128)(2,1)}, bf16[256,2048]{1,0:T(8,128)(2,1)}, bf16[128,4096]{1,0:T(8,128)(2,1)}, f32[8,128]{1,0:T(8,128)}) custom-call(s32[2]{0:T(128)} %pad_add_fusion.1.refs_0_, s32[16,16]{1,0:T(8,128)} %copy-done.49, bf16[4,2,8,256,256]{4,3,2,1,0:T(8,128)(2,1)} %get-tuple-element.131.refs_2_, ...), custom_call_target="tpu_custom_call" | custom-call | flops 100000000 | bytes 1000000 | tf_op jit(solution)/shard_map/attend_backward/pallas_call | solution.py:383
  256.0 3.4 fold.4
  259.5 6.7 %collective-permute-start.35 = (bf16[2,192,768]{2,1,0:T(8,128)(2,1)S(1)}, bf16[2,192,768]{2,1,0:T(8,128)(2,1)S(1)}, u32[]{:S(2)}, u32[]{:S(2)}) collective-permute-start(bf16[2,192,768]{2,1,0:T(8,128)(2,1)S(1)} %get-tuple-element.155), channel_id=1, source_target_pairs={{0,1},{1,0},{2,3},{3,2},{4,5},{5,4},{6,7},{7,6},{8,9},{9,8},{10,11... | collective-permute-start | bytes 1769480 | tf_op jit(solution)/shard_map/ppermute | solution.py:1299
  266.2 6.0 %collective-permute-start.36 = (bf16[2,192,768]{2,1,0:T(8,128)(2,1)}, bf16[2,192,768]{2,1,0:T(8,128)(2,1)}, u32[]{:S(2)}, u32[]{:S(2)}) collective-permute-start(bf16[2,192,768]{2,1,0:T(8,128)(2,1)} %get-tuple-element.156), channel_id=1, source_target_pairs={{0,2},{1,3},{2,0},{3,1},{4,6},{5,7},{6,4},{7,5},{8,10},{9,11},{10,... | collective-permute-start | bytes 1769480 | tf_op jit(solution)/shard_map/ppermute | solution.py:1299
  281.0 7.2 %collective-permute-start.42 = (bf16[2,48,3840]{2,1,0:T(8,128)(2,1)}, bf16[2,48,3840]{2,1,0:T(8,128)(2,1)}, u32[]{:S(2)}, u32[]{:S(2)}) collective-permute-start(bf16[2,48,3840]{2,1,0:T(8,128)(2,1)} %get-tuple-element.162), channel_id=1, source_target_pairs={{0,3},{1,2},{2,1},{3,0},{4,7},{5,6},{6,5},{7,4},{8,11},{9,10},{10,... | collective-permute-start | bytes 2211848 | tf_op jit(solution)/shard_map/ppermute | solution.py:1299
  288.2 22.2 %attend_backward.4 = (bf16[1024,128]{1,0:T(8,128)(2,1)}, bf16[256,2048]{1,0:T(8,128)(2,1)}, bf16[128,4096]{1,0:T(8,128)(2,1)}, f32[8,128]{1,0:T(8,128)}) custom-call(s32[2]{0:T(128)} %pad_add_fusion.1.refs_0_, s32[16,16]{1,0:T(8,128)} %copy-done.49, bf16[4,2,8,256,256]{4,3,2,1,0:T(8,128)(2,1)} %get-tuple-element.134.refs_2_, ...), custom_call_target="tpu_custom_call" | custom-call | flops 100000000 | bytes 1000000 | tf_op jit(solution)/shard_map/attend_backward/pallas_call | solution.py:383
  310.4 10.9 %proj_grads.2 = bf16[768,1024]{1,0:T(8,128)(2,1)} custom-call(bf16[1024,768]{1,0:T(8,128)(2,1)} %bitcast.191, bf16[2048,768]{1,0:T(8,128)(2,1)} %bitcast.193, bf16[4096,768]{1,0:T(8,128)(2,1)} %copy-done.8, bf16[1024,128]{1,0:T(8,128)(2,1)} %get-tuple-element.133.refs_9_.refs_14_.refs_3_.refs_1_, ...), custom_call_target="tpu_custom_call" | custom-call | flops 1000000000 | bytes 1000000 | tf_op jit(solution)/shard_map/proj_grads/pallas_call | solution.py:835
  326.6 4.9 %collective-permute-start.38 = (bf16[192,768]{1,0:T(8,128)(2,1)}, bf16[192,768]{1,0:T(8,128)(2,1)}, u32[]{:S(2)}, u32[]{:S(2)}) collective-permute-start(bf16[192,768]{1,0:T(8,128)(2,1)} %get-tuple-element.158), channel_id=1, source_target_pairs={{0,0},{1,1},{2,2},{3,3},{4,4},{5,5},{6,6},{7,7},{8,16},{9,17},{10,... | collective-permute-start | bytes 884744 | tf_op jit(solution)/shard_map/ppermute | solution.py:1308
  333.8 3.6 collective-permute-start.32
  346.3 22.4 %attend_backward.5 = (bf16[1024,128]{1,0:T(8,128)(2,1)}, bf16[256,2048]{1,0:T(8,128)(2,1)}, bf16[128,4096]{1,0:T(8,128)(2,1)}, f32[8,128]{1,0:T(8,128)}) custom-call(s32[2]{0:T(128)} %pad_add_fusion.1.refs_0_, s32[16,16]{1,0:T(8,128)} %copy-done.49, bf16[4,2,8,256,256]{4,3,2,1,0:T(8,128)(2,1)} %get-tuple-element.125.refs_2_, ...), custom_call_target="tpu_custom_call" | custom-call | flops 100000000 | bytes 1000000 | tf_op jit(solution)/shard_map/attend_backward/pallas_call | solution.py:383
  371.2 9.0 %proj_grads.3 = bf16[768,640]{1,0:T(8,128)(2,1)} custom-call(bf16[1024,768]{1,0:T(8,128)(2,1)} %bitcast.192, bf16[2048,768]{1,0:T(8,128)(2,1)} %bitcast.194, bf16[4096,768]{1,0:T(8,128)(2,1)} %copy-done.8, bf16[1024,128]{1,0:T(8,128)(2,1)} %get-tuple-element.147.refs_3_, bf16[256,2048]{1,0:T(8,128)(2,1)} %get-tuple-element.148.refs_4_.refs_3_, ...), custom_call_target="tpu_custom_call" | custom-call | flops 1000000000 | bytes 1000000 | tf_op jit(solution)/shard_map/proj_grads/pallas_call | solution.py:835
  387.1 4.6 %collective-permute-start.48 = (bf16[4,48,640]{2,1,0:T(8,128)(2,1)S(1)}, bf16[4,48,640]{2,1,0:T(8,128)(2,1)S(1)}, u32[]{:S(2)}, u32[]{:S(2)}) collective-permute-start(bf16[4,48,640]{2,1,0:T(8,128)(2,1)S(1)} %get-tuple-element.272), channel_id=1, source_target_pairs={{0,1},{1,0},{2,3},{3,2},{4,5},{5,4},{6,7},{7,6},{8,9},{9,8},{10,11... | collective-permute-start | bytes 737288 | tf_op jit(solution)/shard_map/ppermute | solution.py:1299
  401.9 3.8 collective-permute-done.50.refs_14_
  415.2 9.7 %collective-permute-done.61 = bf16[48,1664]{1,0:T(8,128)(2,1)S(1)} collective-permute-done((bf16[48,1664]{1,0:T(8,128)(2,1)S(1)}, bf16[48,1664]{1,0:T(8,128)(2,1)S(1)}, u32[]{:S(2)}, u32[]{:S(2)}) %collective-permute-start.61) | collective-permute-done | bytes 159776 | tf_op jit(solution)/shard_map/ppermute | solution.py:1296
  429.7 5.8 %collective-permute-start.55 = (bf16[128,768]{1,0:T(8,128)(2,1)S(1)}, bf16[128,768]{1,0:T(8,128)(2,1)S(1)}, u32[]{:S(2)}, u32[]{:S(2)}) collective-permute-start(bf16[128,768]{1,0:T(8,128)(2,1)S(1)} %get-tuple-element.288), channel_id=1, source_target_pairs={{0,0},{1,1},{2,2},{3,3},{4,4},{5,5},{6,6},{7,7},{8,16},{9,17},{10,... | collective-permute-start | bytes 589832 | tf_op jit(solution)/shard_map/ppermute | solution.py:1308
  439.0 5.0 %collective-permute-done.55 = bf16[128,768]{1,0:T(8,128)(2,1)S(1)} collective-permute-done((bf16[128,768]{1,0:T(8,128)(2,1)S(1)}, bf16[128,768]{1,0:T(8,128)(2,1)S(1)}, u32[]{:S(2)}, u32[]{:S(2)}) %collective-permute-start.55) | collective-permute-done | bytes 196640 | tf_op jit(solution)/shard_map/ppermute | solution.py:1308
  (369 shorter events, 139.7 us)
Async XLA Ops:
  4.8 22.9 %collective-permute-start = (bf16[336,768]{1,0:T(8,128)(2,1)}, bf16[336,768]{1,0:T(8,128)(2,1)S(1)}, u32[]{:S(2)}, u32[]{:S(2)}) collective-permute-start(bf16[336,768]{1,0:T(8,128)(2,1)} %get-tuple-element.97), channel_id=1, source_target_pairs={{0,0},{1,1},{2,2},{3,3},{4,4},{5,5},{6,6},{7,7},{8,16},{9,17},{10,... | collective-permute-start | bytes 1548296 | tf_op jit(solution)/shard_map/ppermute | solution.py:1308
  28.9 20.3 %collective-permute-start.5 = (bf16[336,768]{1,0:T(8,128)(2,1)S(1)}, bf16[336,768]{1,0:T(8,128)(2,1)S(1)}, u32[]{:S(2)}, u32[]{:S(2)}) collective-permute-start(bf16[336,768]{1,0:T(8,128)(2,1)S(1)} %collective-permute-done.4), channel_id=1, source_target_pairs={{0,1},{1,0},{2,3},{3,2},{4,5},{5,4},{6,7},{7,6},{8,9},{9,8},{10,11... | collective-permute-start | bytes 1548296 | tf_op jit(solution)/shard_map/ppermute | solution.py:1299
  29.4 25.3 %collective-permute-start.7 = (bf16[336,768]{1,0:T(8,128)(2,1)S(1)}, bf16[336,768]{1,0:T(8,128)(2,1)S(1)}, u32[]{:S(2)}, u32[]{:S(2)}) collective-permute-start(bf16[336,768]{1,0:T(8,128)(2,1)S(1)} %collective-permute-done.6), channel_id=1, source_target_pairs={{0,1},{1,0},{2,3},{3,2},{4,5},{5,4},{6,7},{7,6},{8,9},{9,8},{10,11... | collective-permute-start | bytes 1548296 | tf_op jit(solution)/shard_map/ppermute | solution.py:1299
  30.7 24.5 %collective-permute-start.2 = (bf16[336,768]{1,0:T(8,128)(2,1)S(1)}, bf16[336,768]{1,0:T(8,128)(2,1)S(1)}, u32[]{:S(2)}, u32[]{:S(2)}) collective-permute-start(bf16[336,768]{1,0:T(8,128)(2,1)S(1)} %collective-permute-done), channel_id=1, source_target_pairs={{0,2},{1,3},{2,0},{3,1},{4,6},{5,7},{6,4},{7,5},{8,10},{9,11},{10,... | collective-permute-start | bytes 1548296 | tf_op jit(solution)/shard_map/ppermute | solution.py:1299
  55.0 22.1 %collective-permute-start.9 = (bf16[4,336,768]{2,1,0:T(8,128)(2,1)S(1)}, bf16[4,336,768]{2,1,0:T(8,128)(2,1)}, u32[]{:S(2)}, u32[]{:S(2)}) collective-permute-start(bf16[4,336,768]{2,1,0:T(8,128)(2,1)S(1)} %pad_maximum_fusion.1.refs_2_), channel_id=1, source_target_pairs={{0,16},{16,0},{1,17},{17,1},{2,18},{18,2},{3,19},{19,3},{4,20},{20... | collective-permute-start | bytes 6193160 | tf_op jit(solution)/shard_map/ppermute | solution.py:1293
  57.0 20.1 %collective-permute-start.8 = (bf16[4,336,768]{2,1,0:T(8,128)(2,1)}, bf16[4,336,768]{2,1,0:T(8,128)(2,1)}, u32[]{:S(2)}, u32[]{:S(2)}) collective-permute-start(bf16[4,336,768]{2,1,0:T(8,128)(2,1)} %pad_maximum_fusion.refs_1_), channel_id=1, source_target_pairs={{0,16},{16,0},{1,17},{17,1},{2,18},{18,2},{3,19},{19,3},{4,20},{20... | collective-permute-start | bytes 6193160 | tf_op jit(solution)/shard_map/ppermute | solution.py:1293
  65.7 28.5 %collective-permute-start.13 = (bf16[448,768]{1,0:T(8,128)(2,1)}, bf16[448,768]{1,0:T(8,128)(2,1)}, u32[]{:S(2)}, u32[]{:S(2)}) collective-permute-start(bf16[448,768]{1,0:T(8,128)(2,1)} %pack_late.1), channel_id=1, source_target_pairs={{0,0},{1,1},{2,2},{3,3},{4,4},{5,5},{6,6},{7,7},{8,16},{9,17},{10,... | collective-permute-start | bytes 2064392 | tf_op jit(solution)/shard_map/ppermute | solution.py:1308
  69.5 33.2 %collective-permute-start.14 = (bf16[448,768]{1,0:T(8,128)(2,1)}, bf16[448,768]{1,0:T(8,128)(2,1)}, u32[]{:S(2)}, u32[]{:S(2)}) collective-permute-start(bf16[448,768]{1,0:T(8,128)(2,1)} %pack_late.1), channel_id=1, source_target_pairs={{0,4},{1,5},{2,6},{3,7},{4,0},{5,1},{6,2},{7,3},{8,20},{9,21},{10,... | collective-permute-start | bytes 2064392 | tf_op jit(solution)/shard_map/ppermute | solution.py:1308
  104.2 56.5 %collective-permute-start.17 = (bf16[2,448,768]{2,1,0:T(8,128)(2,1)S(1)}, bf16[2,448,768]{2,1,0:T(8,128)(2,1)}, u32[]{:S(2)}, u32[]{:S(2)}) collective-permute-start(bf16[2,448,768]{2,1,0:T(8,128)(2,1)S(1)} %hold.1.refs_11_.refs_8_), channel_id=1, source_target_pairs={{0,1},{1,0},{2,3},{3,2},{4,5},{5,4},{6,7},{7,6},{8,9},{9,8},{10,11... | collective-permute-start | bytes 4128776 | tf_op jit(solution)/shard_map/ppermute | solution.py:1299
  104.3 56.5 %collective-permute-start.18 = (bf16[2,448,768]{2,1,0:T(8,128)(2,1)S(1)}, bf16[2,448,768]{2,1,0:T(8,128)(2,1)}, u32[]{:S(2)}, u32[]{:S(2)}) collective-permute-start(bf16[2,448,768]{2,1,0:T(8,128)(2,1)S(1)} %hold.1.refs_11_.refs_8_), channel_id=1, source_target_pairs={{0,2},{1,3},{2,0},{3,1},{4,6},{5,7},{6,4},{7,5},{8,10},{9,11},{10,... | collective-permute-start | bytes 4128776 | tf_op jit(solution)/shard_map/ppermute | solution.py:1299
  105.7 55.0 %collective-permute-start.19 = (bf16[2,448,768]{2,1,0:T(8,128)(2,1)S(1)}, bf16[2,448,768]{2,1,0:T(8,128)(2,1)}, u32[]{:S(2)}, u32[]{:S(2)}) collective-permute-start(bf16[2,448,768]{2,1,0:T(8,128)(2,1)S(1)} %hold.1.refs_11_.refs_8_), channel_id=1, source_target_pairs={{0,3},{1,2},{2,1},{3,0},{4,7},{5,6},{6,5},{7,4},{8,11},{9,10},{10,... | collective-permute-start | bytes 4128776 | tf_op jit(solution)/shard_map/ppermute | solution.py:1299
  107.9 33.7 %collective-permute-start.15 = (bf16[2,128,768]{2,1,0:T(8,128)(2,1)}, bf16[2,128,768]{2,1,0:T(8,128)(2,1)}, u32[]{:S(2)}, u32[]{:S(2)}) collective-permute-start(bf16[2,128,768]{2,1,0:T(8,128)(2,1)} %get-tuple-element.278), channel_id=1, source_target_pairs={{0,0},{1,1},{2,2},{3,3},{4,4},{5,5},{6,6},{7,7},{8,16},{9,17},{10,... | collective-permute-start | bytes 1179656 | tf_op jit(solution)/shard_map/ppermute | solution.py:1308
  109.9 32.8 %collective-permute-start.16 = (bf16[2,128,768]{2,1,0:T(8,128)(2,1)}, bf16[2,128,768]{2,1,0:T(8,128)(2,1)}, u32[]{:S(2)}, u32[]{:S(2)}) collective-permute-start(bf16[2,128,768]{2,1,0:T(8,128)(2,1)} %get-tuple-element.277), channel_id=1, source_target_pairs={{0,4},{1,5},{2,6},{3,7},{4,0},{5,1},{6,2},{7,3},{8,20},{9,21},{10,... | collective-permute-start | bytes 1179656 | tf_op jit(solution)/shard_map/ppermute | solution.py:1308
  160.8 23.2 %collective-permute-start.23 = (bf16[2,448,768]{2,1,0:T(8,128)(2,1)S(1)}, bf16[2,448,768]{2,1,0:T(8,128)(2,1)S(1)}, u32[]{:S(2)}, u32[]{:S(2)}) collective-permute-start(bf16[2,448,768]{2,1,0:T(8,128)(2,1)S(1)} %copy-done.15), channel_id=1, source_target_pairs={{0,16},{16,0},{1,17},{17,1},{2,18},{18,2},{3,19},{19,3},{4,20},{20... | collective-permute-start | bytes 4128776 | tf_op jit(solution)/shard_map/ppermute | solution.py:1293
  160.8 23.1 %collective-permute-start.24 = (bf16[2,448,768]{2,1,0:T(8,128)(2,1)}, bf16[2,448,768]{2,1,0:T(8,128)(2,1)}, u32[]{:S(2)}, u32[]{:S(2)}) collective-permute-start(bf16[2,448,768]{2,1,0:T(8,128)(2,1)} %collective-permute-done.17.refs_11_.refs_9_), channel_id=1, source_target_pairs={{0,16},{16,0},{1,17},{17,1},{2,18},{18,2},{3,19},{19,3},{4,20},{20... | collective-permute-start | bytes 4128776 | tf_op jit(solution)/shard_map/ppermute | solution.py:1293
  161.3 22.6 %collective-permute-start.25 = (bf16[2,448,768]{2,1,0:T(8,128)(2,1)}, bf16[2,448,768]{2,1,0:T(8,128)(2,1)}, u32[]{:S(2)}, u32[]{:S(2)}) collective-permute-start(bf16[2,448,768]{2,1,0:T(8,128)(2,1)} %collective-permute-done.18.refs_12_.refs_10_), channel_id=1, source_target_pairs={{0,16},{16,0},{1,17},{17,1},{2,18},{18,2},{3,19},{19,3},{4,20},{20... | collective-permute-start | bytes 4128776 | tf_op jit(solution)/shard_map/ppermute | solution.py:1293
  161.4 22.6 %collective-permute-start.26 = (bf16[2,448,768]{2,1,0:T(8,128)(2,1)}, bf16[2,448,768]{2,1,0:T(8,128)(2,1)}, u32[]{:S(2)}, u32[]{:S(2)}) collective-permute-start(bf16[2,448,768]{2,1,0:T(8,128)(2,1)} %collective-permute-done.19.refs_13_.refs_11_), channel_id=1, source_target_pairs={{0,16},{16,0},{1,17},{17,1},{2,18},{18,2},{3,19},{19,3},{4,20},{20... | collective-permute-start | bytes 4128776 | tf_op jit(solution)/shard_map/ppermute | solution.py:1293
  217.8 54.5 %collective-permute-start.30 = (bf16[384,3840]{1,0:T(8,128)(2,1)}, bf16[384,3840]{1,0:T(8,128)(2,1)S(1)}, u32[]{:S(2)}, u32[]{:S(2)}) collective-permute-start(bf16[384,3840]{1,0:T(8,128)(2,1)} %get-tuple-element.137), channel_id=1, source_target_pairs={{0,16},{16,0},{1,17},{17,1},{2,18},{18,2},{3,19},{19,3},{4,20},{20... | collective-permute-start | bytes 8847368 | tf_op jit(solution)/shard_map/ppermute | solution.py:1293
  218.2 35.0 %collective-permute-start.31 = (bf16[1536,768]{1,0:T(8,128)(2,1)}, bf16[1536,768]{1,0:T(8,128)(2,1)}, u32[]{:S(2)}, u32[]{:S(2)}) collective-permute-start(bf16[1536,768]{1,0:T(8,128)(2,1)} %get-tuple-element.140), channel_id=1, source_target_pairs={{0,16},{16,0},{1,17},{17,1},{2,18},{18,2},{3,19},{19,3},{4,20},{20... | collective-permute-start | bytes 7077896 | tf_op jit(solution)/shard_map/ppermute | solution.py:1293
  220.7 32.4 %collective-permute-start.27 = (bf16[2,128,768]{2,1,0:T(8,128)(2,1)}, bf16[2,128,768]{2,1,0:T(8,128)(2,1)S(1)}, u32[]{:S(2)}, u32[]{:S(2)}) collective-permute-start(bf16[2,128,768]{2,1,0:T(8,128)(2,1)} %get-tuple-element.276), channel_id=1, source_target_pairs={{0,0},{1,1},{2,2},{3,3},{4,4},{5,5},{6,6},{7,7},{8,16},{9,17},{10,... | collective-permute-start | bytes 1179656 | tf_op jit(solution)/shard_map/ppermute | solution.py:1308
  228.6 24.5 %collective-permute-start.28 = (bf16[2,128,768]{2,1,0:T(8,128)(2,1)}, bf16[2,128,768]{2,1,0:T(8,128)(2,1)S(1)}, u32[]{:S(2)}, u32[]{:S(2)}) collective-permute-start(bf16[2,128,768]{2,1,0:T(8,128)(2,1)} %get-tuple-element.275), channel_id=1, source_target_pairs={{0,4},{1,5},{2,6},{3,7},{4,0},{5,1},{6,2},{7,3},{8,20},{9,21},{10,... | collective-permute-start | bytes 1179656 | tf_op jit(solution)/shard_map/ppermute | solution.py:1308
  259.5 20.7 %collective-permute-start.35 = (bf16[2,192,768]{2,1,0:T(8,128)(2,1)S(1)}, bf16[2,192,768]{2,1,0:T(8,128)(2,1)S(1)}, u32[]{:S(2)}, u32[]{:S(2)}) collective-permute-start(bf16[2,192,768]{2,1,0:T(8,128)(2,1)S(1)} %get-tuple-element.155), channel_id=1, source_target_pairs={{0,1},{1,0},{2,3},{3,2},{4,5},{5,4},{6,7},{7,6},{8,9},{9,8},{10,11... | collective-permute-start | bytes 1769480 | tf_op jit(solution)/shard_map/ppermute | solution.py:1299
  266.2 55.1 %collective-permute-start.36 = (bf16[2,192,768]{2,1,0:T(8,128)(2,1)}, bf16[2,192,768]{2,1,0:T(8,128)(2,1)}, u32[]{:S(2)}, u32[]{:S(2)}) collective-permute-start(bf16[2,192,768]{2,1,0:T(8,128)(2,1)} %get-tuple-element.156), channel_id=1, source_target_pairs={{0,2},{1,3},{2,0},{3,1},{4,6},{5,7},{6,4},{7,5},{8,10},{9,11},{10,... | collective-permute-start | bytes 1769480 | tf_op jit(solution)/shard_map/ppermute | solution.py:1299
  272.2 49.1 %collective-permute-start.37 = (bf16[2,192,768]{2,1,0:T(8,128)(2,1)}, bf16[2,192,768]{2,1,0:T(8,128)(2,1)}, u32[]{:S(2)}, u32[]{:S(2)}) collective-permute-start(bf16[2,192,768]{2,1,0:T(8,128)(2,1)} %get-tuple-element.157), channel_id=1, source_target_pairs={{0,3},{1,2},{2,1},{3,0},{4,7},{5,6},{6,5},{7,4},{8,11},{9,10},{10,... | collective-permute-start | bytes 1769480 | tf_op jit(solution)/shard_map/ppermute | solution.py:1299
  275.2 58.6 %collective-permute-start.40 = (bf16[2,48,3840]{2,1,0:T(8,128)(2,1)}, bf16[2,48,3840]{2,1,0:T(8,128)(2,1)S(1)}, u32[]{:S(2)}, u32[]{:S(2)}) collective-permute-start(bf16[2,48,3840]{2,1,0:T(8,128)(2,1)} %get-tuple-element.160), channel_id=1, source_target_pairs={{0,1},{1,0},{2,3},{3,2},{4,5},{5,4},{6,7},{7,6},{8,9},{9,8},{10,11... | collective-permute-start | bytes 2211848 | tf_op jit(solution)/shard_map/ppermute | solution.py:1299
  276.4 61.0 %collective-permute-start.41 = (bf16[2,48,3840]{2,1,0:T(8,128)(2,1)}, bf16[2,48,3840]{2,1,0:T(8,128)(2,1)}, u32[]{:S(2)}, u32[]{:S(2)}) collective-permute-start(bf16[2,48,3840]{2,1,0:T(8,128)(2,1)} %get-tuple-element.161), channel_id=1, source_target_pairs={{0,2},{1,3},{2,0},{3,1},{4,6},{5,7},{6,4},{7,5},{8,10},{9,11},{10,... | collective-permute-start | bytes 2211848 | tf_op jit(solution)/shard_map/ppermute | solution.py:1299
  281.0 57.8 %collective-permute-start.42 = (bf16[2,48,3840]{2,1,0:T(8,128)(2,1)}, bf16[2,48,3840]{2,1,0:T(8,128)(2,1)}, u32[]{:S(2)}, u32[]{:S(2)}) collective-permute-start(bf16[2,48,3840]{2,1,0:T(8,128)(2,1)} %get-tuple-element.162), channel_id=1, source_target_pairs={{0,3},{1,2},{2,1},{3,0},{4,7},{5,6},{6,5},{7,4},{8,11},{9,10},{10,... | collective-permute-start | bytes 2211848 | tf_op jit(solution)/shard_map/ppermute | solution.py:1299
  333.8 36.5 %collective-permute-start.32 = (bf16[4,48,1024]{2,1,0:T(8,128)(2,1)}, bf16[4,48,1024]{2,1,0:T(8,128)(2,1)}, u32[]{:S(2)}, u32[]{:S(2)}) collective-permute-start(bf16[4,48,1024]{2,1,0:T(8,128)(2,1)} %get-tuple-element.268), channel_id=1, source_target_pairs={{0,1},{1,0},{2,3},{3,2},{4,5},{5,4},{6,7},{7,6},{8,9},{9,8},{10,11... | collective-permute-start | bytes 1179656 | tf_op jit(solution)/shard_map/ppermute | solution.py:1299
  337.4 32.9 %collective-permute-start.33 = (bf16[4,48,1024]{2,1,0:T(8,128)(2,1)}, bf16[4,48,1024]{2,1,0:T(8,128)(2,1)}, u32[]{:S(2)}, u32[]{:S(2)}) collective-permute-start(bf16[4,48,1024]{2,1,0:T(8,128)(2,1)} %get-tuple-element.267), channel_id=1, source_target_pairs={{0,2},{1,3},{2,0},{3,1},{4,6},{5,7},{6,4},{7,5},{8,10},{9,11},{10,... | collective-permute-start | bytes 1179656 | tf_op jit(solution)/shard_map/ppermute | solution.py:1299
  338.8 31.5 %collective-permute-start.34 = (bf16[4,48,1024]{2,1,0:T(8,128)(2,1)}, bf16[4,48,1024]{2,1,0:T(8,128)(2,1)}, u32[]{:S(2)}, u32[]{:S(2)}) collective-permute-start(bf16[4,48,1024]{2,1,0:T(8,128)(2,1)} %get-tuple-element.266), channel_id=1, source_target_pairs={{0,3},{1,2},{2,1},{3,0},{4,7},{5,6},{6,5},{7,4},{8,11},{9,10},{10,... | collective-permute-start | bytes 1179656 | tf_op jit(solution)/shard_map/ppermute | solution.py:1299
  341.8 28.6 %collective-permute-start.43 = (bf16[48,3840]{1,0:T(8,128)(2,1)}, bf16[48,3840]{1,0:T(8,128)(2,1)S(1)}, u32[]{:S(2)}, u32[]{:S(2)}) collective-permute-start(bf16[48,3840]{1,0:T(8,128)(2,1)} %get-tuple-element.163), channel_id=1, source_target_pairs={{0,0},{1,1},{2,2},{3,3},{4,4},{5,5},{6,6},{7,7},{8,16},{9,17},{10,... | collective-permute-start | bytes 1105928 | tf_op jit(solution)/shard_map/ppermute | solution.py:1308
  345.2 25.2 %collective-permute-start.44 = (bf16[48,3840]{1,0:T(8,128)(2,1)}, bf16[48,3840]{1,0:T(8,128)(2,1)S(1)}, u32[]{:S(2)}, u32[]{:S(2)}) collective-permute-start(bf16[48,3840]{1,0:T(8,128)(2,1)} %get-tuple-element.164), channel_id=1, source_target_pairs={{0,4},{1,5},{2,6},{3,7},{4,0},{5,1},{6,2},{7,3},{8,20},{9,21},{10,... | collective-permute-start | bytes 1105928 | tf_op jit(solution)/shard_map/ppermute | solution.py:1308
  (113 other events, 927.4 us)
